TPU v7x, 32 devices: a whole 2x2x4 slice. The times are simulated.
32 devices in a mesh: section: 4 (over y, x), dp: 8 (over z, core).
Axes of the slice: x: 2, y: 2, z: 4, core: 2. Of those that a mesh axis runs over, the one named last changes fastest.
Arguments:
- tokens: bfloat16 [8, 1024, 1024], P('dp'), may hold values from -6 to 6
- lengths: int32 [8], P('dp'), may hold values from 128 to 1024
- cotangent: bfloat16 [8, 1024, 1024], P('dp'), may hold values from -6 to 6
- norm_gain: float32 [2, 1024], P(None, 'dp'), may hold values from 0.5 to 1.5
- norm_shift: float32 [2, 1024], P(None, 'dp'), may hold values from -2 to 2
- average_decay: float32 [2, 16, 1024], P(None, None, 'dp'), may hold values from 2.5 to 7
- average_input: float32 [2, 16, 1024], P(None, None, 'dp'), may hold values from -4 to 4
- average_output: float32 [2, 16, 1024], P(None, None, 'dp'), may hold values from -1.5 to 1.5
- average_skip: float32 [2, 1024], P(None, 'dp'), may hold values from 0.5 to 1.5
- value_weight: bfloat16 [2, 1024, 2048], P(None, 'dp'), may hold values from -0.1875 to 0.1875
- value_bias: float32 [2, 2048], P(None, 'dp'), may hold values from -2 to 2
- base_weight: bfloat16 [2, 1024, 4224], P(None, 'dp'), may hold values from -0.1875 to 0.1875
- base_bias: float32 [2, 4224], P(None, 'dp'), may hold values from -2 to 2
- pair_scale: float32 [2, 2, 128], P(None, None, 'dp'), may hold values from -5 to 5
- query_shift: float32 [2, 128], P(None, 'dp'), may hold values from -3 to 3
- out_weight: bfloat16 [2, 2048, 1024], P(None, 'dp'), may hold values from -0.375 to 0.375
- feed_gain: float32 [2, 1024], P(None, 'dp'), may hold values from 0.5 to 1.5
- feed_shift: float32 [2, 1024], P(None, 'dp'), may hold values from -2 to 2
- feed_in_weight: bfloat16 [2, 1024, 4096], P(None, 'dp'), may hold values from -0.1875 to 0.1875
- feed_in_bias: float32 [2, 4096], P(None, 'dp'), may hold values from -2 to 2
- feed_out_weight: bfloat16 [2, 4096, 1024], P(None, 'dp'), may hold values from -0.09375 to 0.09375
- feed_out_bias: float32 [2, 1024], P(None, 'dp'), may hold values from -2 to 2
Outputs:
- block_out: bfloat16 [8, 1024, 1024], P('dp', 'section')
- input_grad: bfloat16 [8, 1024, 1024], P('dp', 'section')
- grad_norm_gain: float32 [2, 1024], P(None, 'dp')
- grad_norm_shift: float32 [2, 1024], P(None, 'dp')
- grad_average_decay: float32 [2, 16, 1024], P(None, None, 'dp')
- grad_average_input: float32 [2, 16, 1024], P(None, None, 'dp')
- grad_average_output: float32 [2, 16, 1024], P(None, None, 'dp')
- grad_average_skip: float32 [2, 1024], P(None, 'dp')
- grad_value_weight: float32 [2, 1024, 2048], P(None, 'dp')
- grad_value_bias: float32 [2, 2048], P(None, 'dp')
- grad_base_weight: float32 [2, 1024, 4224], P(None, 'dp')
- grad_base_bias: float32 [2, 4224], P(None, 'dp')
- grad_pair_scale: float32 [2, 2, 128], P(None, None, 'dp')
- grad_query_shift: float32 [2, 128], P(None, 'dp')
- grad_out_weight: float32 [2, 2048, 1024], P(None, 'dp')
- grad_feed_gain: float32 [2, 1024], P(None, 'dp')
- grad_feed_shift: float32 [2, 1024], P(None, 'dp')
- grad_feed_in_weight: float32 [2, 1024, 4096], P(None, 'dp')
- grad_feed_in_bias: float32 [2, 4096], P(None, 'dp')
- grad_feed_out_weight: float32 [2, 4096, 1024], P(None, 'dp')
- grad_feed_out_bias: float32 [2, 1024], P(None, 'dp')
Inputs may be any that keep to these rules, and one draw needn't show every extreme that they name: Slot s holds real tokens at positions 0 to lengths[s] - 1; later positions are padding.
All inputs are finite; a program needn't handle non-finite values.
Results may differ from a plain program's by a relative error of at most 0.04.
Values may be sent and summed in bfloat16 or wider, within the bound.
A program may use at most 448 MiB of HBM per device.

v0:
```python
import jax
import jax.numpy as jnp
from jax import lax
from jax.sharding import PartitionSpec as P

EMA = 16
ATT_BLOCK = 128
EMA_BLOCK = 64
MICRO = 8


eps = 1e-05
big_negative = -1000000000.0


def shifted_2(value, axis, steps):
    count = lax.axis_size(axis)
    initial, last = (max(0, -steps), min(count, count - steps))
    return lax.ppermute(value, axis, [(source, source + steps) for source in range(initial, last)])


def product(left, right):

    def plain(left_in, right_in):
        return jnp.dot(
            left_in.astype(jnp.bfloat16),
            right_in.astype(jnp.bfloat16),
            preferred_element_type=jnp.float32,
        )

    def product_keep(left_in, right_in):
        return (
            plain(left_in, right_in),
            (left_in.astype(jnp.bfloat16), right_in.astype(jnp.bfloat16)),
        )

    def product_back(kept, grad):
        left_low, right_low = kept
        rounded = grad.astype(jnp.bfloat16)
        grad_left = lax.dot_general(
            rounded, right_low, (((1,), (1,)), ((), ())), preferred_element_type=jnp.float32
        )
        grad_right = lax.dot_general(
            left_low, rounded, (((0,), (0,)), ((), ())), preferred_element_type=jnp.float32
        )
        return (grad_left, grad_right)

    wrapped = jax.custom_vjp(plain)
    wrapped.defvjp(product_keep, product_back)
    return wrapped(left, right)


def batched(left, right):
    return jax.vmap(product)(left, right)


def layer_norm(rows, gain, shift):
    centre = jnp.mean(rows, axis=-1, keepdims=True)
    centered = rows - centre
    spread = jnp.mean(centered * centered, axis=-1, keepdims=True)
    return centered * lax.rsqrt(spread + eps) * gain + shift


def softmax_rows(scores):
    shifted = scores - jnp.max(scores, axis=-1, keepdims=True)
    raised = jnp.exp(shifted)
    return raised / jnp.sum(raised, axis=-1, keepdims=True)


def moving_average(rows, state, decay, weight_in, weight_out):
    length, width = rows.shape
    block = EMA_BLOCK
    log_rate = -jnp.log1p(jnp.exp(-decay))
    drive = (1.0 - jnp.exp(log_rate)) * weight_in
    steps = jnp.arange(block).astype(jnp.float32)
    powers = jnp.exp(steps[:, None, None] * log_rate[None])
    kernel = jnp.sum(powers * (drive * weight_out)[None], axis=1)
    lag = jnp.arange(block, dtype=jnp.int32)[:, None] - jnp.arange(block, dtype=jnp.int32)[None, :]
    toeplitz = jnp.where((lag >= 0)[:, :, None], kernel[jnp.clip(lag, 0, block - 1)], 0.0)
    pieces = rows.reshape(length // block, block, width)
    inner = jnp.einsum("tsd,nsd->ntd", toeplitz, pieces, precision=lax.Precision.HIGHEST)
    tail = jnp.exp((block - 1.0 - steps)[:, None, None] * log_rate[None]) * drive[None]
    entering = jnp.einsum("sed,nsd->ned", tail, pieces, precision=lax.Precision.HIGHEST)
    full = jnp.exp(block * log_rate)

    def advance(carry, piece):
        return (full * carry + piece, carry)

    last, before = lax.scan(advance, state, entering)
    lead = jnp.exp((steps + 1.0)[:, None, None] * log_rate[None]) * weight_out[None]
    outer = jnp.einsum("ted,ned->ntd", lead, before, precision=lax.Precision.HIGHEST)
    return ((inner + outer).reshape(length, width), last)


def attention_layer(rows, valid, state, weights):
    (
        gain,
        shift,
        decay,
        weight_in,
        weight_out,
        skip,
        value_matrix,
        value_offset,
        base_matrix,
        base_offset,
        scale_pair,
        query_offset,
        out_matrix,
    ) = weights
    length, width = rows.shape
    key_width = scale_pair.shape[-1]
    value_width = value_matrix.shape[-1]
    normed = layer_norm(rows, gain, shift)
    masked = normed * valid[:, None]
    smooth, state_out = moving_average(masked, state, decay, weight_in, weight_out)
    mixed = jax.nn.silu(smooth + skip * masked)
    values = jax.nn.silu(product(normed, value_matrix) + value_offset)
    base = product(mixed, base_matrix) + base_offset
    update = jax.nn.sigmoid(base[:, :width])
    shared = jax.nn.silu(base[:, width : width + key_width])
    reset = jax.nn.silu(base[:, width + key_width : width + key_width + value_width])
    candidate = base[:, width + key_width + value_width :]
    queries = shared * scale_pair[0] + query_offset
    keys = shared * scale_pair[1]
    blocks = length // ATT_BLOCK
    scores = batched(
        queries.reshape(blocks, ATT_BLOCK, key_width),
        keys.reshape(blocks, ATT_BLOCK, key_width).transpose(0, 2, 1),
    ) * key_width ** (-0.5)
    allowed = valid.reshape(blocks, 1, ATT_BLOCK) > 0.5
    probs = softmax_rows(jnp.where(allowed, scores, big_negative))
    attended = (
        batched(probs, values.reshape(blocks, ATT_BLOCK, value_width)).reshape(length, value_width)
        * valid[:, None]
    )
    hidden = jax.nn.silu(candidate + product(attended * reset, out_matrix))
    return (rows + update * (hidden - rows), state_out)


def feed_forward(rows, weights):
    gain, shift, in_matrix, in_offset, out_matrix, out_offset = weights
    normed = layer_norm(rows, gain, shift)
    active = jax.nn.silu(product(normed, in_matrix) + in_offset)
    return rows + product(active, out_matrix) + out_offset


def pick(stack, layer):
    return lax.dynamic_index_in_dim(stack, layer, 0, keepdims=False)


def store(buffer, index, value, flag):
    former = lax.dynamic_index_in_dim(buffer, index, 0, keepdims=False)
    return lax.dynamic_update_index_in_dim(buffer, jnp.where(flag, value, former), index, 0)


def place(part, stack, layer):
    holder = jnp.zeros(stack.shape, jnp.float32)
    return lax.dynamic_update_index_in_dim(holder, part, layer, 0)


def body(
    tokens,
    lengths,
    cotangent,
    norm_gain,
    norm_shift,
    average_decay,
    average_input,
    average_output,
    average_skip,
    value_weight,
    value_bias,
    base_weight,
    base_bias,
    pair_scale,
    query_shift,
    out_weight,
    feed_gain,
    feed_shift,
    feed_in_weight,
    feed_in_bias,
    feed_out_weight,
    feed_out_bias,
):
    sections = lax.axis_size("section")
    section_id = lax.axis_index("section")
    layer = section_id // 2
    attending = section_id % 2 == 0
    slots, slot_len, width = tokens.shape
    part_len = slot_len // MICRO
    count = slots * MICRO
    attention_stacks = (
        norm_gain,
        norm_shift,
        average_decay,
        average_input,
        average_output,
        average_skip,
        value_weight,
        value_bias,
        base_weight,
        base_bias,
        pair_scale,
        query_shift,
        out_weight,
    )
    feed_stacks = (
        feed_gain,
        feed_shift,
        feed_in_weight,
        feed_in_bias,
        feed_out_weight,
        feed_out_bias,
    )
    shards = tuple((pick(stack, layer) for stack in attention_stacks))
    feed_shards = tuple((pick(stack, layer) for stack in feed_stacks))

    def fetch():
        mats = (
            lax.all_gather(shards[6], "dp", axis=0, tiled=True),
            lax.all_gather(shards[8], "dp", axis=0, tiled=True),
            lax.all_gather(shards[12], "dp", axis=0, tiled=True),
        )
        vecs = (
            lax.all_gather(shards[0], "dp", axis=0, tiled=True),
            lax.all_gather(shards[1], "dp", axis=0, tiled=True),
            lax.all_gather(shards[2], "dp", axis=1, tiled=True),
            lax.all_gather(shards[3], "dp", axis=1, tiled=True),
            lax.all_gather(shards[4], "dp", axis=1, tiled=True),
            lax.all_gather(shards[5], "dp", axis=0, tiled=True),
            lax.all_gather(shards[7], "dp", axis=0, tiled=True),
            lax.all_gather(shards[9], "dp", axis=0, tiled=True),
            lax.all_gather(shards[10], "dp", axis=1, tiled=True),
            lax.all_gather(shards[11], "dp", axis=0, tiled=True),
        )
        whole = (
            vecs[0],
            vecs[1],
            vecs[2],
            vecs[3],
            vecs[4],
            vecs[5],
            mats[0],
            vecs[6],
            mats[1],
            vecs[7],
            vecs[8],
            vecs[9],
            mats[2],
        )
        feed_mats = (
            lax.all_gather(feed_shards[2], "dp", axis=0, tiled=True),
            lax.all_gather(feed_shards[4], "dp", axis=0, tiled=True),
        )
        feed_vecs = (
            lax.all_gather(feed_shards[0], "dp", axis=0, tiled=True),
            lax.all_gather(feed_shards[1], "dp", axis=0, tiled=True),
            lax.all_gather(feed_shards[3], "dp", axis=0, tiled=True),
            lax.all_gather(feed_shards[5], "dp", axis=0, tiled=True),
        )
        return (
            whole,
            (feed_vecs[0], feed_vecs[1], feed_mats[0], feed_vecs[2], feed_mats[1], feed_vecs[3]),
        )

    positions = jnp.arange(slot_len, dtype=jnp.int32)
    valid_all = (positions[None, :] < lengths[:, None]).astype(jnp.float32).reshape(count, part_len)
    token_parts = tokens.reshape(count, part_len, width)
    grad_parts = cotangent.reshape(count, part_len, width)
    blank_state = jnp.zeros((EMA, width), jnp.float32)
    attention_full, feed_full = fetch()

    def run_forward(which, rows, valid, begin):

        def resting(rows, valid, begin):
            return (jnp.zeros_like(rows), begin)

        def attend(rows, valid, begin):
            return attention_layer(rows, valid, begin, attention_full)

        def feed(rows, valid, begin):
            return (feed_forward(rows, feed_full), begin)

        return lax.switch(which, (resting, attend, feed), rows, valid, begin)

    def forward_tick(tick, carry):
        sent, kept, starts, results, running = carry
        arriving = shifted_2(sent, "section", 1)
        item = tick - section_id
        live = (item >= 0) & (item < count)
        index = jnp.clip(item, 0, count - 1)
        own = lax.dynamic_index_in_dim(token_parts, index, 0, keepdims=False)
        rows = jnp.where(section_id == 0, own, arriving)
        valid = lax.dynamic_index_in_dim(valid_all, index, 0, keepdims=False)
        begin = jnp.where(index % MICRO == 0, blank_state, running)
        which = jnp.where(live, jnp.where(attending, 1, 2), 0)
        made, after = run_forward(which, rows.astype(jnp.float32), valid, begin)
        made = made.astype(jnp.bfloat16)
        kept = store(kept, index, rows, live)
        starts = store(starts, index, begin, live)
        results = store(results, index, made, live & (section_id == sections - 1))
        running = jnp.where(live, after, running)
        return (made, kept, starts, results, running)

    initial = (
        jnp.zeros((part_len, width), jnp.bfloat16),
        jnp.zeros((count, part_len, width), jnp.bfloat16),
        jnp.zeros((count, EMA, width), jnp.float32),
        jnp.zeros((count, part_len, width), jnp.bfloat16),
        blank_state,
    )
    _, kept, starts, results, _ = lax.fori_loop(0, count + sections - 1, forward_tick, initial)
    final_rows = results.reshape(slots, slot_len, width).astype(jnp.float32)
    block_out = lax.psum_scatter(
        final_rows.astype(jnp.bfloat16), "section", scatter_dimension=1, tiled=True
    )
    back_attention, back_feed = fetch()

    def run_backward(which, rows, valid, begin, incoming, state_grad, sums):

        def resting(rows, valid, begin, incoming, state_grad, sums):
            return (jnp.zeros_like(rows), jnp.zeros_like(begin), sums)

        def attend(rows, valid, begin, incoming, state_grad, sums):
            weights = tuple((matrix.astype(jnp.float32) for matrix in back_attention))

            def attend_local(local_rows, local_begin, local_weights):
                return attention_layer(local_rows, valid, local_begin, local_weights)

            _, pull = jax.vjp(attend_local, rows, begin, weights)
            grad_rows, grad_begin, grad_weights = pull((incoming, state_grad))
            return (grad_rows, grad_begin, (jax.tree.map(jnp.add, sums[0], grad_weights), sums[1]))

        def feed(rows, valid, begin, incoming, state_grad, sums):
            weights = tuple((matrix.astype(jnp.float32) for matrix in back_feed))

            def feed_local(local_rows, local_weights):
                return feed_forward(local_rows, local_weights)

            _, pull = jax.vjp(feed_local, rows, weights)
            grad_rows, grad_weights = pull(incoming)
            return (
                grad_rows,
                jnp.zeros_like(begin),
                (sums[0], jax.tree.map(jnp.add, sums[1], grad_weights)),
            )

        return lax.switch(
            which, (resting, attend, feed), rows, valid, begin, incoming, state_grad, sums
        )

    def backward_tick(tick, carry):
        sent, back_state, sums, input_rows = carry
        arriving = shifted_2(sent, "section", -1)
        item = count - 1 - tick + (sections - 1 - section_id)
        live = (item >= 0) & (item < count)
        index = jnp.clip(item, 0, count - 1)
        own = lax.dynamic_index_in_dim(grad_parts, index, 0, keepdims=False)
        incoming = jnp.where(section_id == sections - 1, own, arriving).astype(jnp.float32)
        rows = lax.dynamic_index_in_dim(kept, index, 0, keepdims=False).astype(jnp.float32)
        valid = lax.dynamic_index_in_dim(valid_all, index, 0, keepdims=False)
        begin = lax.dynamic_index_in_dim(starts, index, 0, keepdims=False)
        state_grad = jnp.where(index % MICRO == MICRO - 1, blank_state, back_state)
        which = jnp.where(live, jnp.where(attending, 1, 2), 0)
        grad_rows, grad_begin, sums = run_backward(
            which, rows, valid, begin, incoming, state_grad, sums
        )
        going = grad_rows.astype(jnp.bfloat16)
        input_rows = store(input_rows, index, going, live & (section_id == 0))
        back_state = jnp.where(live, grad_begin, back_state)
        return (going, back_state, sums, input_rows)

    zero_sums = (
        tuple((jnp.zeros(whole.shape, jnp.float32) for whole in attention_full)),
        tuple((jnp.zeros(whole.shape, jnp.float32) for whole in feed_full)),
    )
    start_back = (
        jnp.zeros((part_len, width), jnp.bfloat16),
        blank_state,
        zero_sums,
        jnp.zeros((count, part_len, width), jnp.bfloat16),
    )
    _, _, sums, input_rows = lax.fori_loop(0, count + sections - 1, backward_tick, start_back)
    first_rows = input_rows.reshape(slots, slot_len, width).astype(jnp.float32)
    input_grad = lax.psum_scatter(
        first_rows.astype(jnp.bfloat16), "section", scatter_dimension=1, tiled=True
    )
    attention_sums, feed_sums = sums
    attention_parts = (
        lax.psum_scatter(
            attention_sums[0].astype(jnp.bfloat16), "dp", scatter_dimension=0, tiled=True
        ).astype(jnp.float32),
        lax.psum_scatter(
            attention_sums[1].astype(jnp.bfloat16), "dp", scatter_dimension=0, tiled=True
        ).astype(jnp.float32),
        lax.psum_scatter(
            attention_sums[2].astype(jnp.bfloat16), "dp", scatter_dimension=1, tiled=True
        ).astype(jnp.float32),
        lax.psum_scatter(
            attention_sums[3].astype(jnp.bfloat16), "dp", scatter_dimension=1, tiled=True
        ).astype(jnp.float32),
        lax.psum_scatter(
            attention_sums[4].astype(jnp.bfloat16), "dp", scatter_dimension=1, tiled=True
        ).astype(jnp.float32),
        lax.psum_scatter(
            attention_sums[5].astype(jnp.bfloat16), "dp", scatter_dimension=0, tiled=True
        ).astype(jnp.float32),
        lax.psum_scatter(
            attention_sums[6].astype(jnp.bfloat16), "dp", scatter_dimension=0, tiled=True
        ).astype(jnp.float32),
        lax.psum_scatter(
            attention_sums[7].astype(jnp.bfloat16), "dp", scatter_dimension=0, tiled=True
        ).astype(jnp.float32),
        lax.psum_scatter(
            attention_sums[8].astype(jnp.bfloat16), "dp", scatter_dimension=0, tiled=True
        ).astype(jnp.float32),
        lax.psum_scatter(
            attention_sums[9].astype(jnp.bfloat16), "dp", scatter_dimension=0, tiled=True
        ).astype(jnp.float32),
        lax.psum_scatter(
            attention_sums[10].astype(jnp.bfloat16), "dp", scatter_dimension=1, tiled=True
        ).astype(jnp.float32),
        lax.psum_scatter(
            attention_sums[11].astype(jnp.bfloat16), "dp", scatter_dimension=0, tiled=True
        ).astype(jnp.float32),
        lax.psum_scatter(
            attention_sums[12].astype(jnp.bfloat16), "dp", scatter_dimension=0, tiled=True
        ).astype(jnp.float32),
    )
    feed_parts = (
        lax.psum_scatter(
            feed_sums[0].astype(jnp.bfloat16), "dp", scatter_dimension=0, tiled=True
        ).astype(jnp.float32),
        lax.psum_scatter(
            feed_sums[1].astype(jnp.bfloat16), "dp", scatter_dimension=0, tiled=True
        ).astype(jnp.float32),
        lax.psum_scatter(
            feed_sums[2].astype(jnp.bfloat16), "dp", scatter_dimension=0, tiled=True
        ).astype(jnp.float32),
        lax.psum_scatter(
            feed_sums[3].astype(jnp.bfloat16), "dp", scatter_dimension=0, tiled=True
        ).astype(jnp.float32),
        lax.psum_scatter(
            feed_sums[4].astype(jnp.bfloat16), "dp", scatter_dimension=0, tiled=True
        ).astype(jnp.float32),
        lax.psum_scatter(
            feed_sums[5].astype(jnp.bfloat16), "dp", scatter_dimension=0, tiled=True
        ).astype(jnp.float32),
    )
    placed = tuple(
        (place(part, stack, layer) for part, stack in zip(attention_parts, attention_stacks))
    )
    feed_placed = tuple((place(part, stack, layer) for part, stack in zip(feed_parts, feed_stacks)))
    totals = (
        lax.psum(placed[0].astype(jnp.bfloat16), "section").astype(jnp.float32),
        lax.psum(placed[1].astype(jnp.bfloat16), "section").astype(jnp.float32),
        lax.psum(placed[2].astype(jnp.bfloat16), "section").astype(jnp.float32),
        lax.psum(placed[3].astype(jnp.bfloat16), "section").astype(jnp.float32),
        lax.psum(placed[4].astype(jnp.bfloat16), "section").astype(jnp.float32),
        lax.psum(placed[5].astype(jnp.bfloat16), "section").astype(jnp.float32),
        lax.psum(placed[6].astype(jnp.bfloat16), "section").astype(jnp.float32),
        lax.psum(placed[7].astype(jnp.bfloat16), "section").astype(jnp.float32),
        lax.psum(placed[8].astype(jnp.bfloat16), "section").astype(jnp.float32),
        lax.psum(placed[9].astype(jnp.bfloat16), "section").astype(jnp.float32),
        lax.psum(placed[10].astype(jnp.bfloat16), "section").astype(jnp.float32),
        lax.psum(placed[11].astype(jnp.bfloat16), "section").astype(jnp.float32),
        lax.psum(placed[12].astype(jnp.bfloat16), "section").astype(jnp.float32),
        lax.psum(feed_placed[0].astype(jnp.bfloat16), "section").astype(jnp.float32),
        lax.psum(feed_placed[1].astype(jnp.bfloat16), "section").astype(jnp.float32),
        lax.psum(feed_placed[2].astype(jnp.bfloat16), "section").astype(jnp.float32),
        lax.psum(feed_placed[3].astype(jnp.bfloat16), "section").astype(jnp.float32),
        lax.psum(feed_placed[4].astype(jnp.bfloat16), "section").astype(jnp.float32),
        lax.psum(feed_placed[5].astype(jnp.bfloat16), "section").astype(jnp.float32),
    )
    return (
        block_out,
        input_grad,
        totals[0],
        totals[1],
        totals[2],
        totals[3],
        totals[4],
        totals[5],
        totals[6],
        totals[7],
        totals[8],
        totals[9],
        totals[10],
        totals[11],
        totals[12],
        totals[13],
        totals[14],
        totals[15],
        totals[16],
        totals[17],
        totals[18],
    )


def solution(mesh):
    in_specs = (
        P("dp", None, None),
        P("dp"),
        P("dp", None, None),
        P(None, "dp"),
        P(None, "dp"),
        P(None, None, "dp"),
        P(None, None, "dp"),
        P(None, None, "dp"),
        P(None, "dp"),
        P(None, "dp", None),
        P(None, "dp"),
        P(None, "dp", None),
        P(None, "dp"),
        P(None, None, "dp"),
        P(None, "dp"),
        P(None, "dp", None),
        P(None, "dp"),
        P(None, "dp"),
        P(None, "dp", None),
        P(None, "dp"),
        P(None, "dp", None),
        P(None, "dp"),
    )
    out_specs = (
        P("dp", "section", None),
        P("dp", "section", None),
        P(None, "dp"),
        P(None, "dp"),
        P(None, None, "dp"),
        P(None, None, "dp"),
        P(None, None, "dp"),
        P(None, "dp"),
        P(None, "dp", None),
        P(None, "dp"),
        P(None, "dp", None),
        P(None, "dp"),
        P(None, None, "dp"),
        P(None, "dp"),
        P(None, "dp", None),
        P(None, "dp"),
        P(None, "dp"),
        P(None, "dp", None),
        P(None, "dp"),
        P(None, "dp", None),
        P(None, "dp"),
    )
    return jax.shard_map(body, mesh=mesh, in_specs=in_specs, out_specs=out_specs, check_vma=False)
```

profile of v0, /device:TPU:0, one launch (start us, length us, event | category | flops | bytes accessed | tf_op | source)
XLA Modules:
  0.0 7443.9 jit_solution(7431609170174911591)
XLA Ops:
  206.5 77.7 %all-gather.33.cloned.1.call-done = bf16[1,4096,1024]{2,1,0:T(8,128)(2,1)} async-done(((bf16[1,512,1024]{2,1,0:T(8,128)(2,1)}), bf16[1,4096,1024]{2,1,0:T(8,128)(2,1)}) %all-gather.33.cloned.1.call-update) | async-done | bytes 8388624 | tf_op jit(solution)/shard_map/all_gather | solution.py:254
  284.3 84.9 %all-gather.25.cloned.1.call-done = bf16[1,1024,4224]{2,1,0:T(8,128)(2,1)} async-done(((bf16[1,128,4224]{2,1,0:T(8,128)(2,1)}), bf16[1,1024,4224]{2,1,0:T(8,128)(2,1)}) %all-gather.25.cloned.1.call-update) | async-done | bytes 8650768 | tf_op jit(solution)/shard_map/all_gather | solution.py:222
  373.9 1583.8 %while.141 = (s32[]{:T(128)}, bf16[128,1024]{1,0:T(8,128)(2,1)}, bf16[8,128,1024]{2,1,0:T(8,128)(2,1)}, f32[8,16,1024]{2,1,0:T(8,128)}, bf16[8,128,1024]{2,1,0:T...) while((s32[]{:T(128)}, bf16[128,1024]{1,0:T(8,128)(2,1)}, ...), condition=%wide.region_13.14_spmd.clone, body=%wide.region_0.13_spmd.clone.sunk | while | flops 2425114880 | bytes 136901392 | solution.py:313
  401.2 175.8 %conditional.6 = (f32[16,1024]{1,0:T(8,128)S(1)}, bf16[128,1024]{1,0:T(8,128)(2,1)}) conditional(s32[]{:T(128)} %clamp.47, f32[16,1024]{1,0:T(8,128)S(1)} %get-tuple-element.4003, (f32[128,1024]{1,0:T(8,128)S(1)}, f32[1024]{0:T(1024)S(1)}, f32[1024]{0:T(1024)S(1)}, f32[8,128]{1,0:T(8,128)S(1)}, s32[]{:T(128)}, ...), branch_computations={%region_1.1_spmd, %region_2.9_spmd, %region_10.12_spmd} | conditional | flops 2424373504 | bytes 131324456 | solution.py:285
  492.2 55.8 fusion.28
  587.6 175.8 %conditional.6 = (f32[16,1024]{1,0:T(8,128)S(1)}, bf16[128,1024]{1,0:T(8,128)(2,1)}) conditional(s32[]{:T(128)} %clamp.47, f32[16,1024]{1,0:T(8,128)S(1)} %get-tuple-element.4003, (f32[128,1024]{1,0:T(8,128)S(1)}, f32[1024]{0:T(1024)S(1)}, f32[1024]{0:T(1024)S(1)}, f32[8,128]{1,0:T(8,128)S(1)}, s32[]{:T(128)}, ...), branch_computations={%region_1.1_spmd, %region_2.9_spmd, %region_10.12_spmd} | conditional | flops 2424373504 | bytes 131324456 | solution.py:285
  678.7 55.8 fusion.28
  774.9 175.8 %conditional.6 = (f32[16,1024]{1,0:T(8,128)S(1)}, bf16[128,1024]{1,0:T(8,128)(2,1)}) conditional(s32[]{:T(128)} %clamp.47, f32[16,1024]{1,0:T(8,128)S(1)} %get-tuple-element.4003, (f32[128,1024]{1,0:T(8,128)S(1)}, f32[1024]{0:T(1024)S(1)}, f32[1024]{0:T(1024)S(1)}, f32[8,128]{1,0:T(8,128)S(1)}, s32[]{:T(128)}, ...), branch_computations={%region_1.1_spmd, %region_2.9_spmd, %region_10.12_spmd} | conditional | flops 2424373504 | bytes 131324456 | solution.py:285
  866.0 55.8 fusion.28
  962.2 175.8 %conditional.6 = (f32[16,1024]{1,0:T(8,128)S(1)}, bf16[128,1024]{1,0:T(8,128)(2,1)}) conditional(s32[]{:T(128)} %clamp.47, f32[16,1024]{1,0:T(8,128)S(1)} %get-tuple-element.4003, (f32[128,1024]{1,0:T(8,128)S(1)}, f32[1024]{0:T(1024)S(1)}, f32[1024]{0:T(1024)S(1)}, f32[8,128]{1,0:T(8,128)S(1)}, s32[]{:T(128)}, ...), branch_computations={%region_1.1_spmd, %region_2.9_spmd, %region_10.12_spmd} | conditional | flops 2424373504 | bytes 131324456 | solution.py:285
  1149.5 175.8 %conditional.6 = (f32[16,1024]{1,0:T(8,128)S(1)}, bf16[128,1024]{1,0:T(8,128)(2,1)}) conditional(s32[]{:T(128)} %clamp.47, f32[16,1024]{1,0:T(8,128)S(1)} %get-tuple-element.4003, (f32[128,1024]{1,0:T(8,128)S(1)}, f32[1024]{0:T(1024)S(1)}, f32[1024]{0:T(1024)S(1)}, f32[8,128]{1,0:T(8,128)S(1)}, s32[]{:T(128)}, ...), branch_computations={%region_1.1_spmd, %region_2.9_spmd, %region_10.12_spmd} | conditional | flops 2424373504 | bytes 131324456 | solution.py:285
  1240.6 55.8 fusion.28
  1336.8 175.8 %conditional.6 = (f32[16,1024]{1,0:T(8,128)S(1)}, bf16[128,1024]{1,0:T(8,128)(2,1)}) conditional(s32[]{:T(128)} %clamp.47, f32[16,1024]{1,0:T(8,128)S(1)} %get-tuple-element.4003, (f32[128,1024]{1,0:T(8,128)S(1)}, f32[1024]{0:T(1024)S(1)}, f32[1024]{0:T(1024)S(1)}, f32[8,128]{1,0:T(8,128)S(1)}, s32[]{:T(128)}, ...), branch_computations={%region_1.1_spmd, %region_2.9_spmd, %region_10.12_spmd} | conditional | flops 2424373504 | bytes 131324456 | solution.py:285
  1427.8 55.8 fusion.28
  1524.0 175.8 %conditional.6 = (f32[16,1024]{1,0:T(8,128)S(1)}, bf16[128,1024]{1,0:T(8,128)(2,1)}) conditional(s32[]{:T(128)} %clamp.47, f32[16,1024]{1,0:T(8,128)S(1)} %get-tuple-element.4003, (f32[128,1024]{1,0:T(8,128)S(1)}, f32[1024]{0:T(1024)S(1)}, f32[1024]{0:T(1024)S(1)}, f32[8,128]{1,0:T(8,128)S(1)}, s32[]{:T(128)}, ...), branch_computations={%region_1.1_spmd, %region_2.9_spmd, %region_10.12_spmd} | conditional | flops 2424373504 | bytes 131324456 | solution.py:285
  1711.3 175.8 %conditional.6 = (f32[16,1024]{1,0:T(8,128)S(1)}, bf16[128,1024]{1,0:T(8,128)(2,1)}) conditional(s32[]{:T(128)} %clamp.47, f32[16,1024]{1,0:T(8,128)S(1)} %get-tuple-element.4003, (f32[128,1024]{1,0:T(8,128)S(1)}, f32[1024]{0:T(1024)S(1)}, f32[1024]{0:T(1024)S(1)}, f32[8,128]{1,0:T(8,128)S(1)}, s32[]{:T(128)}, ...), branch_computations={%region_1.1_spmd, %region_2.9_spmd, %region_10.12_spmd} | conditional | flops 2424373504 | bytes 131324456 | solution.py:285
  1802.4 55.8 fusion.28
  1999.5 4681.7 %while.142 = (s32[]{:T(128)}, bf16[128,1024]{1,0:T(8,128)(2,1)}, f32[16,1024]{1,0:T(8,128)}, f32[1024]{0:T(1024)S(1)}, f32[1024]{0:T(1024)S(1)}, /*index=5*/f32[...) while((s32[]{:T(128)}, bf16[128,1024]{1,0:T(8,128)(2,1)}, ...), condition=%wide.region_56.57_spmd.clone, body=%wide.region_15.56_spmd.clone.sunk | while | flops 7301436416 | bytes 511281856 | solution.py:384
  2004.3 178.5 %collective-permute-done = bf16[128,1024]{1,0:T(8,128)(2,1)S(1)} collective-permute-done((bf16[128,1024]{1,0:T(8,128)(2,1)}, bf16[128,1024]{1,0:T(8,128)(2,1)S(1)}, u32[]{:S(2)}, u32[]{:S(2)}) %collective-permute-start) | collective-permute-done | bytes 262176 | tf_op jit(solution)/shard_map/while/body/eval_jaxpr/ppermute | solution.py:19
  2227.3 570.1 %collective-permute-done = bf16[128,1024]{1,0:T(8,128)(2,1)S(1)} collective-permute-done((bf16[128,1024]{1,0:T(8,128)(2,1)}, bf16[128,1024]{1,0:T(8,128)(2,1)S(1)}, u32[]{:S(2)}, u32[]{:S(2)}) %collective-permute-start) | collective-permute-done | bytes 262176 | tf_op jit(solution)/shard_map/while/body/eval_jaxpr/ppermute | solution.py:19
  2798.4 471.4 %conditional.7 = (f32[16,1024]{1,0:T(8,128)}, f32[1024]{0:T(1024)S(1)}, f32[1024]{0:T(1024)S(1)}, f32[16,1024]{0,1:T(8,128)}, f32[16,1024]{0,1:T(8,128)}, /*inde...) conditional(s32[]{:T(128)} %clamp.48, (f32[1024]{0:T(1024)S(1)}, ...), branch_computations={%region_16.16_spmd, %region_17.46_spmd, %region_47.55_spmd} | conditional | flops 7300858880 | bytes 506753984 | solution.py:349
  2887.0 56.7 fusion.96
  3056.2 56.8 select_bitcast_fusion
  3284.3 471.3 %conditional.7 = (f32[16,1024]{1,0:T(8,128)}, f32[1024]{0:T(1024)S(1)}, f32[1024]{0:T(1024)S(1)}, f32[16,1024]{0,1:T(8,128)}, f32[16,1024]{0,1:T(8,128)}, /*inde...) conditional(s32[]{:T(128)} %clamp.48, (f32[1024]{0:T(1024)S(1)}, ...), branch_computations={%region_16.16_spmd, %region_17.46_spmd, %region_47.55_spmd} | conditional | flops 7300858880 | bytes 506753984 | solution.py:349
  3372.9 56.7 fusion.96
  3542.1 56.8 select_bitcast_fusion
  3770.2 471.3 %conditional.7 = (f32[16,1024]{1,0:T(8,128)}, f32[1024]{0:T(1024)S(1)}, f32[1024]{0:T(1024)S(1)}, f32[16,1024]{0,1:T(8,128)}, f32[16,1024]{0,1:T(8,128)}, /*inde...) conditional(s32[]{:T(128)} %clamp.48, (f32[1024]{0:T(1024)S(1)}, ...), branch_computations={%region_16.16_spmd, %region_17.46_spmd, %region_47.55_spmd} | conditional | flops 7300858880 | bytes 506753984 | solution.py:349
  3858.7 56.7 fusion.96
  4027.9 56.8 select_bitcast_fusion
  4256.0 471.3 %conditional.7 = (f32[16,1024]{1,0:T(8,128)}, f32[1024]{0:T(1024)S(1)}, f32[1024]{0:T(1024)S(1)}, f32[16,1024]{0,1:T(8,128)}, f32[16,1024]{0,1:T(8,128)}, /*inde...) conditional(s32[]{:T(128)} %clamp.48, (f32[1024]{0:T(1024)S(1)}, ...), branch_computations={%region_16.16_spmd, %region_17.46_spmd, %region_47.55_spmd} | conditional | flops 7300858880 | bytes 506753984 | solution.py:349
  4344.6 56.7 fusion.96
  4513.8 56.8 select_bitcast_fusion
  4741.8 471.3 %conditional.7 = (f32[16,1024]{1,0:T(8,128)}, f32[1024]{0:T(1024)S(1)}, f32[1024]{0:T(1024)S(1)}, f32[16,1024]{0,1:T(8,128)}, f32[16,1024]{0,1:T(8,128)}, /*inde...) conditional(s32[]{:T(128)} %clamp.48, (f32[1024]{0:T(1024)S(1)}, ...), branch_computations={%region_16.16_spmd, %region_17.46_spmd, %region_47.55_spmd} | conditional | flops 7300858880 | bytes 506753984 | solution.py:349
  4830.4 56.7 fusion.96
  4999.6 56.8 select_bitcast_fusion
  5227.7 471.3 %conditional.7 = (f32[16,1024]{1,0:T(8,128)}, f32[1024]{0:T(1024)S(1)}, f32[1024]{0:T(1024)S(1)}, f32[16,1024]{0,1:T(8,128)}, f32[16,1024]{0,1:T(8,128)}, /*inde...) conditional(s32[]{:T(128)} %clamp.48, (f32[1024]{0:T(1024)S(1)}, ...), branch_computations={%region_16.16_spmd, %region_17.46_spmd, %region_47.55_spmd} | conditional | flops 7300858880 | bytes 506753984 | solution.py:349
  5316.2 56.7 fusion.96
  5485.4 56.8 select_bitcast_fusion
  5713.5 471.3 %conditional.7 = (f32[16,1024]{1,0:T(8,128)}, f32[1024]{0:T(1024)S(1)}, f32[1024]{0:T(1024)S(1)}, f32[16,1024]{0,1:T(8,128)}, f32[16,1024]{0,1:T(8,128)}, /*inde...) conditional(s32[]{:T(128)} %clamp.48, (f32[1024]{0:T(1024)S(1)}, ...), branch_computations={%region_16.16_spmd, %region_17.46_spmd, %region_47.55_spmd} | conditional | flops 7300858880 | bytes 506753984 | solution.py:349
  5802.1 56.7 fusion.96
  5971.3 56.8 select_bitcast_fusion
  6199.3 471.3 %conditional.7 = (f32[16,1024]{1,0:T(8,128)}, f32[1024]{0:T(1024)S(1)}, f32[1024]{0:T(1024)S(1)}, f32[16,1024]{0,1:T(8,128)}, f32[16,1024]{0,1:T(8,128)}, /*inde...) conditional(s32[]{:T(128)} %clamp.48, (f32[1024]{0:T(1024)S(1)}, ...), branch_computations={%region_16.16_spmd, %region_17.46_spmd, %region_47.55_spmd} | conditional | flops 7300858880 | bytes 506753984 | solution.py:349
  6287.9 56.7 fusion.96
  6457.1 56.8 select_bitcast_fusion
  6787.3 87.9 %reduce-scatter.30.cloned.1.call-done = bf16[128,4096]{1,0:T(8,128)(2,1)} async-done(((bf16[1024,4096]{1,0:T(8,128)(2,1)}), bf16[128,4096]{1,0:T(8,128)(2,1)}) %reduce-scatter.30.cloned.1.call-update) | async-done | bytes 1048592 | tf_op jit(solution)/shard_map/reduce_scatter | solution.py:438
  6876.8 88.7 %reduce-scatter.32.cloned.1.call-done = bf16[512,1024]{1,0:T(8,128)(2,1)} async-done(((bf16[4096,1024]{1,0:T(8,128)(2,1)}), bf16[512,1024]{1,0:T(8,128)(2,1)}) %reduce-scatter.32.cloned.1.call-update) | async-done | bytes 1048592 | tf_op jit(solution)/shard_map/reduce_scatter | solution.py:444
  6969.4 88.8 %reduce-scatter.26.cloned.1.call-done = bf16[128,4224]{1,0:T(8,128)(2,1)} async-done(((bf16[1024,4224]{1,0:T(8,128)(2,1)}), bf16[128,4224]{1,0:T(8,128)(2,1)}) %reduce-scatter.26.cloned.1.call-update) | async-done | bytes 1081360 | tf_op jit(solution)/shard_map/reduce_scatter | solution.py:415
  7207.2 152.5 %all-reduce.24.cloned.1.call-done = (bf16[2,128,2048]{2,1,0:T(8,128)(2,1)}, bf16[2,128,4224]{2,1,0:T(8,128)(2,1)}, bf16[2,256,1024]{2,1,0:T(8,128)(2,1)}, bf16[2...) async-done(((bf16[2,128,2048]{2,1,0:T(8,128)(2,1)}, bf16[2,128,4224]{2,1,0:T(8,128)(2,1)}, bf16[2,256,1024]{2,1,0:T(8,128)(2,1)}, bf16[2,128,4096]{2,1,0:T(8,128)(2,1)}, ...) | async-done | bytes 8454160 | tf_op jit(solution)/shard_map/psum | solution.py:462
  (2916 shorter events, 4809.0 us)
Async XLA Ops:
  7.3 199.3 %all-gather.27.cloned.1.call-start = ((), (), s32[]{:S(2)}) async-start(), calls=%async_computation.19 | async-start | bytes 4718592 | tf_op jit(solution)/shard_map/all_gather | solution.py:221
  9.5 197.0 %all-gather.29.cloned.1.call-start = ((), (), s32[]{:S(2)}) async-start(), calls=%async_computation.20 | async-start | bytes 4718592 | tf_op jit(solution)/shard_map/all_gather | solution.py:223
  11.4 195.1 %all-gather.31.cloned.1.call-start = ((), (), s32[]{:S(2)}) async-start(), calls=%async_computation.21 | async-start | bytes 9437184 | tf_op jit(solution)/shard_map/all_gather | solution.py:253
  13.8 270.5 %all-gather.33.cloned.1.call-start = ((), (), s32[]{:S(2)}) async-start(), calls=%async_computation.22 | async-start | bytes 9437184 | tf_op jit(solution)/shard_map/all_gather | solution.py:254
  16.2 353.0 %all-gather.25.cloned.1.call-start = ((), (), s32[]{:S(2)}) async-start(), calls=%async_computation.18 | async-start | bytes 9732096 | tf_op jit(solution)/shard_map/all_gather | solution.py:222
  17.3 6716.8 %reduce-scatter.24.cloned.1.call-start = ((), (), s32[]{:S(2)}) async-start(), calls=%async_computation.13 | async-start | bytes 4718592 | tf_op jit(solution)/shard_map/reduce_scatter | solution.py:409
  390.5 9.7 collective-permute-start.1
  579.6 7.0 collective-permute-start.1
  766.9 7.0 collective-permute-start.1
  954.2 7.0 collective-permute-start.1
  1141.5 7.0 collective-permute-start.1
  1328.8 7.0 collective-permute-start.1
  1516.1 7.0 collective-permute-start.1
  1703.3 7.0 collective-permute-start.1
  1890.6 7.0 collective-permute-start.1
  1902.9 18.7 collective-permute-start.1
  1926.8 25.2 collective-permute-start.1
  1999.6 183.2 %collective-permute-start = (bf16[128,1024]{1,0:T(8,128)(2,1)}, bf16[128,1024]{1,0:T(8,128)(2,1)S(1)}, u32[]{:S(2)}, u32[]{:S(2)}) collective-permute-start(bf16[128,1024]{1,0:T(8,128)(2,1)} %get-tuple-element.4393), channel_id=1, source_target_pairs={{8,0},{16,8},{24,16},{9,1},{17,9},{25,17},{10,2},{18,10},{26,18},{... | collective-permute-start | bytes 786440 | tf_op jit(solution)/shard_map/while/body/eval_jaxpr/ppermute | solution.py:19
  2188.7 9.4 collective-permute-start
  2203.6 12.6 collective-permute-start
  2221.8 575.6 %collective-permute-start = (bf16[128,1024]{1,0:T(8,128)(2,1)}, bf16[128,1024]{1,0:T(8,128)(2,1)S(1)}, u32[]{:S(2)}, u32[]{:S(2)}) collective-permute-start(bf16[128,1024]{1,0:T(8,128)(2,1)} %get-tuple-element.4393), channel_id=1, source_target_pairs={{8,0},{16,8},{24,16},{9,1},{17,9},{25,17},{10,2},{18,10},{26,18},{... | collective-permute-start | bytes 786440 | tf_op jit(solution)/shard_map/while/body/eval_jaxpr/ppermute | solution.py:19
  2805.2 177.4 %copy-start.126 = (f32[64]{0:T(128)}, f32[64]{0:T(128)S(1)}, u32[]{:S(2)}) copy-start(f32[64]{0:T(128)S(1)} %get-tuple-element.3437) | copy-start | bytes 772 | tf_op jit(solution)/shard_map/while/body/eval_jaxpr/cond
  3274.9 8.5 collective-permute-start
  3291.2 177.3 %copy-start.126 = (f32[64]{0:T(128)}, f32[64]{0:T(128)S(1)}, u32[]{:S(2)}) copy-start(f32[64]{0:T(128)S(1)} %get-tuple-element.3437) | copy-start | bytes 772 | tf_op jit(solution)/shard_map/while/body/eval_jaxpr/cond
  3760.7 8.5 collective-permute-start
  3777.0 177.3 %copy-start.126 = (f32[64]{0:T(128)}, f32[64]{0:T(128)S(1)}, u32[]{:S(2)}) copy-start(f32[64]{0:T(128)S(1)} %get-tuple-element.3437) | copy-start | bytes 772 | tf_op jit(solution)/shard_map/while/body/eval_jaxpr/cond
  4246.5 8.5 collective-permute-start
  4262.8 177.3 %copy-start.126 = (f32[64]{0:T(128)}, f32[64]{0:T(128)S(1)}, u32[]{:S(2)}) copy-start(f32[64]{0:T(128)S(1)} %get-tuple-element.3437) | copy-start | bytes 772 | tf_op jit(solution)/shard_map/while/body/eval_jaxpr/cond
  4732.4 8.5 collective-permute-start
  4748.7 177.3 %copy-start.126 = (f32[64]{0:T(128)}, f32[64]{0:T(128)S(1)}, u32[]{:S(2)}) copy-start(f32[64]{0:T(128)S(1)} %get-tuple-element.3437) | copy-start | bytes 772 | tf_op jit(solution)/shard_map/while/body/eval_jaxpr/cond
  5218.2 8.5 collective-permute-start
  5234.5 177.3 %copy-start.126 = (f32[64]{0:T(128)}, f32[64]{0:T(128)S(1)}, u32[]{:S(2)}) copy-start(f32[64]{0:T(128)S(1)} %get-tuple-element.3437) | copy-start | bytes 772 | tf_op jit(solution)/shard_map/while/body/eval_jaxpr/cond
  5704.0 8.5 collective-permute-start
  5720.3 177.3 %copy-start.126 = (f32[64]{0:T(128)}, f32[64]{0:T(128)S(1)}, u32[]{:S(2)}) copy-start(f32[64]{0:T(128)S(1)} %get-tuple-element.3437) | copy-start | bytes 772 | tf_op jit(solution)/shard_map/while/body/eval_jaxpr/cond
  6189.9 8.5 collective-permute-start
  6206.2 177.3 %copy-start.126 = (f32[64]{0:T(128)}, f32[64]{0:T(128)S(1)}, u32[]{:S(2)}) copy-start(f32[64]{0:T(128)S(1)} %get-tuple-element.3437) | copy-start | bytes 772 | tf_op jit(solution)/shard_map/while/body/eval_jaxpr/cond
  6687.3 97.8 %reduce-scatter.28.cloned.1.call-start = ((), (), s32[]{:S(2)}) async-start(), calls=%async_computation.15 | async-start | bytes 4718592 | tf_op jit(solution)/shard_map/reduce_scatter | solution.py:427
  6693.8 181.5 %reduce-scatter.30.cloned.1.call-start = ((), (), s32[]{:S(2)}) async-start(), calls=%async_computation.16 | async-start | bytes 9437184 | tf_op jit(solution)/shard_map/reduce_scatter | solution.py:438
  6702.9 262.6 %reduce-scatter.32.cloned.1.call-start = ((), (), s32[]{:S(2)}) async-start(), calls=%async_computation.17 | async-start | bytes 9437184 | tf_op jit(solution)/shard_map/reduce_scatter | solution.py:444
  6712.3 345.9 %reduce-scatter.26.cloned.1.call-start = ((), (), s32[]{:S(2)}) async-start(), calls=%async_computation.14 | async-start | bytes 9732096 | tf_op jit(solution)/shard_map/reduce_scatter | solution.py:415
  6721.7 371.5 %reduce-scatter.40.cloned.1.call-start = ((), (), s32[]{:S(2)}) async-start(), calls=%async_computation.26 | async-start | bytes 36864
  6723.1 396.5 %reduce-scatter.34.cloned.1.call-start = ((), (), s32[]{:S(2)}) async-start(), calls=%async_computation.23 | async-start | bytes 294912
  6724.2 426.2 %reduce-scatter.36.cloned.1.call-start = ((), (), s32[]{:S(2)}) async-start(), calls=%async_computation.24 | async-start | bytes 294912
  6725.2 455.8 %reduce-scatter.38.cloned.1.call-start = ((), (), s32[]{:S(2)}) async-start(), calls=%async_computation.25 | async-start | bytes 294912
  6726.3 633.4 %all-reduce.24.cloned.1.call-start = ((), (), s32[]{:S(2)}) async-start(), calls=%async_computation.27 | async-start | bytes 16908288 | tf_op jit(solution)/shard_map/psum | solution.py:462
  6735.3 324.5 %copy-start.47 = (bf16[2,128,2048]{2,1,0:T(8,128)(2,1)}, bf16[2,128,2048]{2,1,0:T(8,128)(2,1)S(1)}, u32[]{:S(2)}) copy-start(bf16[2,128,2048]{2,1,0:T(8,128)(2,1)S(1)} %convert_dynamic-update-slice_fusion.4) | copy-start | bytes 3145732
  7061.2 337.4 %reduce-scatter.20.cloned.1.call-start = ((), (), s32[]{:S(2)}) async-start(), calls=%async_computation.11 | async-start | bytes 2621440 | tf_op jit(solution)/shard_map/reduce_scatter | solution.py:315
  7061.7 375.4 %reduce-scatter.22.cloned.1.call-start = ((), (), s32[]{:S(2)}) async-start(), calls=%async_computation.12 | async-start | bytes 2621440 | tf_op jit(solution)/shard_map/reduce_scatter | solution.py:386
  (701 other events, 16183.7 us)
Sparse Core Ops, SparseCore 0:
  10.3 59.2 all-gather.26
  71.7 46.2 all-gather.28
  120.2 81.4 all-gather.30
  203.7 80.5 all-gather.32
  286.3 82.7 all-gather.24
  6687.4 46.6 reduce-scatter.23
  6736.9 48.1 reduce-scatter.27
  6787.4 87.7 reduce-scatter.29
  6877.5 87.9 reduce-scatter.31
  6967.7 90.4 reduce-scatter.25
  7060.4 28.3 reduce-scatter.39
  7091.0 28.5 reduce-scatter.33
  7121.9 28.4 reduce-scatter.35
  7152.5 28.4 reduce-scatter.37
  7186.4 173.2 all-reduce.23
  7363.4 35.1 reduce-scatter.19
  7402.0 35.1 reduce-scatter.21
where the time goes:
time: 7470 us; the launch traced here: 7440 us
  matrix products  3320 us (44%)
  waiting for transfers between devices  1570 us (21%)
  local copies, waits for them, and re-layouts  1330 us (18%)
  other arithmetic  852 us (11%)
  blocking collectives  224 us (3%)
    dot_general x32, matrix products, moving_average(): jnp.einsum('tsd,nsd->ntd', toeplitz, pieces, precision=lax.Precision.HIGH...  1600 us
    gather x32, local copies, waits for them, and re-layouts, moving_average(): kernel[jnp.clip(lag, 0, block - 1)]  784 us
    ppermute x22, waiting for transfers between devices, shifted_2(): lax.ppermute(value, axis, [(source, source + steps) for source in range(i...  782 us
    dot_general x32, matrix products, moving_average(): jnp.einsum('ted,ned->ntd', lead, before, precision=lax.Precision.HIGHEST)  701 us
    dot_general x32, matrix products, moving_average(): jnp.einsum('sed,nsd->ned', tail, pieces, precision=lax.Precision.HIGHEST)  525 us
    dot_general x80, matrix products, product(): return wrapped(left, right)  293 us
    scatter-add x8, other arithmetic, moving_average(): kernel[jnp.clip(lag, 0, block - 1)]  291 us
    reduce_sum x16, other arithmetic, moving_average(): kernel = jnp.sum(powers * (drive * weight_out)[None], axis=1)  201 us
  transfers between devices with their start and end apart: 39, of which 25 were waited for; matrix products, arithmetic and copies ran while one was open for 3% of the time, Pallas kernels for 0%

commit v1 on v0

v1 whole, which is shorter than its diff:
```python
import functools

import jax
import jax.numpy as jnp
from jax import lax
from jax.experimental import pallas as pl
from jax.experimental.pallas import tpu as pltpu
from jax.sharding import PartitionSpec as P

F32 = jnp.float32
BF16 = jnp.bfloat16
MESH = pl.DeviceIdType.MESH
ATT = 128
LANES = 128
CHUNKS = 8
ROWS = 256
STRIP = 64
EPS = 1e-05
NEGATIVE = -1000000000.0
VMEM_BYTES = 56 * 1024 * 1024


def vmem():
    return pl.BlockSpec(memory_space=pltpu.VMEM)


def smem():
    return pl.BlockSpec(memory_space=pltpu.SMEM)


def hbm():
    return pl.BlockSpec(memory_space=pl.ANY)


def shape(dims, kind):
    return jax.ShapeDtypeStruct(dims, kind)


def sigmoid(v):
    return 0.5 * jnp.tanh(0.5 * v) + 0.5


def silu(v):
    return v * sigmoid(v)


def silu_slope(v):
    s = sigmoid(v)
    return s * (1.0 + v * (1.0 - s))


def dot(left, right, left_dim=1, right_dim=0):
    return lax.dot_general(
        left, right, (((left_dim,), (right_dim,)), ((), ())), preferred_element_type=F32
    )


def normalise(x):
    centred = x - jnp.mean(x, axis=-1, keepdims=True)
    spread = jnp.mean(centred * centred, axis=-1, keepdims=True)
    scale = lax.rsqrt(spread + EPS)
    return centred * scale, scale


def row_valid(start, rows, length):
    place = start + lax.broadcasted_iota(jnp.int32, (rows, 1), 0)
    return (place < length).astype(F32)


def params(**more):
    return pltpu.CompilerParams(vmem_limit_bytes=VMEM_BYTES, **more)


def spread_rows(ref, lanes, count):
    return [ref[n, :, lanes] for n in range(count)]


def on_sublanes(array):
    return jnp.broadcast_to(array[:, None, :], (array.shape[0], CHUNKS, array.shape[1]))


def power(base, exponent):
    result = None
    square = base
    while exponent:
        if exponent % 2:
            result = square if result is None else result * square
        exponent //= 2
        if exponent:
            square = square * square
    return result


def entering(last, rate, steps, reverse=False):
    row = lax.broadcasted_iota(jnp.int32, (CHUNKS, LANES), 0)
    weight = power(rate, steps)
    span = 1
    while span < CHUNKS:
        if reverse:
            moved = jnp.where(row < CHUNKS - span, pltpu.roll(last, CHUNKS - span, 0), 0.0)
        else:
            moved = jnp.where(row >= span, pltpu.roll(last, span, 0), 0.0)
        last = last + weight * moved
        weight = weight * weight
        span *= 2
    if reverse:
        return jnp.where(row < CHUNKS - 1, pltpu.roll(last, CHUNKS - 1, 0), 0.0)
    return jnp.where(row >= 1, pltpu.roll(last, 1, 0), 0.0)


def entering_pair(last, slope, rate, steps):
    row = lax.broadcasted_iota(jnp.int32, (CHUNKS, LANES), 0)
    weight = power(rate, steps)
    tilt = float(steps) * power(rate, steps - 1)
    span = 1
    while span < CHUNKS:
        moved = jnp.where(row >= span, pltpu.roll(last, span, 0), 0.0)
        moved_slope = jnp.where(row >= span, pltpu.roll(slope, span, 0), 0.0)
        slope = slope + weight * moved_slope + tilt * moved
        last = last + weight * moved
        tilt = 2.0 * weight * tilt
        weight = weight * weight
        span *= 2
    first = row >= 1
    return (
        jnp.where(first, pltpu.roll(last, 1, 0), 0.0),
        jnp.where(first, pltpu.roll(slope, 1, 0), 0.0),
    )


def average_forward_kernel(
    length_ref,
    x_ref,
    gain_ref,
    shift_ref,
    rate_ref,
    coef_ref,
    skip_ref,
    normed_ref,
    mixed_ref,
    pre_ref,
    own_ref,
    scale_ref,
    rows_buf,
    m_buf,
    y_buf,
):
    length = length_ref[0]
    count, width = x_ref.shape
    own = mixed_ref.shape[1]
    dims = rate_ref.shape[0]
    steps = count // CHUNKS
    mine = pl.ds(pl.multiple_of(lax.axis_index("section") * own, LANES), own)

    def norm_strip(i, carry):
        start = pl.multiple_of(i * STRIP, STRIP)
        here = pl.ds(start, STRIP)
        n, scale = normalise(x_ref[here, :].astype(F32))
        rows_buf[...] = n
        normed_ref[here, :] = (n * gain_ref[...] + shift_ref[...]).astype(BF16)
        part = rows_buf[:, mine]
        own_ref[here, :] = part
        scale_ref[here, :] = jnp.broadcast_to(scale, (STRIP, LANES))
        masked = (part * gain_ref[:, mine] + shift_ref[:, mine]) * row_valid(start, STRIP, length)
        for group in range(own // LANES):
            m_buf[group, here, :] = masked[:, group * LANES : (group + 1) * LANES]
        return carry

    lax.fori_loop(0, count // STRIP, norm_strip, 0)

    for group in range(own // LANES):
        lanes = slice(group * LANES, (group + 1) * LANES)
        rates = spread_rows(rate_ref, lanes, dims)
        coefs = spread_rows(coef_ref, lanes, dims)
        blank = tuple(jnp.zeros((CHUNKS, LANES), F32) for _ in range(dims))
        m_part, y_part = m_buf.at[group], y_buf.at[group]

        def finals(t, states):
            x = m_part[pl.ds(t, CHUNKS, stride=steps), :]
            return tuple(r * h + x for r, h in zip(rates, states))

        ends = lax.fori_loop(0, steps, finals, blank, unroll=4)
        starts = tuple(entering(h, r, steps) for h, r in zip(ends, rates))

        def outputs(t, states):
            x = m_part[pl.ds(t, CHUNKS, stride=steps), :]
            states = tuple(r * h + x for r, h in zip(rates, states))
            terms = [c * h for c, h in zip(coefs, states)]
            while len(terms) > 1:
                terms = [a + b for a, b in zip(terms[::2], terms[1::2])]
            y_part[pl.ds(t, CHUNKS, stride=steps), :] = terms[0]
            return states

        lax.fori_loop(0, steps, outputs, starts, unroll=4)

    def mix_strip(i, carry):
        here = pl.ds(pl.multiple_of(i * STRIP, STRIP), STRIP)
        for group in range(own // LANES):
            lanes = slice(group * LANES, (group + 1) * LANES)
            pre = y_buf[group, here, :] + skip_ref[:, lanes] * m_buf[group, here, :]
            pre_ref[here, lanes] = pre.astype(BF16)
            mixed_ref[here, lanes] = silu(pre).astype(BF16)
        return carry

    lax.fori_loop(0, count // STRIP, mix_strip, 0)


def average_forward(length, x, gain, shift, rate, coef, skip):
    count, width = x.shape
    own = skip.shape[1]
    groups = own // LANES
    rate, coef = on_sublanes(rate), on_sublanes(coef)
    return pl.pallas_call(
        average_forward_kernel,
        out_shape=(
            shape((count, width), BF16),
            shape((count, own), BF16),
            shape((count, own), BF16),
            shape((count, own), F32),
            shape((count, LANES), F32),
        ),
        in_specs=[smem()] + [vmem()] * 6,
        out_specs=(vmem(),) * 5,
        scratch_shapes=[
            pltpu.VMEM((STRIP, width), F32),
            pltpu.VMEM((groups, count, LANES), F32),
            pltpu.VMEM((groups, count, LANES), F32),
        ],
        compiler_params=params(),
    )(length, x, gain, shift, rate, coef, skip)


def average_backward_kernel(
    length_ref,
    gmixed_ref,
    gvalue_ref,
    pre_ref,
    own_ref,
    scale_ref,
    resid_ref,
    gain_ref,
    shift_ref,
    rate_ref,
    coef_ref,
    skip_ref,
    z_ref,
    stats_ref,
    gh_ref,
    gq_ref,
    sums_ref,
    m_buf,
    g_buf,
    r_buf,
):
    length = length_ref[0]
    count, own = z_ref.shape
    dims = rate_ref.shape[0]
    steps = count // CHUNKS
    groups = own // LANES
    part_size = dims // 2

    def load_strip(i, carry):
        start = pl.multiple_of(i * STRIP, STRIP)
        here = pl.ds(start, STRIP)
        valid = row_valid(start, STRIP, length)
        for group in range(groups):
            lanes = slice(group * LANES, (group + 1) * LANES)
            m_buf[group, here, :] = (
                own_ref[here, lanes] * gain_ref[:, lanes] + shift_ref[:, lanes]
            ) * valid
            slope = silu_slope(pre_ref[here, lanes].astype(F32))
            g_buf[group, here, :] = gmixed_ref[here, lanes] * slope
        return carry

    lax.fori_loop(0, count // STRIP, load_strip, 0)

    zero = jnp.zeros((CHUNKS, LANES), F32)
    for group in range(groups):
        lanes = slice(group * LANES, (group + 1) * LANES)
        rates = spread_rows(rate_ref, lanes, dims)
        coefs = spread_rows(coef_ref, lanes, dims)
        m_part, g_part, r_part = m_buf.at[group], g_buf.at[group], r_buf.at[group]

        for half in range(2):
            some = rates[half * part_size : (half + 1) * part_size]
            blank = (tuple(zero for _ in some), tuple(zero for _ in some))

            def finals(t, carry):
                states, slopes = carry
                x = m_part[pl.ds(t, CHUNKS, stride=steps), :]
                slopes = tuple(r * q + h for r, q, h in zip(some, slopes, states))
                states = tuple(r * h + x for r, h in zip(some, states))
                return states, slopes

            ends, end_slopes = lax.fori_loop(0, steps, finals, blank, unroll=4)
            pairs = [entering_pair(h, q, r, steps) for h, q, r in zip(ends, end_slopes, some)]
            begin = (
                tuple(p[0] for p in pairs),
                tuple(p[1] for p in pairs),
                tuple(zero for _ in some),
                tuple(zero for _ in some),
            )

            def sweep(t, carry):
                states, slopes, of_states, of_slopes = carry
                x = m_part[pl.ds(t, CHUNKS, stride=steps), :]
                g = g_part[pl.ds(t, CHUNKS, stride=steps), :]
                slopes = tuple(r * q + h for r, q, h in zip(some, slopes, states))
                states = tuple(r * h + x for r, h in zip(some, states))
                of_states = tuple(a + g * h for a, h in zip(of_states, states))
                of_slopes = tuple(a + g * q for a, q in zip(of_slopes, slopes))
                return states, slopes, of_states, of_slopes

            _, _, of_states, of_slopes = lax.fori_loop(0, steps, sweep, begin, unroll=4)
            for n in range(part_size):
                row = half * part_size + n
                gh_ref[row : row + 1, lanes] = jnp.sum(of_states[n], axis=0, keepdims=True)
                gq_ref[row : row + 1, lanes] = jnp.sum(of_slopes[n], axis=0, keepdims=True)

        blank = tuple(zero for _ in rates)

        def back_finals(t, states):
            g = g_part[pl.ds(steps - 1 - t, CHUNKS, stride=steps), :]
            return tuple(r * h + g for r, h in zip(rates, states))

        ends = lax.fori_loop(0, steps, back_finals, blank, unroll=4)
        starts = tuple(entering(h, r, steps, reverse=True) for h, r in zip(ends, rates))

        def back_outputs(t, states):
            g = g_part[pl.ds(steps - 1 - t, CHUNKS, stride=steps), :]
            states = tuple(r * h + g for r, h in zip(rates, states))
            terms = [c * h for c, h in zip(coefs, states)]
            while len(terms) > 1:
                terms = [a + b for a, b in zip(terms[::2], terms[1::2])]
            r_part[pl.ds(steps - 1 - t, CHUNKS, stride=steps), :] = terms[0]
            return states

        lax.fori_loop(0, steps, back_outputs, starts, unroll=4)

    ones = jnp.ones((CHUNKS, own), BF16)
    first = lax.broadcasted_iota(jnp.int32, (CHUNKS, LANES), 0) == 0

    def finish(i, carry):
        start = pl.multiple_of(i * LANES, LANES)
        here = pl.ds(start, LANES)
        valid = row_valid(start, LANES, length)
        of_gain, of_shift, of_skip = carry
        smoothed = jnp.concatenate([r_buf[k, here, :] for k in range(groups)], axis=1)
        gpre = jnp.concatenate([g_buf[k, here, :] for k in range(groups)], axis=1)
        masked = jnp.concatenate([m_buf[k, here, :] for k in range(groups)], axis=1)
        n = own_ref[here, :]
        gmasked = skip_ref[...] * gpre + smoothed
        gnormed = gmasked * valid + gvalue_ref[here, :]
        e = gnormed * gain_ref[...]
        z = scale_ref[here, 0:1] * e + resid_ref[here, :]
        z_ref[here, :] = z.astype(BF16)
        mean_row = dot(ones, e.astype(BF16), 1, 1)
        slope_row = dot(ones, (e * n).astype(BF16), 1, 1)
        stats_ref[:, here] = jnp.where(first, mean_row, slope_row)
        return (
            of_gain + jnp.sum(gnormed * n, axis=0, keepdims=True),
            of_shift + jnp.sum(gnormed, axis=0, keepdims=True),
            of_skip + jnp.sum(gpre * masked, axis=0, keepdims=True),
        )

    blank_row = jnp.zeros((1, own), F32)
    of_gain, of_shift, of_skip = lax.fori_loop(
        0, count // LANES, finish, (blank_row, blank_row, blank_row)
    )
    sums_ref[0:1, :] = of_gain
    sums_ref[1:2, :] = of_shift
    sums_ref[2:3, :] = of_skip
    sums_ref[3:8, :] = jnp.zeros((5, own), F32)


def average_backward(
    length, gmixed, gvalue, pre, own_n, scale, resid, gain, shift, rate, coef, skip
):
    count, own = gmixed.shape
    dims = rate.shape[0]
    groups = own // LANES
    rate, coef = on_sublanes(rate), on_sublanes(coef)
    return pl.pallas_call(
        average_backward_kernel,
        out_shape=(
            shape((count, own), BF16),
            shape((CHUNKS, count), F32),
            shape((dims, own), F32),
            shape((dims, own), F32),
            shape((8, own), F32),
        ),
        in_specs=[smem()] + [vmem()] * 11,
        out_specs=(vmem(),) * 5,
        scratch_shapes=[pltpu.VMEM((groups, count, LANES), F32)] * 3,
        compiler_params=params(),
    )(length, gmixed, gvalue, pre, own_n, scale, resid, gain, shift, rate, coef, skip)


def attention_forward_kernel(
    length_ref,
    normed_ref,
    mixed_ref,
    in_ref,
    bias_ref,
    pair_ref,
    offset_ref,
    out_w_ref,
    part_ref,
    update_ref,
    shared_ref,
    reset_ref,
    cand_ref,
    value_ref,
    att_ref,
    gated_ref,
    probs_ref,
):
    length = length_ref[0]
    rows = normed_ref.shape[0]
    wide = value_ref.shape[1]
    own = update_ref.shape[1]
    keyed = shared_ref.shape[1]
    start = pl.program_id(0) * rows
    value = dot(normed_ref[...], in_ref[:, :wide]) + bias_ref[:, :wide]
    value_ref[...] = value.astype(BF16)
    values = silu(value).astype(BF16)
    low = wide
    update = dot(mixed_ref[...], in_ref[:, low : low + own]) + bias_ref[:, low : low + own]
    update_ref[...] = update.astype(BF16)
    low += own
    shared = dot(mixed_ref[...], in_ref[:, low : low + keyed]) + bias_ref[:, low : low + keyed]
    shared_ref[...] = shared.astype(BF16)
    low += keyed
    reset = dot(mixed_ref[...], in_ref[:, low : low + wide]) + bias_ref[:, low : low + wide]
    reset_ref[...] = reset.astype(BF16)
    low += wide
    cand_ref[...] = (
        dot(mixed_ref[...], in_ref[:, low : low + own]) + bias_ref[:, low : low + own]
    ).astype(BF16)
    shared = silu(shared)
    reset = silu(reset)
    queries = (shared * pair_ref[0:1, :] + offset_ref[...]).astype(BF16)
    keys = (shared * pair_ref[1:2, :]).astype(BF16)
    for block in range(rows // ATT):
        here = slice(block * ATT, (block + 1) * ATT)
        begin = start + block * ATT
        scores = dot(queries[here], keys[here], 1, 1) * keyed**-0.5
        key_place = begin + lax.broadcasted_iota(jnp.int32, (ATT, ATT), 1)
        scores = jnp.where(key_place < length, scores, NEGATIVE)
        raised = jnp.exp(scores - jnp.max(scores, axis=-1, keepdims=True))
        probs = (raised / jnp.sum(raised, axis=-1, keepdims=True)).astype(BF16)
        probs_ref[here, :] = probs
        attended = dot(probs, values[here]) * row_valid(begin, ATT, length)
        att_ref[here, :] = attended.astype(BF16)
        gated_ref[here, :] = (attended * reset[here]).astype(BF16)
    part_ref[...] = dot(gated_ref[...], out_w_ref[...]).astype(BF16)


def attention_forward(length, normed, mixed, in_w, bias, pair, offset, out_w, own):
    count, width = normed.shape
    wide = out_w.shape[0]
    keyed = pair.shape[1]

    def rows(columns):
        return pl.BlockSpec((ROWS, columns), lambda i: (i, 0))

    def whole(array):
        return pl.BlockSpec(array.shape, lambda i: (0, 0))

    widths = (width, own, keyed, wide, own, wide, wide, wide, ATT)
    return pl.pallas_call(
        attention_forward_kernel,
        grid=(count // ROWS,),
        out_shape=tuple(shape((count, w), BF16) for w in widths),
        in_specs=[
            smem(),
            rows(width),
            rows(width),
            whole(in_w),
            whole(bias),
            whole(pair),
            whole(offset),
            whole(out_w),
        ],
        out_specs=tuple(rows(w) for w in widths),
        compiler_params=params(),
    )(length, normed, mixed, in_w, bias, pair, offset, out_w)


def attention_backward_kernel(
    length_ref,
    gout_ref,
    gupdate_ref,
    shared_ref,
    reset_ref,
    value_ref,
    att_ref,
    probs_ref,
    in_ref,
    pair_ref,
    offset_ref,
    out_w_ref,
    gmixed_ref,
    gnormed_ref,
    gbase_ref,
    gvalue_ref,
    bias_ref,
    pair_sum_ref,
):
    length = length_ref[0]
    rows = gout_ref.shape[0]
    wide = value_ref.shape[1]
    own = gupdate_ref.shape[1]
    keyed = shared_ref.shape[1]
    start = pl.program_id(0) * rows
    mine = pl.ds(pl.multiple_of(lax.axis_index("section") * own, LANES), own)

    @pl.when(pl.program_id(0) == 0)
    def _():
        bias_ref[...] = jnp.zeros_like(bias_ref)
        pair_sum_ref[...] = jnp.zeros_like(pair_sum_ref)

    valid = row_valid(start, rows, length)
    ggated = dot(gout_ref[...], out_w_ref[...], 1, 1)
    reset = reset_ref[...].astype(F32)
    gattended = (ggated * silu(reset) * valid).astype(BF16)
    greset = ggated * att_ref[...].astype(F32) * silu_slope(reset)
    value = value_ref[...].astype(F32)
    values = silu(value).astype(BF16)
    shared_pre = shared_ref[...].astype(F32)
    shared = silu(shared_pre)
    scale_q, scale_k = pair_ref[0:1, :], pair_ref[1:2, :]
    queries = (shared * scale_q + offset_ref[...]).astype(BF16)
    keys = (shared * scale_k).astype(BF16)
    gq_parts, gk_parts, gv_parts = [], [], []
    for block in range(rows // ATT):
        here = slice(block * ATT, (block + 1) * ATT)
        probs = probs_ref[here, :]
        gprobs = dot(gattended[here], values[here], 1, 1)
        gv_parts.append(dot(probs, gattended[here], 0, 0))
        probs = probs.astype(F32)
        gscores = probs * (gprobs - jnp.sum(probs * gprobs, axis=-1, keepdims=True))
        key_place = start + block * ATT + lax.broadcasted_iota(jnp.int32, (ATT, ATT), 1)
        gscores = jnp.where(key_place < length, gscores, 0.0)
        gscores = (gscores * keyed**-0.5).astype(BF16)
        gq_parts.append(dot(gscores, keys[here]))
        gk_parts.append(dot(gscores, queries[here], 0, 0))
    gqueries = jnp.concatenate(gq_parts, axis=0)
    gkeys = jnp.concatenate(gk_parts, axis=0)
    gvalue = jnp.concatenate(gv_parts, axis=0) * silu_slope(value)
    gshared = (gqueries * scale_q + gkeys * scale_k) * silu_slope(shared_pre)
    pair_sum_ref[0:1, :] += jnp.sum(gqueries * shared, axis=0, keepdims=True)
    pair_sum_ref[1:2, :] += jnp.sum(gkeys * shared, axis=0, keepdims=True)
    pair_sum_ref[2:3, :] += jnp.sum(gqueries, axis=0, keepdims=True)
    gupdate = gupdate_ref[...]
    gcand = gout_ref[:, mine]
    low = 0
    for piece in (gvalue, gupdate, gshared, greset, gcand):
        size = piece.shape[1]
        bias_ref[0:1, low : low + size] += jnp.sum(piece.astype(F32), axis=0, keepdims=True)
        if low:
            gbase_ref[:, low - wide : low - wide + size] = piece.astype(BF16)
        else:
            gvalue_ref[...] = piece.astype(BF16)
        low += size
    gmixed_ref[...] = dot(gbase_ref[...], in_ref[:, wide:], 1, 1).astype(BF16)
    gnormed_ref[...] = dot(gvalue_ref[...], in_ref[:, :wide], 1, 1).astype(BF16)


def attention_backward(length, gout, gupdate, saved, in_w, pair, offset, out_w):
    shared, reset, value, att, probs = saved
    count, width = gout.shape
    own = gupdate.shape[1]
    wide = out_w.shape[0]
    keyed = pair.shape[1]
    total = in_w.shape[1]

    def rows(columns):
        return pl.BlockSpec((ROWS, columns), lambda i: (i, 0))

    def whole(dims):
        return pl.BlockSpec(dims, lambda i: (0, 0))

    return pl.pallas_call(
        attention_backward_kernel,
        grid=(count // ROWS,),
        out_shape=(
            shape((count, width), BF16),
            shape((count, width), BF16),
            shape((count, total - wide), BF16),
            shape((count, wide), BF16),
            shape((8, total), F32),
            shape((8, keyed), F32),
        ),
        in_specs=[
            smem(),
            rows(width),
            rows(own),
            rows(keyed),
            rows(wide),
            rows(wide),
            rows(wide),
            rows(ATT),
            whole(in_w.shape),
            whole(pair.shape),
            whole(offset.shape),
            whole(out_w.shape),
        ],
        out_specs=(
            rows(width),
            rows(width),
            rows(total - wide),
            rows(wide),
            whole((8, total)),
            whole((8, keyed)),
        ),
        compiler_params=params(),
    )(length, gout, gupdate, shared, reset, value, att, probs, in_w, pair, offset, out_w)


def feed_forward_kernel(
    x_ref, gain_ref, shift_ref, in_ref, bias_ref, out_w_ref, part_ref, pre_ref, n_ref, normed_ref, scale_ref
):
    n, scale = normalise(x_ref[...].astype(F32))
    n_ref[...] = n.astype(BF16)
    scale_ref[...] = jnp.broadcast_to(scale, scale_ref.shape)
    normed_ref[...] = (n * gain_ref[...] + shift_ref[...]).astype(BF16)
    pre = dot(normed_ref[...], in_ref[...]) + bias_ref[...]
    pre_ref[...] = pre.astype(BF16)
    part_ref[...] = dot(silu(pre).astype(BF16), out_w_ref[...]).astype(BF16)


def feed_forward(x, gain, shift, in_w, bias, out_w):
    count, width = x.shape
    hidden = in_w.shape[1]

    def rows(columns):
        return pl.BlockSpec((ROWS, columns), lambda i: (i, 0))

    def whole(array):
        return pl.BlockSpec(array.shape, lambda i: (0, 0))

    return pl.pallas_call(
        feed_forward_kernel,
        grid=(count // ROWS,),
        out_shape=(
            shape((count, width), BF16),
            shape((count, hidden), BF16),
            shape((count, width), BF16),
            shape((count, width), BF16),
            shape((count, LANES), F32),
        ),
        in_specs=[rows(width)] + [whole(a) for a in (gain, shift, in_w, bias, out_w)],
        out_specs=(rows(width), rows(hidden), rows(width), rows(width), rows(LANES)),
        compiler_params=params(),
    )(x, gain, shift, in_w, bias, out_w)


def feed_backward_kernel(corrected, *refs):
    if corrected:
        z_ref, means_ref, x_ref = refs[:3]
        refs = refs[3:]
    else:
        g_in_ref = refs[0]
        refs = refs[1:]
    pre_ref, n_ref, gain_ref, in_ref, out_w_ref = refs[:5]
    refs = refs[5:]
    part_ref, stats_ref, gpre_ref, act_ref, sums_ref, bias_ref = refs[:6]
    width = n_ref.shape[1]

    @pl.when(pl.program_id(0) == 0)
    def _():
        sums_ref[...] = jnp.zeros_like(sums_ref)
        bias_ref[...] = jnp.zeros_like(bias_ref)

    if corrected:
        g_ref = refs[6]
        xn, xscale = normalise(x_ref[...].astype(F32))
        means = means_ref[...].T * (1.0 / width)
        g = z_ref[...].astype(F32) - xscale * (means[:, 0:1] + xn * means[:, 1:2])
        g_ref[...] = g.astype(BF16)
    else:
        g_ref = g_in_ref
    g = g_ref[...]
    pre = pre_ref[...].astype(F32)
    s = sigmoid(pre)
    act_ref[...] = (pre * s).astype(BF16)
    gpre = dot(g, out_w_ref[...], 1, 1) * (s * (1.0 + pre * (1.0 - s)))
    bias_ref[0:1, :] += jnp.sum(gpre, axis=0, keepdims=True)
    gpre_ref[...] = gpre.astype(BF16)
    part = dot(gpre_ref[...], in_ref[...], 1, 1)
    part_ref[...] = part.astype(BF16)
    n = n_ref[...].astype(F32)
    sums_ref[0:1, :] += jnp.sum(part * n, axis=0, keepdims=True)
    sums_ref[1:2, :] += jnp.sum(part, axis=0, keepdims=True)
    sums_ref[2:3, :] += jnp.sum(g.astype(F32), axis=0, keepdims=True)
    e = part * gain_ref[...]
    ones = jnp.ones((CHUNKS, width), BF16)
    mean_row = dot(ones, e.astype(BF16), 1, 1)
    slope_row = dot(ones, (e * n).astype(BF16), 1, 1)
    first = lax.broadcasted_iota(jnp.int32, mean_row.shape, 0) == 0
    stats_ref[...] = jnp.where(first, mean_row, slope_row)


def feed_backward(given, pre, n, gain, in_w, out_w):
    corrected = isinstance(given, tuple)
    count, width = n.shape
    hidden = in_w.shape[1]

    def rows(columns):
        return pl.BlockSpec((ROWS, columns), lambda i: (i, 0))

    def whole(dims):
        return pl.BlockSpec(dims, lambda i: (0, 0))

    stats_spec = pl.BlockSpec((CHUNKS, ROWS), lambda i: (0, i))
    given = given if corrected else (given,)
    given_specs = [rows(width), stats_spec, rows(width)] if corrected else [rows(width)]
    extra = ((shape((count, width), BF16),), (rows(width),)) if corrected else ((), ())
    return pl.pallas_call(
        functools.partial(feed_backward_kernel, corrected),
        grid=(count // ROWS,),
        out_shape=(
            shape((count, width), BF16),
            shape((CHUNKS, count), F32),
            shape((count, hidden), BF16),
            shape((count, hidden), BF16),
            shape((8, width), F32),
            shape((8, hidden), F32),
        )
        + extra[0],
        in_specs=given_specs
        + [rows(hidden), rows(width), whole(gain.shape), whole(in_w.shape), whole(out_w.shape)],
        out_specs=(
            rows(width),
            stats_spec,
            rows(hidden),
            rows(hidden),
            whole((8, width)),
            whole((8, hidden)),
        )
        + extra[1],
        compiler_params=params(),
    )(*given, pre, n, gain, in_w, out_w)


def plane():
    me = lax.axis_index("section")
    across = me + 1 - 2 * (me % 2)
    along = me + 2 - 4 * (me // 2)
    return me, across, along, across + along - me


def greet(*others):
    barrier = pltpu.get_barrier_semaphore()
    for other in others:
        pl.semaphore_signal(barrier, inc=1, device_id={"section": other}, device_id_type=MESH)
    pl.semaphore_wait(barrier, len(others))


def link(source, target, sems, index, other):
    send, recv = sems
    return pltpu.make_async_remote_copy(
        src_ref=source,
        dst_ref=target,
        send_sem=send.at[index],
        recv_sem=recv.at[index],
        device_id={"section": other},
        device_id_type=MESH,
    )


def strips(count, work):
    def one(i, carry):
        work(pl.multiple_of(i * STRIP, STRIP))
        return carry

    lax.fori_loop(0, count // STRIP, one, 0)


def reduce_begin(part, piece, peers, slots, sems):
    me, across, along, far = peers
    early, direct, _, _ = slots
    started = []
    for half, first in enumerate((across, along)):
        started.append(link(part.at[piece(far, half)], early.at[half], sems, half, first))
        started[-1].start()
    for half, first in enumerate((across, along)):
        started.append(link(part.at[piece(first, half)], direct.at[half], sems, 2 + half, first))
        started[-1].start()
    return started


def reduce_forward(part, piece, peers, slots, sems, started):
    me, across, along, far = peers
    early, _, late, stage = slots
    for half, second in enumerate((along, across)):
        started[half].wait_recv()
        row, column = piece(second, half)

        def add(start):
            here = pl.ds(start, STRIP)
            mine = part[pl.ds(row.start + start, STRIP), column].astype(F32)
            stage[half, here, :] = (mine + early[half, here, :].astype(F32)).astype(BF16)

        strips(early.shape[1], add)
        started.append(link(stage.at[half], late.at[half], sems, 4 + half, second))
        started[-1].start()


def reduce_arrived(started, half):
    started[2 + half].wait_recv()
    started[4 + half].wait_recv()


def reduced(part, piece, me, slots, half, start):
    _, direct, late, _ = slots
    row, column = piece(me, half)
    here = pl.ds(start, STRIP)
    total = part[pl.ds(row.start + start, STRIP), column].astype(F32)
    return total + direct[half, here, :].astype(F32) + late[half, here, :].astype(F32)


def gather_begin(out, piece, peers, sems, half):
    me, across, along, far = peers
    here = out.at[piece(me, half)]
    order = ((along, 0), (across, 1)) if half == 0 else ((across, 1), (along, 0))
    started = {}
    for other, way in order:
        copy = link(here, here, sems, 2 * half + way, other)
        copy.start()
        started[way] = copy
    return started


def gather_finish(out, piece, peers, sems, zero, one):
    me, across, along, far = peers
    zero[0].wait_recv()
    passing = out.at[piece(along, 0)]
    first = link(passing, passing, sems, 4, across)
    first.start()
    one[1].wait_recv()
    passing = out.at[piece(across, 1)]
    second = link(passing, passing, sems, 5, along)
    second.start()
    zero[1].wait_recv()
    one[0].wait_recv()
    first.wait_recv()
    second.wait_recv()
    for copy in (zero[0], zero[1], one[0], one[1], first, second):
        copy.wait_send()


def column_piece(count, own):
    def piece(owner, half):
        size = count // 2
        return pl.ds(half * size, size), pl.ds(pl.multiple_of(owner * own, LANES), own)

    return piece


def row_piece(count, width):
    def piece(owner, half):
        size = count // 4
        return (
            pl.ds(pl.multiple_of(owner * size, size), size),
            pl.ds(half * (width // 2), width // 2),
        )

    return piece


def reduce_scratch(rows, columns):
    return [pltpu.VMEM((2, rows, columns), BF16)] * 4


def copy_sems(count):
    return [pltpu.SemaphoreType.DMA((count,)), pltpu.SemaphoreType.DMA((count,))]


def comm_params(ident):
    return params(collective_id=ident, has_side_effects=True)


def own_slice(source, target, sem, own):
    start = pl.multiple_of(lax.axis_index("section") * own, LANES)
    return pltpu.make_async_copy(source.at[:, pl.ds(start, own)], target, sem)


def gather_kernel(own_ref, out_ref, send, recv):
    count, own = own_ref.shape
    peers = plane()
    piece = column_piece(count, own)
    mine = pl.ds(pl.multiple_of(peers[0] * own, LANES), own)
    out_ref[:, mine] = own_ref[...]
    greet(peers[1], peers[2])
    zero = gather_begin(out_ref, piece, peers, (send, recv), 0)
    one = gather_begin(out_ref, piece, peers, (send, recv), 1)
    gather_finish(out_ref, piece, peers, (send, recv), zero, one)


def gather_columns(own, sections, ident):
    count, width = own.shape
    return pl.pallas_call(
        gather_kernel,
        out_shape=shape((count, width * sections), BF16),
        in_specs=[vmem()],
        out_specs=vmem(),
        scratch_shapes=copy_sems(6),
        compiler_params=comm_params(ident),
    )(own)


def stats_total(stats, got, stage, peers, sems, index):
    me, across, along, far = peers
    first = link(stats, got.at[0], sems, index, across)
    first.start()
    first.wait_recv()
    stage[...] = stats[...] + got[0]
    second = link(stage, got.at[1], sems, index + 1, along)
    second.start()
    second.wait_recv()
    first.wait_send()
    second.wait_send()
    return stage[...] + got[1]


def gather_stats_kernel(own_ref, stats_ref, out_ref, total_ref, got, stage, send, recv):
    count, own = own_ref.shape
    peers = plane()
    piece = column_piece(count, own)
    mine = pl.ds(pl.multiple_of(peers[0] * own, LANES), own)
    out_ref[:, mine] = own_ref[...]
    greet(peers[1], peers[2])
    sems = (send, recv)
    zero = gather_begin(out_ref, piece, peers, sems, 0)
    one = gather_begin(out_ref, piece, peers, sems, 1)
    total_ref[...] = stats_total(stats_ref, got, stage, peers, sems, 6)
    gather_finish(out_ref, piece, peers, sems, zero, one)


def gather_stats(own, stats, sections, ident):
    count, width = own.shape
    return pl.pallas_call(
        gather_stats_kernel,
        out_shape=(shape((count, width * sections), BF16), shape(stats.shape, F32)),
        in_specs=[vmem()] * 2,
        out_specs=(vmem(), vmem()),
        scratch_shapes=[pltpu.VMEM((2,) + stats.shape, F32), pltpu.VMEM(stats.shape, F32)]
        + copy_sems(8),
        compiler_params=comm_params(ident),
    )(own, stats)


def attention_join_kernel(
    part_ref,
    update_ref,
    cand_ref,
    x_ref,
    out_ref,
    hidden_ref,
    early,
    direct,
    late,
    stage,
    x_own,
    local_sem,
    send,
    recv,
    send_g,
    recv_g,
):
    count, own = update_ref.shape
    peers = plane()
    me = peers[0]
    piece = column_piece(count, own)
    slots = (early, direct, late, stage)
    fetch = own_slice(x_ref, x_own, local_sem, own)
    fetch.start()
    greet(peers[1], peers[2])
    started = reduce_begin(part_ref, piece, peers, slots, (send, recv))
    fetch.wait()
    reduce_forward(part_ref, piece, peers, slots, (send, recv), started)
    begun = []
    mine = pl.ds(pl.multiple_of(me * own, LANES), own)
    for half in range(2):
        reduce_arrived(started, half)

        def finish(start):
            here = pl.ds(half * (count // 2) + start, STRIP)
            pre = cand_ref[here, :].astype(F32) + reduced(part_ref, piece, me, slots, half, start)
            hidden_ref[here, :] = pre.astype(BF16)
            x = x_own[here, :].astype(F32)
            made = x + sigmoid(update_ref[here, :].astype(F32)) * (silu(pre) - x)
            out_ref[here, mine] = made.astype(BF16)

        strips(count // 2, finish)
        begun.append(gather_begin(out_ref, piece, peers, (send_g, recv_g), half))
    gather_finish(out_ref, piece, peers, (send_g, recv_g), begun[0], begun[1])
    for copy in started:
        copy.wait_send()


def attention_join(part, update, cand, x, ident):
    count, width = part.shape
    own = update.shape[1]
    return pl.pallas_call(
        attention_join_kernel,
        out_shape=(shape((count, width), BF16), shape((count, own), BF16)),
        in_specs=[vmem(), vmem(), vmem(), hbm()],
        out_specs=(vmem(), vmem()),
        scratch_shapes=reduce_scratch(count // 2, own)
        + [pltpu.VMEM((count, own), BF16), pltpu.SemaphoreType.DMA]
        + copy_sems(6)
        + copy_sems(6),
        compiler_params=comm_params(ident),
    )(part, update, cand, x)


def feed_join_kernel(
    part_ref,
    bias_ref,
    x_ref,
    out_ref,
    early,
    direct,
    late,
    stage,
    x_own,
    local_sem,
    send,
    recv,
    send_g,
    recv_g,
):
    count = part_ref.shape[0]
    own = bias_ref.shape[1]
    peers = plane()
    me = peers[0]
    piece = column_piece(count, own)
    slots = (early, direct, late, stage)
    fetch = own_slice(x_ref, x_own, local_sem, own)
    fetch.start()
    greet(peers[1], peers[2])
    started = reduce_begin(part_ref, piece, peers, slots, (send, recv))
    fetch.wait()
    reduce_forward(part_ref, piece, peers, slots, (send, recv), started)
    begun = []
    mine = pl.ds(pl.multiple_of(me * own, LANES), own)
    for half in range(2):
        reduce_arrived(started, half)

        def finish(start):
            here = pl.ds(half * (count // 2) + start, STRIP)
            total = reduced(part_ref, piece, me, slots, half, start)
            made = x_own[here, :].astype(F32) + total + bias_ref[...]
            out_ref[here, mine] = made.astype(BF16)

        strips(count // 2, finish)
        begun.append(gather_begin(out_ref, piece, peers, (send_g, recv_g), half))
    gather_finish(out_ref, piece, peers, (send_g, recv_g), begun[0], begun[1])
    for copy in started:
        copy.wait_send()


def feed_join(part, bias, x, ident):
    count, width = part.shape
    own = bias.shape[1]
    return pl.pallas_call(
        feed_join_kernel,
        out_shape=shape((count, width), BF16),
        in_specs=[vmem(), vmem(), hbm()],
        out_specs=vmem(),
        scratch_shapes=reduce_scratch(count // 2, own)
        + [pltpu.VMEM((count, own), BF16), pltpu.SemaphoreType.DMA]
        + copy_sems(6)
        + copy_sems(6),
        compiler_params=comm_params(ident),
    )(part, bias, x)


def feed_last_kernel(
    part_ref, bias_ref, x_ref, out_ref, early, direct, late, stage, x_own, local_sem, send, recv
):
    count, width = part_ref.shape
    quarter = count // 4
    peers = plane()
    me = peers[0]
    piece = row_piece(count, width)
    slots = (early, direct, late, stage)
    mine = pl.ds(pl.multiple_of(me * quarter, quarter), quarter)
    fetch = pltpu.make_async_copy(x_ref.at[mine, :], x_own, local_sem)
    fetch.start()
    greet(peers[1], peers[2])
    started = reduce_begin(part_ref, piece, peers, slots, (send, recv))
    fetch.wait()
    reduce_forward(part_ref, piece, peers, slots, (send, recv), started)
    for half in range(2):
        reduce_arrived(started, half)
        lanes = slice(half * (width // 2), (half + 1) * (width // 2))

        def finish(start):
            here = pl.ds(start, STRIP)
            total = reduced(part_ref, piece, me, slots, half, start)
            made = x_own[here, lanes].astype(F32) + total + bias_ref[:, lanes]
            out_ref[here, lanes] = made.astype(BF16)

        strips(quarter, finish)
    for copy in started:
        copy.wait_send()


def feed_last(part, bias, x, ident):
    count, width = part.shape
    quarter = count // 4
    return pl.pallas_call(
        feed_last_kernel,
        out_shape=shape((quarter, width), BF16),
        in_specs=[vmem(), vmem(), hbm()],
        out_specs=vmem(),
        scratch_shapes=reduce_scratch(quarter, width // 2)
        + [pltpu.VMEM((quarter, width), BF16), pltpu.SemaphoreType.DMA]
        + copy_sems(6),
        compiler_params=comm_params(ident),
    )(part, bias, x)


def back_join_kernel(
    part_ref,
    stats_ref,
    scale_ref,
    gain_ref,
    update_ref,
    hidden_ref,
    g_ref,
    n_ref,
    x_ref,
    out_ref,
    gupdate_ref,
    resid_ref,
    early,
    direct,
    late,
    stage,
    g_own,
    n_own,
    x_own,
    got,
    stats_stage,
    means,
    local_sem,
    send,
    recv,
    send_g,
    recv_g,
    send_s,
    recv_s,
):
    count, width = part_ref.shape
    own = update_ref.shape[1]
    peers = plane()
    me = peers[0]
    piece = column_piece(count, own)
    slots = (early, direct, late, stage)
    fetches = [
        own_slice(source, target, local_sem.at[i], own)
        for i, (source, target) in enumerate(((g_ref, g_own), (n_ref, n_own), (x_ref, x_own)))
    ]
    for fetch in fetches:
        fetch.start()
    greet(peers[1], peers[2])
    started = reduce_begin(part_ref, piece, peers, slots, (send, recv))
    total = stats_total(stats_ref, got, stats_stage, peers, (send_s, recv_s), 0)
    means[...] = total.T * (1.0 / width)
    for fetch in fetches:
        fetch.wait()
    reduce_forward(part_ref, piece, peers, slots, (send, recv), started)
    begun = []
    mine = pl.ds(pl.multiple_of(me * own, LANES), own)
    for half in range(2):
        reduce_arrived(started, half)

        def finish(start):
            here = pl.ds(half * (count // 2) + start, STRIP)
            e = reduced(part_ref, piece, me, slots, half, start) * gain_ref[...]
            n = n_own[here, :].astype(F32)
            inner = e - means[here, 0:1] - n * means[here, 1:2]
            g = g_own[here, :].astype(F32) + scale_ref[here, 0:1] * inner
            g = g.astype(BF16).astype(F32)
            u = sigmoid(update_ref[here, :].astype(F32))
            pre = hidden_ref[here, :].astype(F32)
            s = sigmoid(pre)
            x = x_own[here, :].astype(F32)
            gupdate_ref[here, :] = (g * (pre * s - x) * (u * (1.0 - u))).astype(BF16)
            resid_ref[here, :] = g * (1.0 - u)
            out_ref[here, mine] = (g * u * (s * (1.0 + pre * (1.0 - s)))).astype(BF16)

        strips(count // 2, finish)
        begun.append(gather_begin(out_ref, piece, peers, (send_g, recv_g), half))
    gather_finish(out_ref, piece, peers, (send_g, recv_g), begun[0], begun[1])
    for copy in started:
        copy.wait_send()


def back_join(part, stats, scale, gain, update, hidden, g, n, x, ident):
    count, width = part.shape
    own = update.shape[1]
    return pl.pallas_call(
        back_join_kernel,
        out_shape=(
            shape((count, width), BF16),
            shape((count, own), BF16),
            shape((count, own), F32),
        ),
        in_specs=[vmem()] * 6 + [hbm()] * 3,
        out_specs=(vmem(),) * 3,
        scratch_shapes=reduce_scratch(count // 2, own)
        + [pltpu.VMEM((count, own), BF16)] * 3
        + [
            pltpu.VMEM((2, CHUNKS, count), F32),
            pltpu.VMEM((CHUNKS, count), F32),
            pltpu.VMEM((count, CHUNKS), F32),
            pltpu.SemaphoreType.DMA((3,)),
        ]
        + copy_sems(6)
        + copy_sems(6)
        + copy_sems(2),
        compiler_params=comm_params(ident),
    )(part, stats, scale, gain, update, hidden, g, n, x)


def reduce_two_kernel(
    one_ref, two_ref, out_one, out_two, e1, d1, l1, s1, e2, d2, l2, s2, sa, ra, sb, rb
):
    count, own = out_one.shape
    peers = plane()
    me = peers[0]
    piece = column_piece(count, own)
    jobs = (
        (one_ref, out_one, (e1, d1, l1, s1), (sa, ra)),
        (two_ref, out_two, (e2, d2, l2, s2), (sb, rb)),
    )
    greet(peers[1], peers[2])
    begun = [reduce_begin(part, piece, peers, slots, sems) for part, _, slots, sems in jobs]
    for (part, _, slots, sems), started in zip(jobs, begun):
        reduce_forward(part, piece, peers, slots, sems, started)
    for (part, out, slots, sems), started in zip(jobs, begun):
        for half in range(2):
            reduce_arrived(started, half)

            def finish(start):
                here = pl.ds(half * (count // 2) + start, STRIP)
                out[here, :] = reduced(part, piece, me, slots, half, start)

            strips(count // 2, finish)
        for copy in started:
            copy.wait_send()


def reduce_two(one, two, own, ident):
    count = one.shape[0]
    return pl.pallas_call(
        reduce_two_kernel,
        out_shape=(shape((count, own), F32),) * 2,
        in_specs=[vmem()] * 2,
        out_specs=(vmem(),) * 2,
        scratch_shapes=reduce_scratch(count // 2, own) * 2 + copy_sems(6) + copy_sems(6),
        compiler_params=comm_params(ident),
    )(one, two)


def last_rows_kernel(
    z_ref, stats_ref, x_ref, out_ref, land, x_own, got, stats_stage, total_buf, local_sem, send, recv
):
    count, own = z_ref.shape
    quarter, width = out_ref.shape
    peers = plane()
    me = peers[0]

    def rows(owner):
        return pl.ds(pl.multiple_of(owner * quarter, quarter), quarter)

    mine = pl.ds(pl.multiple_of(me * own, LANES), own)
    fetch = pltpu.make_async_copy(x_ref.at[rows(me), :], x_own, local_sem)
    fetch.start()
    land[:, mine] = z_ref[rows(me), :]
    greet(*peers[1:])
    sems = (send, recv)
    copies = []
    for index, other in enumerate(peers[1:]):
        copies.append(link(z_ref.at[rows(other), :], land.at[:, mine], sems, 2 + index, other))
        copies[-1].start()
    total_buf[...] = stats_total(stats_ref, got, stats_stage, peers, sems, 0)
    part = total_buf[:, pl.ds(pl.multiple_of(me * quarter, LANES), quarter)]
    means = part.T * (1.0 / width)
    fetch.wait()
    for copy in copies:
        copy.wait_recv()
    n, scale = normalise(x_own[...].astype(F32))
    g = land[...].astype(F32) - scale * (means[:, 0:1] + n * means[:, 1:2])
    out_ref[...] = g.astype(BF16)
    for copy in copies:
        copy.wait_send()


def last_rows(z, stats, x, ident):
    count, own = z.shape
    width = x.shape[1]
    quarter = count // 4
    return pl.pallas_call(
        last_rows_kernel,
        out_shape=shape((quarter, width), BF16),
        in_specs=[vmem(), vmem(), hbm()],
        out_specs=vmem(),
        scratch_shapes=[
            pltpu.VMEM((quarter, width), BF16),
            pltpu.VMEM((quarter, width), BF16),
            pltpu.VMEM((2,) + stats.shape, F32),
            pltpu.VMEM(stats.shape, F32),
            pltpu.VMEM(stats.shape, F32),
            pltpu.SemaphoreType.DMA,
        ]
        + copy_sems(5),
        compiler_params=comm_params(ident),
    )(z, stats, x)


def interleaved(array, shards, sections, section):
    lead = array.shape[:-1]
    split = array.reshape(lead + (shards, sections, -1))
    return lax.dynamic_index_in_dim(split, section, len(lead) + 1, keepdims=False).reshape(
        lead + (-1,)
    )


def contiguous(array, sections, section):
    size = array.shape[-1] // sections
    return lax.dynamic_slice_in_dim(array, section * size, size, axis=array.ndim - 1)


def put_interleaved(own, shards, sections, section):
    lead = own.shape[:-1]
    own = own.reshape(lead + (shards, 1, -1))
    holder = jnp.zeros(lead + (shards, sections, own.shape[-1]), own.dtype)
    holder = lax.dynamic_update_slice_in_dim(holder, own, section, len(lead) + 1)
    return holder.reshape(lead + (-1,))


def put_contiguous(own, sections, section):
    size = own.shape[-1]
    holder = jnp.zeros(own.shape[:-1] + (size * sections,), own.dtype)
    return lax.dynamic_update_slice_in_dim(holder, own, section * size, own.ndim - 1)


def body(
    tokens,
    lengths,
    cotangent,
    norm_gain,
    norm_shift,
    average_decay,
    average_input,
    average_output,
    average_skip,
    value_weight,
    value_bias,
    base_weight,
    base_bias,
    pair_scale,
    query_shift,
    out_weight,
    feed_gain,
    feed_shift,
    feed_in_weight,
    feed_in_bias,
    feed_out_weight,
    feed_out_bias,
):
    sections = lax.axis_size("section")
    shards = lax.axis_size("dp")
    section = lax.axis_index("section")
    _, count, width = tokens.shape
    layers = norm_gain.shape[0]
    own = width // sections
    wide = value_weight.shape[2]
    keyed = pair_scale.shape[2] * shards
    hidden = feed_in_weight.shape[2]

    base_parts = (
        contiguous(base_weight[..., :width], sections, section),
        base_weight[..., width : width + keyed],
        interleaved(base_weight[..., width + keyed : width + keyed + wide], shards, sections, section),
        contiguous(base_weight[..., width + keyed + wide :], sections, section),
    )
    in_shard = jnp.concatenate(
        (interleaved(value_weight, shards, sections, section),) + base_parts, axis=2
    )

    def quarter_rows(array):
        split = array.reshape(layers, sections, -1, array.shape[2])
        return lax.dynamic_index_in_dim(split, section, 1, keepdims=False)

    out_shard = quarter_rows(out_weight)
    feed_in_shard = interleaved(feed_in_weight, shards, sections, section)
    feed_out_shard = quarter_rows(feed_out_weight)

    def over_dp(array):
        return lax.all_gather(array, "dp", axis=0, tiled=True)

    weights = []
    for layer in range(layers):
        weights.append(
            (
                over_dp(in_shard[layer]),
                over_dp(out_shard[layer]),
                over_dp(feed_in_shard[layer]),
                over_dp(feed_out_shard[layer]),
            )
        )

    smalls = (
        norm_gain,
        norm_shift,
        average_decay,
        average_input,
        average_output,
        average_skip,
        value_bias,
        base_bias,
        pair_scale,
        query_shift,
        feed_gain,
        feed_shift,
        feed_in_bias,
        feed_out_bias,
    )
    packed = jnp.concatenate([a.reshape(layers, -1) for a in smalls], axis=1)
    everyone = lax.all_gather(packed, "dp", axis=0)
    full = []
    low = 0
    for a in smalls:
        size = a.size // layers
        piece = everyone[:, :, low : low + size].reshape((shards,) + a.shape)
        piece = jnp.moveaxis(piece, 0, a.ndim - 1)
        full.append(piece.reshape(a.shape[:-1] + (-1,)))
        low += size
    (
        gain_all,
        shift_all,
        decay_all,
        input_all,
        output_all,
        skip_all,
        value_bias_all,
        base_bias_all,
        pair_all,
        offset_all,
        feed_gain_all,
        feed_shift_all,
        feed_in_bias_all,
        feed_out_bias_all,
    ) = full
    rate_all = jax.nn.sigmoid(contiguous(decay_all, sections, section))
    input_own = contiguous(input_all, sections, section)
    output_own = contiguous(output_all, sections, section)
    drive_all = (1.0 - rate_all) * input_own
    coef_all = drive_all * output_own
    skip_own = contiguous(skip_all, sections, section)
    gain_own = contiguous(gain_all, sections, section)
    shift_own = contiguous(shift_all, sections, section)
    in_bias = jnp.concatenate(
        (
            interleaved(value_bias_all, shards, sections, section),
            contiguous(base_bias_all[:, :width], sections, section),
            base_bias_all[:, width : width + keyed],
            interleaved(
                base_bias_all[:, width + keyed : width + keyed + wide], shards, sections, section
            ),
            contiguous(base_bias_all[:, width + keyed + wide :], sections, section),
        ),
        axis=1,
    )
    feed_in_bias_own = interleaved(feed_in_bias_all, shards, sections, section)
    feed_out_bias_own = contiguous(feed_out_bias_all, sections, section)
    feed_gain_own = contiguous(feed_gain_all, sections, section)

    idents = iter(range(64))
    x = tokens[0]
    kept = []
    for layer in range(layers):
        in_w, out_w, feed_in_w, feed_out_w = weights[layer]
        row = slice(layer, layer + 1)
        normed, mixed_own, pre, own_n, scale = average_forward(
            lengths,
            x,
            gain_all[row],
            shift_all[row],
            rate_all[layer],
            coef_all[layer],
            skip_own[row],
        )
        mixed = gather_columns(mixed_own, sections, next(idents))
        part, update, shared, reset, cand, value, att, gated, probs = attention_forward(
            lengths,
            normed,
            mixed,
            in_w,
            in_bias[row],
            pair_all[layer],
            offset_all[row],
            out_w,
            own,
        )
        middle, hidden_pre = attention_join(part, update, cand, x, next(idents))
        feed_part, feed_pre, feed_n, feed_normed, feed_scale = feed_forward(
            middle,
            feed_gain_all[row],
            feed_shift_all[row],
            feed_in_w,
            feed_in_bias_own[row],
            feed_out_w,
        )
        kept.append(
            dict(
                x=x,
                normed=normed,
                mixed=mixed,
                pre=pre,
                own_n=own_n,
                scale=scale,
                update=update,
                saved=(shared, reset, value, att, probs),
                gated=gated,
                hidden=hidden_pre,
                feed_pre=feed_pre,
                feed_n=feed_n,
                feed_normed=feed_normed,
                feed_scale=feed_scale,
            )
        )
        if layer + 1 < layers:
            x = feed_join(feed_part, feed_out_bias_own[row], middle, next(idents))
        else:
            block_out = feed_last(feed_part, feed_out_bias_all[row], middle, next(idents))

    def weight_grad(left, right):
        return dot(left, right, 0, 0).astype(BF16)

    def scattered(grad):
        return lax.psum_scatter(grad, "dp", scatter_dimension=0, tiled=True)

    given = cotangent[0]
    big = [None] * layers
    small = [None] * layers
    for layer in reversed(range(layers)):
        in_w, out_w, feed_in_w, feed_out_w = weights[layer]
        k = kept[layer]
        row = slice(layer, layer + 1)
        done = feed_backward(
            given, k["feed_pre"], k["feed_n"], feed_gain_all[row], feed_in_w, feed_out_w
        )
        part, stats, gpre, act, feed_sums, feed_bias = done[:6]
        g = done[6] if isinstance(given, tuple) else given
        gout, gupdate, resid = back_join(
            part,
            stats,
            k["feed_scale"],
            feed_gain_own[row],
            k["update"],
            k["hidden"],
            g,
            k["feed_n"],
            k["x"],
            next(idents),
        )
        feed_in_grad = scattered(weight_grad(k["feed_normed"], gpre))
        feed_out_grad = scattered(weight_grad(act, g))
        gmixed_part, gvalue_part, gbase, gvalue, bias_sums, pair_sums = attention_backward(
            lengths,
            gout,
            gupdate,
            k["saved"],
            in_w,
            pair_all[layer],
            offset_all[row],
            out_w,
        )
        gmixed, gnormed = reduce_two(gmixed_part, gvalue_part, own, next(idents))
        in_grad = scattered(
            jnp.concatenate(
                (weight_grad(k["normed"], gvalue), weight_grad(k["mixed"], gbase)), axis=1
            )
        )
        out_grad = scattered(weight_grad(k["gated"], gout))
        z, zstats, of_states, of_slopes, channel_sums = average_backward(
            lengths,
            gmixed,
            gnormed,
            k["pre"],
            k["own_n"],
            k["scale"],
            resid,
            gain_own[row],
            shift_own[row],
            rate_all[layer],
            coef_all[layer],
            skip_own[row],
        )
        if layer:
            whole_z, total = gather_stats(z, zstats, sections, next(idents))
            given = (whole_z, total, k["x"])
        else:
            input_grad = last_rows(z, zstats, k["x"], next(idents))
        big[layer] = (in_grad, out_grad, feed_in_grad, feed_out_grad)

        rate, drive = rate_all[layer], drive_all[layer]
        gdrive = output_own[layer] * of_states
        grate = coef_all[layer] * of_slopes - input_own[layer] * gdrive
        half_wide = wide // sections
        offsets = (half_wide, half_wide + own, half_wide + own + keyed)
        bias = bias_sums[0]
        base_bias_grad = jnp.concatenate(
            (
                put_contiguous(bias[offsets[0] : offsets[1]], sections, section),
                bias[offsets[1] : offsets[2]],
                put_interleaved(
                    bias[offsets[2] : offsets[2] + half_wide], shards, sections, section
                ),
                put_contiguous(bias[offsets[2] + half_wide :], sections, section),
            )
        )
        alone = (section == 0).astype(F32)
        small[layer] = (
            put_contiguous(channel_sums[0], sections, section),
            put_contiguous(channel_sums[1], sections, section),
            put_contiguous(grate * rate * (1.0 - rate), sections, section),
            put_contiguous((1.0 - rate) * gdrive, sections, section),
            put_contiguous(drive * of_states, sections, section),
            put_contiguous(channel_sums[2], sections, section),
            put_interleaved(bias[:half_wide], shards, sections, section),
            base_bias_grad,
            pair_sums[0:2],
            pair_sums[2],
            feed_sums[0],
            feed_sums[1],
            put_interleaved(feed_bias[0], shards, sections, section),
            feed_sums[2] * alone,
        )

    def to_shards(array):
        lead = array.shape[:-1]
        split = array.reshape(lead + (shards, -1))
        return jnp.moveaxis(split, len(lead), 0).reshape(shards, -1)

    small_totals = []
    for layer in range(layers):
        rows = jnp.concatenate([to_shards(a) for a in small[layer]], axis=1)
        mine = lax.psum_scatter(rows, "dp", scatter_dimension=0, tiled=True)
        small_totals.append(lax.psum(mine[0], "section"))
    small_outs = []
    low = 0
    for a in smalls:
        size = a.size // layers
        small_outs.append(
            jnp.stack([t[low : low + size].reshape(a.shape[1:]) for t in small_totals])
        )
        low += size

    def over_sections(array):
        return lax.all_gather(array, "section", axis=0)

    def join_interleaved(array):
        split = array.reshape(array.shape[:2] + (shards, -1))
        return split.transpose(1, 2, 0, 3).reshape(array.shape[1], -1)

    def join_contiguous(array):
        return array.transpose(1, 0, 2).reshape(array.shape[1], -1)

    value_grads, base_grads, out_grads, feed_in_grads, feed_out_grads = [], [], [], [], []
    half_wide = wide // sections
    for layer in range(layers):
        in_grad, out_grad, feed_in_grad, feed_out_grad = (over_sections(a) for a in big[layer])
        value_grads.append(join_interleaved(in_grad[..., :half_wide]).astype(F32))
        low = half_wide + own
        base_grads.append(
            jnp.concatenate(
                (
                    join_contiguous(in_grad[..., half_wide:low]).astype(F32),
                    jnp.sum(in_grad[..., low : low + keyed].astype(F32), axis=0),
                    join_interleaved(in_grad[..., low + keyed : low + keyed + half_wide]).astype(F32),
                    join_contiguous(in_grad[..., low + keyed + half_wide :]).astype(F32),
                ),
                axis=1,
            )
        )
        out_grads.append(out_grad.reshape(-1, width).astype(F32))
        feed_in_grads.append(join_interleaved(feed_in_grad).astype(F32))
        feed_out_grads.append(feed_out_grad.reshape(-1, width).astype(F32))
    (
        g_gain,
        g_shift,
        g_decay,
        g_input,
        g_output,
        g_skip,
        g_value_bias,
        g_base_bias,
        g_pair,
        g_query,
        g_feed_gain,
        g_feed_shift,
        g_feed_in_bias,
        g_feed_out_bias,
    ) = small_outs
    return (
        block_out[None],
        input_grad[None],
        g_gain,
        g_shift,
        g_decay,
        g_input,
        g_output,
        g_skip,
        jnp.stack(value_grads),
        g_value_bias,
        jnp.stack(base_grads),
        g_base_bias,
        g_pair,
        g_query,
        jnp.stack(out_grads),
        g_feed_gain,
        g_feed_shift,
        jnp.stack(feed_in_grads),
        g_feed_in_bias,
        jnp.stack(feed_out_grads),
        g_feed_out_bias,
    )


def solution(mesh):
    row, row2 = P(None, "dp"), P(None, "dp", None)
    deep = P(None, None, "dp")
    in_specs = (
        P("dp", None, None),
        P("dp"),
        P("dp", None, None),
        row,
        row,
        deep,
        deep,
        deep,
        row,
        row2,
        row,
        row2,
        row,
        deep,
        row,
        row2,
        row,
        row,
        row2,
        row,
        row2,
        row,
    )
    out_specs = (
        P("dp", "section", None),
        P("dp", "section", None),
        row,
        row,
        deep,
        deep,
        deep,
        row,
        row2,
        row,
        row2,
        row,
        deep,
        row,
        row2,
        row,
        row,
        row2,
        row,
        row2,
        row,
    )
    return jax.shard_map(body, mesh=mesh, in_specs=in_specs, out_specs=out_specs, check_vma=False)
```

time: 7470 us -> 1200 us (0.16)
  matrix products: 3320 us -> 44.6 us
  local copies, waits for them, and re-layouts: 1330 us -> 106 us
  waiting for transfers between devices: 1570 us -> 424 us
  other arithmetic: 852 us -> 36.5 us
  Pallas kernels: 0 us -> 522 us
  blocking collectives: 224 us -> 38.5 us
    dot_general x248 -> x10, matrix products: 3320 us -> 44.6 us  [dot(): lax.dot_general(left, right, (((left_dim,), (right_dim,)), ((), ())), pre...]
    gather x32 -> x0, local copies, waits for them, and re-layouts: 784 us -> none  [moving_average(): kernel[jnp.clip(lag, 0, block - 1)]]
    ppermute x22 -> x0, waiting for transfers between devices: 782 us -> none  [shifted_2(): lax.ppermute(value, axis, [(source, source + steps) for source in range(i...]
    pallas_call x0 -> x24, Pallas kernels: none -> 522 us  [the longest x2 82.7 us: back_join(): pl.pallas_call(back_join_kernel, out_shape=(shape((count, width), BF16),...]
    scatter-add x8 -> x0, other arithmetic: 291 us -> none  [moving_average(): kernel[jnp.clip(lag, 0, block - 1)]]
    reduce_sum x96 -> x2, other arithmetic: 223 us -> 1.98 us  [body(): jnp.sum(in_grad[..., low:low + keyed].astype(F32), axis=0)]
    select_n x24 -> x0, local copies, waits for them, and re-layouts: 198 us -> none  [the longest x8 197 us: moving_average(): jnp.where((lag >= 0)[:, :, None], kernel[jnp.clip(lag, 0, block - 1)], 0.0)]
    reduce_scatter x7 -> x8, waiting for transfers between devices: 387 us -> 227 us  [scattered(): return lax.psum_scatter(grad, 'dp', scatter_dimension=0, tiled=True)]
  transfers between devices with their start and end apart: 39 -> 24, of which waited for: 25 -> 16; matrix products, arithmetic and copies ran while one was open for 3% -> 11% of each run, Pallas kernels for 0% -> 21%
where the time goes in v1:
time: 1200 us; the launch traced here: 1190 us
  Pallas kernels  522 us (44%)
  waiting for transfers between devices  424 us (35%)
  local copies, waits for them, and re-layouts  106 us (9%)
  matrix products  44.6 us (4%)
  blocking collectives  38.5 us (3%)
  other arithmetic  36.5 us (3%)
  between operations  16.7 us (1%)
    reduce_scatter x8, waiting for transfers between devices, scattered(): return lax.psum_scatter(grad, 'dp', scatter_dimension=0, tiled=True)  227 us
    all_gather x6, waiting for transfers between devices, over_sections(): return lax.all_gather(array, 'section', axis=0)  150 us
    pallas_call x2, Pallas kernels, back_join(): pl.pallas_call(back_join_kernel, out_shape=(shape((count, width), BF16),...  82.7 us
    pallas_call x2, Pallas kernels, attention_join(): pl.pallas_call(attention_join_kernel, out_shape=(shape((count, width), BF...  78.2 us
    pallas_call x2, Pallas kernels, reduce_two(): pl.pallas_call(reduce_two_kernel, out_shape=(shape((count, own), F32),) *...  57.3 us
    dot_general x10, matrix products, dot(): lax.dot_general(left, right, (((left_dim,), (right_dim,)), ((), ())), pre...  44.6 us
    pallas_call x2, Pallas kernels, average_backward(): pl.pallas_call(average_backward_kernel, out_shape=(shape((count, own), BF...  43.3 us
    pallas_call x2, Pallas kernels, gather_columns(): pl.pallas_call(gather_kernel, out_shape=shape((count, width * sections),...  43.3 us
  transfers between devices with their start and end apart: 24, of which 16 were waited for; matrix products, arithmetic and copies ran while one was open for 11% of the time, Pallas kernels for 21%

profile of v1, /device:TPU:0, one launch (start us, length us, event | category | flops | bytes accessed | tf_op | source)
XLA Modules:
  0.0 1189.0 jit_solution(2105069431301242834)
XLA Ops:
  28.9 16.6 %all-gather.15 = f32[8,2,8256]{2,1,0:T(2,128)S(1)} all-gather(f32[1,2,8256]{2,1,0:T(2,128)S(1)} %bitcast.450), channel_id=2, replica_groups=mesh['section'=4,'dp'=8] {'dp'}, dimensions={0}, use_global_device_ids=true | all-gather | bytes 594432 | tf_op jit(solution)/shard_map/all_gather | solution.py:1438
  50.3 13.6 %shard_map.373 = (bf16[1024,1024]{1,0:T(8,128)(2,1)}, bf16[1024,256]{1,0:T(8,128)(2,1)}, bf16[1024,256]{1,0:T(8,128)(2,1)}, f32[1024,256]{1,0:T(8,128)}, f32[1024,128]{1,0:T(8,128)}) custom-call(s32[1]{0:T(128)S(6)} %copy.210.length_ref, bf16[1024,1024]{1,0:T(8,128)(2,1)} %bitcast.393, f32[1,1024]{1,0:T(1,128)} %get-tuple-element.346.gain_ref, ...), custom_call_target="tpu_custom_call" | custom-call | tf_op jit(solution)/shard_map/pallas_call | solution.py:213
  63.9 24.5 %shard_map.374.mixed_ref = bf16[1024,1024]{1,0:T(8,128)(2,1)} custom-call(bf16[1024,256]{1,0:T(8,128)(2,1)} %get-tuple-element.111.own_ref), custom_call_target="tpu_custom_call" | custom-call | tf_op jit(solution)/shard_map/pallas_call | solution.py:904
  96.8 11.8 shard_map.375
  108.6 41.4 %shard_map.376 = (bf16[1024,1024]{1,0:T(8,128)(2,1)}, bf16[1024,256]{1,0:T(8,128)(2,1)}) custom-call(bf16[1024,1024]{1,0:T(8,128)(2,1)} %get-tuple-element.112.part_ref, bf16[1024,256]{1,0:T(8,128)(2,1)} %get-tuple-element.113.update_ref, bf16[1024,256]{1,0:T(8,128)(2,1)} %get-tuple-element.114.cand_ref, bf16[1024,1024]{1,0:T(8,128)(2,1)} %bitcast.394), custom_call_target="tpu_custom_call" | custom-call | tf_op jit(solution)/shard_map/pallas_call | solution.py:1007
  150.1 10.1 shard_map.377
  160.2 37.2 %shard_map.378.x_ref.refs_2_ = bf16[1024,1024]{1,0:T(8,128)(2,1)} custom-call(bf16[1024,1024]{1,0:T(8,128)(2,1)} %get-tuple-element.116.part_ref, f32[1,256]{1,0:T(1,128)} %constant_dynamic-slice_fusion.7.bias_ref, bf16[1024,1024]{1,0:T(8,128)(2,1)} %get-tuple-element.115.x_ref), custom_call_target="tpu_custom_call" | custom-call | tf_op jit(solution)/shard_map/pallas_call | solution.py:1069
  198.8 13.4 %shard_map.379 = (bf16[1024,1024]{1,0:T(8,128)(2,1)}, bf16[1024,256]{1,0:T(8,128)(2,1)}, bf16[1024,256]{1,0:T(8,128)(2,1)}, f32[1024,256]{1,0:T(8,128)}, f32[1024,128]{1,0:T(8,128)}) custom-call(s32[1]{0:T(128)S(6)} %copy.210.length_ref, bf16[1024,1024]{1,0:T(8,128)(2,1)} %shard_map.378.x_ref.refs_2_, f32[1,1024]{1,0:T(1,128)} %get-tuple-element.345.gain_ref, ...), custom_call_target="tpu_custom_call" | custom-call | tf_op jit(solution)/shard_map/pallas_call | solution.py:213
  212.2 18.8 %shard_map.380.mixed_ref = bf16[1024,1024]{1,0:T(8,128)(2,1)} custom-call(bf16[1024,256]{1,0:T(8,128)(2,1)} %get-tuple-element.118.own_ref), custom_call_target="tpu_custom_call" | custom-call | tf_op jit(solution)/shard_map/pallas_call | solution.py:904
  231.1 11.8 shard_map.381
  242.9 36.8 %shard_map.382 = (bf16[1024,1024]{1,0:T(8,128)(2,1)}, bf16[1024,256]{1,0:T(8,128)(2,1)}) custom-call(bf16[1024,1024]{1,0:T(8,128)(2,1)} %get-tuple-element.119.part_ref, bf16[1024,256]{1,0:T(8,128)(2,1)} %get-tuple-element.120.update_ref, bf16[1024,256]{1,0:T(8,128)(2,1)} %get-tuple-element.121.cand_ref, bf16[1024,1024]{1,0:T(8,128)(2,1)} %shard_map.378.x_ref.refs_2_), custom_call_target="tpu_custom_call" | custom-call | tf_op jit(solution)/shard_map/pallas_call | solution.py:1007
  279.8 10.1 shard_map.383
  289.9 11.6 shard_map.385
  301.5 42.0 %shard_map.386 = (bf16[1024,1024]{1,0:T(8,128)(2,1)}, bf16[1024,256]{1,0:T(8,128)(2,1)}, f32[1024,256]{1,0:T(8,128)}) custom-call(bf16[1024,1024]{1,0:T(8,128)(2,1)} %get-tuple-element.126.part_ref, f32[8,1024]{1,0:T(8,128)} %get-tuple-element.127.stats_ref, f32[1024,128]{1,0:T(8,128)} %get-tuple-element.128.scale_ref, ...), custom_call_target="tpu_custom_call" | custom-call | tf_op jit(solution)/shard_map/pallas_call | solution.py:1208
  343.5 13.8 %shard_map.387 = (bf16[1024,1024]{1,0:T(8,128)(2,1)}, bf16[1024,1024]{1,0:T(8,128)(2,1)}, bf16[1024,1152]{1,0:T(8,128)(2,1)}, bf16[1024,512]{1,0:T(8,128)(2,1)}, f32[8,1664]{1,0:T(8,128)}, /*index=5*/f32[8,128]{1,0:T(8,128)}) custom-call(s32[1]{0:T(128)S(6)} %copy.210.length_ref, bf16[1024,1024]{1,0:T(8,128)(2,1)} %get-tuple-element.130.gout_ref, ...), custom_call_target="tpu_custom_call" | custom-call | tf_op jit(solution)/shard_map/pallas_call | solution.py:584
  360.9 32.2 %shard_map.388 = (f32[1024,256]{1,0:T(8,128)}, f32[1024,256]{1,0:T(8,128)}) custom-call(bf16[1024,1024]{1,0:T(8,128)(2,1)} %get-tuple-element.137.one_ref, bf16[1024,1024]{1,0:T(8,128)(2,1)} %get-tuple-element.138.two_ref), custom_call_target="tpu_custom_call" | custom-call | tf_op jit(solution)/shard_map/pallas_call | solution.py:1262
  393.1 21.7 %shard_map.389 = (bf16[1024,256]{1,0:T(8,128)(2,1)}, f32[8,1024]{1,0:T(8,128)}, f32[16,256]{1,0:T(8,128)}, f32[16,256]{1,0:T(8,128)}, f32[8,256]{1,0:T(8,128)}) custom-call(s32[1]{0:T(128)S(6)} %copy.210.length_ref, f32[1024,256]{1,0:T(8,128)} %get-tuple-element.139.gmixed_ref, f32[1024,256]{1,0:T(8,128)} %get-tuple-element.140.gvalue_ref, ...), custom_call_target="tpu_custom_call" | custom-call | tf_op jit(solution)/shard_map/pallas_call | solution.py:383
  414.8 22.9 %shard_map.390 = (bf16[1024,1024]{1,0:T(8,128)(2,1)}, f32[8,1024]{1,0:T(8,128)}) custom-call(bf16[1024,256]{1,0:T(8,128)(2,1)} %get-tuple-element.145.own_ref, f32[8,1024]{1,0:T(8,128)} %get-tuple-element.146.stats_ref), custom_call_target="tpu_custom_call" | custom-call | tf_op jit(solution)/shard_map/pallas_call | solution.py:944
  437.7 14.0 %shard_map.391 = (bf16[1024,1024]{1,0:T(8,128)(2,1)}, f32[8,1024]{1,0:T(8,128)}, bf16[1024,1024]{1,0:T(8,128)(2,1)}, bf16[1024,1024]{1,0:T(8,128)(2,1)}, f32[8,1...) custom-call(bf16[1024,1024]{1,0:T(8,128)(2,1)} %get-tuple-element.147.refs_0_, ...), custom_call_target="tpu_custom_call" | custom-call | tf_op jit(solution)/shard_map/pallas_call | solution.py:720
  451.6 40.7 %shard_map.392 = (bf16[1024,1024]{1,0:T(8,128)(2,1)}, bf16[1024,256]{1,0:T(8,128)(2,1)}, f32[1024,256]{1,0:T(8,128)}) custom-call(bf16[1024,1024]{1,0:T(8,128)(2,1)} %get-tuple-element.151.part_ref, f32[8,1024]{1,0:T(8,128)} %get-tuple-element.152.stats_ref, f32[1024,128]{1,0:T(8,128)} %get-tuple-element.153.scale_ref, ...), custom_call_target="tpu_custom_call" | custom-call | tf_op jit(solution)/shard_map/pallas_call | solution.py:1208
  492.3 13.4 %shard_map.393 = (bf16[1024,1024]{1,0:T(8,128)(2,1)}, bf16[1024,1024]{1,0:T(8,128)(2,1)}, bf16[1024,1152]{1,0:T(8,128)(2,1)}, bf16[1024,512]{1,0:T(8,128)(2,1)}, f32[8,1664]{1,0:T(8,128)}, /*index=5*/f32[8,128]{1,0:T(8,128)}) custom-call(s32[1]{0:T(128)S(6)} %copy.210.length_ref, bf16[1024,1024]{1,0:T(8,128)(2,1)} %get-tuple-element.156.gout_ref, ...), custom_call_target="tpu_custom_call" | custom-call | tf_op jit(solution)/shard_map/pallas_call | solution.py:584
  512.2 25.1 %shard_map.394 = (f32[1024,256]{1,0:T(8,128)}, f32[1024,256]{1,0:T(8,128)}) custom-call(bf16[1024,1024]{1,0:T(8,128)(2,1)} %get-tuple-element.163.one_ref, bf16[1024,1024]{1,0:T(8,128)(2,1)} %get-tuple-element.164.two_ref), custom_call_target="tpu_custom_call" | custom-call | tf_op jit(solution)/shard_map/pallas_call | solution.py:1262
  537.3 21.7 %shard_map.395 = (bf16[1024,256]{1,0:T(8,128)(2,1)}, f32[8,1024]{1,0:T(8,128)}, f32[16,256]{1,0:T(8,128)}, f32[16,256]{1,0:T(8,128)}, f32[8,256]{1,0:T(8,128)}) custom-call(s32[1]{0:T(128)S(6)} %copy.210.length_ref, f32[1024,256]{1,0:T(8,128)} %get-tuple-element.165.gmixed_ref, f32[1024,256]{1,0:T(8,128)} %get-tuple-element.166.gvalue_ref, ...), custom_call_target="tpu_custom_call" | custom-call | tf_op jit(solution)/shard_map/pallas_call | solution.py:383
  568.9 5.9 convolution_convert_fusion.4
  576.5 5.3 convolution_convert_fusion.5
  583.4 5.3 convolution_convert_fusion.2
  590.3 5.4 convolution_convert_fusion.3
  614.4 5.8 convolution_convert_fusion.1
  640.5 21.7 %reduce-scatter.19.cloned.1.call-done = bf16[128,1024]{1,0:T(8,128)(2,1)} async-done(((bf16[1024,1024]{1,0:T(8,128)(2,1)}), bf16[128,1024]{1,0:T(8,128)(2,1)}) %reduce-scatter.19.cloned.1.call-update) | async-done | bytes 262160 | tf_op jit(solution)/shard_map/reduce_scatter | solution.py:1550
  662.2 36.7 %reduce-scatter.17.cloned.1.call-done = bf16[128,1024]{1,0:T(8,128)(2,1)} async-done(((bf16[1024,1024]{1,0:T(8,128)(2,1)}), bf16[128,1024]{1,0:T(8,128)(2,1)}) %reduce-scatter.17.cloned.1.call-update) | async-done | bytes 262160 | tf_op jit(solution)/shard_map/reduce_scatter | solution.py:1550
  699.0 36.6 %reduce-scatter.23.cloned.1.call-done = bf16[128,1024]{1,0:T(8,128)(2,1)} async-done(((bf16[1024,1024]{1,0:T(8,128)(2,1)}), bf16[128,1024]{1,0:T(8,128)(2,1)}) %reduce-scatter.23.cloned.1.call-update) | async-done | bytes 262160 | tf_op jit(solution)/shard_map/reduce_scatter | solution.py:1550
  735.7 36.7 %reduce-scatter.21.cloned.1.call-done = bf16[128,1024]{1,0:T(8,128)(2,1)} async-done(((bf16[1024,1024]{1,0:T(8,128)(2,1)}), bf16[128,1024]{1,0:T(8,128)(2,1)}) %reduce-scatter.21.cloned.1.call-update) | async-done | bytes 262160 | tf_op jit(solution)/shard_map/reduce_scatter | solution.py:1550
  773.1 20.3 %shard_map.384 = bf16[256,1024]{1,0:T(8,128)(2,1)} custom-call(bf16[1024,1024]{1,0:T(8,128)(2,1)} %get-tuple-element.123.part_ref, f32[1,1024]{1,0:T(1,128)} %slice_bitcast_fusion.26.bias_ref, bf16[1024,1024]{1,0:T(8,128)(2,1)} %get-tuple-element.122.x_ref), custom_call_target="tpu_custom_call" | custom-call | tf_op jit(solution)/shard_map/pallas_call | solution.py:1116
  793.4 12.7 %shard_map.396 = bf16[256,1024]{1,0:T(8,128)(2,1)} custom-call(bf16[1024,256]{1,0:T(8,128)(2,1)} %get-tuple-element.171.z_ref, f32[8,1024]{1,0:T(8,128)} %get-tuple-element.172.stats_ref, bf16[1024,1024]{1,0:T(8,128)(2,1)} %bitcast.396), custom_call_target="tpu_custom_call" | custom-call | tf_op jit(solution)/shard_map/pallas_call | solution.py:1310
  806.1 10.3 reduce-scatter.11.cloned.1.call-done
  816.6 42.5 %all-reduce.9.cloned.1.call-done = (f32[8256]{0:T(1024)}, f32[8256]{0:T(1024)}) async-done(((f32[8256]{0:T(1024)}, f32[8256]{0:T(1024)}), (f32[8256]{0:T(1024)}, f32[8256]{0:T(1024)})) %all-reduce.9.cloned.1.call-update) | async-done | bytes 66064 | tf_op jit(solution)/shard_map/psum | solution.py:1659
  876.7 29.2 %reduce-scatter.9.cloned.1.call-done = bf16[128,1664]{1,0:T(8,128)(2,1)} async-done(((bf16[1024,1664]{1,0:T(8,128)(2,1)}), bf16[128,1664]{1,0:T(8,128)(2,1)}) %reduce-scatter.9.cloned.1.call-update) | async-done | bytes 426000 | tf_op jit(solution)/shard_map/reduce_scatter | solution.py:1550
  907.2 32.5 %reduce-scatter.15.cloned.1.call-done = bf16[64,1024]{1,0:T(8,128)(2,1)} async-done(((bf16[512,1024]{1,0:T(8,128)(2,1)}), bf16[64,1024]{1,0:T(8,128)(2,1)}) %reduce-scatter.15.cloned.1.call-update) | async-done | bytes 131088 | tf_op jit(solution)/shard_map/reduce_scatter | solution.py:1550
  939.7 10.5 all-gather.10
  950.1 23.1 %reduce-scatter.13.cloned.1.call-done = bf16[64,1024]{1,0:T(8,128)(2,1)} async-done(((bf16[512,1024]{1,0:T(8,128)(2,1)}), bf16[64,1024]{1,0:T(8,128)(2,1)}) %reduce-scatter.13.cloned.1.call-update) | async-done | bytes 131088 | tf_op jit(solution)/shard_map/reduce_scatter | solution.py:1550
  973.2 11.5 all-gather.9
  986.2 13.9 %all-gather.53.cloned.1.call-done = bf16[512,1024]{1,0:T(8,128)(2,1)} async-done(((bf16[128,1024]{1,0:T(8,128)(2,1)}), bf16[512,1024]{1,0:T(8,128)(2,1)}) %all-gather.53.cloned.1.call-update) | async-done | bytes 1048592 | tf_op jit(solution)/shard_map/all_gather | solution.py:1670
  1003.8 24.7 %all-gather.51.cloned.1.call-done = bf16[512,1024]{1,0:T(8,128)(2,1)} async-done(((bf16[128,1024]{1,0:T(8,128)(2,1)}), bf16[512,1024]{1,0:T(8,128)(2,1)}) %all-gather.51.cloned.1.call-update) | async-done | bytes 1048592 | tf_op jit(solution)/shard_map/all_gather | solution.py:1670
  1032.3 24.9 %all-gather.57.cloned.1.call-done = bf16[512,1024]{1,0:T(8,128)(2,1)} async-done(((bf16[128,1024]{1,0:T(8,128)(2,1)}), bf16[512,1024]{1,0:T(8,128)(2,1)}) %all-gather.57.cloned.1.call-update) | async-done | bytes 1048592 | tf_op jit(solution)/shard_map/all_gather | solution.py:1670
  1057.2 28.6 %all-gather.55.cloned.1.call-done = bf16[512,1024]{1,0:T(8,128)(2,1)} async-done(((bf16[128,1024]{1,0:T(8,128)(2,1)}), bf16[512,1024]{1,0:T(8,128)(2,1)}) %all-gather.55.cloned.1.call-update) | async-done | bytes 1048592 | tf_op jit(solution)/shard_map/all_gather | solution.py:1670
  1091.9 28.0 %all-gather.49.cloned.1.call-done = bf16[512,1664]{1,0:T(8,128)(2,1)} async-done(((bf16[128,1664]{1,0:T(8,128)(2,1)}), bf16[512,1664]{1,0:T(8,128)(2,1)}) %all-gather.49.cloned.1.call-update) | async-done | bytes 1703952 | tf_op jit(solution)/shard_map/all_gather | solution.py:1670
  1123.8 30.1 %all-gather.47.cloned.1.call-done = bf16[512,1664]{1,0:T(8,128)(2,1)} async-done(((bf16[128,1664]{1,0:T(8,128)(2,1)}), bf16[512,1664]{1,0:T(8,128)(2,1)}) %all-gather.47.cloned.1.call-update) | async-done | bytes 1703952 | tf_op jit(solution)/shard_map/all_gather | solution.py:1670
  1174.3 5.8 copy.128
  (387 shorter events, 159.0 us)
Async XLA Ops:
  7.2 89.6 %all-gather.37.cloned.1.call-start = ((), (), s32[]{:S(2)}) async-start(), calls=%async_computation.19 | async-start | bytes 1179648 | tf_op jit(solution)/shard_map/all_gather | solution.py:1408
  9.0 87.8 %all-gather.35.cloned.1.call-start = ((), (), s32[]{:S(2)}) async-start(), calls=%async_computation.18 | async-start | bytes 3833856 | tf_op jit(solution)/shard_map/all_gather | solution.py:1408
  9.8 5.4 copy-start.4
  16.4 133.7 %all-gather.31.cloned.1.call-start = ((), (), s32[]{:S(2)}) async-start(), calls=%async_computation.8 | async-start | bytes 2359296 | tf_op jit(solution)/shard_map/all_gather | solution.py:1408
  22.8 5.7 copy-start.19
  22.8 5.7 copy-start.25
  22.9 5.8 copy-start.20
  22.9 5.8 copy-start.21
  22.9 5.8 copy-start.22
  22.9 5.8 copy-start.23
  22.9 5.8 copy-start.24
  22.9 5.8 copy-start.26
  22.9 5.8 copy-start.27
  22.9 5.8 copy-start.28
  23.0 5.8 copy-start.29
  23.0 5.8 copy-start.30
  23.0 5.8 copy-start.31
  23.0 5.8 copy-start.32
  23.8 126.4 %all-gather.39.cloned.1.call-start = ((), (), s32[]{:S(2)}) async-start(), calls=%async_computation.20 | async-start | bytes 2359296 | tf_op jit(solution)/shard_map/all_gather | solution.py:1408
  25.7 205.4 %all-gather.43.cloned.1.call-start = ((), (), s32[]{:S(2)}) async-start(), calls=%async_computation.22 | async-start | bytes 1179648 | tf_op jit(solution)/shard_map/all_gather | solution.py:1408
  26.3 204.8 %all-gather.41.cloned.1.call-start = ((), (), s32[]{:S(2)}) async-start(), calls=%async_computation.21 | async-start | bytes 3833856 | tf_op jit(solution)/shard_map/all_gather | solution.py:1408
  26.9 252.9 %all-gather.33.cloned.1.call-start = ((), (), s32[]{:S(2)}) async-start(), calls=%async_computation.9 | async-start | bytes 2359296 | tf_op jit(solution)/shard_map/all_gather | solution.py:1408
  27.7 252.1 %all-gather.45.cloned.1.call-start = ((), (), s32[]{:S(2)}) async-start(), calls=%async_computation.23 | async-start | bytes 2359296 | tf_op jit(solution)/shard_map/all_gather | solution.py:1408
  28.5 594.4 %all-reduce.7.cloned.1.call-start = ((), (), s32[]{:S(2)}) async-start(), calls=%async_computation.30 | async-start | bytes 1064960
  492.3 17.8 %copy-start.17 = (f32[16,256]{1,0:T(8,128)S(1)}, f32[16,256]{1,0:T(8,128)}, u32[]{:S(2)}) copy-start(f32[16,256]{1,0:T(8,128)} %get-tuple-element.182) | copy-start | bytes 49156
  492.3 17.8 %copy-start.18 = (f32[16,256]{1,0:T(8,128)S(1)}, f32[16,256]{1,0:T(8,128)}, u32[]{:S(2)}) copy-start(f32[16,256]{1,0:T(8,128)} %get-tuple-element.181) | copy-start | bytes 49156
  568.9 93.3 %reduce-scatter.19.cloned.1.call-start = ((), (), s32[]{:S(2)}) async-start(), calls=%async_computation.15 | async-start | bytes 2359296 | tf_op jit(solution)/shard_map/reduce_scatter | solution.py:1550
  574.9 124.1 %reduce-scatter.17.cloned.1.call-start = ((), (), s32[]{:S(2)}) async-start(), calls=%async_computation.14 | async-start | bytes 2359296 | tf_op jit(solution)/shard_map/reduce_scatter | solution.py:1550
  581.8 153.8 %reduce-scatter.23.cloned.1.call-start = ((), (), s32[]{:S(2)}) async-start(), calls=%async_computation.17 | async-start | bytes 2359296 | tf_op jit(solution)/shard_map/reduce_scatter | solution.py:1550
  588.7 183.7 %reduce-scatter.21.cloned.1.call-start = ((), (), s32[]{:S(2)}) async-start(), calls=%async_computation.16 | async-start | bytes 2359296 | tf_op jit(solution)/shard_map/reduce_scatter | solution.py:1550
  590.3 5.7 copy-start.34
  595.7 220.8 %reduce-scatter.11.cloned.1.call-start = ((), (), s32[]{:S(2)}) async-start(), calls=%async_computation.11 | async-start | bytes 3833856 | tf_op jit(solution)/shard_map/reduce_scatter | solution.py:1550
  599.5 1.9 copy-start.2
  608.3 250.7 %all-reduce.9.cloned.1.call-start = ((), (), s32[]{:S(2)}) async-start(), calls=%async_computation.31 | async-start | bytes 147456 | tf_op jit(solution)/shard_map/psum | solution.py:1659
  627.5 278.5 %reduce-scatter.9.cloned.1.call-start = ((), (), s32[]{:S(2)}) async-start(), calls=%async_computation.10 | async-start | bytes 3833856 | tf_op jit(solution)/shard_map/reduce_scatter | solution.py:1550
  631.2 308.5 %reduce-scatter.15.cloned.1.call-start = ((), (), s32[]{:S(2)}) async-start(), calls=%async_computation.13 | async-start | bytes 1179648 | tf_op jit(solution)/shard_map/reduce_scatter | solution.py:1550
  632.9 3.6 copy-start.16
  636.5 336.7 %reduce-scatter.13.cloned.1.call-start = ((), (), s32[]{:S(2)}) async-start(), calls=%async_computation.12 | async-start | bytes 1179648 | tf_op jit(solution)/shard_map/reduce_scatter | solution.py:1550
  640.4 359.6 %all-gather.53.cloned.1.call-start = ((), (), s32[]{:S(2)}) async-start(), calls=%async_computation.27 | async-start | bytes 1310720 | tf_op jit(solution)/shard_map/all_gather | solution.py:1670
  662.2 366.3 %all-gather.51.cloned.1.call-start = ((), (), s32[]{:S(2)}) async-start(), calls=%async_computation.26 | async-start | bytes 1310720 | tf_op jit(solution)/shard_map/all_gather | solution.py:1670
  699.0 358.2 %all-gather.57.cloned.1.call-start = ((), (), s32[]{:S(2)}) async-start(), calls=%async_computation.29 | async-start | bytes 1310720 | tf_op jit(solution)/shard_map/all_gather | solution.py:1670
  735.7 350.2 %all-gather.55.cloned.1.call-start = ((), (), s32[]{:S(2)}) async-start(), calls=%async_computation.28 | async-start | bytes 1310720 | tf_op jit(solution)/shard_map/all_gather | solution.py:1670
  772.4 347.5 %all-gather.49.cloned.1.call-start = ((), (), s32[]{:S(2)}) async-start(), calls=%async_computation.25 | async-start | bytes 2129920 | tf_op jit(solution)/shard_map/all_gather | solution.py:1670
  816.5 337.3 %all-gather.47.cloned.1.call-start = ((), (), s32[]{:S(2)}) async-start(), calls=%async_computation.24 | async-start | bytes 2129920 | tf_op jit(solution)/shard_map/all_gather | solution.py:1670
  1119.9 3.0 copy-start.15
  1166.7 2.2 copy-start.13
  1174.3 5.8 copy-start.14
  1174.3 6.6 copy-start.8
  (14 other events, 21.3 us)
Sparse Core Ops, SparseCore 0:
  10.2 24.7 all-gather.36
  37.3 40.0 all-gather.34
  79.5 27.9 all-gather.30
  109.5 28.6 all-gather.38
  139.7 21.5 all-gather.42
  162.8 40.1 all-gather.40
  204.5 27.8 all-gather.32
  234.1 28.5 all-gather.44
  569.0 53.7 all-reduce.6
  625.0 37.1 reduce-scatter.18
  664.5 34.4 reduce-scatter.16
  701.1 34.4 reduce-scatter.22
  737.9 34.4 reduce-scatter.20
  775.2 41.2 reduce-scatter.10
  819.9 39.1 all-reduce.8
  861.9 43.9 reduce-scatter.8
  908.7 30.8 reduce-scatter.14
  942.5 30.7 reduce-scatter.12
  975.2 24.7 all-gather.52
  1001.9 26.6 all-gather.50
  1030.5 26.6 all-gather.56
  1059.2 26.6 all-gather.54
  1087.8 32.0 all-gather.48
  1121.8 32.0 all-gather.46

commit v2 on v1

--- a/solution.py
+++ b/solution.py
@@ -15,6 +15,9 @@
 CHUNKS = 8
 ROWS = 256
 STRIP = 64
+TILE = 128
+UNROLL = 16
+SMALL = 16
 EPS = 1e-05
 NEGATIVE = -1000000000.0
 VMEM_BYTES = 56 * 1024 * 1024
@@ -67,16 +70,20 @@
     return (place < length).astype(F32)
 
 
+def lasting(microseconds):
+    return pl.CostEstimate(
+        flops=int(microseconds * 1.0e9),
+        bytes_accessed=int(microseconds * 3.0e6),
+        transcendentals=0,
+    )
+
+
 def params(**more):
     return pltpu.CompilerParams(vmem_limit_bytes=VMEM_BYTES, **more)
 
 
 def spread_rows(ref, lanes, count):
     return [ref[n, :, lanes] for n in range(count)]
-
-
-def on_sublanes(array):
-    return jnp.broadcast_to(array[:, None, :], (array.shape[0], CHUNKS, array.shape[1]))
 
 
 def power(base, exponent):
@@ -150,6 +157,7 @@
     own = mixed_ref.shape[1]
     dims = rate_ref.shape[0]
     steps = count // CHUNKS
+    pitch = steps + 1
     mine = pl.ds(pl.multiple_of(lax.axis_index("section") * own, LANES), own)
 
     def norm_strip(i, carry):
@@ -163,7 +171,7 @@
         scale_ref[here, :] = jnp.broadcast_to(scale, (STRIP, LANES))
         masked = (part * gain_ref[:, mine] + shift_ref[:, mine]) * row_valid(start, STRIP, length)
         for group in range(own // LANES):
-            m_buf[group, here, :] = masked[:, group * LANES : (group + 1) * LANES]
+            m_buf[group, pl.ds(start + start // steps, STRIP), :] = masked[:, group * LANES : (group + 1) * LANES]
         return carry
 
     lax.fori_loop(0, count // STRIP, norm_strip, 0)
@@ -176,28 +184,30 @@
         m_part, y_part = m_buf.at[group], y_buf.at[group]
 
         def finals(t, states):
-            x = m_part[pl.ds(t, CHUNKS, stride=steps), :]
+            x = m_part[pl.ds(t, CHUNKS, stride=pitch), :]
             return tuple(r * h + x for r, h in zip(rates, states))
 
-        ends = lax.fori_loop(0, steps, finals, blank, unroll=4)
+        ends = lax.fori_loop(0, steps, finals, blank, unroll=UNROLL)
         starts = tuple(entering(h, r, steps) for h, r in zip(ends, rates))
 
         def outputs(t, states):
-            x = m_part[pl.ds(t, CHUNKS, stride=steps), :]
+            x = m_part[pl.ds(t, CHUNKS, stride=pitch), :]
             states = tuple(r * h + x for r, h in zip(rates, states))
             terms = [c * h for c, h in zip(coefs, states)]
             while len(terms) > 1:
                 terms = [a + b for a, b in zip(terms[::2], terms[1::2])]
-            y_part[pl.ds(t, CHUNKS, stride=steps), :] = terms[0]
+            y_part[pl.ds(t, CHUNKS, stride=pitch), :] = terms[0]
             return states
 
-        lax.fori_loop(0, steps, outputs, starts, unroll=4)
+        lax.fori_loop(0, steps, outputs, starts, unroll=UNROLL)
 
     def mix_strip(i, carry):
-        here = pl.ds(pl.multiple_of(i * STRIP, STRIP), STRIP)
+        start = pl.multiple_of(i * STRIP, STRIP)
+        here = pl.ds(start, STRIP)
+        there = pl.ds(start + start // steps, STRIP)
         for group in range(own // LANES):
             lanes = slice(group * LANES, (group + 1) * LANES)
-            pre = y_buf[group, here, :] + skip_ref[:, lanes] * m_buf[group, here, :]
+            pre = y_buf[group, there, :] + skip_ref[:, lanes] * m_buf[group, there, :]
             pre_ref[here, lanes] = pre.astype(BF16)
             mixed_ref[here, lanes] = silu(pre).astype(BF16)
         return carry
@@ -209,7 +219,6 @@
     count, width = x.shape
     own = skip.shape[1]
     groups = own // LANES
-    rate, coef = on_sublanes(rate), on_sublanes(coef)
     return pl.pallas_call(
         average_forward_kernel,
         out_shape=(
@@ -223,14 +232,19 @@
         out_specs=(vmem(),) * 5,
         scratch_shapes=[
             pltpu.VMEM((STRIP, width), F32),
-            pltpu.VMEM((groups, count, LANES), F32),
-            pltpu.VMEM((groups, count, LANES), F32),
+            pltpu.VMEM((groups, count + CHUNKS, LANES), F32),
+            pltpu.VMEM((groups, count + CHUNKS, LANES), F32),
         ],
+        cost_estimate=lasting(13),
         compiler_params=params(),
     )(length, x, gain, shift, rate, coef, skip)
 
 
-def average_backward_kernel(
+def average_backward_kernel(waits, *refs):
+    average_backward_work(*refs[waits:])
+
+
+def average_backward_work(
     length_ref,
     gmixed_ref,
     gvalue_ref,
@@ -238,24 +252,23 @@
     own_ref,
     scale_ref,
     resid_ref,
-    gain_ref,
-    shift_ref,
+    norm_ref,
     rate_ref,
     coef_ref,
     skip_ref,
     z_ref,
     stats_ref,
-    gh_ref,
-    gq_ref,
     sums_ref,
     m_buf,
     g_buf,
     r_buf,
 ):
     length = length_ref[0]
+    gain_ref, shift_ref = norm_ref.at[0:1, :], norm_ref.at[1:2, :]
     count, own = z_ref.shape
     dims = rate_ref.shape[0]
     steps = count // CHUNKS
+    pitch = steps + 1
     groups = own // LANES
     part_size = dims // 2
 
@@ -263,13 +276,14 @@
         start = pl.multiple_of(i * STRIP, STRIP)
         here = pl.ds(start, STRIP)
         valid = row_valid(start, STRIP, length)
+        there = pl.ds(start + start // steps, STRIP)
         for group in range(groups):
             lanes = slice(group * LANES, (group + 1) * LANES)
-            m_buf[group, here, :] = (
+            m_buf[group, there, :] = (
                 own_ref[here, lanes] * gain_ref[:, lanes] + shift_ref[:, lanes]
             ) * valid
             slope = silu_slope(pre_ref[here, lanes].astype(F32))
-            g_buf[group, here, :] = gmixed_ref[here, lanes] * slope
+            g_buf[group, there, :] = gmixed_ref[here, lanes] * slope
         return carry
 
     lax.fori_loop(0, count // STRIP, load_strip, 0)
@@ -281,61 +295,57 @@
         coefs = spread_rows(coef_ref, lanes, dims)
         m_part, g_part, r_part = m_buf.at[group], g_buf.at[group], r_buf.at[group]
 
+        blank = tuple(zero for _ in rates)
+
+        def back_finals(t, carry):
+            states, slopes = carry
+            g = g_part[pl.ds(steps - 1 - t, CHUNKS, stride=pitch), :]
+            slopes = tuple(r * w + h for r, w, h in zip(rates, slopes, states))
+            states = tuple(r * h + g for r, h in zip(rates, states))
+            return states, slopes
+
+        ends, end_slopes = lax.fori_loop(0, steps, back_finals, (blank, blank), unroll=UNROLL)
+        starts = tuple(entering(h, r, steps, reverse=True) for h, r in zip(ends, rates))
+
         for half in range(2):
             some = rates[half * part_size : (half + 1) * part_size]
-            blank = (tuple(zero for _ in some), tuple(zero for _ in some))
-
-            def finals(t, carry):
-                states, slopes = carry
-                x = m_part[pl.ds(t, CHUNKS, stride=steps), :]
-                slopes = tuple(r * q + h for r, q, h in zip(some, slopes, states))
-                states = tuple(r * h + x for r, h in zip(some, states))
-                return states, slopes
-
-            ends, end_slopes = lax.fori_loop(0, steps, finals, blank, unroll=4)
-            pairs = [entering_pair(h, q, r, steps) for h, q, r in zip(ends, end_slopes, some)]
-            begin = (
-                tuple(p[0] for p in pairs),
-                tuple(p[1] for p in pairs),
-                tuple(zero for _ in some),
-                tuple(zero for _ in some),
-            )
+            empty = tuple(zero for _ in some)
 
             def sweep(t, carry):
                 states, slopes, of_states, of_slopes = carry
-                x = m_part[pl.ds(t, CHUNKS, stride=steps), :]
-                g = g_part[pl.ds(t, CHUNKS, stride=steps), :]
+                x = m_part[pl.ds(t, CHUNKS, stride=pitch), :]
+                g = g_part[pl.ds(t, CHUNKS, stride=pitch), :]
                 slopes = tuple(r * q + h for r, q, h in zip(some, slopes, states))
                 states = tuple(r * h + x for r, h in zip(some, states))
                 of_states = tuple(a + g * h for a, h in zip(of_states, states))
                 of_slopes = tuple(a + g * q for a, q in zip(of_slopes, slopes))
                 return states, slopes, of_states, of_slopes
 
-            _, _, of_states, of_slopes = lax.fori_loop(0, steps, sweep, begin, unroll=4)
+            states, slopes, of_states, of_slopes = lax.fori_loop(
+                0, steps, sweep, (empty,) * 4, unroll=UNROLL
+            )
             for n in range(part_size):
                 row = half * part_size + n
-                gh_ref[row : row + 1, lanes] = jnp.sum(of_states[n], axis=0, keepdims=True)
-                gq_ref[row : row + 1, lanes] = jnp.sum(of_slopes[n], axis=0, keepdims=True)
-
-        blank = tuple(zero for _ in rates)
-
-        def back_finals(t, states):
-            g = g_part[pl.ds(steps - 1 - t, CHUNKS, stride=steps), :]
-            return tuple(r * h + g for r, h in zip(rates, states))
-
-        ends = lax.fori_loop(0, steps, back_finals, blank, unroll=4)
-        starts = tuple(entering(h, r, steps, reverse=True) for h, r in zip(ends, rates))
+                rate, back, back_slope = rates[row], ends[row], end_slopes[row]
+                state, slope = entering_pair(states[n], slopes[n], rate, steps)
+                of_state = of_states[n] + state * (rate * back)
+                of_slope = (
+                    of_slopes[n] + slope * (rate * back) + state * (back + rate * back_slope)
+                )
+                sums_ref[row : row + 1, lanes] = jnp.sum(of_state, axis=0, keepdims=True)
+                row += dims
+                sums_ref[row : row + 1, lanes] = jnp.sum(of_slope, axis=0, keepdims=True)
 
         def back_outputs(t, states):
-            g = g_part[pl.ds(steps - 1 - t, CHUNKS, stride=steps), :]
+            g = g_part[pl.ds(steps - 1 - t, CHUNKS, stride=pitch), :]
             states = tuple(r * h + g for r, h in zip(rates, states))
             terms = [c * h for c, h in zip(coefs, states)]
             while len(terms) > 1:
                 terms = [a + b for a, b in zip(terms[::2], terms[1::2])]
-            r_part[pl.ds(steps - 1 - t, CHUNKS, stride=steps), :] = terms[0]
+            r_part[pl.ds(steps - 1 - t, CHUNKS, stride=pitch), :] = terms[0]
             return states
 
-        lax.fori_loop(0, steps, back_outputs, starts, unroll=4)
+        lax.fori_loop(0, steps, back_outputs, starts, unroll=UNROLL)
 
     ones = jnp.ones((CHUNKS, own), BF16)
     first = lax.broadcasted_iota(jnp.int32, (CHUNKS, LANES), 0) == 0
@@ -344,10 +354,11 @@
         start = pl.multiple_of(i * LANES, LANES)
         here = pl.ds(start, LANES)
         valid = row_valid(start, LANES, length)
+        there = pl.ds(start + start // steps, LANES)
         of_gain, of_shift, of_skip = carry
-        smoothed = jnp.concatenate([r_buf[k, here, :] for k in range(groups)], axis=1)
-        gpre = jnp.concatenate([g_buf[k, here, :] for k in range(groups)], axis=1)
-        masked = jnp.concatenate([m_buf[k, here, :] for k in range(groups)], axis=1)
+        smoothed = jnp.concatenate([r_buf[k, there, :] for k in range(groups)], axis=1)
+        gpre = jnp.concatenate([g_buf[k, there, :] for k in range(groups)], axis=1)
+        masked = jnp.concatenate([m_buf[k, there, :] for k in range(groups)], axis=1)
         n = own_ref[here, :]
         gmasked = skip_ref[...] * gpre + smoothed
         gnormed = gmasked * valid + gvalue_ref[here, :]
@@ -367,36 +378,48 @@
     of_gain, of_shift, of_skip = lax.fori_loop(
         0, count // LANES, finish, (blank_row, blank_row, blank_row)
     )
-    sums_ref[0:1, :] = of_gain
-    sums_ref[1:2, :] = of_shift
-    sums_ref[2:3, :] = of_skip
-    sums_ref[3:8, :] = jnp.zeros((5, own), F32)
+    last = 2 * dims
+    sums_ref[last : last + 1, :] = of_gain
+    sums_ref[last + 1 : last + 2, :] = of_shift
+    sums_ref[last + 2 : last + 3, :] = of_skip
+    sums_ref[last + 3 : last + 8, :] = jnp.zeros((5, own), F32)
 
 
 def average_backward(
-    length, gmixed, gvalue, pre, own_n, scale, resid, gain, shift, rate, coef, skip
+    length, gmixed, gvalue, pre, own_n, scale, resid, norm, rate, coef, skip, after=()
 ):
     count, own = gmixed.shape
     dims = rate.shape[0]
     groups = own // LANES
-    rate, coef = on_sublanes(rate), on_sublanes(coef)
     return pl.pallas_call(
-        average_backward_kernel,
+        functools.partial(average_backward_kernel, len(after)),
         out_shape=(
             shape((count, own), BF16),
             shape((CHUNKS, count), F32),
-            shape((dims, own), F32),
-            shape((dims, own), F32),
-            shape((8, own), F32),
+            shape((2 * dims + 8, own), F32),
         ),
-        in_specs=[smem()] + [vmem()] * 11,
-        out_specs=(vmem(),) * 5,
-        scratch_shapes=[pltpu.VMEM((groups, count, LANES), F32)] * 3,
+        in_specs=[hbm()] * len(after) + [smem()] + [vmem()] * 10,
+        out_specs=(vmem(),) * 3,
+        scratch_shapes=[pltpu.VMEM((groups, count + CHUNKS, LANES), F32)] * 3,
+        cost_estimate=lasting(21),
         compiler_params=params(),
-    )(length, gmixed, gvalue, pre, own_n, scale, resid, gain, shift, rate, coef, skip)
+    )(*after, length, gmixed, gvalue, pre, own_n, scale, resid, norm, rate, coef, skip)
+
+
+def unfold(packed, out_w, shards):
+    wide, width = out_w.shape
+    few = wide // shards
+    low = packed.shape[1] - width // 2
+    for shard in range(shards):
+        for half in range(2):
+            start = shard * (width // shards) + half * few
+            out_w[
+                shard * few : (shard + 1) * few, half * (width // 2) : (half + 1) * (width // 2)
+            ] = packed[start : start + few, low:]
 
 
 def attention_forward_kernel(
+    shards,
     length_ref,
     normed_ref,
     mixed_ref,
@@ -404,7 +427,6 @@
     bias_ref,
     pair_ref,
     offset_ref,
-    out_w_ref,
     part_ref,
     update_ref,
     shared_ref,
@@ -414,8 +436,14 @@
     att_ref,
     gated_ref,
     probs_ref,
+    out_w_ref,
 ):
     length = length_ref[0]
+
+    @pl.when(pl.program_id(0) == 0)
+    def _():
+        unfold(in_ref, out_w_ref, shards)
+
     rows = normed_ref.shape[0]
     wide = value_ref.shape[1]
     own = update_ref.shape[1]
@@ -456,9 +484,9 @@
     part_ref[...] = dot(gated_ref[...], out_w_ref[...]).astype(BF16)
 
 
-def attention_forward(length, normed, mixed, in_w, bias, pair, offset, out_w, own):
+def attention_forward(length, normed, mixed, in_w, bias, pair, offset, own, shards):
     count, width = normed.shape
-    wide = out_w.shape[0]
+    wide = width // 2
     keyed = pair.shape[1]
 
     def rows(columns):
@@ -469,7 +497,7 @@
 
     widths = (width, own, keyed, wide, own, wide, wide, wide, ATT)
     return pl.pallas_call(
-        attention_forward_kernel,
+        functools.partial(attention_forward_kernel, shards),
         grid=(count // ROWS,),
         out_shape=tuple(shape((count, w), BF16) for w in widths),
         in_specs=[
@@ -480,14 +508,24 @@
             whole(bias),
             whole(pair),
             whole(offset),
-            whole(out_w),
         ],
         out_specs=tuple(rows(w) for w in widths),
+        scratch_shapes=[pltpu.VMEM((wide, width), BF16)],
+        cost_estimate=lasting(12),
         compiler_params=params(),
-    )(length, normed, mixed, in_w, bias, pair, offset, out_w)
+    )(length, normed, mixed, in_w, bias, pair, offset)
 
 
 def attention_backward_kernel(
+    shards,
+    waits,
+    *refs,
+):
+    attention_backward_work(shards, *refs[waits:])
+
+
+def attention_backward_work(
+    shards,
     length_ref,
     gout_ref,
     gupdate_ref,
@@ -499,16 +537,17 @@
     in_ref,
     pair_ref,
     offset_ref,
-    out_w_ref,
     gmixed_ref,
     gnormed_ref,
     gbase_ref,
     gvalue_ref,
     bias_ref,
     pair_sum_ref,
+    out_w_ref,
 ):
     length = length_ref[0]
     rows = gout_ref.shape[0]
+    total = bias_ref.shape[1]
     wide = value_ref.shape[1]
     own = gupdate_ref.shape[1]
     keyed = shared_ref.shape[1]
@@ -519,6 +558,7 @@
     def _():
         bias_ref[...] = jnp.zeros_like(bias_ref)
         pair_sum_ref[...] = jnp.zeros_like(pair_sum_ref)
+        unfold(in_ref, out_w_ref, shards)
 
     valid = row_valid(start, rows, length)
     ggated = dot(gout_ref[...], out_w_ref[...], 1, 1)
@@ -563,17 +603,17 @@
         else:
             gvalue_ref[...] = piece.astype(BF16)
         low += size
-    gmixed_ref[...] = dot(gbase_ref[...], in_ref[:, wide:], 1, 1).astype(BF16)
+    gmixed_ref[...] = dot(gbase_ref[...], in_ref[:, wide:total], 1, 1).astype(BF16)
     gnormed_ref[...] = dot(gvalue_ref[...], in_ref[:, :wide], 1, 1).astype(BF16)
 
 
-def attention_backward(length, gout, gupdate, saved, in_w, pair, offset, out_w):
+def attention_backward(length, gout, gupdate, saved, in_w, pair, offset, shards, after=()):
     shared, reset, value, att, probs = saved
     count, width = gout.shape
     own = gupdate.shape[1]
-    wide = out_w.shape[0]
+    wide = width // 2
     keyed = pair.shape[1]
-    total = in_w.shape[1]
+    total = in_w.shape[1] - width // 2
 
     def rows(columns):
         return pl.BlockSpec((ROWS, columns), lambda i: (i, 0))
@@ -582,7 +622,7 @@
         return pl.BlockSpec(dims, lambda i: (0, 0))
 
     return pl.pallas_call(
-        attention_backward_kernel,
+        functools.partial(attention_backward_kernel, shards, len(after)),
         grid=(count // ROWS,),
         out_shape=(
             shape((count, width), BF16),
@@ -592,7 +632,8 @@
             shape((8, total), F32),
             shape((8, keyed), F32),
         ),
-        in_specs=[
+        in_specs=[hbm()] * len(after)
+        + [
             smem(),
             rows(width),
             rows(own),
@@ -604,7 +645,6 @@
             whole(in_w.shape),
             whole(pair.shape),
             whole(offset.shape),
-            whole(out_w.shape),
         ],
         out_specs=(
             rows(width),
@@ -614,25 +654,28 @@
             whole((8, total)),
             whole((8, keyed)),
         ),
+        scratch_shapes=[pltpu.VMEM((wide, width), BF16)],
+        cost_estimate=lasting(13),
         compiler_params=params(),
-    )(length, gout, gupdate, shared, reset, value, att, probs, in_w, pair, offset, out_w)
+    )(*after, length, gout, gupdate, shared, reset, value, att, probs, in_w, pair, offset)
 
 
 def feed_forward_kernel(
-    x_ref, gain_ref, shift_ref, in_ref, bias_ref, out_w_ref, part_ref, pre_ref, n_ref, normed_ref, scale_ref
+    x_ref, gain_ref, shift_ref, w_ref, bias_ref, part_ref, pre_ref, n_ref, normed_ref, scale_ref
 ):
+    hidden = pre_ref.shape[1]
     n, scale = normalise(x_ref[...].astype(F32))
     n_ref[...] = n.astype(BF16)
     scale_ref[...] = jnp.broadcast_to(scale, scale_ref.shape)
     normed_ref[...] = (n * gain_ref[...] + shift_ref[...]).astype(BF16)
-    pre = dot(normed_ref[...], in_ref[...]) + bias_ref[...]
+    pre = dot(normed_ref[...], w_ref[:, :hidden]) + bias_ref[...]
     pre_ref[...] = pre.astype(BF16)
-    part_ref[...] = dot(silu(pre).astype(BF16), out_w_ref[...]).astype(BF16)
-
-
-def feed_forward(x, gain, shift, in_w, bias, out_w):
+    part_ref[...] = dot(silu(pre).astype(BF16), w_ref[:, hidden:]).astype(BF16)
+
+
+def feed_forward(x, gain, shift, weights, bias):
     count, width = x.shape
-    hidden = in_w.shape[1]
+    hidden = bias.shape[1]
 
     def rows(columns):
         return pl.BlockSpec((ROWS, columns), lambda i: (i, 0))
@@ -650,21 +693,24 @@
             shape((count, width), BF16),
             shape((count, LANES), F32),
         ),
-        in_specs=[rows(width)] + [whole(a) for a in (gain, shift, in_w, bias, out_w)],
+        in_specs=[rows(width)] + [whole(a) for a in (gain, shift, weights, bias)],
         out_specs=(rows(width), rows(hidden), rows(width), rows(width), rows(LANES)),
+        cost_estimate=lasting(10),
         compiler_params=params(),
-    )(x, gain, shift, in_w, bias, out_w)
-
-
-def feed_backward_kernel(corrected, *refs):
+    )(x, gain, shift, weights, bias)
+
+
+def feed_backward_kernel(corrected, waits, *refs):
+    refs = refs[waits:]
     if corrected:
         z_ref, means_ref, x_ref = refs[:3]
         refs = refs[3:]
     else:
         g_in_ref = refs[0]
         refs = refs[1:]
-    pre_ref, n_ref, gain_ref, in_ref, out_w_ref = refs[:5]
-    refs = refs[5:]
+    pre_ref, n_ref, gain_ref, w_ref = refs[:4]
+    refs = refs[4:]
+    hidden = pre_ref.shape[1]
     part_ref, stats_ref, gpre_ref, act_ref, sums_ref, bias_ref = refs[:6]
     width = n_ref.shape[1]
 
@@ -685,10 +731,10 @@
     pre = pre_ref[...].astype(F32)
     s = sigmoid(pre)
     act_ref[...] = (pre * s).astype(BF16)
-    gpre = dot(g, out_w_ref[...], 1, 1) * (s * (1.0 + pre * (1.0 - s)))
+    gpre = dot(g, w_ref[:, hidden:], 1, 1) * (s * (1.0 + pre * (1.0 - s)))
     bias_ref[0:1, :] += jnp.sum(gpre, axis=0, keepdims=True)
     gpre_ref[...] = gpre.astype(BF16)
-    part = dot(gpre_ref[...], in_ref[...], 1, 1)
+    part = dot(gpre_ref[...], w_ref[:, :hidden], 1, 1)
     part_ref[...] = part.astype(BF16)
     n = n_ref[...].astype(F32)
     sums_ref[0:1, :] += jnp.sum(part * n, axis=0, keepdims=True)
@@ -702,10 +748,10 @@
     stats_ref[...] = jnp.where(first, mean_row, slope_row)
 
 
-def feed_backward(given, pre, n, gain, in_w, out_w):
+def feed_backward(given, pre, n, gain, weights, after=()):
     corrected = isinstance(given, tuple)
     count, width = n.shape
-    hidden = in_w.shape[1]
+    hidden = pre.shape[1]
 
     def rows(columns):
         return pl.BlockSpec((ROWS, columns), lambda i: (i, 0))
@@ -718,7 +764,7 @@
     given_specs = [rows(width), stats_spec, rows(width)] if corrected else [rows(width)]
     extra = ((shape((count, width), BF16),), (rows(width),)) if corrected else ((), ())
     return pl.pallas_call(
-        functools.partial(feed_backward_kernel, corrected),
+        functools.partial(feed_backward_kernel, corrected, len(after)),
         grid=(count // ROWS,),
         out_shape=(
             shape((count, width), BF16),
@@ -729,8 +775,9 @@
             shape((8, hidden), F32),
         )
         + extra[0],
-        in_specs=given_specs
-        + [rows(hidden), rows(width), whole(gain.shape), whole(in_w.shape), whole(out_w.shape)],
+        in_specs=[hbm()] * len(after)
+        + given_specs
+        + [rows(hidden), rows(width), whole(gain.shape), whole(weights.shape)],
         out_specs=(
             rows(width),
             stats_spec,
@@ -740,8 +787,9 @@
             whole((8, hidden)),
         )
         + extra[1],
+        cost_estimate=lasting(13),
         compiler_params=params(),
-    )(*given, pre, n, gain, in_w, out_w)
+    )(*after, *given, pre, n, gain, weights)
 
 
 def plane():
@@ -776,6 +824,22 @@
         return carry
 
     lax.fori_loop(0, count // STRIP, one, 0)
+
+
+def widen(block):
+    rows, columns = block.shape
+    if columns < LANES:
+        block = jnp.concatenate((block, jnp.zeros((rows, LANES - columns), F32)), axis=1)
+    return block.astype(BF16)
+
+
+def grad_tiles(left, right, store, begin, end):
+    def one(i, carry):
+        rows = pl.ds(pl.multiple_of(i * TILE, TILE), TILE)
+        store(rows, dot(left[:, rows], right[...], 0, 0).astype(BF16))
+        return carry
+
+    lax.fori_loop(begin, end, one, 0)
 
 
 def reduce_begin(part, piece, peers, slots, sems):
@@ -833,7 +897,7 @@
     return started
 
 
-def gather_finish(out, piece, peers, sems, zero, one):
+def gather_forward(out, piece, peers, sems, zero, one):
     me, across, along, far = peers
     zero[0].wait_recv()
     passing = out.at[piece(along, 0)]
@@ -843,6 +907,11 @@
     passing = out.at[piece(across, 1)]
     second = link(passing, passing, sems, 5, along)
     second.start()
+    return first, second
+
+
+def gather_finish(out, piece, peers, sems, zero, one, passed=None):
+    first, second = passed or gather_forward(out, piece, peers, sems, zero, one)
     zero[1].wait_recv()
     one[0].wait_recv()
     first.wait_recv()
@@ -907,6 +976,7 @@
         in_specs=[vmem()],
         out_specs=vmem(),
         scratch_shapes=copy_sems(6),
+        cost_estimate=lasting(18),
         compiler_params=comm_params(ident),
     )(own)
 
@@ -948,6 +1018,7 @@
         out_specs=(vmem(), vmem()),
         scratch_shapes=[pltpu.VMEM((2,) + stats.shape, F32), pltpu.VMEM(stats.shape, F32)]
         + copy_sems(8),
+        cost_estimate=lasting(20),
         compiler_params=comm_params(ident),
     )(own, stats)
 
@@ -1013,6 +1084,7 @@
         + [pltpu.VMEM((count, own), BF16), pltpu.SemaphoreType.DMA]
         + copy_sems(6)
         + copy_sems(6),
+        cost_estimate=lasting(37),
         compiler_params=comm_params(ident),
     )(part, update, cand, x)
 
@@ -1075,6 +1147,7 @@
         + [pltpu.VMEM((count, own), BF16), pltpu.SemaphoreType.DMA]
         + copy_sems(6)
         + copy_sems(6),
+        cost_estimate=lasting(36),
         compiler_params=comm_params(ident),
     )(part, bias, x)
 
@@ -1121,28 +1194,40 @@
         scratch_shapes=reduce_scratch(quarter, width // 2)
         + [pltpu.VMEM((quarter, width), BF16), pltpu.SemaphoreType.DMA]
         + copy_sems(6),
+        cost_estimate=lasting(20),
         compiler_params=comm_params(ident),
     )(part, bias, x)
 
 
 def back_join_kernel(
+    shards,
     part_ref,
     stats_ref,
     scale_ref,
     gain_ref,
     update_ref,
     hidden_ref,
-    g_ref,
+    normed_hbm,
+    gpre_hbm,
+    act_hbm,
+    g_hbm,
+    sums_ref,
+    bias_ref,
     n_ref,
     x_ref,
     out_ref,
     gupdate_ref,
     resid_ref,
+    grad_hbm,
+    normed_ref,
+    gpre_ref,
+    act_ref,
+    g_ref,
+    grad_ref,
     early,
     direct,
     late,
     stage,
-    g_own,
     n_own,
     x_own,
     got,
@@ -1164,17 +1249,54 @@
     slots = (early, direct, late, stage)
     fetches = [
         own_slice(source, target, local_sem.at[i], own)
-        for i, (source, target) in enumerate(((g_ref, g_own), (n_ref, n_own), (x_ref, x_own)))
+        for i, (source, target) in enumerate(((n_ref, n_own), (x_ref, x_own)))
     ]
-    for fetch in fetches:
+    later = [
+        pltpu.make_async_copy(source, target, local_sem.at[2 + i])
+        for i, (source, target) in enumerate(
+            (
+                (normed_hbm, normed_ref),
+                (gpre_hbm, gpre_ref),
+                (g_hbm, g_ref),
+                (act_hbm, act_ref),
+            )
+        )
+    ]
+    for fetch in fetches + later:
         fetch.start()
+    hidden = gpre_ref.shape[1]
+
+    def in_grad(rows, value):
+        grad_ref[rows, :hidden] = value
+
+    def out_grad(rows, value):
+        grad_ref[rows, hidden : hidden + width] = value
+
+    def small_grads():
+        grad_ref[:, hidden + width :] = jnp.zeros((width, LANES), BF16)
+        size = width // shards
+        for shard in range(shards):
+            lanes = slice(shard * size, (shard + 1) * size)
+            block = jnp.concatenate(
+                (sums_ref[0:3, lanes], bias_ref[0:1, lanes], jnp.zeros((SMALL - 4, size), F32)),
+                axis=0,
+            )
+            grad_ref[shard * size : shard * size + SMALL, hidden + width :] = widen(block)
+
     greet(peers[1], peers[2])
     started = reduce_begin(part_ref, piece, peers, slots, (send, recv))
+    small_grads()
+    later[0].wait()
+    later[1].wait()
+    grad_tiles(normed_ref, gpre_ref, in_grad, 0, width // (2 * TILE))
     total = stats_total(stats_ref, got, stats_stage, peers, (send_s, recv_s), 0)
     means[...] = total.T * (1.0 / width)
     for fetch in fetches:
         fetch.wait()
     reduce_forward(part_ref, piece, peers, slots, (send, recv), started)
+    later[2].wait()
+    later[3].wait()
+    grad_tiles(normed_ref, gpre_ref, in_grad, width // (2 * TILE), width // TILE)
     begun = []
     mine = pl.ds(pl.multiple_of(me * own, LANES), own)
     for half in range(2):
@@ -1182,10 +1304,10 @@
 
         def finish(start):
             here = pl.ds(half * (count // 2) + start, STRIP)
-            e = reduced(part_ref, piece, me, slots, half, start) * gain_ref[...]
+            e = reduced(part_ref, piece, me, slots, half, start) * gain_ref[2:3, :]
             n = n_own[here, :].astype(F32)
             inner = e - means[here, 0:1] - n * means[here, 1:2]
-            g = g_own[here, :].astype(F32) + scale_ref[here, 0:1] * inner
+            g = g_ref[here, mine].astype(F32) + scale_ref[here, 0:1] * inner
             g = g.astype(BF16).astype(F32)
             u = sigmoid(update_ref[here, :].astype(F32))
             pre = hidden_ref[here, :].astype(F32)
@@ -1197,42 +1319,100 @@
 
         strips(count // 2, finish)
         begun.append(gather_begin(out_ref, piece, peers, (send_g, recv_g), half))
+    grad_tiles(act_ref, g_ref, out_grad, 0, hidden // TILE)
+    store = pltpu.make_async_copy(grad_ref, grad_hbm, local_sem.at[6])
+    store.start()
     gather_finish(out_ref, piece, peers, (send_g, recv_g), begun[0], begun[1])
     for copy in started:
         copy.wait_send()
-
-
-def back_join(part, stats, scale, gain, update, hidden, g, n, x, ident):
+    store.wait()
+
+
+def back_join(
+    part, stats, scale, gain, update, hidden, normed, gpre, act, g, sums, bias, n, x, shards, ident
+):
     count, width = part.shape
     own = update.shape[1]
+    wide = gpre.shape[1]
     return pl.pallas_call(
-        back_join_kernel,
+        functools.partial(back_join_kernel, shards),
         out_shape=(
             shape((count, width), BF16),
             shape((count, own), BF16),
             shape((count, own), F32),
+            shape((width, wide + width + LANES), BF16),
         ),
-        in_specs=[vmem()] * 6 + [hbm()] * 3,
-        out_specs=(vmem(),) * 3,
-        scratch_shapes=reduce_scratch(count // 2, own)
-        + [pltpu.VMEM((count, own), BF16)] * 3
+        in_specs=[vmem()] * 6 + [hbm()] * 4 + [vmem()] * 2 + [hbm()] * 2,
+        out_specs=(vmem(),) * 3 + (hbm(),),
+        scratch_shapes=[
+            pltpu.VMEM((count, width), BF16),
+            pltpu.VMEM((count, wide), BF16),
+            pltpu.VMEM((count, wide), BF16),
+            pltpu.VMEM((count, width), BF16),
+            pltpu.VMEM((width, wide + width + LANES), BF16),
+        ]
+        + reduce_scratch(count // 2, own)
+        + [pltpu.VMEM((count, own), BF16)] * 2
         + [
             pltpu.VMEM((2, CHUNKS, count), F32),
             pltpu.VMEM((CHUNKS, count), F32),
             pltpu.VMEM((count, CHUNKS), F32),
-            pltpu.SemaphoreType.DMA((3,)),
+            pltpu.SemaphoreType.DMA((7,)),
         ]
         + copy_sems(6)
         + copy_sems(6)
         + copy_sems(2),
+        cost_estimate=lasting(43),
         compiler_params=comm_params(ident),
-    )(part, stats, scale, gain, update, hidden, g, n, x)
-
-
-def reduce_two_kernel(
-    one_ref, two_ref, out_one, out_two, e1, d1, l1, s1, e2, d2, l2, s2, sa, ra, sb, rb
+    )(part, stats, scale, gain, update, hidden, normed, gpre, act, g, sums, bias, n, x)
+
+
+def reduce_two_kernel(shards, waits, *refs):
+    reduce_two_work(shards, *refs[waits:])
+
+
+def reduce_two_work(
+    shards,
+    one_ref,
+    two_ref,
+    normed_hbm,
+    gvalue_hbm,
+    mixed_hbm,
+    gbase_hbm,
+    gated_hbm,
+    gout_hbm,
+    bias_ref,
+    pair_ref,
+    out_one,
+    out_two,
+    grad_hbm,
+    normed_ref,
+    gvalue_ref,
+    mixed_ref,
+    gbase_ref,
+    gated_ref,
+    gout_ref,
+    grad_ref,
+    local_sem,
+    e1,
+    d1,
+    l1,
+    s1,
+    e2,
+    d2,
+    l2,
+    s2,
+    sa,
+    ra,
+    sb,
+    rb,
 ):
     count, own = out_one.shape
+    width = normed_ref.shape[1]
+    wide = gvalue_ref.shape[1]
+    total = wide + gbase_ref.shape[1]
+    block_rows = width // shards
+    few = wide // shards
     peers = plane()
     me = peers[0]
     piece = column_piece(count, own)
@@ -1240,10 +1420,60 @@
         (one_ref, out_one, (e1, d1, l1, s1), (sa, ra)),
         (two_ref, out_two, (e2, d2, l2, s2), (sb, rb)),
     )
+
+    fetches = [
+        pltpu.make_async_copy(source, target, local_sem.at[i])
+        for i, (source, target) in enumerate(
+            (
+                (mixed_hbm, mixed_ref),
+                (gbase_hbm, gbase_ref),
+                (normed_hbm, normed_ref),
+                (gvalue_hbm, gvalue_ref),
+                (gated_hbm, gated_ref),
+                (gout_hbm, gout_ref),
+            )
+        )
+    ]
+    for fetch in fetches:
+        fetch.start()
+
+    def value_grad(rows, value):
+        grad_ref[rows, :wide] = value
+
+    def base_grad(rows, value):
+        grad_ref[rows, wide:total] = value
+
+    def out_grad(rows, value):
+        for i in range(TILE // few):
+            start = (rows.start // few + i) * block_rows
+            for half in range(2):
+                here = pl.ds(pl.multiple_of(start + half * few, few), few)
+                grad_ref[here, total : total + width // 2] = value[
+                    i * few : (i + 1) * few, half * (width // 2) : (half + 1) * (width // 2)
+                ]
+
+    def small_grads():
+        last = total + width // 2
+        grad_ref[:, last:] = jnp.zeros((width, LANES), BF16)
+        rows = [bias_ref[0:1, i * LANES : (i + 1) * LANES] for i in range(total // LANES)]
+        block = jnp.concatenate(rows + [pair_ref[0:3, :]], axis=0).astype(BF16)
+        for shard in range(shards):
+            grad_ref[shard * block_rows : shard * block_rows + SMALL, last:] = block
+
     greet(peers[1], peers[2])
     begun = [reduce_begin(part, piece, peers, slots, sems) for part, _, slots, sems in jobs]
+    small_grads()
+    fetches[0].wait()
+    fetches[1].wait()
+    grad_tiles(mixed_ref, gbase_ref, base_grad, 0, width // TILE)
     for (part, _, slots, sems), started in zip(jobs, begun):
         reduce_forward(part, piece, peers, slots, sems, started)
+    for fetch in fetches[2:]:
+        fetch.wait()
+    grad_tiles(normed_ref, gvalue_ref, value_grad, 0, width // TILE)
+    grad_tiles(gated_ref, gout_ref, out_grad, 0, wide // TILE)
+    store = pltpu.make_async_copy(grad_ref, grad_hbm, local_sem.at[6])
+    store.start()
     for (part, out, slots, sems), started in zip(jobs, begun):
         for half in range(2):
             reduce_arrived(started, half)
@@ -1255,23 +1485,45 @@
             strips(count // 2, finish)
         for copy in started:
             copy.wait_send()
-
-
-def reduce_two(one, two, own, ident):
-    count = one.shape[0]
+    store.wait()
+
+
+def reduce_two(
+    one, two, normed, gvalue, mixed, gbase, gated, gout, bias, pair, own, shards, ident, after=()
+):
+    count, width = one.shape
+    columns = gvalue.shape[1] + gbase.shape[1] + width // 2 + LANES
     return pl.pallas_call(
-        reduce_two_kernel,
-        out_shape=(shape((count, own), F32),) * 2,
-        in_specs=[vmem()] * 2,
-        out_specs=(vmem(),) * 2,
-        scratch_shapes=reduce_scratch(count // 2, own) * 2 + copy_sems(6) + copy_sems(6),
+        functools.partial(reduce_two_kernel, shards, len(after)),
+        out_shape=(shape((count, own), F32),) * 2 + (shape((width, columns), BF16),),
+        in_specs=[hbm()] * len(after) + [vmem()] * 2 + [hbm()] * 6 + [vmem()] * 2,
+        out_specs=(vmem(),) * 2 + (hbm(),),
+        scratch_shapes=[
+            pltpu.VMEM(a.shape, BF16) for a in (normed, gvalue, mixed, gbase, gated, gout)
+        ]
+        + [pltpu.VMEM((width, columns), BF16), pltpu.SemaphoreType.DMA((7,))]
+        + reduce_scratch(count // 2, own) * 2
+        + copy_sems(6)
+        + copy_sems(6),
+        cost_estimate=lasting(36),
         compiler_params=comm_params(ident),
-    )(one, two)
-
-
-def last_rows_kernel(
-    z_ref, stats_ref, x_ref, out_ref, land, x_own, got, stats_stage, total_buf, local_sem, send, recv
-):
+    )(*after, one, two, normed, gvalue, mixed, gbase, gated, gout, bias, pair)
+
+
+def block_piece(whole):
+    def piece(owner, half):
+        size = whole.shape[1] // 2
+        return owner, pl.ds(half * size, size), slice(None)
+
+    return piece
+
+
+def final_kernel(number, z_ref, stats_ref, x_ref, *refs):
+    blocks, refs = refs[:number], refs[number:]
+    out_ref, refs = refs[0], refs[1:]
+    gathered, refs = refs[:number], refs[number:]
+    land, x_own, got, stats_stage, total_buf, local_sem, send, recv = refs[:8]
+    block_sems = [refs[8 + 2 * i : 10 + 2 * i] for i in range(number)]
     count, own = z_ref.shape
     quarter, width = out_ref.shape
     peers = plane()
@@ -1284,6 +1536,8 @@
     fetch = pltpu.make_async_copy(x_ref.at[rows(me), :], x_own, local_sem)
     fetch.start()
     land[:, mine] = z_ref[rows(me), :]
+    for block, whole in zip(blocks, gathered):
+        whole[me] = block[...]
     greet(*peers[1:])
     sems = (send, recv)
     copies = []
@@ -1291,6 +1545,10 @@
         copies.append(link(z_ref.at[rows(other), :], land.at[:, mine], sems, 2 + index, other))
         copies[-1].start()
     total_buf[...] = stats_total(stats_ref, got, stats_stage, peers, sems, 0)
+    begun = [
+        [gather_begin(whole, block_piece(whole), peers, k, half) for half in range(2)]
+        for whole, k in zip(gathered, block_sems)
+    ]
     part = total_buf[:, pl.ds(pl.multiple_of(me * quarter, LANES), quarter)]
     means = part.T * (1.0 / width)
     fetch.wait()
@@ -1299,19 +1557,27 @@
     n, scale = normalise(x_own[...].astype(F32))
     g = land[...].astype(F32) - scale * (means[:, 0:1] + n * means[:, 1:2])
     out_ref[...] = g.astype(BF16)
+    passed = [
+        gather_forward(whole, block_piece(whole), peers, k, zero, one)
+        for whole, k, (zero, one) in zip(gathered, block_sems, begun)
+    ]
+    for whole, k, (zero, one), two in zip(gathered, block_sems, begun, passed):
+        gather_finish(whole, block_piece(whole), peers, k, zero, one, two)
     for copy in copies:
         copy.wait_send()
 
 
-def last_rows(z, stats, x, ident):
+def final_exchange(z, stats, x, blocks, sections, ident):
     count, own = z.shape
     width = x.shape[1]
     quarter = count // 4
+    number = len(blocks)
     return pl.pallas_call(
-        last_rows_kernel,
-        out_shape=shape((quarter, width), BF16),
-        in_specs=[vmem(), vmem(), hbm()],
-        out_specs=vmem(),
+        functools.partial(final_kernel, number),
+        out_shape=(shape((quarter, width), BF16),)
+        + tuple(shape((sections,) + a.shape, BF16) for a in blocks),
+        in_specs=[vmem(), vmem(), hbm()] + [vmem()] * number,
+        out_specs=(vmem(),) * (1 + number),
         scratch_shapes=[
             pltpu.VMEM((quarter, width), BF16),
             pltpu.VMEM((quarter, width), BF16),
@@ -1320,36 +1586,417 @@
             pltpu.VMEM(stats.shape, F32),
             pltpu.SemaphoreType.DMA,
         ]
-        + copy_sems(5),
+        + copy_sems(5)
+        + copy_sems(6) * number,
+        cost_estimate=lasting(10 + 20 * number),
         compiler_params=comm_params(ident),
-    )(z, stats, x)
-
-
-def interleaved(array, shards, sections, section):
-    lead = array.shape[:-1]
-    split = array.reshape(lead + (shards, sections, -1))
-    return lax.dynamic_index_in_dim(split, section, len(lead) + 1, keepdims=False).reshape(
-        lead + (-1,)
+    )(z, stats, x, *blocks)
+
+
+def sums_kernel(shards, holders, sums_ref, block_ref, channels_ref, whole_ref, *refs):
+    sums_land, send_s, recv_s, send_c, recv_c, send, recv = refs
+    peers = plane()
+    me = peers[0]
+    slot = lax.axis_index("dp")
+    holding = slot // holders == me
+    whole_ref[me] = block_ref[...]
+    barrier = pltpu.get_barrier_semaphore()
+    for other in peers[1:]:
+        pl.semaphore_signal(barrier, inc=1, device_id={"section": other}, device_id_type=MESH)
+    for step in range(1, shards):
+        other = (slot + step) % shards
+        pl.semaphore_signal(barrier, inc=1, device_id={"dp": other}, device_id_type=MESH)
+    pl.semaphore_wait(barrier, shards + 2)
+
+    def sums_copy(target, index, place):
+        return pltpu.make_async_remote_copy(
+            src_ref=sums_ref,
+            dst_ref=sums_land.at[place],
+            send_sem=send_s.at[index],
+            recv_sem=recv_s.at[place],
+            device_id={"dp": target},
+            device_id_type=MESH,
+        )
+
+    def sums_out(index):
+        target = me * holders + index
+        place = jnp.maximum((slot - target + shards) % shards - 1, 0)
+        return target, sums_copy(target, index, place)
+
+    for index in range(holders):
+        target, copy = sums_out(index)
+
+        @pl.when(target != slot)
+        def _():
+            copy.start()
+
+    piece = block_piece(whole_ref)
+    zero, one = (gather_begin(whole_ref, piece, peers, (send, recv), half) for half in range(2))
+    passed = gather_forward(whole_ref, piece, peers, (send, recv), zero, one)
+
+    def channels_copy(other, index):
+        return link(channels_ref, channels_ref, (send_c, recv_c), index, other)
+
+    @pl.when(holding)
+    def _():
+        summed = sums_ref[...]
+        for step in range(1, shards):
+            sums_copy((slot + step) % shards, 0, step - 1).wait_recv()
+            summed = summed + sums_land[step - 1]
+        channels_ref[...] = summed
+        for index, other in enumerate(peers[1:]):
+            channels_copy(other, index).start()
+
+    gather_finish(whole_ref, piece, peers, (send, recv), zero, one, passed)
+
+    for index, other in enumerate(peers[1:]):
+
+        @pl.when(slot // holders == other)
+        def _():
+            channels_copy(other, index).wait_recv()
+
+    @pl.when(holding)
+    def _():
+        for index, other in enumerate(peers[1:]):
+            channels_copy(other, index).wait_send()
+
+    for index in range(holders):
+        target, copy = sums_out(index)
+
+        @pl.when(target != slot)
+        def _():
+            copy.wait_send()
+
+
+def gather_sums(sums, block, sections, shards, holders, ident):
+    return pl.pallas_call(
+        functools.partial(sums_kernel, shards, holders),
+        out_shape=(shape(sums.shape, F32), shape((sections,) + block.shape, BF16)),
+        in_specs=[vmem()] * 2,
+        out_specs=(vmem(),) * 2,
+        scratch_shapes=[pltpu.VMEM((shards - 1,) + sums.shape, F32)]
+        + copy_sems(max(shards - 1, holders))
+        + copy_sems(3)
+        + copy_sems(6),
+        cost_estimate=lasting(25),
+        compiler_params=comm_params(ident),
+    )(sums, block)
+
+
+def assemble_kernel(layers, shards, *refs):
+    gathered = refs[: 2 * layers]
+    value_ref, base_ref, out_ref, feed_in_ref, feed_out_ref, small_ref, feed_small_ref = refs[
+        2 * layers :
+    ]
+    sections = gathered[0].shape[0]
+    width = out_ref.shape[2]
+    wide = value_ref.shape[2] // sections
+    hidden = feed_in_ref.shape[2] // sections
+    own = width // sections
+    keyed = base_ref.shape[2] - 2 * width - wide * sections
+    edge = wide + own
+    total = edge + keyed + wide + own
+    few = wide // shards
+
+    def woven(part, here, low, size):
+        step = size // shards
+        return jnp.concatenate(
+            [
+                part[k, here, low + d * step : low + (d + 1) * step].astype(F32)
+                for d in range(shards)
+                for k in range(sections)
+            ],
+            axis=1,
+        )
+
+    def joined(part, here, low, size):
+        return jnp.concatenate(
+            [part[k, here, low : low + size].astype(F32) for k in range(sections)], axis=1
+        )
+
+    def emit(part, feed):
+        def strip(i, carry):
+            here = pl.ds(pl.multiple_of(i * SMALL, SMALL), SMALL)
+            value_ref[0, here, :] = woven(part, here, 0, wide)
+            base_ref[0, here, :width] = joined(part, here, wide, own)
+            shared = part[0, here, edge : edge + keyed].astype(F32)
+            for k in range(1, sections):
+                shared += part[k, here, edge : edge + keyed].astype(F32)
+            low = width
+            base_ref[0, here, low : low + keyed] = shared
+            low += keyed
+            base_ref[0, here, low : low + wide * sections] = woven(part, here, edge + keyed, wide)
+            low += wide * sections
+            base_ref[0, here, low:] = joined(part, here, edge + keyed + wide, own)
+            feed_in_ref[0, here, :] = woven(feed, here, 0, hidden)
+            return carry
+
+        lax.fori_loop(0, value_ref.shape[1] // SMALL, strip, 0)
+        rows = feed.shape[1]
+        for k in range(sections):
+            feed_out_ref[0, k * rows : (k + 1) * rows, :] = feed[
+                k, :, hidden : hidden + width
+            ].astype(F32)
+            for half in range(2):
+                out_ref[
+                    0, k * few : (k + 1) * few, half * (width // 2) : (half + 1) * (width // 2)
+                ] = part[k, half * few : (half + 1) * few, total : total + width // 2].astype(F32)
+            small_ref[0, k] = part[k, :SMALL, total + width // 2 :].astype(F32)
+            feed_small_ref[0, k] = feed[k, :SMALL, hidden + width :].astype(F32)
+
+    for layer in range(layers):
+
+        @pl.when(pl.program_id(0) == layer)
+        def _():
+            emit(gathered[2 * layer], gathered[2 * layer + 1])
+
+
+def assemble(gathered, shards, width, wide, base, hidden):
+    layers = len(gathered)
+    flat = [array for pair in gathered for array in pair]
+    sections, rows, _ = flat[0].shape
+    dims = (
+        (rows, wide),
+        (rows, base),
+        (wide // shards, width),
+        (rows, hidden),
+        (hidden // shards, width),
+        (sections, SMALL, LANES),
+        (sections, SMALL, LANES),
     )
-
-
-def contiguous(array, sections, section):
-    size = array.shape[-1] // sections
-    return lax.dynamic_slice_in_dim(array, section * size, size, axis=array.ndim - 1)
-
-
-def put_interleaved(own, shards, sections, section):
-    lead = own.shape[:-1]
-    own = own.reshape(lead + (shards, 1, -1))
-    holder = jnp.zeros(lead + (shards, sections, own.shape[-1]), own.dtype)
-    holder = lax.dynamic_update_slice_in_dim(holder, own, section, len(lead) + 1)
-    return holder.reshape(lead + (-1,))
-
-
-def put_contiguous(own, sections, section):
-    size = own.shape[-1]
-    holder = jnp.zeros(own.shape[:-1] + (size * sections,), own.dtype)
-    return lax.dynamic_update_slice_in_dim(holder, own, section * size, own.ndim - 1)
+    return pl.pallas_call(
+        functools.partial(assemble_kernel, layers, shards),
+        grid=(layers,),
+        out_shape=tuple(shape((layers,) + d, F32) for d in dims),
+        in_specs=[pl.BlockSpec(a.shape, lambda i: (0, 0, 0)) for a in flat],
+        out_specs=tuple(
+            pl.BlockSpec((1,) + d, lambda i, n=len(d): (i,) + (0,) * n) for d in dims
+        ),
+        cost_estimate=lasting(9),
+        compiler_params=params(),
+    )(*flat)
+
+
+def chosen(pieces):
+    section = lax.axis_index("section")
+    result = pieces[0]
+    for k in range(1, len(pieces)):
+        result = jnp.where(section == k, pieces[k], result)
+    return result
+
+
+def pick(ref, index, low, size, shards, sections):
+    step = size // (shards * sections)
+    parts = []
+    for shard in range(shards):
+        start = low + shard * sections * step
+        parts.append(
+            chosen([ref[index + (slice(start + k * step, start + (k + 1) * step),)] for k in range(sections)])
+        )
+    return jnp.concatenate(parts, axis=-1)
+
+
+def pack_attention_kernel(shards, sections, value_ref, base_ref, out_ref, packed_ref):
+    rows, wide_all = value_ref.shape[1:]
+    few_all, width = out_ref.shape[1:]
+    wide, own, few = wide_all // sections, width // sections, few_all // sections
+    keyed = base_ref.shape[2] - 2 * width - wide_all
+    section = lax.axis_index("section")
+    low = wide + own + keyed
+
+    def strip(i, carry):
+        here = pl.ds(pl.multiple_of(i * SMALL, SMALL), SMALL)
+
+        def base(start, size):
+            return base_ref[0, here, pl.ds(pl.multiple_of(start, LANES), size)]
+
+        packed_ref[here, :wide] = pick(value_ref, (0, here), 0, wide_all, shards, sections)
+        packed_ref[here, wide : wide + own] = base(section * own, own)
+        packed_ref[here, wide + own : low] = base(width, keyed)
+        packed_ref[here, low : low + wide] = pick(
+            base_ref, (0, here), width + keyed, wide_all, shards, sections
+        )
+        packed_ref[here, low + wide : low + wide + own] = base(
+            width + keyed + wide_all + section * own, own
+        )
+        return carry
+
+    lax.fori_loop(0, rows // SMALL, strip, 0)
+    low += wide + own
+    mine = pl.ds(pl.multiple_of(section * few, few), few)
+    for half in range(2):
+        packed_ref[half * few : (half + 1) * few, low:] = out_ref[
+            0, mine, half * (width // 2) : (half + 1) * (width // 2)
+        ]
+
+
+def pack_feed_kernel(shards, sections, in_ref, out_ref, packed_ref):
+    rows, hidden_all = in_ref.shape[1:]
+    hidden = hidden_all // sections
+    size = out_ref.shape[1] // sections
+
+    def strip(i, carry):
+        here = pl.ds(pl.multiple_of(i * SMALL, SMALL), SMALL)
+        packed_ref[here, :hidden] = pick(in_ref, (0, here), 0, hidden_all, shards, sections)
+        return carry
+
+    lax.fori_loop(0, rows // SMALL, strip, 0)
+    start = pl.multiple_of(lax.axis_index("section") * size, size)
+    packed_ref[:, hidden:] = out_ref[0, pl.ds(start, size), :]
+
+
+def pack(kernel, layer, columns, shards, sections, *arrays):
+    rows = arrays[0].shape[1]
+    return pl.pallas_call(
+        functools.partial(kernel, shards, sections),
+        grid=(1,),
+        out_shape=shape((rows, columns), BF16),
+        in_specs=[pl.BlockSpec((1,) + a.shape[1:], lambda i: (layer, 0, 0)) for a in arrays],
+        out_specs=pl.BlockSpec((rows, columns), lambda i: (0, 0)),
+        cost_estimate=lasting(3),
+        compiler_params=params(),
+    )(*arrays)
+
+
+def unpack_kernel(layers, shards, sections, places, everyone_ref, *refs):
+    base_buf = refs[-1]
+    section = lax.axis_index("section")
+    outs = 14
+    for layer in range(layers):
+        (
+            gain_ref,
+            shift_ref,
+            feed_gain_ref,
+            feed_shift_ref,
+            feed_out_ref,
+            own_ref,
+            rate_ref,
+            coef_ref,
+            bias_ref,
+            feed_in_ref,
+            pair_ref,
+            offset_ref,
+            skip_ref,
+            own_out_ref,
+        ) = refs[layer * outs : (layer + 1) * outs]
+        width = gain_ref.shape[1]
+        own = width // sections
+        mine = pl.ds(pl.multiple_of(section * own, LANES), own)
+        row = slice(layer, layer + 1)
+
+        def joined(low, size):
+            return jnp.concatenate(
+                [everyone_ref[d, row, low : low + size] for d in range(shards)], axis=1
+            )
+
+        def share(low, size):
+            step = size // sections
+            return jnp.concatenate(
+                [
+                    chosen(
+                        [
+                            everyone_ref[d, row, low + k * step : low + (k + 1) * step]
+                            for k in range(sections)
+                        ]
+                    )
+                    for d in range(shards)
+                ],
+                axis=1,
+            )
+
+        def channels(low):
+            size = width // shards
+            count = own // size
+            return jnp.concatenate(
+                [everyone_ref[section * count + d, row, low : low + size] for d in range(count)],
+                axis=1,
+            )
+
+        size = width // shards
+        gain_ref[...] = joined(places["norm_gain"], size)
+        shift_ref[...] = joined(places["norm_shift"], size)
+        feed_gain_ref[...] = joined(places["feed_gain"], size)
+        feed_shift_ref[...] = joined(places["feed_shift"], size)
+        feed_out_ref[...] = joined(places["feed_out_bias"], size)
+        own_ref[0:1, :] = gain_ref[:, mine]
+        own_ref[1:2, :] = shift_ref[:, mine]
+        own_ref[2:3, :] = feed_gain_ref[:, mine]
+        own_ref[3:8, :] = jnp.zeros((5, own), F32)
+        own_out_ref[...] = feed_out_ref[:, mine]
+        skip_ref[...] = channels(places["average_skip"])
+        for n in range(rate_ref.shape[0]):
+            rate = sigmoid(channels(places["average_decay"] + n * size))
+            drive = (1.0 - rate) * channels(places["average_input"] + n * size)
+            coef = drive * channels(places["average_output"] + n * size)
+            rate_ref[n] = jnp.broadcast_to(rate, (CHUNKS, own))
+            coef_ref[n] = jnp.broadcast_to(coef, (CHUNKS, own))
+        keyed = offset_ref.shape[1]
+        step = keyed // shards
+        for r in range(2):
+            pair_ref[r : r + 1, :] = joined(places["pair_scale"] + r * step, step)
+        offset_ref[...] = joined(places["query_shift"], step)
+        feed_in_ref[...] = share(
+            places["feed_in_bias"], feed_in_ref.shape[1] * sections // shards
+        )
+        total = bias_ref.shape[1]
+        wide = (total - keyed - 2 * own) // 2
+        base_all = 2 * width + keyed + wide * sections
+        base_buf[...] = joined(places["base_bias"], base_all // shards)
+        low = wide + own + keyed
+        bias_ref[:, :wide] = share(places["value_bias"], wide * sections // shards)
+        bias_ref[:, wide : wide + own] = base_buf[:, mine]
+        bias_ref[:, wide + own : low] = base_buf[:, width : width + keyed]
+        bias_ref[:, low : low + wide] = pick(
+            base_buf, (slice(None),), width + keyed, wide * sections, shards, sections
+        )
+        start = pl.multiple_of(width + keyed + wide * sections + section * own, LANES)
+        bias_ref[:, low + wide :] = base_buf[:, pl.ds(start, own)]
+
+
+def unpack(everyone, places, sizes, sections):
+    shards, layers = everyone.shape[:2]
+    width, dims, total, hidden, keyed, base = sizes
+    own = width // sections
+    one_layer = (
+        [shape((1, width), F32)] * 5
+        + [shape((8, own), F32)]
+        + [shape((dims, CHUNKS, own), F32)] * 2
+        + [
+            shape((1, total), F32),
+            shape((1, hidden), F32),
+            shape((2, keyed), F32),
+            shape((1, keyed), F32),
+            shape((1, own), F32),
+            shape((1, own), F32),
+        ]
+    )
+    outs = pl.pallas_call(
+        functools.partial(unpack_kernel, layers, shards, sections, places),
+        out_shape=tuple(one_layer * layers),
+        in_specs=[vmem()],
+        out_specs=(vmem(),) * (len(one_layer) * layers),
+        scratch_shapes=[pltpu.VMEM((1, base), F32)],
+        cost_estimate=lasting(3),
+        compiler_params=params(),
+    )(everyone)
+    names = (
+        "gain",
+        "shift",
+        "feed_gain",
+        "feed_shift",
+        "feed_out",
+        "own",
+        "rate",
+        "coef",
+        "bias",
+        "feed_in",
+        "pair",
+        "offset",
+        "skip",
+        "own_out",
+    )
+    count = len(one_layer)
+    return [dict(zip(names, outs[k * count : (k + 1) * count])) for k in range(layers)]
 
 
 def body(
@@ -1386,139 +2033,81 @@
     keyed = pair_scale.shape[2] * shards
     hidden = feed_in_weight.shape[2]
 
-    base_parts = (
-        contiguous(base_weight[..., :width], sections, section),
-        base_weight[..., width : width + keyed],
-        interleaved(base_weight[..., width + keyed : width + keyed + wide], shards, sections, section),
-        contiguous(base_weight[..., width + keyed + wide :], sections, section),
-    )
-    in_shard = jnp.concatenate(
-        (interleaved(value_weight, shards, sections, section),) + base_parts, axis=2
-    )
-
-    def quarter_rows(array):
-        split = array.reshape(layers, sections, -1, array.shape[2])
-        return lax.dynamic_index_in_dim(split, section, 1, keepdims=False)
-
-    out_shard = quarter_rows(out_weight)
-    feed_in_shard = interleaved(feed_in_weight, shards, sections, section)
-    feed_out_shard = quarter_rows(feed_out_weight)
+    share = wide // sections
+    total = share + own + keyed + share + own
 
     def over_dp(array):
         return lax.all_gather(array, "dp", axis=0, tiled=True)
 
     weights = []
     for layer in range(layers):
-        weights.append(
-            (
-                over_dp(in_shard[layer]),
-                over_dp(out_shard[layer]),
-                over_dp(feed_in_shard[layer]),
-                over_dp(feed_out_shard[layer]),
-            )
-        )
-
-    smalls = (
-        norm_gain,
-        norm_shift,
-        average_decay,
-        average_input,
-        average_output,
-        average_skip,
-        value_bias,
-        base_bias,
-        pair_scale,
-        query_shift,
-        feed_gain,
-        feed_shift,
-        feed_in_bias,
-        feed_out_bias,
+        attention = pack(
+            pack_attention_kernel,
+            layer,
+            total + width // 2,
+            shards,
+            sections,
+            value_weight,
+            base_weight,
+            out_weight,
+        )
+        feed = pack(
+            pack_feed_kernel,
+            layer,
+            hidden // sections + width,
+            shards,
+            sections,
+            feed_in_weight,
+            feed_out_weight,
+        )
+        weights.append((over_dp(attention), over_dp(feed)))
+
+    smalls = dict(
+        norm_gain=norm_gain,
+        norm_shift=norm_shift,
+        average_decay=average_decay,
+        average_input=average_input,
+        average_output=average_output,
+        average_skip=average_skip,
+        feed_gain=feed_gain,
+        feed_shift=feed_shift,
+        feed_out_bias=feed_out_bias,
+        value_bias=value_bias,
+        feed_in_bias=feed_in_bias,
+        base_bias=base_bias,
+        pair_scale=pair_scale,
+        query_shift=query_shift,
     )
-    packed = jnp.concatenate([a.reshape(layers, -1) for a in smalls], axis=1)
-    everyone = lax.all_gather(packed, "dp", axis=0)
-    full = []
+    packed = jnp.concatenate([a.reshape(layers, -1) for a in smalls.values()], axis=1)
+    places = {}
     low = 0
-    for a in smalls:
-        size = a.size // layers
-        piece = everyone[:, :, low : low + size].reshape((shards,) + a.shape)
-        piece = jnp.moveaxis(piece, 0, a.ndim - 1)
-        full.append(piece.reshape(a.shape[:-1] + (-1,)))
-        low += size
-    (
-        gain_all,
-        shift_all,
-        decay_all,
-        input_all,
-        output_all,
-        skip_all,
-        value_bias_all,
-        base_bias_all,
-        pair_all,
-        offset_all,
-        feed_gain_all,
-        feed_shift_all,
-        feed_in_bias_all,
-        feed_out_bias_all,
-    ) = full
-    rate_all = jax.nn.sigmoid(contiguous(decay_all, sections, section))
-    input_own = contiguous(input_all, sections, section)
-    output_own = contiguous(output_all, sections, section)
-    drive_all = (1.0 - rate_all) * input_own
-    coef_all = drive_all * output_own
-    skip_own = contiguous(skip_all, sections, section)
-    gain_own = contiguous(gain_all, sections, section)
-    shift_own = contiguous(shift_all, sections, section)
-    in_bias = jnp.concatenate(
-        (
-            interleaved(value_bias_all, shards, sections, section),
-            contiguous(base_bias_all[:, :width], sections, section),
-            base_bias_all[:, width : width + keyed],
-            interleaved(
-                base_bias_all[:, width + keyed : width + keyed + wide], shards, sections, section
-            ),
-            contiguous(base_bias_all[:, width + keyed + wide :], sections, section),
-        ),
-        axis=1,
+    for name, array in smalls.items():
+        places[name] = low
+        low += array.size // layers
+    dims = average_decay.shape[1]
+    small = unpack(
+        lax.all_gather(packed, "dp", axis=0),
+        places,
+        (width, dims, total, hidden // sections, keyed, base_weight.shape[2]),
+        sections,
     )
-    feed_in_bias_own = interleaved(feed_in_bias_all, shards, sections, section)
-    feed_out_bias_own = contiguous(feed_out_bias_all, sections, section)
-    feed_gain_own = contiguous(feed_gain_all, sections, section)
 
     idents = iter(range(64))
-    x = tokens[0]
+    x0 = x = tokens[0]
     kept = []
     for layer in range(layers):
-        in_w, out_w, feed_in_w, feed_out_w = weights[layer]
-        row = slice(layer, layer + 1)
+        attention_w, feed_w = weights[layer]
+        p = small[layer]
         normed, mixed_own, pre, own_n, scale = average_forward(
-            lengths,
-            x,
-            gain_all[row],
-            shift_all[row],
-            rate_all[layer],
-            coef_all[layer],
-            skip_own[row],
+            lengths, x, p["gain"], p["shift"], p["rate"], p["coef"], p["skip"]
         )
         mixed = gather_columns(mixed_own, sections, next(idents))
         part, update, shared, reset, cand, value, att, gated, probs = attention_forward(
-            lengths,
-            normed,
-            mixed,
-            in_w,
-            in_bias[row],
-            pair_all[layer],
-            offset_all[row],
-            out_w,
-            own,
+            lengths, normed, mixed, attention_w, p["bias"], p["pair"], p["offset"], own, shards
         )
         middle, hidden_pre = attention_join(part, update, cand, x, next(idents))
         feed_part, feed_pre, feed_n, feed_normed, feed_scale = feed_forward(
-            middle,
-            feed_gain_all[row],
-            feed_shift_all[row],
-            feed_in_w,
-            feed_in_bias_own[row],
-            feed_out_w,
+            middle, p["feed_gain"], p["feed_shift"], feed_w, p["feed_in"]
         )
         kept.append(
             dict(
@@ -1539,60 +2128,85 @@
             )
         )
         if layer + 1 < layers:
-            x = feed_join(feed_part, feed_out_bias_own[row], middle, next(idents))
+            x = feed_join(feed_part, p["own_out"], middle, next(idents))
         else:
-            block_out = feed_last(feed_part, feed_out_bias_all[row], middle, next(idents))
-
-    def weight_grad(left, right):
-        return dot(left, right, 0, 0).astype(BF16)
+            block_out = feed_last(feed_part, p["feed_out"], middle, next(idents))
 
     def scattered(grad):
         return lax.psum_scatter(grad, "dp", scatter_dimension=0, tiled=True)
 
+    def over_sections(array):
+        return lax.all_gather(array, "section", axis=0)
+
     given = cotangent[0]
-    big = [None] * layers
-    small = [None] * layers
+    feed_grads = [None] * layers
+    attention_grads = [None] * layers
+    channel_sums = [None] * layers
+    feed_one = None
     for layer in reversed(range(layers)):
-        in_w, out_w, feed_in_w, feed_out_w = weights[layer]
-        k = kept[layer]
-        row = slice(layer, layer + 1)
+        attention_w, feed_w = weights[layer]
+        k, p = kept[layer], small[layer]
+        own_rows = p["own"]
         done = feed_backward(
-            given, k["feed_pre"], k["feed_n"], feed_gain_all[row], feed_in_w, feed_out_w
+            given,
+            k["feed_pre"],
+            k["feed_n"],
+            p["feed_gain"],
+            feed_w,
+            () if layer else (feed_one,),
         )
         part, stats, gpre, act, feed_sums, feed_bias = done[:6]
         g = done[6] if isinstance(given, tuple) else given
-        gout, gupdate, resid = back_join(
+        gout, gupdate, resid, feed_grad = back_join(
             part,
             stats,
             k["feed_scale"],
-            feed_gain_own[row],
+            own_rows,
             k["update"],
             k["hidden"],
+            k["feed_normed"],
+            gpre,
+            act,
             g,
+            feed_sums,
+            feed_bias,
             k["feed_n"],
             k["x"],
+            shards,
             next(idents),
         )
-        feed_in_grad = scattered(weight_grad(k["feed_normed"], gpre))
-        feed_out_grad = scattered(weight_grad(act, g))
+        feed_grads[layer] = scattered(feed_grad)
         gmixed_part, gvalue_part, gbase, gvalue, bias_sums, pair_sums = attention_backward(
             lengths,
             gout,
             gupdate,
             k["saved"],
-            in_w,
-            pair_all[layer],
-            offset_all[row],
-            out_w,
-        )
-        gmixed, gnormed = reduce_two(gmixed_part, gvalue_part, own, next(idents))
-        in_grad = scattered(
-            jnp.concatenate(
-                (weight_grad(k["normed"], gvalue), weight_grad(k["mixed"], gbase)), axis=1
-            )
-        )
-        out_grad = scattered(weight_grad(k["gated"], gout))
-        z, zstats, of_states, of_slopes, channel_sums = average_backward(
+            attention_w,
+            p["pair"],
+            p["offset"],
+            shards,
+            () if layer else (attention_grads[1],),
+        )
+        gmixed, gnormed, attention_grad = reduce_two(
+            gmixed_part,
+            gvalue_part,
+            k["normed"],
+            gvalue,
+            k["mixed"],
+            gbase,
+            k["gated"],
+            gout,
+            bias_sums,
+            pair_sums,
+            own,
+            shards,
+            next(idents),
+        )
+        attention_grads[layer] = scattered(attention_grad)
+        if layer:
+            held, gmixed = lax.optimization_barrier((feed_grads[layer], gmixed))
+            feed_one = over_sections(held)
+        z, zstats, channel_sums[layer] = average_backward(
             lengths,
             gmixed,
             gnormed,
@@ -1600,118 +2214,78 @@
             k["own_n"],
             k["scale"],
             resid,
-            gain_own[row],
-            shift_own[row],
-            rate_all[layer],
-            coef_all[layer],
-            skip_own[row],
+            own_rows,
+            p["rate"],
+            p["coef"],
+            p["skip"],
+            () if layer else (feed_grads[0],),
         )
         if layer:
-            whole_z, total = gather_stats(z, zstats, sections, next(idents))
-            given = (whole_z, total, k["x"])
-        else:
-            input_grad = last_rows(z, zstats, k["x"], next(idents))
-        big[layer] = (in_grad, out_grad, feed_in_grad, feed_out_grad)
-
-        rate, drive = rate_all[layer], drive_all[layer]
-        gdrive = output_own[layer] * of_states
-        grate = coef_all[layer] * of_slopes - input_own[layer] * gdrive
-        half_wide = wide // sections
-        offsets = (half_wide, half_wide + own, half_wide + own + keyed)
-        bias = bias_sums[0]
-        base_bias_grad = jnp.concatenate(
+            whole_z, means = gather_stats(z, zstats, sections, next(idents))
+            given = (whole_z, means, k["x"])
+
+    input_grad, attention_one, feed_zero = final_exchange(
+        z, zstats, x0, [attention_grads[1], feed_grads[0]], sections, next(idents)
+    )
+    channels, attention_zero = gather_sums(
+        jnp.concatenate(channel_sums, axis=0),
+        attention_grads[0],
+        sections,
+        shards,
+        own * shards // width,
+        next(idents),
+    )
+    shard = lax.axis_index("dp")
+    size = width // shards
+    rows = channels.shape[0]
+    channels = lax.dynamic_slice_in_dim(channels, shard * size % own, size, axis=1)
+    channels = channels.reshape(layers, rows // layers, size)
+    g_value, g_base, g_out, g_feed_in, g_feed_out, smalls_out, feed_smalls = assemble(
+        ((attention_zero, feed_zero), (attention_one, feed_one)),
+        shards,
+        width,
+        wide,
+        base_weight.shape[2],
+        hidden,
+    )
+
+    def of_shard(array):
+        part = array.shape[-1] // shards
+        return lax.dynamic_slice_in_dim(array, shard * part, part, axis=array.ndim - 1)
+
+    def woven(array):
+        split = array.reshape(layers, sections, shards, -1)
+        return split.transpose(0, 2, 1, 3).reshape(layers, -1)
+
+    of_states, of_slopes, sums = channels[:, :dims], channels[:, dims : 2 * dims], channels[:, 2 * dims :]
+    rate = jax.nn.sigmoid(average_decay)
+    gdrive = average_output * of_states
+    drive = (1.0 - rate) * average_input
+    grate = drive * average_output * of_slopes - average_input * gdrive
+    g_gain, g_shift, g_skip = sums[:, 0], sums[:, 1], sums[:, 2]
+    g_decay, g_input, g_output = grate * rate * (1.0 - rate), (1.0 - rate) * gdrive, drive * of_states
+
+    edge = share + own
+    bias_rows = total // LANES
+    bias = smalls_out[:, :, :bias_rows].reshape(layers, sections, total)
+    pairs = of_shard(jnp.sum(smalls_out[:, :, bias_rows : bias_rows + 3], axis=1))
+    g_pair, g_query = pairs[:, :2], pairs[:, 2]
+    g_value_bias = of_shard(woven(bias[..., :share]))
+    g_base_bias = of_shard(
+        jnp.concatenate(
             (
-                put_contiguous(bias[offsets[0] : offsets[1]], sections, section),
-                bias[offsets[1] : offsets[2]],
-                put_interleaved(
-                    bias[offsets[2] : offsets[2] + half_wide], shards, sections, section
-                ),
-                put_contiguous(bias[offsets[2] + half_wide :], sections, section),
-            )
-        )
-        alone = (section == 0).astype(F32)
-        small[layer] = (
-            put_contiguous(channel_sums[0], sections, section),
-            put_contiguous(channel_sums[1], sections, section),
-            put_contiguous(grate * rate * (1.0 - rate), sections, section),
-            put_contiguous((1.0 - rate) * gdrive, sections, section),
-            put_contiguous(drive * of_states, sections, section),
-            put_contiguous(channel_sums[2], sections, section),
-            put_interleaved(bias[:half_wide], shards, sections, section),
-            base_bias_grad,
-            pair_sums[0:2],
-            pair_sums[2],
-            feed_sums[0],
-            feed_sums[1],
-            put_interleaved(feed_bias[0], shards, sections, section),
-            feed_sums[2] * alone,
-        )
-
-    def to_shards(array):
-        lead = array.shape[:-1]
-        split = array.reshape(lead + (shards, -1))
-        return jnp.moveaxis(split, len(lead), 0).reshape(shards, -1)
-
-    small_totals = []
-    for layer in range(layers):
-        rows = jnp.concatenate([to_shards(a) for a in small[layer]], axis=1)
-        mine = lax.psum_scatter(rows, "dp", scatter_dimension=0, tiled=True)
-        small_totals.append(lax.psum(mine[0], "section"))
-    small_outs = []
-    low = 0
-    for a in smalls:
-        size = a.size // layers
-        small_outs.append(
-            jnp.stack([t[low : low + size].reshape(a.shape[1:]) for t in small_totals])
-        )
-        low += size
-
-    def over_sections(array):
-        return lax.all_gather(array, "section", axis=0)
-
-    def join_interleaved(array):
-        split = array.reshape(array.shape[:2] + (shards, -1))
-        return split.transpose(1, 2, 0, 3).reshape(array.shape[1], -1)
-
-    def join_contiguous(array):
-        return array.transpose(1, 0, 2).reshape(array.shape[1], -1)
-
-    value_grads, base_grads, out_grads, feed_in_grads, feed_out_grads = [], [], [], [], []
-    half_wide = wide // sections
-    for layer in range(layers):
-        in_grad, out_grad, feed_in_grad, feed_out_grad = (over_sections(a) for a in big[layer])
-        value_grads.append(join_interleaved(in_grad[..., :half_wide]).astype(F32))
-        low = half_wide + own
-        base_grads.append(
-            jnp.concatenate(
-                (
-                    join_contiguous(in_grad[..., half_wide:low]).astype(F32),
-                    jnp.sum(in_grad[..., low : low + keyed].astype(F32), axis=0),
-                    join_interleaved(in_grad[..., low + keyed : low + keyed + half_wide]).astype(F32),
-                    join_contiguous(in_grad[..., low + keyed + half_wide :]).astype(F32),
-                ),
-                axis=1,
-            )
-        )
-        out_grads.append(out_grad.reshape(-1, width).astype(F32))
-        feed_in_grads.append(join_interleaved(feed_in_grad).astype(F32))
-        feed_out_grads.append(feed_out_grad.reshape(-1, width).astype(F32))
-    (
-        g_gain,
-        g_shift,
-        g_decay,
-        g_input,
-        g_output,
-        g_skip,
-        g_value_bias,
-        g_base_bias,
-        g_pair,
-        g_query,
-        g_feed_gain,
-        g_feed_shift,
-        g_feed_in_bias,
-        g_feed_out_bias,
-    ) = small_outs
+                bias[..., share:edge].reshape(layers, -1),
+                jnp.sum(bias[..., edge : edge + keyed], axis=1),
+                woven(bias[..., edge + keyed : edge + keyed + share]),
+                bias[..., edge + keyed + share :].reshape(layers, -1),
+            ),
+            axis=1,
+        )
+    )
+    g_feed_gain = jnp.sum(feed_smalls[:, :, 0, :size], axis=1)
+    g_feed_shift = jnp.sum(feed_smalls[:, :, 1, :size], axis=1)
+    g_feed_out_bias = feed_smalls[:, 0, 2, :size]
+    g_feed_in_bias = feed_smalls[:, :, 3, :size].reshape(layers, -1)
     return (
         block_out[None],
         input_grad[None],
@@ -1721,18 +2295,18 @@
         g_input,
         g_output,
         g_skip,
-        jnp.stack(value_grads),
+        g_value,
         g_value_bias,
-        jnp.stack(base_grads),
+        g_base,
         g_base_bias,
         g_pair,
         g_query,
-        jnp.stack(out_grads),
+        g_out,
         g_feed_gain,
         g_feed_shift,
-        jnp.stack(feed_in_grads),
+        g_feed_in,
         g_feed_in_bias,
-        jnp.stack(feed_out_grads),
+        g_feed_out,
         g_feed_out_bias,
     )
 

time: 1200 us -> 679 us (0.57)
  waiting for transfers between devices: 424 us -> 9.23 us
  Pallas kernels: 522 us -> 621 us
  local copies, waits for them, and re-layouts: 106 us -> 8.31 us
  matrix products: 44.6 us -> 0 us
  other arithmetic: 36.5 us -> 4.24 us
  blocking collectives: 38.5 us -> 19.9 us
    reduce_scatter x8 -> x4, waiting for transfers between devices: 227 us -> 8.3 us  [scattered(): return lax.psum_scatter(grad, 'dp', scatter_dimension=0, tiled=True)]
    all_gather x6 -> x1, waiting for transfers between devices: 150 us -> 0.02 us  [over_sections(): return lax.all_gather(array, 'section', axis=0)]
    pallas_call x13 -> x20, Pallas kernels: 272 us -> 368 us  [the longest x2 84.4 us: back_join(): pl.pallas_call(functools.partial(back_join_kernel, shards), out_shape=(sh...]
    dot_general x10 -> x0, matrix products: 44.6 us -> none  [dot(): lax.dot_general(left, right, (((left_dim,), (right_dim,)), ((), ())), pre...]
    psum x1 -> x0, waiting for transfers between devices: 42.5 us -> none  [body(): small_totals.append(lax.psum(mine[0], 'section'))]
    slice x51 -> x5, local copies, waits for them, and re-layouts: 35.5 us -> 3.13 us  [the longest x2 1.29 us: body(): g_pair, g_query = (pairs[:, :2], pairs[:, 2])]
    unnamed x105 -> x49, local copies, waits for them, and re-layouts: 29.2 us -> 2.32 us
    another operation x21 -> x0, other arithmetic: 20.7 us -> none  [the longest x14 8.17 us: body(): jnp.stack([t[low:low + size].reshape(a.shape[1:]) for t in small_totals])]
  transfers between devices with their start and end apart: 24 -> 9, of which waited for: 16 -> 1; matrix products, arithmetic and copies ran while one was open for 11% -> 0% of each run, Pallas kernels for 21% -> 75%
where the time goes in v2:
time: 679 us; the launch traced here: 678 us
  Pallas kernels  621 us (91%)
  blocking collectives  19.9 us (3%)
  between operations  15 us (2%)
  waiting for transfers between devices  9.23 us (1%)
  local copies, waits for them, and re-layouts  8.31 us (1%)
    pallas_call x2, Pallas kernels, back_join(): pl.pallas_call(functools.partial(back_join_kernel, shards), out_shape=(sh...  84.4 us
    pallas_call x2, Pallas kernels, attention_join(): pl.pallas_call(attention_join_kernel, out_shape=(shape((count, width), BF...  77.5 us
    pallas_call x2, Pallas kernels, reduce_two(): pl.pallas_call(functools.partial(reduce_two_kernel, shards, len(after)),...  66.3 us
    pallas_call x1, Pallas kernels, final_exchange(): pl.pallas_call(functools.partial(final_kernel, number), out_shape=(shape(...  48 us
    pallas_call x2, Pallas kernels, gather_columns(): pl.pallas_call(gather_kernel, out_shape=shape((count, width * sections),...  43 us
    pallas_call x1, Pallas kernels, feed_join(): pl.pallas_call(feed_join_kernel, out_shape=shape((count, width), BF16), i...  36.8 us
    pallas_call x1, Pallas kernels, gather_stats(): pl.pallas_call(gather_stats_kernel, out_shape=(shape((count, width * sect...  35.4 us
    pallas_call x1, Pallas kernels, gather_sums(): pl.pallas_call(functools.partial(sums_kernel, shards, holders), out_shape...  34.4 us
  transfers between devices with their start and end apart: 9, of which 1 were waited for; matrix products, arithmetic and copies ran while one was open for 0% of the time, Pallas kernels for 75%

profile of v2, /device:TPU:0, one launch (start us, length us, event | category | flops | bytes accessed | tf_op | source)
XLA Modules:
  0.0 678.0 jit_solution(2478210849967926003)
XLA Ops:
  7.2 4.7 shard_map.376
  12.0 2.5 shard_map.379
  14.6 4.7 shard_map.384
  19.5 2.5 shard_map.387
  23.1 19.9 %all-gather.2.everyone_ref = f32[8,2,8256]{2,1,0:T(2,128)} all-gather(f32[1,2,8256]{2,1,0:T(2,128)S(1)} %bitcast.37), channel_id=2, replica_groups=mesh['section'=4,'dp'=8] {'dp'}, dimensions={0}, use_global_device_ids=true | all-gather | bytes 594432 | tf_op jit(solution)/shard_map/all_gather | solution.py:2089
  43.1 2.7 shard_map.373
  45.8 11.8 %shard_map.374 = (bf16[1024,1024]{1,0:T(8,128)(2,1)}, bf16[1024,256]{1,0:T(8,128)(2,1)}, bf16[1024,256]{1,0:T(8,128)(2,1)}, f32[1024,256]{1,0:T(8,128)}, f32[1024,128]{1,0:T(8,128)}) custom-call(s32[1]{0:T(128)S(6)} %copy.71.length_ref.refs_0_.refs_1_, bf16[1024,1024]{1,0:T(8,128)(2,1)} %bitcast.60, f32[1,1024]{1,0:T(1,128)} %get-tuple-element.150.gain_ref, ...), custom_call_target="tpu_custom_call" | custom-call | flops 12999999488 | bytes 39000000 | tf_op jit(solution)/shard_map/pallas_call | solution.py:222
  57.6 24.5 %shard_map.375.mixed_ref.refs_4_ = bf16[1024,1024]{1,0:T(8,128)(2,1)} custom-call(bf16[1024,256]{1,0:T(8,128)(2,1)} %get-tuple-element.156.own_ref), custom_call_target="tpu_custom_call" | custom-call | flops 17999998976 | bytes 54000000 | tf_op jit(solution)/shard_map/pallas_call | solution.py:973
  82.1 11.9 %shard_map.377 = (bf16[1024,1024]{1,0:T(8,128)(2,1)}, bf16[1024,256]{1,0:T(8,128)(2,1)}, bf16[1024,128]{1,0:T(8,128)(2,1)}, bf16[1024,512]{1,0:T(8,128)(2,1)}, b...) custom-call(s32[1]{0:T(128)S(6)} %copy.71.length_ref.refs_0_.refs_1_, ...), custom_call_target="tpu_custom_call" | custom-call | flops 12000000000 | bytes 36000000 | tf_op jit(solution)/shard_map/pallas_call | solution.py:499
  94.1 41.3 %shard_map.378 = (bf16[1024,1024]{1,0:T(8,128)(2,1)}, bf16[1024,256]{1,0:T(8,128)(2,1)}) custom-call(bf16[1024,1024]{1,0:T(8,128)(2,1)} %get-tuple-element.160.part_ref, bf16[1024,256]{1,0:T(8,128)(2,1)} %get-tuple-element.161.update_ref, bf16[1024,256]{1,0:T(8,128)(2,1)} %get-tuple-element.162.cand_ref, bf16[1024,1024]{1,0:T(8,128)(2,1)} %bitcast.61), custom_call_target="tpu_custom_call" | custom-call | flops 36999999488 | bytes 111000000 | tf_op jit(solution)/shard_map/pallas_call | solution.py:1078
  135.4 10.1 %shard_map.380 = (bf16[1024,1024]{1,0:T(8,128)(2,1)}, bf16[1024,1024]{1,0:T(8,128)(2,1)}, bf16[1024,1024]{1,0:T(8,128)(2,1)}, bf16[1024,1024]{1,0:T(8,128)(2,1)}, f32[1024,128]{1,0:T(8,128)}) custom-call(bf16[1024,1024]{1,0:T(8,128)(2,1)} %get-tuple-element.163.x_ref, f32[1,1024]{1,0:T(1,128)} %get-tuple-element.164.gain_ref.refs_6_, ...), custom_call_target="tpu_custom_call" | custom-call | flops 10000000000 | bytes 30000000 | tf_op jit(solution)/shard_map/pallas_call | solution.py:686
  145.5 36.8 %shard_map.381.x_ref.refs_3_ = bf16[1024,1024]{1,0:T(8,128)(2,1)} custom-call(bf16[1024,1024]{1,0:T(8,128)(2,1)} %get-tuple-element.167.part_ref, f32[1,256]{1,0:T(1,128)} %get-tuple-element.168.bias_ref, bf16[1024,1024]{1,0:T(8,128)(2,1)} %get-tuple-element.163.x_ref), custom_call_target="tpu_custom_call" | custom-call | flops 35999997952 | bytes 108000000 | tf_op jit(solution)/shard_map/pallas_call | solution.py:1141
  182.4 11.8 %shard_map.382 = (bf16[1024,1024]{1,0:T(8,128)(2,1)}, bf16[1024,256]{1,0:T(8,128)(2,1)}, bf16[1024,256]{1,0:T(8,128)(2,1)}, f32[1024,256]{1,0:T(8,128)}, f32[1024,128]{1,0:T(8,128)}) custom-call(s32[1]{0:T(128)S(6)} %copy.71.length_ref.refs_0_.refs_1_, bf16[1024,1024]{1,0:T(8,128)(2,1)} %shard_map.381.x_ref.refs_3_, f32[1,1024]{1,0:T(1,128)} %get-tuple-element.169.gain_ref, ...), custom_call_target="tpu_custom_call" | custom-call | flops 12999999488 | bytes 39000000 | tf_op jit(solution)/shard_map/pallas_call | solution.py:222
  194.2 18.5 %shard_map.383.mixed_ref.refs_4_ = bf16[1024,1024]{1,0:T(8,128)(2,1)} custom-call(bf16[1024,256]{1,0:T(8,128)(2,1)} %get-tuple-element.175.own_ref), custom_call_target="tpu_custom_call" | custom-call | flops 17999998976 | bytes 54000000 | tf_op jit(solution)/shard_map/pallas_call | solution.py:973
  212.7 11.9 %shard_map.385 = (bf16[1024,1024]{1,0:T(8,128)(2,1)}, bf16[1024,256]{1,0:T(8,128)(2,1)}, bf16[1024,128]{1,0:T(8,128)(2,1)}, bf16[1024,512]{1,0:T(8,128)(2,1)}, b...) custom-call(s32[1]{0:T(128)S(6)} %copy.71.length_ref.refs_0_.refs_1_, ...), custom_call_target="tpu_custom_call" | custom-call | flops 12000000000 | bytes 36000000 | tf_op jit(solution)/shard_map/pallas_call | solution.py:499
  224.6 36.2 %shard_map.386 = (bf16[1024,1024]{1,0:T(8,128)(2,1)}, bf16[1024,256]{1,0:T(8,128)(2,1)}) custom-call(bf16[1024,1024]{1,0:T(8,128)(2,1)} %get-tuple-element.179.part_ref, bf16[1024,256]{1,0:T(8,128)(2,1)} %get-tuple-element.180.update_ref, bf16[1024,256]{1,0:T(8,128)(2,1)} %get-tuple-element.181.cand_ref, bf16[1024,1024]{1,0:T(8,128)(2,1)} %shard_map.381.x_ref.refs_3_), custom_call_target="tpu_custom_call" | custom-call | flops 36999999488 | bytes 111000000 | tf_op jit(solution)/shard_map/pallas_call | solution.py:1078
  260.9 10.0 %shard_map.388 = (bf16[1024,1024]{1,0:T(8,128)(2,1)}, bf16[1024,1024]{1,0:T(8,128)(2,1)}, bf16[1024,1024]{1,0:T(8,128)(2,1)}, bf16[1024,1024]{1,0:T(8,128)(2,1)}, f32[1024,128]{1,0:T(8,128)}) custom-call(bf16[1024,1024]{1,0:T(8,128)(2,1)} %get-tuple-element.182.x_ref, f32[1,1024]{1,0:T(1,128)} %get-tuple-element.183.gain_ref.refs_3_, ...), custom_call_target="tpu_custom_call" | custom-call | flops 10000000000 | bytes 30000000 | tf_op jit(solution)/shard_map/pallas_call | solution.py:686
  270.9 11.5 %shard_map.390 = (bf16[1024,1024]{1,0:T(8,128)(2,1)}, f32[8,1024]{1,0:T(8,128)}, bf16[1024,1024]{1,0:T(8,128)(2,1)}, bf16[1024,1024]{1,0:T(8,128)(2,1)}, f32[8,1024]{1,0:T(8,128)}, /*index=5*/f32[8,1024]{1,0:T(8,128)}) custom-call(bf16[1024,1024]{1,0:T(8,128)(2,1)} %bitcast.58, bf16[1024,1024]{1,0:T(8,128)(2,1)} %get-tuple-element.188.refs_1_, ...), custom_call_target="tpu_custom_call" | custom-call | flops 12999999488 | bytes 39000000 | tf_op jit(solution)/shard_map/pallas_call | solution.py:766
  282.4 42.3 %shard_map.391 = (bf16[1024,1024]{1,0:T(8,128)(2,1)}, bf16[1024,256]{1,0:T(8,128)(2,1)}, f32[1024,256]{1,0:T(8,128)}, bf16[1024,2176]{1,0:T(8,128)(2,1)}) custom-call(bf16[1024,1024]{1,0:T(8,128)(2,1)} %get-tuple-element.190.part_ref, f32[8,1024]{1,0:T(8,128)} %get-tuple-element.191.stats_ref, f32[1024,128]{1,0:T(8,128)} %get-tuple-element.192.scale_ref, ...), custom_call_target="tpu_custom_call" | custom-call | flops 43000000512 | bytes 129000000 | tf_op jit(solution)/shard_map/pallas_call | solution.py:1337
  324.8 13.4 %shard_map.392 = (bf16[1024,1024]{1,0:T(8,128)(2,1)}, bf16[1024,1024]{1,0:T(8,128)(2,1)}, bf16[1024,1152]{1,0:T(8,128)(2,1)}, bf16[1024,512]{1,0:T(8,128)(2,1)}, f32[8,1664]{1,0:T(8,128)}, /*index=5*/f32[8,128]{1,0:T(8,128)}) custom-call(s32[1]{0:T(128)S(6)} %copy.71.length_ref.refs_0_.refs_1_, bf16[1024,1024]{1,0:T(8,128)(2,1)} %get-tuple-element.201.refs_1_.refs_7_, ...), custom_call_target="tpu_custom_call" | custom-call | flops 12999999488 | bytes 39000000 | tf_op jit(solution)/shard_map/pallas_call | solution.py:624
  338.2 31.5 %shard_map.393 = (f32[1024,256]{1,0:T(8,128)}, f32[1024,256]{1,0:T(8,128)}, bf16[1024,2304]{1,0:T(8,128)(2,1)}) custom-call(bf16[1024,1024]{1,0:T(8,128)(2,1)} %get-tuple-element.208.refs_0_, bf16[1024,1024]{1,0:T(8,128)(2,1)} %get-tuple-element.209.refs_1_, bf16[1024,1024]{1,0:T(8,128)(2,1)} %get-tuple-element.174.normed_ref.refs_2_, ...), custom_call_target="tpu_custom_call" | custom-call | flops 35999997952 | bytes 108000000 | tf_op jit(solution)/shard_map/pallas_call | solution.py:1496
  369.7 8.3 %reduce-scatter.5.cloned.1.call-done = bf16[128,2176]{1,0:T(8,128)(2,1)} async-done(((bf16[1024,2176]{1,0:T(8,128)(2,1)}), bf16[128,2176]{1,0:T(8,128)(2,1)}) %reduce-scatter.5.cloned.1.call-update) | async-done | bytes 557072 | tf_op jit(solution)/shard_map/reduce_scatter | solution.py:2136
  378.1 0.7 reduce-scatter.9.cloned.1.call-update
  378.8 15.1 %shard_map.394 = (bf16[1024,256]{1,0:T(8,128)(2,1)}, f32[8,1024]{1,0:T(8,128)}, f32[40,256]{1,0:T(8,128)}) custom-call(s32[1]{0:T(128)S(6)} %copy.71.length_ref.refs_0_.refs_1_, f32[1024,256]{1,0:T(8,128)} %get-tuple-element.217.refs_1_, f32[1024,256]{1,0:T(8,128)} %get-tuple-element.218.refs_2_, bf16[1024,256]{1,0:T(8,128)(2,1)} %get-tuple-element.219.refs_3_, ...), custom_call_target="tpu_custom_call" | custom-call | flops 20999999488 | bytes 63000000 | tf_op jit(solution)/shard_map/pallas_call | solution.py:394
  393.9 35.4 %shard_map.395 = (bf16[1024,1024]{1,0:T(8,128)(2,1)}, f32[8,1024]{1,0:T(8,128)}) custom-call(bf16[1024,256]{1,0:T(8,128)(2,1)} %get-tuple-element.223.own_ref, f32[8,1024]{1,0:T(8,128)} %get-tuple-element.224.stats_ref), custom_call_target="tpu_custom_call" | custom-call | flops 20000000000 | bytes 60000000 | tf_op jit(solution)/shard_map/pallas_call | solution.py:1014
  429.4 14.1 %shard_map.396 = (bf16[1024,1024]{1,0:T(8,128)(2,1)}, f32[8,1024]{1,0:T(8,128)}, bf16[1024,1024]{1,0:T(8,128)(2,1)}, bf16[1024,1024]{1,0:T(8,128)(2,1)}, f32[8,1...) custom-call(bf16[4,128,2176]{2,1,0:T(8,128)(2,1)} %bitcast.56, ...), custom_call_target="tpu_custom_call" | custom-call | flops 12999999488 | bytes 39000000 | tf_op jit(solution)/shard_map/pallas_call | solution.py:766
  443.5 42.1 %shard_map.397 = (bf16[1024,1024]{1,0:T(8,128)(2,1)}, bf16[1024,256]{1,0:T(8,128)(2,1)}, f32[1024,256]{1,0:T(8,128)}, bf16[1024,2176]{1,0:T(8,128)(2,1)}) custom-call(bf16[1024,1024]{1,0:T(8,128)(2,1)} %get-tuple-element.229.part_ref, f32[8,1024]{1,0:T(8,128)} %get-tuple-element.230.stats_ref, f32[1024,128]{1,0:T(8,128)} %get-tuple-element.231.scale_ref, ...), custom_call_target="tpu_custom_call" | custom-call | flops 43000000512 | bytes 129000000 | tf_op jit(solution)/shard_map/pallas_call | solution.py:1337
  485.8 13.6 %shard_map.398 = (bf16[1024,1024]{1,0:T(8,128)(2,1)}, bf16[1024,1024]{1,0:T(8,128)(2,1)}, bf16[1024,1152]{1,0:T(8,128)(2,1)}, bf16[1024,512]{1,0:T(8,128)(2,1)}, f32[8,1664]{1,0:T(8,128)}, /*index=5*/f32[8,128]{1,0:T(8,128)}) custom-call(bf16[128,2304]{1,0:T(8,128)(2,1)} %reduce-scatter.9.cloned.1.call-done.refs_0_, s32[1]{0:T(128)S(6)} %copy.71.length_ref.refs_0_.refs_1_, ...), custom_call_target="tpu_custom_call" | custom-call | flops 12999999488 | bytes 39000000 | tf_op jit(solution)/shard_map/pallas_call | solution.py:624
  499.4 34.7 %shard_map.399 = (f32[1024,256]{1,0:T(8,128)}, f32[1024,256]{1,0:T(8,128)}, bf16[1024,2304]{1,0:T(8,128)(2,1)}) custom-call(bf16[1024,1024]{1,0:T(8,128)(2,1)} %get-tuple-element.249.refs_0_, bf16[1024,1024]{1,0:T(8,128)(2,1)} %get-tuple-element.250.refs_1_, bf16[1024,1024]{1,0:T(8,128)(2,1)} %get-tuple-element.155.normed_ref.refs_2_, ...), custom_call_target="tpu_custom_call" | custom-call | flops 35999997952 | bytes 108000000 | tf_op jit(solution)/shard_map/pallas_call | solution.py:1496
  534.2 16.6 %shard_map.389 = bf16[256,1024]{1,0:T(8,128)(2,1)} custom-call(bf16[1024,1024]{1,0:T(8,128)(2,1)} %get-tuple-element.186.part_ref, f32[1,1024]{1,0:T(1,128)} %get-tuple-element.187.bias_ref, bf16[1024,1024]{1,0:T(8,128)(2,1)} %get-tuple-element.182.x_ref), custom_call_target="tpu_custom_call" | custom-call | flops 20000000000 | bytes 60000000 | tf_op jit(solution)/shard_map/pallas_call | solution.py:1189
  550.9 15.1 %shard_map.400 = (bf16[1024,256]{1,0:T(8,128)(2,1)}, f32[8,1024]{1,0:T(8,128)}, f32[40,256]{1,0:T(8,128)}) custom-call(bf16[128,2176]{1,0:T(8,128)(2,1)} %reduce-scatter.7.cloned.1.call-done.refs_0_.refs_1_, s32[1]{0:T(128)S(6)} %copy.71.length_ref.refs_0_.refs_1_, f32[1024,256]{1,0:T(8,128)} %get-tuple-element.256.refs_2_, ...), custom_call_target="tpu_custom_call" | custom-call | flops 20999999488 | bytes 63000000 | tf_op jit(solution)/shard_map/pallas_call | solution.py:394
  566.0 48.0 %shard_map.401 = (bf16[256,1024]{1,0:T(8,128)(2,1)}, bf16[4,128,2304]{2,1,0:T(8,128)(2,1)}, bf16[4,128,2176]{2,1,0:T(8,128)(2,1)}) custom-call(bf16[1024,256]{1,0:T(8,128)(2,1)} %get-tuple-element.262.z_ref, f32[8,1024]{1,0:T(8,128)} %get-tuple-element.263.stats_ref, bf16[1024,1024]{1,0:T(8,128)(2,1)} %bitcast.63, ...), custom_call_target="tpu_custom_call" | custom-call | flops 49999998976 | bytes 150000000 | tf_op jit(solution)/shard_map/pallas_call | solution.py:1575
  614.0 0.6 pad_maximum_fusion.sums_ref
  614.7 34.4 %shard_map.402 = (f32[80,256]{1,0:T(8,128)}, bf16[4,128,2304]{2,1,0:T(8,128)(2,1)}) custom-call(f32[80,256]{1,0:T(8,128)} %pad_maximum_fusion.sums_ref, bf16[128,2304]{1,0:T(8,128)(2,1)} %reduce-scatter.11.cloned.1.call-done.block_ref), custom_call_target="tpu_custom_call" | custom-call | flops 24999999488 | bytes 75000000 | tf_op jit(solution)/shard_map/pallas_call | solution.py:1672
  649.1 0.8 constant_dynamic-slice_fusion.3
  650.5 0.6 slice_multiply_fusion.1
  651.1 10.8 %shard_map.403 = (f32[2,128,2048]{2,1,0:T(8,128)}, f32[2,128,4224]{2,1,0:T(8,128)}, f32[2,256,1024]{2,1,0:T(8,128)}, f32[2,128,4096]{2,1,0:T(8,128)}, f32[2,512,...) custom-call(bf16[4,128,2304]{2,1,0:T(8,128)(2,1)} %get-tuple-element.269.refs_0_, ...), custom_call_target="tpu_custom_call" | custom-call | flops 8999999488 | bytes 27000000 | tf_op jit(solution)/shard_map/pallas_call | solution.py:1767
  661.9 0.9 reshape.83
  662.8 0.8 slice_reduce_fusion
  663.6 1.5 slice_reduce_fusion.2
  665.1 1.3 slice.75
  666.7 0.7 constant_dynamic-slice_fusion
  667.4 0.6 constant_dynamic-slice_fusion.1
  668.0 0.6 copy.68
  668.6 0.6 constant_dynamic-slice_fusion.2
  669.2 0.7 fusion.6
  669.9 0.8 copy.72
  670.7 0.8 copy.73
  (83 shorter events, 2.0 us)
Async XLA Ops:
  7.2 75.0 %all-gather.9.cloned.1.call-start = ((), (), s32[]{:S(2)}) async-start(), calls=%async_computation.4 | async-start | bytes 5013504 | tf_op jit(solution)/shard_map/all_gather | solution.py:2040
  11.9 123.5 %all-gather.11.cloned.1.call-start = ((), (), s32[]{:S(2)}) async-start(), calls=%async_computation.5 | async-start | bytes 4718592 | tf_op jit(solution)/shard_map/all_gather | solution.py:2040
  14.5 198.2 %all-gather.13.cloned.1.call-start = ((), (), s32[]{:S(2)}) async-start(), calls=%async_computation.6 | async-start | bytes 5013504 | tf_op jit(solution)/shard_map/all_gather | solution.py:2040
  19.3 3.5 copy-start.2
  19.3 3.5 copy-start.13
  19.3 3.6 copy-start.4
  19.3 3.6 copy-start.6
  19.4 3.6 copy-start.10
  19.4 3.6 copy-start.11
  19.4 3.6 copy-start.12
  19.4 3.6 copy-start.14
  19.4 3.6 copy-start.15
  19.4 3.6 copy-start.16
  19.4 3.6 copy-start.17
  19.4 3.6 copy-start.18
  19.5 3.6 copy-start.19
  19.5 3.6 copy-start.20
  19.5 241.4 %all-gather.15.cloned.1.call-start = ((), (), s32[]{:S(2)}) async-start(), calls=%async_computation.7 | async-start | bytes 4718592 | tf_op jit(solution)/shard_map/all_gather | solution.py:2040
  22.1 355.9 %reduce-scatter.5.cloned.1.call-start = ((), (), s32[]{:S(2)}) async-start(), calls=%async_computation.8 | async-start | bytes 5013504 | tf_op jit(solution)/shard_map/reduce_scatter | solution.py:2136
  324.7 104.7 %all-gather.17.cloned.1.call-start = ((), (), s32[]{:S(2)}) async-start(), calls=%async_computation.12 | async-start | bytes 2785280 | tf_op jit(solution)/shard_map/all_gather | solution.py:2139
  378.0 107.7 %reduce-scatter.9.cloned.1.call-start = ((), (), s32[]{:S(2)}) async-start(), calls=%async_computation.10 | async-start | bytes 5308416 | tf_op jit(solution)/shard_map/reduce_scatter | solution.py:2136
  378.8 172.1 %reduce-scatter.7.cloned.1.call-start = ((), (), s32[]{:S(2)}) async-start(), calls=%async_computation.9 | async-start | bytes 5013504 | tf_op jit(solution)/shard_map/reduce_scatter | solution.py:2136
  485.7 129.0 %reduce-scatter.11.cloned.1.call-start = ((), (), s32[]{:S(2)}) async-start(), calls=%async_computation.11 | async-start | bytes 5308416 | tf_op jit(solution)/shard_map/reduce_scatter | solution.py:2136
  566.0 48.0 %copy-start.8 = (f32[40,256]{1,0:T(8,128)S(1)}, f32[40,256]{1,0:T(8,128)}, u32[]{:S(2)}) copy-start(f32[40,256]{1,0:T(8,128)} %get-tuple-element.266) | copy-start | bytes 122884
  566.0 48.0 %copy-start.9 = (f32[40,256]{1,0:T(8,128)S(1)}, f32[40,256]{1,0:T(8,128)}, u32[]{:S(2)}) copy-start(f32[40,256]{1,0:T(8,128)} %get-tuple-element.265) | copy-start | bytes 122884
  614.7 35.8 %copy-start.3 = (f32[2,16,128]{2,1,0:T(8,128)S(1)}, f32[2,16,128]{2,1,0:T(8,128)}, u32[]{:S(2)}) copy-start(f32[2,16,128]{2,1,0:T(8,128)} %param.27) | copy-start | bytes 49156
  614.7 35.8 %copy-start.5 = (f32[2,16,128]{2,1,0:T(8,128)S(1)}, f32[2,16,128]{2,1,0:T(8,128)}, u32[]{:S(2)}) copy-start(f32[2,16,128]{2,1,0:T(8,128)} %param.29) | copy-start | bytes 49156
  614.7 35.8 %copy-start.7 = (f32[2,16,128]{2,1,0:T(8,128)S(1)}, f32[2,16,128]{2,1,0:T(8,128)}, u32[]{:S(2)}) copy-start(f32[2,16,128]{2,1,0:T(8,128)} %param.28) | copy-start | bytes 49156
  651.1 18.8 %copy-start = (bf16[256,1024]{1,0:T(8,128)(2,1)S(1)}, bf16[256,1024]{1,0:T(8,128)(2,1)}, u32[]{:S(2)}) copy-start(bf16[256,1024]{1,0:T(8,128)(2,1)} %shard_map.389) | copy-start | bytes 1572868
  661.9 8.8 %copy-start.1 = (bf16[256,1024]{1,0:T(8,128)(2,1)S(1)}, bf16[256,1024]{1,0:T(8,128)(2,1)}, u32[]{:S(2)}) copy-start(bf16[256,1024]{1,0:T(8,128)(2,1)} %get-tuple-element.264) | copy-start | bytes 1572868
Sparse Core Ops, SparseCore 0:
  12.1 56.3 all-gather.8
  70.7 45.9 all-gather.10
  118.9 48.2 all-gather.12
  168.6 45.9 all-gather.14
  324.8 53.1 reduce-scatter.4
  379.7 43.5 all-gather.16
  425.6 53.3 reduce-scatter.8
  485.8 54.9 reduce-scatter.6
  543.1 53.1 reduce-scatter.10

commit v3 on v2

v3 whole, which is shorter than its diff:
```python
import functools
import types

import jax
import jax.numpy as jnp
from jax import lax
from jax.experimental import pallas as pl
from jax.experimental.pallas import tpu as pltpu
from jax.sharding import PartitionSpec as P

F32 = jnp.float32
BF16 = jnp.bfloat16
MESH = pl.DeviceIdType.MESH
ATT = 128
LANES = 128
CHUNKS = 8
ROWS = 256
STRIP = 64
TILE = 128
LOCAL = "local"
UNROLL = 16
SMALL = 16
SMEM, VMEM, RAW, FETCH, BLOCKS, LATE, OWN_PART, STORE = range(8)
EPS = 1e-05
NEGATIVE = -1000000000.0
VMEM_BYTES = 56 * 1024 * 1024


def vmem():
    return pl.BlockSpec(memory_space=pltpu.VMEM)


def smem():
    return pl.BlockSpec(memory_space=pltpu.SMEM)


def hbm():
    return pl.BlockSpec(memory_space=pl.ANY)


def shape(dims, kind):
    return jax.ShapeDtypeStruct(dims, kind)


def sigmoid(v):
    return 0.5 * jnp.tanh(0.5 * v) + 0.5


def silu(v):
    return v * sigmoid(v)


def silu_slope(v):
    s = sigmoid(v)
    return s * (1.0 + v * (1.0 - s))


def dot(left, right, left_dim=1, right_dim=0):
    return lax.dot_general(
        left, right, (((left_dim,), (right_dim,)), ((), ())), preferred_element_type=F32
    )


def normalise(x):
    centred = x - jnp.mean(x, axis=-1, keepdims=True)
    spread = jnp.mean(centred * centred, axis=-1, keepdims=True)
    scale = lax.rsqrt(spread + EPS)
    return centred * scale, scale


def row_valid(start, rows, length):
    place = start + lax.broadcasted_iota(jnp.int32, (rows, 1), 0)
    return (place < length).astype(F32)


def lasting(microseconds):
    return pl.CostEstimate(
        flops=int(microseconds * 1.0e9),
        bytes_accessed=int(microseconds * 3.0e6),
        transcendentals=0,
    )


def params(**more):
    return pltpu.CompilerParams(vmem_limit_bytes=VMEM_BYTES, **more)


def power(base, exponent):
    result = None
    square = base
    while exponent:
        if exponent % 2:
            result = square if result is None else result * square
        exponent //= 2
        if exponent:
            square = square * square
    return result


def shifted(array, span, reverse=False):
    row = lax.broadcasted_iota(jnp.int32, array.shape, 1)
    if reverse:
        return jnp.where(row < CHUNKS - span, pltpu.roll(array, CHUNKS - span, 1), 0.0)
    return jnp.where(row >= span, pltpu.roll(array, span, 1), 0.0)


def entering(last, rate, steps, reverse=False):
    weight = power(rate, steps)
    span = 1
    while span < CHUNKS:
        last = last + weight * shifted(last, span, reverse)
        weight = weight * weight
        span *= 2
    return shifted(last, 1, reverse)


def entering_pair(last, slope, rate, steps):
    weight = power(rate, steps)
    tilt = float(steps) * power(rate, steps - 1)
    span = 1
    while span < CHUNKS:
        moved = shifted(last, span)
        slope = slope + weight * shifted(slope, span) + tilt * moved
        last = last + weight * moved
        tilt = 2.0 * weight * tilt
        weight = weight * weight
        span *= 2
    return shifted(last, 1), shifted(slope, 1)


def average_forward_kernel(
    length_ref,
    x_ref,
    gain_ref,
    shift_ref,
    rate_ref,
    coef_ref,
    skip_ref,
    normed_ref,
    mixed_ref,
    pre_ref,
    own_ref,
    scale_ref,
    rows_buf,
    m_buf,
    y_buf,
):
    length = length_ref[0]
    count, width = x_ref.shape
    own = mixed_ref.shape[1]
    dims = rate_ref.shape[0]
    steps = count // CHUNKS
    pitch = steps + 1
    mine = pl.ds(pl.multiple_of(lax.axis_index("section") * own, LANES), own)

    def norm_strip(i, carry):
        start = pl.multiple_of(i * STRIP, STRIP)
        here = pl.ds(start, STRIP)
        n, scale = normalise(x_ref[here, :].astype(F32))
        rows_buf[...] = n
        normed_ref[here, :] = (n * gain_ref[...] + shift_ref[...]).astype(BF16)
        part = rows_buf[:, mine]
        own_ref[here, :] = part
        scale_ref[here, :] = jnp.broadcast_to(scale, (STRIP, LANES))
        masked = (part * gain_ref[:, mine] + shift_ref[:, mine]) * row_valid(start, STRIP, length)
        for group in range(own // LANES):
            m_buf[group, pl.ds(start + start // steps, STRIP), :] = masked[:, group * LANES : (group + 1) * LANES]
        return carry

    lax.fori_loop(0, count // STRIP, norm_strip, 0)

    for group in range(own // LANES):
        lanes = slice(group * LANES, (group + 1) * LANES)
        rates = rate_ref[:, :, lanes]
        coefs = coef_ref[:, :, lanes]
        m_part, y_part = m_buf.at[group], y_buf.at[group]

        def finals(t, states):
            return rates * states + m_part[pl.ds(t, CHUNKS, stride=pitch), :]

        ends = lax.fori_loop(0, steps, finals, jnp.zeros_like(rates), unroll=UNROLL)

        def outputs(t, states):
            states = rates * states + m_part[pl.ds(t, CHUNKS, stride=pitch), :]
            y_part[pl.ds(t, CHUNKS, stride=pitch), :] = jnp.sum(coefs * states, axis=0)
            return states

        lax.fori_loop(0, steps, outputs, entering(ends, rates, steps), unroll=UNROLL)

    def mix_strip(i, carry):
        start = pl.multiple_of(i * STRIP, STRIP)
        here = pl.ds(start, STRIP)
        there = pl.ds(start + start // steps, STRIP)
        for group in range(own // LANES):
            lanes = slice(group * LANES, (group + 1) * LANES)
            pre = y_buf[group, there, :] + skip_ref[:, lanes] * m_buf[group, there, :]
            pre_ref[here, lanes] = pre.astype(BF16)
            mixed_ref[here, lanes] = silu(pre).astype(BF16)
        return carry

    lax.fori_loop(0, count // STRIP, mix_strip, 0)


def average_forward(length, x, gain, shift, rate, coef, skip):
    count, width = x.shape
    own = skip.shape[1]
    groups = own // LANES
    return pl.pallas_call(
        average_forward_kernel,
        out_shape=(
            shape((count, width), BF16),
            shape((count, own), BF16),
            shape((count, own), BF16),
            shape((count, own), F32),
            shape((count, LANES), F32),
        ),
        in_specs=[smem()] + [vmem()] * 6,
        out_specs=(vmem(),) * 5,
        scratch_shapes=[
            pltpu.VMEM((STRIP, width), F32),
            pltpu.VMEM((groups, count + CHUNKS, LANES), F32),
            pltpu.VMEM((groups, count + CHUNKS, LANES), F32),
        ],
        cost_estimate=lasting(13),
        compiler_params=params(),
    )(length, x, gain, shift, rate, coef, skip)


def average_backward_work(r):
    length = r.length[0]
    count, own = r.z.shape
    dims = r.rate.shape[0]
    steps = count // CHUNKS
    pitch = steps + 1
    groups = own // LANES
    part_size = dims // 2
    gain_ref, shift_ref = r.norm.at[0:1, :], r.norm.at[1:2, :]
    peers = plane()
    sems, piece = (r.send, r.recv), block_piece(r.whole)
    r.whole[peers[0]] = r.block[...]
    greet(peers[1], peers[2])
    begun = [gather_begin(r.whole, piece, peers, sems, half) for half in range(2)]

    def load_strip(i, carry):
        start = pl.multiple_of(i * STRIP, STRIP)
        here = pl.ds(start, STRIP)
        valid = row_valid(start, STRIP, length)
        there = pl.ds(start + start // steps, STRIP)
        for group in range(groups):
            lanes = slice(group * LANES, (group + 1) * LANES)
            r.m_buf[group, there, :] = (
                r.own_n[here, lanes] * gain_ref[:, lanes] + shift_ref[:, lanes]
            ) * valid
            slope = silu_slope(r.pre[here, lanes].astype(F32))
            r.g_buf[group, there, :] = r.gmixed[here, lanes] * slope
        return carry

    lax.fori_loop(0, count // STRIP, load_strip, 0)

    passed = None
    for group in range(groups):
        lanes = slice(group * LANES, (group + 1) * LANES)
        rates = r.rate[:, :, lanes]
        coefs = r.coef[:, :, lanes]
        m_part, g_part, r_part = r.m_buf.at[group], r.g_buf.at[group], r.r_buf.at[group]
        blank = jnp.zeros_like(rates)

        def back_finals(t, carry):
            states, slopes = carry
            g = g_part[pl.ds(steps - 1 - t, CHUNKS, stride=pitch), :]
            return rates * states + g, rates * slopes + states

        ends, end_slopes = lax.fori_loop(0, steps, back_finals, (blank, blank), unroll=UNROLL)
        starts = entering(ends, rates, steps, reverse=True)

        for half in range(2):
            first = half * part_size
            some = r.rate[first : first + part_size, :, lanes]
            empty = jnp.zeros_like(some)

            def sweep(t, carry):
                states, slopes, of_states, of_slopes = carry
                x = m_part[pl.ds(t, CHUNKS, stride=pitch), :]
                g = g_part[pl.ds(t, CHUNKS, stride=pitch), :]
                slopes = some * slopes + states
                states = some * states + x
                return states, slopes, of_states + g * states, of_slopes + g * slopes

            states, slopes, of_states, of_slopes = lax.fori_loop(
                0, steps, sweep, (empty,) * 4, unroll=UNROLL
            )
            back, back_slope = ends[first : first + part_size], end_slopes[first : first + part_size]
            state, slope = entering_pair(states, slopes, some, steps)
            of_states = of_states + state * (some * back)
            of_slopes = of_slopes + slope * (some * back) + state * (back + some * back_slope)
            r.sums[first : first + part_size, lanes] = jnp.sum(of_states, axis=1)
            r.sums[dims + first : dims + first + part_size, lanes] = jnp.sum(of_slopes, axis=1)

        def back_outputs(t, states):
            here = pl.ds(steps - 1 - t, CHUNKS, stride=pitch)
            states = rates * states + g_part[here, :]
            r_part[here, :] = jnp.sum(coefs * states, axis=0)
            return states

        lax.fori_loop(0, steps, back_outputs, starts, unroll=UNROLL)
        if passed is None:
            passed = gather_forward(r.whole, piece, peers, sems, *begun)

    ones = jnp.ones((CHUNKS, own), BF16)
    first = lax.broadcasted_iota(jnp.int32, (CHUNKS, LANES), 0) == 0

    def finish(i, carry):
        start = pl.multiple_of(i * LANES, LANES)
        here = pl.ds(start, LANES)
        valid = row_valid(start, LANES, length)
        there = pl.ds(start + start // steps, LANES)
        of_gain, of_shift, of_skip = carry
        smoothed = jnp.concatenate([r.r_buf[k, there, :] for k in range(groups)], axis=1)
        gpre = jnp.concatenate([r.g_buf[k, there, :] for k in range(groups)], axis=1)
        masked = jnp.concatenate([r.m_buf[k, there, :] for k in range(groups)], axis=1)
        n = r.own_n[here, :]
        gmasked = r.skip[...] * gpre + smoothed
        gnormed = gmasked * valid + r.gvalue[here, :]
        e = gnormed * gain_ref[...]
        z = r.scale[here, 0:1] * e + r.resid[here, :]
        r.z[here, :] = z.astype(BF16)
        mean_row = dot(ones, e.astype(BF16), 1, 1)
        slope_row = dot(ones, (e * n).astype(BF16), 1, 1)
        r.stats[:, here] = jnp.where(first, mean_row, slope_row)
        return (
            of_gain + jnp.sum(gnormed * n, axis=0, keepdims=True),
            of_shift + jnp.sum(gnormed, axis=0, keepdims=True),
            of_skip + jnp.sum(gpre * masked, axis=0, keepdims=True),
        )

    blank_row = jnp.zeros((1, own), F32)
    of_gain, of_shift, of_skip = lax.fori_loop(
        0, count // LANES, finish, (blank_row, blank_row, blank_row)
    )
    last = 2 * dims
    r.sums[last : last + 1, :] = of_gain
    r.sums[last + 1 : last + 2, :] = of_shift
    r.sums[last + 2 : last + 3, :] = of_skip
    r.sums[last + 3 : last + 8, :] = jnp.zeros((5, own), F32)
    gather_finish(r.whole, piece, peers, sems, *begun, passed)


def average_backward(
    length, gmixed, gvalue, k, resid, norm, rate, coef, skip, block, ident, after=()
):
    count, own = gmixed.shape
    dims = rate.shape[0]
    buffer = pltpu.VMEM((own // LANES, count + CHUNKS, LANES), F32)
    sems = pltpu.SemaphoreType.DMA((6,))
    given = dict(
        gmixed=gmixed,
        gvalue=gvalue,
        pre=k.pre,
        own_n=k.own_n,
        scale=k.scale,
        resid=resid,
        norm=norm,
        rate=rate,
        coef=coef,
        skip=skip,
        block=block,
    )
    return transfer(
        average_backward_work,
        dict(length=(length, SMEM), **{name: (a, VMEM) for name, a in given.items()}),
        dict(
            z=(shape((count, own), BF16), VMEM),
            stats=(shape((CHUNKS, count), F32), VMEM),
            sums=(shape((2 * dims + 8, own), F32), VMEM),
            whole=(shape((4,) + block.shape, BF16), VMEM),
        ),
        dict(m_buf=buffer, g_buf=buffer, r_buf=buffer, send=sems, recv=sems),
        ident,
        17,
        after,
    )


def unfold(packed, in_w, out_w, shards, sems):
    wide, width = out_w.shape
    few = wide // shards
    low = in_w.shape[1]
    copies = [pltpu.make_async_copy(packed.at[:, pl.ds(0, low)], in_w, sems.at[0])]
    for shard in range(shards):
        for half in range(2):
            start = shard * (width // shards) + half * few
            columns = pl.ds(half * (width // 2), width // 2)
            copies.append(
                pltpu.make_async_copy(
                    packed.at[pl.ds(start, few), pl.ds(low, width // 2)],
                    out_w.at[pl.ds(shard * few, few), columns],
                    sems.at[len(copies)],
                )
            )
    return copies


def attention_forward_block(
    length,
    start,
    normed_ref,
    mixed_ref,
    in_ref,
    bias_ref,
    pair_ref,
    offset_ref,
    part_ref,
    update_ref,
    shared_ref,
    reset_ref,
    cand_ref,
    value_ref,
    att_ref,
    gated_ref,
    probs_ref,
    out_w_ref,
):
    rows = normed_ref.shape[0]
    wide = value_ref.shape[1]
    own = update_ref.shape[1]
    keyed = shared_ref.shape[1]
    value = dot(normed_ref[...], in_ref[:, :wide]) + bias_ref[:, :wide]
    value_ref[...] = value.astype(BF16)
    values = silu(value).astype(BF16)
    low = wide
    update = dot(mixed_ref[...], in_ref[:, low : low + own]) + bias_ref[:, low : low + own]
    update_ref[...] = update.astype(BF16)
    low += own
    shared = dot(mixed_ref[...], in_ref[:, low : low + keyed]) + bias_ref[:, low : low + keyed]
    shared_ref[...] = shared.astype(BF16)
    low += keyed
    reset = dot(mixed_ref[...], in_ref[:, low : low + wide]) + bias_ref[:, low : low + wide]
    reset_ref[...] = reset.astype(BF16)
    low += wide
    cand_ref[...] = (
        dot(mixed_ref[...], in_ref[:, low : low + own]) + bias_ref[:, low : low + own]
    ).astype(BF16)
    shared = silu(shared)
    reset = silu(reset)
    queries = (shared * pair_ref[0:1, :] + offset_ref[...]).astype(BF16)
    keys = (shared * pair_ref[1:2, :]).astype(BF16)
    for block in range(rows // ATT):
        here = slice(block * ATT, (block + 1) * ATT)
        begin = start + block * ATT
        scores = dot(queries[here], keys[here], 1, 1) * keyed**-0.5
        key_place = begin + lax.broadcasted_iota(jnp.int32, (ATT, ATT), 1)
        scores = jnp.where(key_place < length, scores, NEGATIVE)
        raised = jnp.exp(scores - jnp.max(scores, axis=-1, keepdims=True))
        probs = (raised / jnp.sum(raised, axis=-1, keepdims=True)).astype(BF16)
        probs_ref[here, :] = probs
        attended = dot(probs, values[here]) * row_valid(begin, ATT, length)
        att_ref[here, :] = attended.astype(BF16)
        gated_ref[here, :] = (attended * reset[here]).astype(BF16)
    part_ref[...] = dot(gated_ref[...], out_w_ref[...]).astype(BF16)


def attention_backward_block(
    length,
    start,
    mine,
    gout_ref,
    gupdate_ref,
    shared_ref,
    reset_ref,
    value_ref,
    att_ref,
    probs_ref,
    in_ref,
    pair_ref,
    offset_ref,
    gmixed_ref,
    gnormed_ref,
    gbase_ref,
    gvalue_ref,
    bias_ref,
    pair_sum_ref,
    out_w_ref,
):
    rows = gout_ref.shape[0]
    total = bias_ref.shape[1]
    wide = value_ref.shape[1]
    own = gupdate_ref.shape[1]
    keyed = shared_ref.shape[1]
    valid = row_valid(start, rows, length)
    ggated = dot(gout_ref[...], out_w_ref[...], 1, 1)
    reset = reset_ref[...].astype(F32)
    gattended = (ggated * silu(reset) * valid).astype(BF16)
    greset = ggated * att_ref[...].astype(F32) * silu_slope(reset)
    value = value_ref[...].astype(F32)
    values = silu(value).astype(BF16)
    shared_pre = shared_ref[...].astype(F32)
    shared = silu(shared_pre)
    scale_q, scale_k = pair_ref[0:1, :], pair_ref[1:2, :]
    queries = (shared * scale_q + offset_ref[...]).astype(BF16)
    keys = (shared * scale_k).astype(BF16)
    gq_parts, gk_parts, gv_parts = [], [], []
    for block in range(rows // ATT):
        here = slice(block * ATT, (block + 1) * ATT)
        probs = probs_ref[here, :]
        gprobs = dot(gattended[here], values[here], 1, 1)
        gv_parts.append(dot(probs, gattended[here], 0, 0))
        probs = probs.astype(F32)
        gscores = probs * (gprobs - jnp.sum(probs * gprobs, axis=-1, keepdims=True))
        key_place = start + block * ATT + lax.broadcasted_iota(jnp.int32, (ATT, ATT), 1)
        gscores = jnp.where(key_place < length, gscores, 0.0)
        gscores = (gscores * keyed**-0.5).astype(BF16)
        gq_parts.append(dot(gscores, keys[here]))
        gk_parts.append(dot(gscores, queries[here], 0, 0))
    gqueries = jnp.concatenate(gq_parts, axis=0)
    gkeys = jnp.concatenate(gk_parts, axis=0)
    gvalue = jnp.concatenate(gv_parts, axis=0) * silu_slope(value)
    gshared = (gqueries * scale_q + gkeys * scale_k) * silu_slope(shared_pre)
    pair_sum_ref[0:1, :] += jnp.sum(gqueries * shared, axis=0, keepdims=True)
    pair_sum_ref[1:2, :] += jnp.sum(gkeys * shared, axis=0, keepdims=True)
    pair_sum_ref[2:3, :] += jnp.sum(gqueries, axis=0, keepdims=True)
    gupdate = gupdate_ref[...]
    gcand = gout_ref[:, mine]
    low = 0
    for piece in (gvalue, gupdate, gshared, greset, gcand):
        size = piece.shape[1]
        bias_ref[0:1, low : low + size] += jnp.sum(piece.astype(F32), axis=0, keepdims=True)
        if low:
            gbase_ref[:, low - wide : low - wide + size] = piece.astype(BF16)
        else:
            gvalue_ref[...] = piece.astype(BF16)
        low += size
    gmixed_ref[...] = dot(gbase_ref[...], in_ref[:, wide:total], 1, 1).astype(BF16)
    gnormed_ref[...] = dot(gvalue_ref[...], in_ref[:, :wide], 1, 1).astype(BF16)


def feed_forward_kernel(
    x_ref, gain_ref, shift_ref, w_ref, bias_ref, part_ref, pre_ref, n_ref, normed_ref, scale_ref
):
    hidden = pre_ref.shape[1]
    n, scale = normalise(x_ref[...].astype(F32))
    n_ref[...] = n.astype(BF16)
    scale_ref[...] = jnp.broadcast_to(scale, scale_ref.shape)
    normed_ref[...] = (n * gain_ref[...] + shift_ref[...]).astype(BF16)
    pre = dot(normed_ref[...], w_ref[:, :hidden]) + bias_ref[...]
    pre_ref[...] = pre.astype(BF16)
    part_ref[...] = dot(silu(pre).astype(BF16), w_ref[:, hidden:]).astype(BF16)


def feed_backward_block(
    g_ref, pre_ref, n_ref, gain_ref, w_ref, part_ref, stats_ref, gpre_ref, act_ref, sums_ref, bias_ref, lanes
):
    hidden = pre_ref.shape[1]
    width = n_ref.shape[1]
    g = g_ref[...]
    pre = pre_ref[...].astype(F32)
    s = sigmoid(pre)
    act_ref[...] = (pre * s).astype(BF16)
    gpre = dot(g, w_ref[:, hidden:], 1, 1) * (s * (1.0 + pre * (1.0 - s)))
    bias_ref[0:1, :] += jnp.sum(gpre, axis=0, keepdims=True)
    gpre_ref[...] = gpre.astype(BF16)
    part = dot(gpre_ref[...], w_ref[:, :hidden], 1, 1)
    part_ref[...] = part.astype(BF16)
    n = n_ref[...].astype(F32)
    sums_ref[0:1, :] += jnp.sum(part * n, axis=0, keepdims=True)
    sums_ref[1:2, :] += jnp.sum(part, axis=0, keepdims=True)
    sums_ref[2:3, :] += jnp.sum(g.astype(F32), axis=0, keepdims=True)
    e = part * gain_ref[...]
    ones = jnp.ones((CHUNKS, width), BF16)
    mean_row = dot(ones, e.astype(BF16), 1, 1)
    slope_row = dot(ones, (e * n).astype(BF16), 1, 1)
    first = lax.broadcasted_iota(jnp.int32, mean_row.shape, 0) == 0
    stats_ref[:, lanes] = jnp.where(first, mean_row, slope_row)


def plane():
    me = lax.axis_index("section")
    across = me + 1 - 2 * (me % 2)
    along = me + 2 - 4 * (me // 2)
    return me, across, along, across + along - me


def greet(*others):
    barrier = pltpu.get_barrier_semaphore()
    for other in others:
        pl.semaphore_signal(barrier, inc=1, device_id={"section": other}, device_id_type=MESH)
    pl.semaphore_wait(barrier, len(others))


def link(source, target, sems, index, other):
    send, recv = sems
    return pltpu.make_async_remote_copy(
        src_ref=source,
        dst_ref=target,
        send_sem=send.at[index],
        recv_sem=recv.at[index],
        device_id={"section": other},
        device_id_type=MESH,
    )


def strips(count, work):
    def one(i, carry):
        work(pl.multiple_of(i * STRIP, STRIP))
        return carry

    lax.fori_loop(0, count // STRIP, one, 0)


def widen(block):
    rows, columns = block.shape
    if columns < LANES:
        block = jnp.concatenate((block, jnp.zeros((rows, LANES - columns), F32)), axis=1)
    return block.astype(BF16)


def grad_tiles(left, right, store, begin, end):
    def one(i, carry):
        rows = pl.ds(pl.multiple_of(i * TILE, TILE), TILE)
        store(rows, dot(left[:, rows], right[...], 0, 0).astype(BF16))
        return carry

    lax.fori_loop(begin, end, one, 0)


def gather_begin(out, piece, peers, sems, half):
    me, across, along, far = peers
    here = out.at[piece(me, half)]
    order = ((along, 0), (across, 1)) if half == 0 else ((across, 1), (along, 0))
    started = {}
    for other, way in order:
        copy = link(here, here, sems, 2 * half + way, other)
        copy.start()
        started[way] = copy
    return started


def gather_forward(out, piece, peers, sems, zero, one):
    me, across, along, far = peers
    zero[0].wait_recv()
    passing = out.at[piece(along, 0)]
    first = link(passing, passing, sems, 4, across)
    first.start()
    one[1].wait_recv()
    passing = out.at[piece(across, 1)]
    second = link(passing, passing, sems, 5, along)
    second.start()
    return first, second


def gather_finish(out, piece, peers, sems, zero, one, passed=None):
    first, second = passed or gather_forward(out, piece, peers, sems, zero, one)
    zero[1].wait_recv()
    one[0].wait_recv()
    first.wait_recv()
    second.wait_recv()
    for copy in (zero[0], zero[1], one[0], one[1], first, second):
        copy.wait_send()


def copy_sems(count):
    return [pltpu.SemaphoreType.DMA((count,)), pltpu.SemaphoreType.DMA((count,))]


def comm_params(ident):
    return params(collective_id=ident, has_side_effects=True)


def own_slice(source, target, sem, own):
    start = pl.multiple_of(lax.axis_index("section") * own, LANES)
    return pltpu.make_async_copy(source.at[:, pl.ds(start, own)], target, sem)


def stats_total(stats, got, stage, peers, sems, index):
    me, across, along, far = peers
    first = link(stats, got.at[0], sems, index, across)
    first.start()
    first.wait_recv()
    stage[...] = stats[...] + got[0]
    second = link(stage, got.at[1], sems, index + 1, along)
    second.start()
    second.wait_recv()
    first.wait_send()
    second.wait_send()
    return stage[...] + got[1]


def transfer(work, ins, outs, scratch, ident, microseconds, after=(), first=None):
    order = [n for kind in (FETCH, BLOCKS, LATE, OWN_PART) for n in ins if ins[n][1] == kind]
    stored = [n for n, (_, how) in outs.items() if how == STORE]
    buffers, places, low = {}, {}, 0
    for name in order + stored:
        if name in stored:
            buffers[name] = pltpu.VMEM(outs[name][0].shape, outs[name][0].dtype)
        else:
            array, how = ins[name]
            columns = array.shape[1] // (4 if how == OWN_PART else 1)
            buffers[name] = pltpu.VMEM((array.shape[0], columns), array.dtype)
        places[name] = low
        low += ins[name][0].shape[0] // ROWS if name in ins and ins[name][1] == BLOCKS else 1
    by_blocks = [n for n in order if ins[n][1] == BLOCKS]

    def kernel(*refs):
        refs = refs[len(after) :]
        names = list(ins) + list(outs)
        given = dict(zip(names, refs))
        refs = refs[len(names) :]
        own_names = list(buffers) + [LOCAL] + list(scratch)
        held = dict(zip(own_names, refs))
        r = types.SimpleNamespace(**{**given, **held})
        local = held[LOCAL]

        def copy(name):
            sem = local.at[places[name]]
            if name in stored:
                return pltpu.make_async_copy(held[name], given[name], sem)
            if ins[name][1] == OWN_PART:
                return own_slice(given[name], held[name], sem, held[name].shape[1])
            return pltpu.make_async_copy(given[name], held[name], sem)

        def block_copy(name, block):
            here = rows_of(block)
            source, target = given[name].at[here, :], held[name].at[here, :]
            return pltpu.make_async_copy(source, target, local.at[places[name] + block])

        def start(*kinds):
            for name in order:
                if ins[name][1] in kinds:
                    copy(name).start()

        def wait_block(block):
            for name in by_blocks:
                block_copy(name, block).wait()

        start(FETCH)
        if first:
            first(r)
        if by_blocks:
            for block in range(ins[by_blocks[0]][0].shape[0] // ROWS):
                for name in by_blocks:
                    block_copy(name, block).start()
        start(LATE, OWN_PART)
        r.wait = lambda *which: [copy(n).wait() for n in which]
        r.store = lambda *which: [copy(n).start() for n in which]
        r.wait_block = wait_block
        work(r)
        for name in stored:
            copy(name).wait()

    spec = {SMEM: smem, VMEM: vmem}
    return pl.pallas_call(
        kernel,
        out_shape=tuple(o for o, _ in outs.values()),
        in_specs=[hbm()] * len(after) + [spec.get(how, hbm)() for _, how in ins.values()],
        out_specs=tuple(spec.get(how, hbm)() for _, how in outs.values()),
        scratch_shapes=list(buffers.values())
        + [pltpu.SemaphoreType.DMA((max(low, 1),))]
        + list(scratch.values()),
        cost_estimate=lasting(microseconds),
        compiler_params=comm_params(ident),
    )(*after, *[a for a, _ in ins.values()])


def rows_of(block):
    return pl.ds(pl.multiple_of(block * ROWS, ROWS), ROWS)


def half_rows(block):
    return pl.ds(pl.multiple_of(block * (ROWS // 2), ROWS // 2), ROWS // 2)


def owned(block, owner, half, own):
    start = pl.multiple_of(block * ROWS + half * (ROWS // 2), ROWS // 2)
    return pl.ds(start, ROWS // 2), pl.ds(pl.multiple_of(owner * own, LANES), own)


def sum_scratch(name, count, own):
    buffer = pltpu.VMEM((2, count // 2, own), BF16)
    sems = pltpu.SemaphoreType.DMA((6 * (count // ROWS),))
    return {
        name + "_early": buffer,
        name + "_direct": buffer,
        name + "_late": buffer,
        name + "_stage": buffer,
        name + "_send": sems,
        name + "_recv": sems,
    }


def block_sum(r, name, part, peers, own, piece=None, place=half_rows):
    if piece is None:
        piece = functools.partial(owned, own=own)
    me, across, along, far = peers
    early, direct, late, stage, send, recv = (
        getattr(r, name + end) for end in ("_early", "_direct", "_late", "_stage", "_send", "_recv")
    )
    sems = (send, recv)
    ways = ((across, along), (along, across))

    def early_copy(block, half):
        source = part.at[piece(block, far, half)]
        target = early.at[half, place(block)]
        return link(source, target, sems, block * 6 + half, ways[half][0])

    def direct_copy(block, half):
        first = ways[half][0]
        source = part.at[piece(block, first, half)]
        target = direct.at[half, place(block)]
        return link(source, target, sems, block * 6 + 2 + half, first)

    def late_copy(block, half):
        source = stage.at[half, place(block)]
        target = late.at[half, place(block)]
        return link(source, target, sems, block * 6 + 4 + half, ways[half][1])

    def begin(block):
        for half in range(2):
            early_copy(block, half).start()
        for half in range(2):
            direct_copy(block, half).start()

    def forward(block):
        for half in range(2):
            early_copy(block, half).wait_recv()
            here = place(block)
            passed = part[piece(block, ways[half][1], half)].astype(F32)
            stage[half, here, :] = (passed + early[half, here, :].astype(F32)).astype(BF16)
            late_copy(block, half).start()

    def arrived(block, half):
        direct_copy(block, half).wait_recv()
        late_copy(block, half).wait_recv()

    def total(block, half, start):
        row, column = piece(block, me, half)
        here = pl.ds(place(block).start + start, STRIP)
        mine = part[pl.ds(row.start + start, STRIP), column].astype(F32)
        return mine + direct[half, here, :].astype(F32) + late[half, here, :].astype(F32)

    def end(block):
        for half in range(2):
            early_copy(block, half).wait_send()
            direct_copy(block, half).wait_send()
            late_copy(block, half).wait_send()

    return types.SimpleNamespace(begin=begin, forward=forward, arrived=arrived, total=total, end=end)


def gather_sems(count):
    return pltpu.SemaphoreType.DMA((6 * (count // ROWS),))


def block_gather(out, peers, own, sems):
    me, across, along, far = peers

    def copy(block, owner, half, index, other):
        place = out.at[owned(block, owner, half, own)]
        return link(place, place, sems, block * 6 + index, other)

    def own_copy(block, half, way):
        return copy(block, me, half, 2 * half + way, (along, across)[way])

    def pass_copy(block, half):
        return copy(block, (along, across)[half], half, 4 + half, (across, along)[half])

    def begin(block):
        for half, way in ((0, 0), (1, 1), (1, 0), (0, 1)):
            own_copy(block, half, way).start()

    def forward(block):
        for half in range(2):
            own_copy(block, half, half).wait_recv()
            pass_copy(block, half).start()

    def arrive(block):
        own_copy(block, 0, 1).wait_recv()
        own_copy(block, 1, 0).wait_recv()
        for half in range(2):
            pass_copy(block, half).wait_recv()

    def sent(block):
        for half in range(2):
            pass_copy(block, half).wait_send()
            for way in range(2):
                own_copy(block, half, way).wait_send()

    return types.SimpleNamespace(begin=begin, forward=forward, arrive=arrive, sent=sent)


def pipeline(count, compute, sums, finish, gather, extra=None, between=None, before=None):
    blocks = count // ROWS
    if before:
        before.begin(0)
        before.begin(1)
        before.forward(0)

    def tick(i, carry):
        if before:

            @pl.when(i < blocks - 2)
            def _():
                before.begin(i + 2)

            @pl.when(i < blocks - 1)
            def _():
                before.forward(i + 1)

            @pl.when(i < blocks)
            def _():
                before.arrive(i)

        @pl.when(i < blocks)
        def _():
            compute(i)
            for one in sums:
                one.begin(i)

        if between:
            between(i)

        @pl.when((i >= 1) & (i <= blocks))
        def _():
            for one in sums:
                one.forward(i - 1)

        @pl.when((i >= 2) & (i <= blocks + 1))
        def _():
            finish(i - 2)
            if gather:
                gather.begin(i - 2)

        if gather:

            @pl.when(i >= 3)
            def _():
                gather.forward(i - 3)

        if extra:
            extra(i)
        return carry

    lax.fori_loop(0, blocks + (3 if gather else 2), tick, 0)

    def close(i, carry):
        for one in sums:
            one.end(i)
        if gather:
            gather.arrive(i)
            gather.sent(i)
        if before:
            before.sent(i)
        return carry

    lax.fori_loop(0, blocks, close, 0)


def finish_strips(one, block, work):
    for half in range(2):
        one.arrived(block, half)

        def strip(start):
            row = pl.multiple_of(block * ROWS + half * (ROWS // 2), ROWS // 2) + start
            work(pl.ds(row, STRIP), one.total(block, half, start))

        strips(ROWS // 2, strip)


def views(refs, block):
    return [ref.at[rows_of(block), :] for ref in refs]


def attention_forward(length, normed, mixed_own, packed, bias, pair, offset, x, shards, ident):
    count, width = normed.shape
    own = width // 4
    wide = width // 2
    keyed = pair.shape[1]
    low = packed.shape[1] - width // 2

    def weights(r):
        return unfold(r.packed, r.in_w, r.out_w, shards, r.fold)

    def first(r):
        for copy in weights(r):
            copy.start()

    def work(r):
        peers = plane()
        mine = pl.ds(pl.multiple_of(peers[0] * own, LANES), own)
        real = r.length[0]
        r.mixed[:, mine] = r.mixed_own[...]
        greet(peers[1], peers[2])
        mixing = block_gather(r.mixed, peers, own, (r.mixed_send, r.mixed_recv))
        total = block_sum(r, "sum", r.part, peers, own)
        gather = block_gather(r.out, peers, own, (r.gather_send, r.gather_recv))
        saved = (r.update, r.shared, r.reset, r.cand, r.value, r.att, r.gated, r.probs)

        def compute(block):
            @pl.when(block == 0)
            def _():
                for copy in weights(r):
                    copy.wait()

            r.wait_block(block)
            attention_forward_block(
                real,
                block * ROWS,
                *views((r.normed, r.mixed), block),
                r.in_w,
                r.bias,
                r.pair,
                r.offset,
                *views((r.part,) + saved, block),
                r.out_w,
            )

        def finish(block):
            def strip(here, summed):
                pre = r.cand[here, :].astype(F32) + summed
                r.hidden[here, :] = pre.astype(BF16)
                old = r.x[here, :].astype(F32)
                made = old + sigmoid(r.update[here, :].astype(F32)) * (silu(pre) - old)
                r.out[here, mine] = made.astype(BF16)

            finish_strips(total, block, strip)

        def extra(i):
            @pl.when(i == 0)
            def _():
                r.wait("x")

            @pl.when(i == count // ROWS)
            def _():
                r.store("mixed", "update", "shared", "reset", "value", "att", "gated", "probs")

        pipeline(count, compute, (total,), finish, gather, extra, before=mixing)

    rows = lambda columns: (shape((count, columns), BF16), STORE)
    return transfer(
        work,
        dict(
            length=(length, SMEM),
            packed=(packed, RAW),
            normed=(normed, BLOCKS),
            mixed_own=(mixed_own, VMEM),
            x=(x, OWN_PART),
            bias=(bias, VMEM),
            pair=(pair, VMEM),
            offset=(offset, VMEM),
        ),
        dict(
            out=(shape((count, width), BF16), VMEM),
            hidden=(shape((count, own), BF16), VMEM),
            mixed=rows(width),
            update=rows(own),
            shared=rows(keyed),
            reset=rows(wide),
            value=rows(wide),
            att=rows(wide),
            gated=rows(wide),
            probs=rows(ATT),
        ),
        dict(
            part=pltpu.VMEM((count, width), BF16),
            cand=pltpu.VMEM((count, own), BF16),
            in_w=pltpu.VMEM((width, low), BF16),
            out_w=pltpu.VMEM((wide, width), BF16),
            fold=pltpu.SemaphoreType.DMA((2 * shards + 1,)),
            mixed_send=gather_sems(count),
            mixed_recv=gather_sems(count),
            **sum_scratch("sum", count, own),
            gather_send=gather_sems(count),
            gather_recv=gather_sems(count),
        ),
        ident,
        54,
        first=first,
    )


def feed_forward_joined(x, gain, shift, weights, bias, own_out, ident):
    count, width = x.shape
    hidden = bias.shape[1]
    own = width // 4

    def work(r):
        peers = plane()
        mine = pl.ds(pl.multiple_of(peers[0] * own, LANES), own)
        greet(peers[1], peers[2])
        r.wait("weights")
        total = block_sum(r, "sum", r.part, peers, own)
        gather = block_gather(r.out, peers, own, (r.gather_send, r.gather_recv))

        def compute(block):
            r.wait_block(block)
            x_rows, *outs = views((r.x, r.part, r.pre, r.n, r.normed, r.scale), block)
            feed_forward_kernel(x_rows, r.gain, r.shift, r.weights, r.bias, *outs)

        def finish(block):
            def strip(here, summed):
                made = r.x[here, mine].astype(F32) + summed + r.own_out[...]
                r.out[here, mine] = made.astype(BF16)

            finish_strips(total, block, strip)

        def extra(i):
            @pl.when(i == count // ROWS)
            def _():
                r.store("pre", "n", "normed", "scale")

        pipeline(count, compute, (total,), finish, gather, extra)

    rows = lambda columns, kind=BF16: (shape((count, columns), kind), STORE)
    return transfer(
        work,
        dict(
            x=(x, BLOCKS),
            weights=(weights, FETCH),
            gain=(gain, VMEM),
            shift=(shift, VMEM),
            bias=(bias, VMEM),
            own_out=(own_out, VMEM),
        ),
        dict(
            out=(shape((count, width), BF16), VMEM),
            pre=rows(hidden),
            n=rows(width),
            normed=rows(width),
            scale=rows(LANES, F32),
        ),
        dict(
            part=pltpu.VMEM((count, width), BF16),
            **sum_scratch("sum", count, own),
            gather_send=gather_sems(count),
            gather_recv=gather_sems(count),
        ),
        ident,
        40,
    )


def feed_backward(given, k, p, weights, shards, ident, after=()):
    corrected = isinstance(given, tuple)
    both_ways = k.feed_pre is None
    count, width = k.middle.shape
    own = width // 4
    hidden = p.feed_in.shape[1]
    norms, gain = p.own, p.feed_gain
    blocks = count // ROWS

    def work(r):
        peers = plane()
        me, across, along, far = peers
        mine = pl.ds(pl.multiple_of(me * own, LANES), own)
        if corrected:
            r.z[:, mine] = r.z_own[...]
        greet(across, along)
        before = None
        if corrected:
            before = block_gather(r.z, peers, own, (r.z_send, r.z_recv))
        r.sums[...] = jnp.zeros_like(r.sums)
        r.bias[...] = jnp.zeros_like(r.bias)
        total = block_sum(r, "sum", r.part, peers, own)
        gather = block_gather(r.out, peers, own, (r.gather_send, r.gather_recv))

        def quarter(block, owner, half):
            size = count // 4
            return (
                pl.ds(pl.multiple_of(owner * size, size), size),
                pl.ds(half * (width // 2), width // 2),
            )

        if both_ways:
            last = block_sum(
                r, "last", r.made, peers, own, quarter, lambda block: pl.ds(0, count // 4)
            )

        def last_rows():
            for half in range(2):
                last.arrived(0, half)
                lanes = slice(half * (width // 2), (half + 1) * (width // 2))

                def strip(start):
                    here = pl.ds(start, STRIP)
                    row = pl.ds(pl.multiple_of(me * (count // 4), STRIP) + start, STRIP)
                    made = r.middle[row, lanes].astype(F32) + last.total(0, half, start)
                    r.block_out[here, lanes] = (made + r.out_bias[:, lanes]).astype(BF16)

                strips(count // 4, strip)

        def stats_copy(block, step):
            lanes = rows_of(block)
            source = (r.stats, r.stats_stage)[step].at[:, lanes]
            sems = (r.stats_send, r.stats_recv)
            other = (across, along)[step]
            return link(source, r.stats_got.at[step, :, lanes], sems, 2 * block + step, other)

        def compute(block):
            here = rows_of(block)

            @pl.when(block == 0)
            def _():
                r.wait("weights")
                if corrected:
                    sems = (r.means_send, r.means_recv)
                    r.means[...] = stats_total(
                        r.z_stats, r.means_got, r.means_stage, peers, sems, 0
                    )

            r.wait_block(block)
            if corrected:
                xn, xscale = normalise(r.x_full[here, :].astype(F32))
                means = r.means[:, here].T * (1.0 / width)
                z = r.z[here, :].astype(F32)
                g = z - xscale * (means[:, 0:1] + xn * means[:, 1:2])
                r.g[here, :] = g.astype(BF16)
            if both_ways:
                x_rows, *made = views((r.middle, r.made, r.pre, r.n, r.normed, r.scale), block)
                feed_forward_kernel(x_rows, r.gain, r.shift, r.weights, r.in_bias, *made)
            g_rows, pre_rows, n_rows = views((r.g, r.pre, r.n), block)
            part, gpre, act = views((r.part, r.gpre, r.act), block)
            feed_backward_block(
                g_rows,
                pre_rows,
                n_rows,
                r.gain,
                r.weights,
                part,
                r.stats,
                gpre,
                act,
                r.sums,
                r.bias,
                here,
            )
            stats_copy(block, 0).start()

        def finish(block):
            here = rows_of(block)
            stats_copy(block, 1).wait_recv()
            every = r.stats_stage[:, here] + r.stats_got[1, :, here]
            r.columns[here, :] = every.T * (1.0 / width)

            def strip(here, summed):
                e = summed * r.norms[2:3, :]
                n_own = r.n[here, mine].astype(F32)
                inner = e - r.columns[here, 0:1] - n_own * r.columns[here, 1:2]
                g = r.g[here, mine].astype(F32) + r.scale[here, 0:1] * inner
                g = g.astype(BF16).astype(F32)
                u = sigmoid(r.update[here, :].astype(F32))
                pre = r.hidden[here, :].astype(F32)
                s = sigmoid(pre)
                x = r.x[here, :].astype(F32)
                r.gupdate[here, :] = (g * (pre * s - x) * (u * (1.0 - u))).astype(BF16)
                r.resid[here, :] = g * (1.0 - u)
                r.out[here, mine] = (g * u * (s * (1.0 + pre * (1.0 - s)))).astype(BF16)

            finish_strips(total, block, strip)

        def small_grads():
            r.grad[:, hidden + width :] = jnp.zeros((width, LANES), BF16)
            size = width // shards
            for shard in range(shards):
                lanes = slice(shard * size, (shard + 1) * size)
                block = jnp.concatenate(
                    (r.sums[0:3, lanes], r.bias[0:1, lanes], jnp.zeros((SMALL - 4, size), F32)),
                    axis=0,
                )
                r.grad[shard * size : shard * size + SMALL, hidden + width :] = widen(block)

        def in_grad(rows, value):
            r.grad[rows, :hidden] = value

        def out_grad(rows, value):
            r.grad[rows, hidden : hidden + width] = value

        def extra(i):
            @pl.when((i >= 1) & (i <= blocks))
            def _():
                here = rows_of(i - 1)
                stats_copy(i - 1, 0).wait_recv()
                r.stats_stage[:, here] = r.stats[:, here] + r.stats_got[0, :, here]
                stats_copy(i - 1, 1).start()

            @pl.when(i == 0)
            def _():
                r.wait("update", "hidden", "x")
                if not both_ways:
                    r.wait("scale", "normed")

            if both_ways:

                @pl.when(i == blocks - 1)
                def _():
                    last.begin(0)

                @pl.when(i == blocks)
                def _():
                    last.forward(0)

                @pl.when(i == blocks + 2)
                def _():
                    last_rows()
                    last.end(0)

            @pl.when(i == blocks + 1)
            def _():
                r.store("gupdate", "resid")

        def between(i):
            @pl.when(i == blocks)
            def _():
                grad_tiles(r.normed, r.gpre, in_grad, 0, width // TILE)
                small_grads()
                grad_tiles(r.act, r.g, out_grad, 0, hidden // TILE)
                r.store("grad")

        pipeline(count, compute, (total,), finish, gather, extra, between, before)

        def close(i, carry):
            stats_copy(i, 0).wait_send()
            stats_copy(i, 1).wait_send()
            return carry

        lax.fori_loop(0, blocks, close, 0)

    if corrected:
        z_own, z_stats, x_full = given
        first = dict(z_own=(z_own, VMEM), x_full=(x_full, BLOCKS), z_stats=(z_stats, VMEM))
        both = pltpu.SemaphoreType.DMA((2,))
        extra_scratch = dict(
            g=pltpu.VMEM((count, width), BF16),
            z=pltpu.VMEM((count, width), BF16),
            z_send=gather_sems(count),
            z_recv=gather_sems(count),
            means=pltpu.VMEM((CHUNKS, count), F32),
            means_stage=pltpu.VMEM((CHUNKS, count), F32),
            means_got=pltpu.VMEM((2, CHUNKS, count), F32),
            means_send=both,
            means_recv=both,
        )
    else:
        first = dict(g=(given, BLOCKS))
        extra_scratch = {}
    extra_outs = {}
    if both_ways:
        saved = {}
        first.update(
            middle=(k.middle, BLOCKS),
            shift=(p.feed_shift, VMEM),
            in_bias=(p.feed_in, VMEM),
            out_bias=(p.feed_out, VMEM),
        )
        extra_outs.update(block_out=(shape((count // 4, width), BF16), VMEM))
        rows = pltpu.VMEM((count, width), BF16)
        slot = pltpu.VMEM((2, count // 4, width // 2), BF16)
        ends = pltpu.SemaphoreType.DMA((6,))
        extra_scratch.update(
            made=rows,
            pre=pltpu.VMEM((count, hidden), BF16),
            n=rows,
            normed=rows,
            scale=pltpu.VMEM((count, LANES), F32),
            last_early=slot,
            last_direct=slot,
            last_late=slot,
            last_stage=slot,
            last_send=ends,
            last_recv=ends,
        )
    else:
        saved = dict(
            pre=(k.feed_pre, BLOCKS),
            n=(k.feed_n, BLOCKS),
            scale=(k.feed_scale, LATE),
            normed=(k.feed_normed, LATE),
        )
    sems = pltpu.SemaphoreType.DMA((2 * blocks,))
    return transfer(
        work,
        dict(
            weights=(weights, FETCH),
            **first,
            **saved,
            update=(k.update, LATE),
            hidden=(k.hidden, LATE),
            x=(k.x, OWN_PART),
            gain=(gain, VMEM),
            norms=(norms, VMEM),
        ),
        dict(
            out=(shape((count, width), BF16), VMEM),
            gupdate=(shape((count, own), BF16), STORE),
            resid=(shape((count, own), F32), STORE),
            grad=(shape((width, hidden + width + LANES), BF16), STORE),
            **extra_outs,
        ),
        dict(
            part=pltpu.VMEM((count, width), BF16),
            gpre=pltpu.VMEM((count, hidden), BF16),
            act=pltpu.VMEM((count, hidden), BF16),
            sums=pltpu.VMEM((8, width), F32),
            bias=pltpu.VMEM((8, hidden), F32),
            stats=pltpu.VMEM((CHUNKS, count), F32),
            stats_stage=pltpu.VMEM((CHUNKS, count), F32),
            stats_got=pltpu.VMEM((2, CHUNKS, count), F32),
            columns=pltpu.VMEM((count, CHUNKS), F32),
            stats_send=sems,
            stats_recv=sems,
            **extra_scratch,
            **sum_scratch("sum", count, own),
            gather_send=gather_sems(count),
            gather_recv=gather_sems(count),
        ),
        ident,
        46,
        after,
    )


def attention_backward(length, gout, gupdate, k, packed, pair, offset, shards, ident, after=()):
    shared, reset, value, att, probs = k.saved
    count, width = gout.shape
    own = width // 4
    wide = width // 2
    keyed = pair.shape[1]
    total = packed.shape[1] - width // 2
    blocks = count // ROWS
    few = wide // shards
    block_rows = width // shards

    def weights(r):
        return unfold(r.packed, r.in_w, r.out_w, shards, r.fold)

    def first(r):
        for copy in weights(r):
            copy.start()

    def work(r):
        peers = plane()
        mine = pl.ds(pl.multiple_of(peers[0] * own, LANES), own)
        real = r.length[0]
        greet(peers[1], peers[2])
        r.bias[...] = jnp.zeros_like(r.bias)
        r.pairs[...] = jnp.zeros_like(r.pairs)
        one = block_sum(r, "one", r.gmixed_part, peers, own)
        two = block_sum(r, "two", r.gvalue_part, peers, own)

        def compute(block):
            @pl.when(block == 0)
            def _():
                for copy in weights(r):
                    copy.wait()

            r.wait_block(block)
            attention_backward_block(
                real,
                block * ROWS,
                mine,
                *views((r.gout, r.gupdate, r.shared, r.reset, r.value, r.att, r.probs), block),
                r.in_w,
                r.pair,
                r.offset,
                *views((r.gmixed_part, r.gvalue_part, r.gbase, r.gvalue), block),
                r.bias,
                r.pairs,
                r.out_w,
            )

        def finish(block):
            def keep(out):
                def strip(here, summed):
                    out[here, :] = summed

                return strip

            finish_strips(one, block, keep(r.gmixed))
            finish_strips(two, block, keep(r.gnormed))

        def value_grad(rows, value):
            r.grad[rows, :wide] = value

        def base_grad(rows, value):
            r.grad[rows, wide:total] = value

        def out_grad(rows, value):
            for i in range(TILE // few):
                start = (rows.start // few + i) * block_rows
                for half in range(2):
                    here = pl.ds(pl.multiple_of(start + half * few, few), few)
                    r.grad[here, total : total + width // 2] = value[
                        i * few : (i + 1) * few, half * (width // 2) : (half + 1) * (width // 2)
                    ]

        def small_grads():
            last = total + width // 2
            r.grad[:, last:] = jnp.zeros((width, LANES), BF16)
            rows = [r.bias[0:1, i * LANES : (i + 1) * LANES] for i in range(total // LANES)]
            block = jnp.concatenate(rows + [r.pairs[0:3, :]], axis=0).astype(BF16)
            for shard in range(shards):
                r.grad[shard * block_rows : shard * block_rows + SMALL, last:] = block

        def extra(i):
            @pl.when(i == 0)
            def _():
                r.wait("normed", "mixed", "gated")

        def between(i):
            @pl.when(i == blocks)
            def _():
                small_grads()
                grad_tiles(r.mixed, r.gbase, base_grad, 0, width // TILE)
                grad_tiles(r.normed, r.gvalue, value_grad, 0, width // TILE)
                grad_tiles(r.gated, r.gout, out_grad, 0, wide // TILE)
                r.store("grad")

        pipeline(count, compute, (one, two), finish, None, extra, between)

    return transfer(
        work,
        dict(
            length=(length, SMEM),
            packed=(packed, RAW),
            gout=(gout, BLOCKS),
            gupdate=(gupdate, BLOCKS),
            shared=(shared, BLOCKS),
            reset=(reset, BLOCKS),
            value=(value, BLOCKS),
            att=(att, BLOCKS),
            probs=(probs, BLOCKS),
            normed=(k.normed, LATE),
            mixed=(k.mixed, LATE),
            gated=(k.gated, LATE),
            pair=(pair, VMEM),
            offset=(offset, VMEM),
        ),
        dict(
            gmixed=(shape((count, own), F32), VMEM),
            gnormed=(shape((count, own), F32), VMEM),
            grad=(shape((width, total + width // 2 + LANES), BF16), STORE),
        ),
        dict(
            gmixed_part=pltpu.VMEM((count, width), BF16),
            gvalue_part=pltpu.VMEM((count, width), BF16),
            gbase=pltpu.VMEM((count, total - wide), BF16),
            gvalue=pltpu.VMEM((count, wide), BF16),
            bias=pltpu.VMEM((8, total), F32),
            pairs=pltpu.VMEM((8, keyed), F32),
            in_w=pltpu.VMEM((width, total), BF16),
            out_w=pltpu.VMEM((wide, width), BF16),
            fold=pltpu.SemaphoreType.DMA((2 * shards + 1,)),
            **sum_scratch("one", count, own),
            **sum_scratch("two", count, own),
        ),
        ident,
        40,
        after,
        first,
    )


def block_piece(whole):
    def piece(owner, half):
        size = whole.shape[1] // 2
        return owner, pl.ds(half * size, size), slice(None)

    return piece


def final_kernel(number, z_ref, stats_ref, x_ref, *refs):
    blocks, refs = refs[:number], refs[number:]
    out_ref, refs = refs[0], refs[1:]
    gathered, refs = refs[:number], refs[number:]
    land, x_own, got, stats_stage, total_buf, local_sem, send, recv = refs[:8]
    block_sems = [refs[8 + 2 * i : 10 + 2 * i] for i in range(number)]
    count, own = z_ref.shape
    quarter, width = out_ref.shape
    peers = plane()
    me = peers[0]

    def rows(owner):
        return pl.ds(pl.multiple_of(owner * quarter, quarter), quarter)

    mine = pl.ds(pl.multiple_of(me * own, LANES), own)
    fetch = pltpu.make_async_copy(x_ref.at[rows(me), :], x_own, local_sem)
    fetch.start()
    land[:, mine] = z_ref[rows(me), :]
    for block, whole in zip(blocks, gathered):
        whole[me] = block[...]
    greet(*peers[1:])
    sems = (send, recv)
    copies = []
    for index, other in enumerate(peers[1:]):
        copies.append(link(z_ref.at[rows(other), :], land.at[:, mine], sems, 2 + index, other))
        copies[-1].start()
    total_buf[...] = stats_total(stats_ref, got, stats_stage, peers, sems, 0)
    begun = [
        [gather_begin(whole, block_piece(whole), peers, k, half) for half in range(2)]
        for whole, k in zip(gathered, block_sems)
    ]
    part = total_buf[:, pl.ds(pl.multiple_of(me * quarter, LANES), quarter)]
    means = part.T * (1.0 / width)
    fetch.wait()
    for copy in copies:
        copy.wait_recv()
    n, scale = normalise(x_own[...].astype(F32))
    g = land[...].astype(F32) - scale * (means[:, 0:1] + n * means[:, 1:2])
    out_ref[...] = g.astype(BF16)
    passed = [
        gather_forward(whole, block_piece(whole), peers, k, zero, one)
        for whole, k, (zero, one) in zip(gathered, block_sems, begun)
    ]
    for whole, k, (zero, one), two in zip(gathered, block_sems, begun, passed):
        gather_finish(whole, block_piece(whole), peers, k, zero, one, two)
    for copy in copies:
        copy.wait_send()


def final_exchange(z, stats, x, blocks, sections, ident):
    count, own = z.shape
    width = x.shape[1]
    quarter = count // 4
    number = len(blocks)
    return pl.pallas_call(
        functools.partial(final_kernel, number),
        out_shape=(shape((quarter, width), BF16),)
        + tuple(shape((sections,) + a.shape, BF16) for a in blocks),
        in_specs=[vmem(), vmem(), hbm()] + [vmem()] * number,
        out_specs=(vmem(),) * (1 + number),
        scratch_shapes=[
            pltpu.VMEM((quarter, width), BF16),
            pltpu.VMEM((quarter, width), BF16),
            pltpu.VMEM((2,) + stats.shape, F32),
            pltpu.VMEM(stats.shape, F32),
            pltpu.VMEM(stats.shape, F32),
            pltpu.SemaphoreType.DMA,
        ]
        + copy_sems(5)
        + copy_sems(6) * number,
        cost_estimate=lasting(10 + 20 * number),
        compiler_params=comm_params(ident),
    )(z, stats, x, *blocks)


def sums_kernel(shards, holders, sums_ref, block_ref, channels_ref, whole_ref, *refs):
    sums_land, send_s, recv_s, send_c, recv_c, send, recv = refs
    peers = plane()
    me = peers[0]
    slot = lax.axis_index("dp")
    holding = slot // holders == me
    whole_ref[me] = block_ref[...]
    barrier = pltpu.get_barrier_semaphore()
    for other in peers[1:]:
        pl.semaphore_signal(barrier, inc=1, device_id={"section": other}, device_id_type=MESH)
    for step in range(1, shards):
        other = (slot + step) % shards
        pl.semaphore_signal(barrier, inc=1, device_id={"dp": other}, device_id_type=MESH)
    pl.semaphore_wait(barrier, shards + 2)

    def sums_copy(target, index, place):
        return pltpu.make_async_remote_copy(
            src_ref=sums_ref,
            dst_ref=sums_land.at[place],
            send_sem=send_s.at[index],
            recv_sem=recv_s.at[place],
            device_id={"dp": target},
            device_id_type=MESH,
        )

    def sums_out(index):
        target = me * holders + index
        place = jnp.maximum((slot - target + shards) % shards - 1, 0)
        return target, sums_copy(target, index, place)

    for index in range(holders):
        target, copy = sums_out(index)

        @pl.when(target != slot)
        def _():
            copy.start()

    piece = block_piece(whole_ref)
    zero, one = (gather_begin(whole_ref, piece, peers, (send, recv), half) for half in range(2))
    passed = gather_forward(whole_ref, piece, peers, (send, recv), zero, one)

    def channels_copy(other, index):
        return link(channels_ref, channels_ref, (send_c, recv_c), index, other)

    @pl.when(holding)
    def _():
        summed = sums_ref[...]
        for step in range(1, shards):
            sums_copy((slot + step) % shards, 0, step - 1).wait_recv()
            summed = summed + sums_land[step - 1]
        channels_ref[...] = summed
        for index, other in enumerate(peers[1:]):
            channels_copy(other, index).start()

    gather_finish(whole_ref, piece, peers, (send, recv), zero, one, passed)

    for index, other in enumerate(peers[1:]):

        @pl.when(slot // holders == other)
        def _():
            channels_copy(other, index).wait_recv()

    @pl.when(holding)
    def _():
        for index, other in enumerate(peers[1:]):
            channels_copy(other, index).wait_send()

    for index in range(holders):
        target, copy = sums_out(index)

        @pl.when(target != slot)
        def _():
            copy.wait_send()


def gather_sums(sums, block, sections, shards, holders, ident):
    return pl.pallas_call(
        functools.partial(sums_kernel, shards, holders),
        out_shape=(shape(sums.shape, F32), shape((sections,) + block.shape, BF16)),
        in_specs=[vmem()] * 2,
        out_specs=(vmem(),) * 2,
        scratch_shapes=[pltpu.VMEM((shards - 1,) + sums.shape, F32)]
        + copy_sems(max(shards - 1, holders))
        + copy_sems(3)
        + copy_sems(6),
        cost_estimate=lasting(25),
        compiler_params=comm_params(ident),
    )(sums, block)


def woven_parts(part, here, low, size, shards):
    step = size // shards
    return jnp.concatenate(
        [
            part[k, here, low + d * step : low + (d + 1) * step].astype(F32)
            for d in range(shards)
            for k in range(part.shape[0])
        ],
        axis=1,
    )


def joined_parts(part, here, low, size):
    return jnp.concatenate(
        [part[k, here, low : low + size].astype(F32) for k in range(part.shape[0])], axis=1
    )


def by_strips(rows, work):
    def strip(i, carry):
        work(pl.ds(pl.multiple_of(i * SMALL, SMALL), SMALL))
        return carry

    lax.fori_loop(0, rows // SMALL, strip, 0)


def attention_outputs(shards, part, value_ref, base_ref, out_ref, small_ref):
    sections = part.shape[0]
    width = out_ref.shape[2]
    wide = value_ref.shape[2] // sections
    own = width // sections
    keyed = base_ref.shape[2] - 2 * width - wide * sections
    edge = wide + own
    total = edge + keyed + wide + own
    few = wide // shards

    def strip(here):
        value_ref[0, here, :] = woven_parts(part, here, 0, wide, shards)
        base_ref[0, here, :width] = joined_parts(part, here, wide, own)
        shared = part[0, here, edge : edge + keyed].astype(F32)
        for k in range(1, sections):
            shared += part[k, here, edge : edge + keyed].astype(F32)
        low = width
        base_ref[0, here, low : low + keyed] = shared
        low += keyed
        base_ref[0, here, low : low + wide * sections] = woven_parts(
            part, here, edge + keyed, wide, shards
        )
        low += wide * sections
        base_ref[0, here, low:] = joined_parts(part, here, edge + keyed + wide, own)

    by_strips(value_ref.shape[1], strip)
    for k in range(sections):
        for half in range(2):
            columns = slice(half * (width // 2), (half + 1) * (width // 2))
            out_ref[0, k * few : (k + 1) * few, columns] = part[
                k, half * few : (half + 1) * few, total : total + width // 2
            ].astype(F32)
        small_ref[0, k] = part[k, :SMALL, total + width // 2 :].astype(F32)


def feed_outputs(shards, feed, in_ref, out_ref, small_ref):
    sections, rows = feed.shape[:2]
    width = out_ref.shape[2]
    hidden = in_ref.shape[2] // sections

    def strip(here):
        in_ref[0, here, :] = woven_parts(feed, here, 0, hidden, shards)

    by_strips(rows, strip)
    for k in range(sections):
        out_ref[0, k * rows : (k + 1) * rows, :] = feed[k, :, hidden : hidden + width].astype(F32)
        small_ref[0, k] = feed[k, :SMALL, hidden + width :].astype(F32)


def assemble_kernel(work, shards, layers, *refs):
    for layer in range(layers):

        @pl.when(pl.program_id(0) == layer)
        def _():
            work(shards, refs[layer], *refs[layers:])


def assemble(work, gathered, dims, shards):
    layers = len(gathered)
    dims = dims + ((gathered[0].shape[0], SMALL, LANES),)
    return pl.pallas_call(
        functools.partial(assemble_kernel, work, shards, layers),
        grid=(layers,),
        out_shape=tuple(shape((layers,) + d, F32) for d in dims),
        in_specs=[pl.BlockSpec(a.shape, lambda i: (0, 0, 0)) for a in gathered],
        out_specs=tuple(
            pl.BlockSpec((1,) + d, lambda i, n=len(d): (i,) + (0,) * n) for d in dims
        ),
        cost_estimate=lasting(6),
        compiler_params=params(),
    )(*gathered)


def chosen(pieces):
    section = lax.axis_index("section")
    result = pieces[0]
    for k in range(1, len(pieces)):
        result = jnp.where(section == k, pieces[k], result)
    return result


def pick(ref, index, low, size, shards, sections):
    step = size // (shards * sections)
    parts = []
    for shard in range(shards):
        start = low + shard * sections * step
        parts.append(
            chosen([ref[index + (slice(start + k * step, start + (k + 1) * step),)] for k in range(sections)])
        )
    return jnp.concatenate(parts, axis=-1)


def pack_attention_kernel(shards, sections, value_ref, base_ref, out_ref, packed_ref):
    rows, wide_all = value_ref.shape[1:]
    few_all, width = out_ref.shape[1:]
    wide, own, few = wide_all // sections, width // sections, few_all // sections
    keyed = base_ref.shape[2] - 2 * width - wide_all
    section = lax.axis_index("section")
    low = wide + own + keyed

    def strip(i, carry):
        here = pl.ds(pl.multiple_of(i * SMALL, SMALL), SMALL)

        def base(start, size):
            return base_ref[0, here, pl.ds(pl.multiple_of(start, LANES), size)]

        packed_ref[here, :wide] = pick(value_ref, (0, here), 0, wide_all, shards, sections)
        packed_ref[here, wide : wide + own] = base(section * own, own)
        packed_ref[here, wide + own : low] = base(width, keyed)
        packed_ref[here, low : low + wide] = pick(
            base_ref, (0, here), width + keyed, wide_all, shards, sections
        )
        packed_ref[here, low + wide : low + wide + own] = base(
            width + keyed + wide_all + section * own, own
        )
        return carry

    lax.fori_loop(0, rows // SMALL, strip, 0)
    low += wide + own
    mine = pl.ds(pl.multiple_of(section * few, few), few)
    for half in range(2):
        packed_ref[half * few : (half + 1) * few, low:] = out_ref[
            0, mine, half * (width // 2) : (half + 1) * (width // 2)
        ]


def pack_feed_kernel(shards, sections, in_ref, out_ref, packed_ref):
    rows, hidden_all = in_ref.shape[1:]
    hidden = hidden_all // sections
    size = out_ref.shape[1] // sections

    def strip(i, carry):
        here = pl.ds(pl.multiple_of(i * SMALL, SMALL), SMALL)
        packed_ref[here, :hidden] = pick(in_ref, (0, here), 0, hidden_all, shards, sections)
        return carry

    lax.fori_loop(0, rows // SMALL, strip, 0)
    start = pl.multiple_of(lax.axis_index("section") * size, size)
    packed_ref[:, hidden:] = out_ref[0, pl.ds(start, size), :]


def pack(kernel, layer, columns, shards, sections, *arrays):
    rows = arrays[0].shape[1]
    return pl.pallas_call(
        functools.partial(kernel, shards, sections),
        grid=(1,),
        out_shape=shape((rows, columns), BF16),
        in_specs=[pl.BlockSpec((1,) + a.shape[1:], lambda i: (layer, 0, 0)) for a in arrays],
        out_specs=pl.BlockSpec((rows, columns), lambda i: (0, 0)),
        cost_estimate=lasting(3),
        compiler_params=params(),
    )(*arrays)


def unpack_kernel(layers, shards, sections, places, everyone_ref, *refs):
    base_buf = refs[-1]
    section = lax.axis_index("section")
    outs = 14
    for layer in range(layers):
        (
            gain_ref,
            shift_ref,
            feed_gain_ref,
            feed_shift_ref,
            feed_out_ref,
            own_ref,
            rate_ref,
            coef_ref,
            bias_ref,
            feed_in_ref,
            pair_ref,
            offset_ref,
            skip_ref,
            own_out_ref,
        ) = refs[layer * outs : (layer + 1) * outs]
        width = gain_ref.shape[1]
        own = width // sections
        mine = pl.ds(pl.multiple_of(section * own, LANES), own)
        row = slice(layer, layer + 1)

        def joined(low, size):
            return jnp.concatenate(
                [everyone_ref[d, row, low : low + size] for d in range(shards)], axis=1
            )

        def share(low, size):
            step = size // sections
            return jnp.concatenate(
                [
                    chosen(
                        [
                            everyone_ref[d, row, low + k * step : low + (k + 1) * step]
                            for k in range(sections)
                        ]
                    )
                    for d in range(shards)
                ],
                axis=1,
            )

        def channels(low):
            size = width // shards
            count = own // size
            return jnp.concatenate(
                [everyone_ref[section * count + d, row, low : low + size] for d in range(count)],
                axis=1,
            )

        size = width // shards
        gain_ref[...] = joined(places["norm_gain"], size)
        shift_ref[...] = joined(places["norm_shift"], size)
        feed_gain_ref[...] = joined(places["feed_gain"], size)
        feed_shift_ref[...] = joined(places["feed_shift"], size)
        feed_out_ref[...] = joined(places["feed_out_bias"], size)
        own_ref[0:1, :] = gain_ref[:, mine]
        own_ref[1:2, :] = shift_ref[:, mine]
        own_ref[2:3, :] = feed_gain_ref[:, mine]
        own_ref[3:8, :] = jnp.zeros((5, own), F32)
        own_out_ref[...] = feed_out_ref[:, mine]
        skip_ref[...] = channels(places["average_skip"])
        for n in range(rate_ref.shape[0]):
            rate = sigmoid(channels(places["average_decay"] + n * size))
            drive = (1.0 - rate) * channels(places["average_input"] + n * size)
            coef = drive * channels(places["average_output"] + n * size)
            rate_ref[n] = jnp.broadcast_to(rate, (CHUNKS, own))
            coef_ref[n] = jnp.broadcast_to(coef, (CHUNKS, own))
        keyed = offset_ref.shape[1]
        step = keyed // shards
        for r in range(2):
            pair_ref[r : r + 1, :] = joined(places["pair_scale"] + r * step, step)
        offset_ref[...] = joined(places["query_shift"], step)
        feed_in_ref[...] = share(
            places["feed_in_bias"], feed_in_ref.shape[1] * sections // shards
        )
        total = bias_ref.shape[1]
        wide = (total - keyed - 2 * own) // 2
        base_all = 2 * width + keyed + wide * sections
        base_buf[...] = joined(places["base_bias"], base_all // shards)
        low = wide + own + keyed
        bias_ref[:, :wide] = share(places["value_bias"], wide * sections // shards)
        bias_ref[:, wide : wide + own] = base_buf[:, mine]
        bias_ref[:, wide + own : low] = base_buf[:, width : width + keyed]
        bias_ref[:, low : low + wide] = pick(
            base_buf, (slice(None),), width + keyed, wide * sections, shards, sections
        )
        start = pl.multiple_of(width + keyed + wide * sections + section * own, LANES)
        bias_ref[:, low + wide :] = base_buf[:, pl.ds(start, own)]


def unpack(everyone, places, sizes, sections):
    shards, layers = everyone.shape[:2]
    width, dims, total, hidden, keyed, base = sizes
    own = width // sections
    one_layer = (
        [shape((1, width), F32)] * 5
        + [shape((8, own), F32)]
        + [shape((dims, CHUNKS, own), F32)] * 2
        + [
            shape((1, total), F32),
            shape((1, hidden), F32),
            shape((2, keyed), F32),
            shape((1, keyed), F32),
            shape((1, own), F32),
            shape((1, own), F32),
        ]
    )
    outs = pl.pallas_call(
        functools.partial(unpack_kernel, layers, shards, sections, places),
        out_shape=tuple(one_layer * layers),
        in_specs=[vmem()],
        out_specs=(vmem(),) * (len(one_layer) * layers),
        scratch_shapes=[pltpu.VMEM((1, base), F32)],
        cost_estimate=lasting(3),
        compiler_params=params(),
    )(everyone)
    names = (
        "gain",
        "shift",
        "feed_gain",
        "feed_shift",
        "feed_out",
        "own",
        "rate",
        "coef",
        "bias",
        "feed_in",
        "pair",
        "offset",
        "skip",
        "own_out",
    )
    count = len(one_layer)
    return [
        types.SimpleNamespace(**dict(zip(names, outs[k * count : (k + 1) * count])))
        for k in range(layers)
    ]


def body(
    tokens,
    lengths,
    cotangent,
    norm_gain,
    norm_shift,
    average_decay,
    average_input,
    average_output,
    average_skip,
    value_weight,
    value_bias,
    base_weight,
    base_bias,
    pair_scale,
    query_shift,
    out_weight,
    feed_gain,
    feed_shift,
    feed_in_weight,
    feed_in_bias,
    feed_out_weight,
    feed_out_bias,
):
    sections = lax.axis_size("section")
    shards = lax.axis_size("dp")
    section = lax.axis_index("section")
    _, count, width = tokens.shape
    layers = norm_gain.shape[0]
    own = width // sections
    wide = value_weight.shape[2]
    keyed = pair_scale.shape[2] * shards
    hidden = feed_in_weight.shape[2]

    share = wide // sections
    total = share + own + keyed + share + own

    def over_dp(array):
        return lax.all_gather(array, "dp", axis=0, tiled=True)

    weights = []
    for layer in range(layers):
        attention = pack(
            pack_attention_kernel,
            layer,
            total + width // 2,
            shards,
            sections,
            value_weight,
            base_weight,
            out_weight,
        )
        feed = pack(
            pack_feed_kernel,
            layer,
            hidden // sections + width,
            shards,
            sections,
            feed_in_weight,
            feed_out_weight,
        )
        weights.append((over_dp(attention), over_dp(feed)))

    smalls = dict(
        norm_gain=norm_gain,
        norm_shift=norm_shift,
        average_decay=average_decay,
        average_input=average_input,
        average_output=average_output,
        average_skip=average_skip,
        feed_gain=feed_gain,
        feed_shift=feed_shift,
        feed_out_bias=feed_out_bias,
        value_bias=value_bias,
        feed_in_bias=feed_in_bias,
        base_bias=base_bias,
        pair_scale=pair_scale,
        query_shift=query_shift,
    )
    packed = jnp.concatenate([a.reshape(layers, -1) for a in smalls.values()], axis=1)
    places = {}
    low = 0
    for name, array in smalls.items():
        places[name] = low
        low += array.size // layers
    dims = average_decay.shape[1]
    small = unpack(
        lax.all_gather(packed, "dp", axis=0),
        places,
        (width, dims, total, hidden // sections, keyed, base_weight.shape[2]),
        sections,
    )

    idents = iter(range(64))
    x0 = x = tokens[0]
    kept = []
    for layer in range(layers):
        attention_w, feed_w = weights[layer]
        p = small[layer]
        normed, mixed_own, pre, own_n, scale = average_forward(
            lengths, x, p.gain, p.shift, p.rate, p.coef, p.skip
        )
        middle, hidden_pre, mixed, update, shared, reset, value, att, gated, probs = attention_forward(
            lengths,
            normed,
            mixed_own,
            attention_w,
            p.bias,
            p.pair,
            p.offset,
            x,
            shards,
            next(idents),
        )
        feed_saved = [None] * 4
        x_next = None
        if layer + 1 < layers:
            x_next, *feed_saved = feed_forward_joined(
                middle, p.feed_gain, p.feed_shift, feed_w, p.feed_in, p.own_out, next(idents)
            )
        feed_pre, feed_n, feed_normed, feed_scale = feed_saved
        kept.append(
            types.SimpleNamespace(
                x=x,
                middle=middle,
                normed=normed,
                mixed=mixed,
                pre=pre,
                own_n=own_n,
                scale=scale,
                update=update,
                saved=(shared, reset, value, att, probs),
                gated=gated,
                hidden=hidden_pre,
                feed_pre=feed_pre,
                feed_n=feed_n,
                feed_normed=feed_normed,
                feed_scale=feed_scale,
            )
        )
        x = x_next

    def scattered(grad):
        return lax.psum_scatter(grad, "dp", scatter_dimension=0, tiled=True)

    given = cotangent[0]
    feed_grads = [None] * layers
    attention_grads = [None] * layers
    channel_sums = [None] * layers
    gathered = [None] * layers
    for layer in reversed(range(layers)):
        attention_w, feed_w = weights[layer]
        k, p = kept[layer], small[layer]
        gout, gupdate, resid, feed_grad, *last = feed_backward(
            given, k, p, feed_w, shards, next(idents)
        )
        if last:
            block_out = last[0]
        feed_grads[layer] = scattered(feed_grad)
        gmixed, gnormed, attention_grad = attention_backward(
            lengths,
            gout,
            gupdate,
            k,
            attention_w,
            p.pair,
            p.offset,
            shards,
            next(idents),
            () if layer else (attention_grads[1],),
        )
        attention_grads[layer] = scattered(attention_grad)
        z, zstats, channel_sums[layer], gathered[layer] = average_backward(
            lengths,
            gmixed,
            gnormed,
            k,
            resid,
            p.own,
            p.rate,
            p.coef,
            p.skip,
            feed_grads[1] if layer else attention_grads[1],
            next(idents),
        )
        if layer:
            given = (z, zstats, k.x)

    attention_one, feed_one = gathered
    input_grad, feed_zero = final_exchange(
        z, zstats, x0, [feed_grads[0]], sections, next(idents)
    )
    channels, attention_zero = gather_sums(
        jnp.concatenate(channel_sums, axis=0),
        attention_grads[0],
        sections,
        shards,
        own * shards // width,
        next(idents),
    )
    shard = lax.axis_index("dp")
    size = width // shards
    rows = channels.shape[0]
    channels = lax.dynamic_slice_in_dim(channels, shard * size % own, size, axis=1)
    channels = channels.reshape(layers, rows // layers, size)
    g_feed_in, g_feed_out, feed_smalls = assemble(
        feed_outputs,
        (feed_zero, feed_one),
        ((size, hidden), (hidden // shards, width)),
        shards,
    )
    g_value, g_base, g_out, smalls_out = assemble(
        attention_outputs,
        (attention_zero, attention_one),
        ((size, wide), (size, base_weight.shape[2]), (wide // shards, width)),
        shards,
    )

    def of_shard(array):
        part = array.shape[-1] // shards
        return lax.dynamic_slice_in_dim(array, shard * part, part, axis=array.ndim - 1)

    def woven(array):
        split = array.reshape(layers, sections, shards, -1)
        return split.transpose(0, 2, 1, 3).reshape(layers, -1)

    of_states, of_slopes, sums = channels[:, :dims], channels[:, dims : 2 * dims], channels[:, 2 * dims :]
    rate = jax.nn.sigmoid(average_decay)
    gdrive = average_output * of_states
    drive = (1.0 - rate) * average_input
    grate = drive * average_output * of_slopes - average_input * gdrive
    g_gain, g_shift, g_skip = sums[:, 0], sums[:, 1], sums[:, 2]
    g_decay, g_input, g_output = grate * rate * (1.0 - rate), (1.0 - rate) * gdrive, drive * of_states

    edge = share + own
    bias_rows = total // LANES
    bias = smalls_out[:, :, :bias_rows].reshape(layers, sections, total)
    pairs = of_shard(jnp.sum(smalls_out[:, :, bias_rows : bias_rows + 3], axis=1))
    g_pair, g_query = pairs[:, :2], pairs[:, 2]
    g_value_bias = of_shard(woven(bias[..., :share]))
    g_base_bias = of_shard(
        jnp.concatenate(
            (
                bias[..., share:edge].reshape(layers, -1),
                jnp.sum(bias[..., edge : edge + keyed], axis=1),
                woven(bias[..., edge + keyed : edge + keyed + share]),
                bias[..., edge + keyed + share :].reshape(layers, -1),
            ),
            axis=1,
        )
    )
    g_feed_gain = jnp.sum(feed_smalls[:, :, 0, :size], axis=1)
    g_feed_shift = jnp.sum(feed_smalls[:, :, 1, :size], axis=1)
    g_feed_out_bias = feed_smalls[:, 0, 2, :size]
    g_feed_in_bias = feed_smalls[:, :, 3, :size].reshape(layers, -1)
    return (
        block_out[None],
        input_grad[None],
        g_gain,
        g_shift,
        g_decay,
        g_input,
        g_output,
        g_skip,
        g_value,
        g_value_bias,
        g_base,
        g_base_bias,
        g_pair,
        g_query,
        g_out,
        g_feed_gain,
        g_feed_shift,
        g_feed_in,
        g_feed_in_bias,
        g_feed_out,
        g_feed_out_bias,
    )


def solution(mesh):
    row, row2 = P(None, "dp"), P(None, "dp", None)
    deep = P(None, None, "dp")
    in_specs = (
        P("dp", None, None),
        P("dp"),
        P("dp", None, None),
        row,
        row,
        deep,
        deep,
        deep,
        row,
        row2,
        row,
        row2,
        row,
        deep,
        row,
        row2,
        row,
        row,
        row2,
        row,
        row2,
        row,
    )
    out_specs = (
        P("dp", "section", None),
        P("dp", "section", None),
        row,
        row,
        deep,
        deep,
        deep,
        row,
        row2,
        row,
        row2,
        row,
        deep,
        row,
        row2,
        row,
        row,
        row2,
        row,
        row2,
        row,
    )
    return jax.shard_map(body, mesh=mesh, in_specs=in_specs, out_specs=out_specs, check_vma=False)
```

time: 679 us -> 610 us (0.90)
  Pallas kernels: 621 us -> 543 us
  waiting for transfers between devices: 9.23 us -> 18.2 us
    pallas_call x22 -> x11, Pallas kernels: 498 us -> 439 us  [the longest x9 426 us: transfer(): pl.pallas_call(kernel, out_shape=tuple((o for o, _ in outs.values())), in...]
    pallas_call x1, Pallas kernels: 48 us -> 29.9 us  [final_exchange(): pl.pallas_call(functools.partial(final_kernel, number), out_shape=(shape(...]
    all_gather x4, waiting for transfers between devices: 0.08 us -> 10.7 us  [over_dp(): return lax.all_gather(array, 'dp', axis=0, tiled=True)]
  transfers between devices with their start and end apart: 9 -> 8, of which waited for: 1 -> 3; matrix products, arithmetic and copies ran while one was open for 0% -> 1% of each run, Pallas kernels for 75% -> 72%
where the time goes in v3:
time: 610 us; the launch traced here: 609 us
  Pallas kernels  543 us (89%)
  blocking collectives  19.9 us (3%)
  waiting for transfers between devices  18.2 us (3%)
  between operations  15.3 us (3%)
  local copies, waits for them, and re-layouts  7.54 us (1%)
    pallas_call x9, Pallas kernels, transfer(): pl.pallas_call(kernel, out_shape=tuple((o for o, _ in outs.values())), in...  426 us
    pallas_call x1, Pallas kernels, gather_sums(): pl.pallas_call(functools.partial(sums_kernel, shards, holders), out_shape...  32.8 us
    pallas_call x1, Pallas kernels, final_exchange(): pl.pallas_call(functools.partial(final_kernel, number), out_shape=(shape(...  29.9 us
    pallas_call x2, Pallas kernels, average_forward(): pl.pallas_call(average_forward_kernel, out_shape=(shape((count, width), B...  23.9 us
    all_gather x1, blocking collectives, body(): lax.all_gather(packed, 'dp', axis=0)  19.9 us
    pallas_call x4, Pallas kernels, pack(): pl.pallas_call(functools.partial(kernel, shards, sections), grid=(1,), ou...  14.4 us
    pallas_call x2, Pallas kernels, assemble(): pl.pallas_call(functools.partial(assemble_kernel, work, shards, layers),...  12.8 us
  transfers between devices with their start and end apart: 8, of which 3 were waited for; matrix products, arithmetic and copies ran while one was open for 1% of the time, Pallas kernels for 72%

profile of v3, /device:TPU:0, one launch (start us, length us, event | category | flops | bytes accessed | tf_op | source)
XLA Modules:
  0.0 608.8 jit_solution(315159684018927435)
XLA Ops:
  7.2 4.7 shard_map.375
  11.9 0.0 all-gather.13.cloned.1.call-start
  12.0 2.5 shard_map.379
  14.5 0.0 all-gather.9.cloned.1.call-start
  14.6 4.7 shard_map.374
  19.5 0.0 all-gather.7.cloned.1.call-start
  19.5 2.5 shard_map.373
  22.2 0.1 reshape.81
  22.4 0.1 concatenate.9
  22.5 19.9 %all-gather.1.everyone_ref = f32[8,2,8256]{2,1,0:T(2,128)} all-gather(f32[1,2,8256]{2,1,0:T(2,128)S(1)} %bitcast.36), channel_id=2, replica_groups=mesh['section'=4,'dp'=8] {'dp'}, dimensions={0}, use_global_device_ids=true | all-gather | bytes 594432 | tf_op jit(solution)/shard_map/all_gather | solution.py:2144
  42.4 2.7 shard_map.376
  45.8 12.0 %shard_map.377 = (bf16[1024,1024]{1,0:T(8,128)(2,1)}, bf16[1024,256]{1,0:T(8,128)(2,1)}, bf16[1024,256]{1,0:T(8,128)(2,1)}, f32[1024,256]{1,0:T(8,128)}, f32[1024,128]{1,0:T(8,128)}) custom-call(s32[1]{0:T(128)S(6)} %copy.71.length_ref.refs_0_.refs_1_, bf16[1024,1024]{1,0:T(8,128)(2,1)} %bitcast.56, f32[1,1024]{1,0:T(1,128)} %get-tuple-element.116.gain_ref, ...), custom_call_target="tpu_custom_call" | custom-call | flops 12999999488 | bytes 39000000 | tf_op jit(solution)/shard_map/pallas_call | solution.py:208
  57.8 10.7 %all-gather.11.cloned.1.call-done.refs_1_.refs_2_ = bf16[1024,2176]{1,0:T(8,128)(2,1)} async-done(((bf16[128,2176]{1,0:T(8,128)(2,1)}), bf16[1024,2176]{1,0:T(8,128)(2,1)}) %all-gather.11.cloned.1.call-update) | async-done | bytes 4456464 | tf_op jit(solution)/shard_map/all_gather | solution.py:2095
  68.4 58.6 %shard_map.378 = (bf16[1024,1024]{1,0:T(8,128)(2,1)}, bf16[1024,256]{1,0:T(8,128)(2,1)}, bf16[1024,1024]{1,0:T(8,128)(2,1)}, bf16[1024,256]{1,0:T(8,128)(2,1)}, ...) custom-call(s32[1]{0:T(128)S(6)} %copy.71.length_ref.refs_0_.refs_1_, ...), custom_call_target="tpu_custom_call" | custom-call | flops 54000001024 | bytes 162000000 | tf_op jit(solution)/shard_map/pallas_call | solution.py:750
  127.0 42.3 %shard_map.380 = (bf16[1024,1024]{1,0:T(8,128)(2,1)}, bf16[1024,1024]{1,0:T(8,128)(2,1)}, bf16[1024,1024]{1,0:T(8,128)(2,1)}, bf16[1024,1024]{1,0:T(8,128)(2,1)}, f32[1024,128]{1,0:T(8,128)}) custom-call(bf16[1024,1024]{1,0:T(8,128)(2,1)} %get-tuple-element.126.refs_0_, bf16[1024,2048]{1,0:T(8,128)(2,1)} %all-gather.13.cloned.1.call-done.refs_1_.refs_0_, ...), custom_call_target="tpu_custom_call" | custom-call | flops 40000000000 | bytes 120000000 | tf_op jit(solution)/shard_map/pallas_call | solution.py:750
  169.4 11.9 %shard_map.381 = (bf16[1024,1024]{1,0:T(8,128)(2,1)}, bf16[1024,256]{1,0:T(8,128)(2,1)}, bf16[1024,256]{1,0:T(8,128)(2,1)}, f32[1024,256]{1,0:T(8,128)}, f32[1024,128]{1,0:T(8,128)}) custom-call(s32[1]{0:T(128)S(6)} %copy.71.length_ref.refs_0_.refs_1_, bf16[1024,1024]{1,0:T(8,128)(2,1)} %get-tuple-element.131.x_ref.refs_4_.refs_8_.refs_2_, ...), custom_call_target="tpu_custom_call" | custom-call | flops 12999999488 | bytes 39000000 | tf_op jit(solution)/shard_map/pallas_call | solution.py:208
  181.3 57.5 %shard_map.382 = (bf16[1024,1024]{1,0:T(8,128)(2,1)}, bf16[1024,256]{1,0:T(8,128)(2,1)}, bf16[1024,1024]{1,0:T(8,128)(2,1)}, bf16[1024,256]{1,0:T(8,128)(2,1)}, ...) custom-call(s32[1]{0:T(128)S(6)} %copy.71.length_ref.refs_0_.refs_1_, ...), custom_call_target="tpu_custom_call" | custom-call | flops 54000001024 | bytes 162000000 | tf_op jit(solution)/shard_map/pallas_call | solution.py:750
  238.8 61.1 %shard_map.383 = (bf16[1024,1024]{1,0:T(8,128)(2,1)}, bf16[1024,256]{1,0:T(8,128)(2,1)}, f32[1024,256]{1,0:T(8,128)}, bf16[1024,2176]{1,0:T(8,128)(2,1)}, bf16[256,1024]{1,0:T(8,128)(2,1)}) custom-call(bf16[1024,2048]{1,0:T(8,128)(2,1)} %all-gather.7.cloned.1.call-done.refs_0_, bf16[1024,1024]{1,0:T(8,128)(2,1)} %bitcast.55, ...), custom_call_target="tpu_custom_call" | custom-call | flops 46000001024 | bytes 138000000 | tf_op jit(solution)/shard_map/pallas_call | solution.py:750
  300.0 49.8 %shard_map.384 = (f32[1024,256]{1,0:T(8,128)}, f32[1024,256]{1,0:T(8,128)}, bf16[1024,2304]{1,0:T(8,128)(2,1)}) custom-call(s32[1]{0:T(128)S(6)} %copy.71.length_ref.refs_0_.refs_1_, bf16[1024,2176]{1,0:T(8,128)(2,1)} %all-gather.9.cloned.1.call-done.refs_1_, bf16[1024,1024]{1,0:T(8,128)(2,1)} %get-tuple-element.151.refs_2_, ...), custom_call_target="tpu_custom_call" | custom-call | flops 40000000000 | bytes 120000000 | tf_op jit(solution)/shard_map/pallas_call | solution.py:750
  349.8 0.0 reduce-scatter.9.cloned.1.call-start
  349.8 1.3 reduce-scatter.7.cloned.1.call-done.refs_11_
  351.1 27.3 %shard_map.385 = (bf16[1024,256]{1,0:T(8,128)(2,1)}, f32[8,1024]{1,0:T(8,128)}, f32[40,256]{1,0:T(8,128)}, bf16[4,128,2176]{2,1,0:T(8,128)(2,1)}) custom-call(s32[1]{0:T(128)S(6)} %copy.71.length_ref.refs_0_.refs_1_, f32[1024,256]{1,0:T(8,128)} %get-tuple-element.161.refs_1_, f32[1024,256]{1,0:T(8,128)} %get-tuple-element.162.refs_2_, ...), custom_call_target="tpu_custom_call" | custom-call | flops 16999999488 | bytes 51000000 | tf_op jit(solution)/shard_map/pallas_call | solution.py:750
  378.4 62.5 %shard_map.386 = (bf16[1024,1024]{1,0:T(8,128)(2,1)}, bf16[1024,256]{1,0:T(8,128)(2,1)}, f32[1024,256]{1,0:T(8,128)}, bf16[1024,2176]{1,0:T(8,128)(2,1)}) custom-call(bf16[1024,2048]{1,0:T(8,128)(2,1)} %all-gather.13.cloned.1.call-done.refs_1_.refs_0_, bf16[1024,256]{1,0:T(8,128)(2,1)} %get-tuple-element.168.refs_1_, ...), custom_call_target="tpu_custom_call" | custom-call | flops 46000001024 | bytes 138000000 | tf_op jit(solution)/shard_map/pallas_call | solution.py:750
  441.0 43.8 %shard_map.387 = (f32[1024,256]{1,0:T(8,128)}, f32[1024,256]{1,0:T(8,128)}, bf16[1024,2304]{1,0:T(8,128)(2,1)}) custom-call(bf16[128,2304]{1,0:T(8,128)(2,1)} %reduce-scatter.5.cloned.1.call-done.refs_0_.refs_11_, s32[1]{0:T(128)S(6)} %copy.71.length_ref.refs_0_.refs_1_, bf16[1024,2176]{1,0:T(8,128)(2,1)} %all-gather.11.cloned.1.call-done.refs_1_.refs_2_, ...), custom_call_target="tpu_custom_call" | custom-call | flops 40000000000 | bytes 120000000 | tf_op jit(solution)/shard_map/pallas_call | solution.py:750
  484.9 23.2 %shard_map.388 = (bf16[1024,256]{1,0:T(8,128)(2,1)}, f32[8,1024]{1,0:T(8,128)}, f32[40,256]{1,0:T(8,128)}, bf16[4,128,2304]{2,1,0:T(8,128)(2,1)}) custom-call(s32[1]{0:T(128)S(6)} %copy.71.length_ref.refs_0_.refs_1_, f32[1024,256]{1,0:T(8,128)} %get-tuple-element.186.refs_1_, f32[1024,256]{1,0:T(8,128)} %get-tuple-element.187.refs_2_, ...), custom_call_target="tpu_custom_call" | custom-call | flops 16999999488 | bytes 51000000 | tf_op jit(solution)/shard_map/pallas_call | solution.py:750
  508.2 1.4 pad_maximum_fusion.sums_ref
  509.6 29.9 %shard_map.389 = (bf16[256,1024]{1,0:T(8,128)(2,1)}, bf16[4,128,2176]{2,1,0:T(8,128)(2,1)}) custom-call(bf16[1024,256]{1,0:T(8,128)(2,1)} %get-tuple-element.192.z_ref, f32[8,1024]{1,0:T(8,128)} %get-tuple-element.193.stats_ref, bf16[1024,1024]{1,0:T(8,128)(2,1)} %bitcast.59, bf16[128,2176]{1,0:T(8,128)(2,1)} %reduce-scatter.9.cloned.1.call-done.refs_0_), custom_call_target="tpu_custom_call" | custom-call | flops 30000001024 | bytes 90000000 | tf_op jit(solution)/shard_map/pallas_call | solution.py:1622
  539.5 6.0 shard_map.392
  545.5 1.3 slice.75
  546.8 1.5 slice_reduce_fusion.2
  548.3 0.6 copy.68
  548.9 5.9 reduce-scatter.11.cloned.1.call-done.block_ref
  554.8 32.8 %shard_map.390 = (f32[80,256]{1,0:T(8,128)}, bf16[4,128,2304]{2,1,0:T(8,128)(2,1)}) custom-call(f32[80,256]{1,0:T(8,128)} %pad_maximum_fusion.sums_ref, bf16[128,2304]{1,0:T(8,128)(2,1)} %reduce-scatter.11.cloned.1.call-done.block_ref), custom_call_target="tpu_custom_call" | custom-call | flops 24999999488 | bytes 75000000 | tf_op jit(solution)/shard_map/pallas_call | solution.py:1719
  587.6 6.7 %shard_map.391 = (f32[2,128,2048]{2,1,0:T(8,128)}, f32[2,128,4224]{2,1,0:T(8,128)}, f32[2,256,1024]{2,1,0:T(8,128)}, f32[2,4,16,128]{3,2,1,0:T(8,128)}) custom-call(bf16[4,128,2304]{2,1,0:T(8,128)(2,1)} %get-tuple-element.200.refs_0_, bf16[4,128,2304]{2,1,0:T(8,128)(2,1)} %get-tuple-element.201.refs_1_), custom_call_target="tpu_custom_call" | custom-call | flops 6000000000 | bytes 18000000 | tf_op jit(solution)/shard_map/pallas_call | solution.py:1819
  594.4 0.9 reshape.83
  595.4 0.8 slice_reduce_fusion
  596.2 0.6 slice_multiply_fusion.1
  596.8 0.6 fusion.8
  597.4 0.1 reshape.87
  597.5 0.1 reshape.88
  597.6 0.1 reshape.84
  597.7 0.1 reshape.85
  597.8 0.7 constant_dynamic-slice_fusion
  598.5 0.6 constant_dynamic-slice_fusion.1
  599.1 0.6 constant_dynamic-slice_fusion.2
  599.7 0.7 fusion.6
  600.4 0.8 copy.72
  601.2 0.8 copy.73
  (69 shorter events, 0.6 us)
Async XLA Ops:
  7.2 61.3 %all-gather.11.cloned.1.call-start = ((), (), s32[]{:S(2)}) async-start(), calls=%async_computation.6 | async-start | bytes 5013504 | tf_op jit(solution)/shard_map/all_gather | solution.py:2095
  11.9 115.1 %all-gather.13.cloned.1.call-start = ((), (), s32[]{:S(2)}) async-start(), calls=%async_computation.7 | async-start | bytes 4718592 | tf_op jit(solution)/shard_map/all_gather | solution.py:2095
  14.5 166.7 %all-gather.9.cloned.1.call-start = ((), (), s32[]{:S(2)}) async-start(), calls=%async_computation.5 | async-start | bytes 5013504 | tf_op jit(solution)/shard_map/all_gather | solution.py:2095
  19.3 2.8 copy-start.2
  19.3 2.8 copy-start.13
  19.3 2.9 copy-start.4
  19.3 2.9 copy-start.6
  19.4 2.9 copy-start.10
  19.4 2.9 copy-start.11
  19.4 2.9 copy-start.12
  19.4 2.9 copy-start.14
  19.4 2.9 copy-start.15
  19.4 2.9 copy-start.16
  19.4 2.9 copy-start.17
  19.4 2.9 copy-start.18
  19.5 2.9 copy-start.19
  19.5 2.9 copy-start.20
  19.5 219.3 %all-gather.7.cloned.1.call-start = ((), (), s32[]{:S(2)}) async-start(), calls=%async_computation.4 | async-start | bytes 4718592 | tf_op jit(solution)/shard_map/all_gather | solution.py:2095
  22.1 329.1 %reduce-scatter.7.cloned.1.call-start = ((), (), s32[]{:S(2)}) async-start(), calls=%async_computation.9 | async-start | bytes 5013504 | tf_op jit(solution)/shard_map/reduce_scatter | solution.py:2200
  299.9 141.1 %reduce-scatter.5.cloned.1.call-start = ((), (), s32[]{:S(2)}) async-start(), calls=%async_computation.8 | async-start | bytes 5308416 | tf_op jit(solution)/shard_map/reduce_scatter | solution.py:2200
  349.8 159.8 %reduce-scatter.9.cloned.1.call-start = ((), (), s32[]{:S(2)}) async-start(), calls=%async_computation.10 | async-start | bytes 5013504 | tf_op jit(solution)/shard_map/reduce_scatter | solution.py:2200
  441.0 113.8 %reduce-scatter.11.cloned.1.call-start = ((), (), s32[]{:S(2)}) async-start(), calls=%async_computation.11 | async-start | bytes 5308416 | tf_op jit(solution)/shard_map/reduce_scatter | solution.py:2200
  484.9 23.2 %copy-start.8 = (f32[40,256]{1,0:T(8,128)S(1)}, f32[40,256]{1,0:T(8,128)}, u32[]{:S(2)}) copy-start(f32[40,256]{1,0:T(8,128)} %get-tuple-element.197) | copy-start | bytes 122884
  587.6 8.5 %copy-start.9 = (f32[80,256]{1,0:T(8,128)S(1)}, f32[80,256]{1,0:T(8,128)}, u32[]{:S(2)}) copy-start(f32[80,256]{1,0:T(8,128)} %get-tuple-element.199) | copy-start | bytes 245764
  587.6 8.6 %copy-start.3 = (f32[2,16,128]{2,1,0:T(8,128)S(1)}, f32[2,16,128]{2,1,0:T(8,128)}, u32[]{:S(2)}) copy-start(f32[2,16,128]{2,1,0:T(8,128)} %param.27) | copy-start | bytes 49156
  587.6 8.6 %copy-start.5 = (f32[2,16,128]{2,1,0:T(8,128)S(1)}, f32[2,16,128]{2,1,0:T(8,128)}, u32[]{:S(2)}) copy-start(f32[2,16,128]{2,1,0:T(8,128)} %param.29) | copy-start | bytes 49156
  587.6 8.6 %copy-start.7 = (f32[2,16,128]{2,1,0:T(8,128)S(1)}, f32[2,16,128]{2,1,0:T(8,128)}, u32[]{:S(2)}) copy-start(f32[2,16,128]{2,1,0:T(8,128)} %param.28) | copy-start | bytes 49156
  587.6 12.8 %copy-start = (bf16[256,1024]{1,0:T(8,128)(2,1)S(1)}, bf16[256,1024]{1,0:T(8,128)(2,1)}, u32[]{:S(2)}) copy-start(bf16[256,1024]{1,0:T(8,128)(2,1)} %get-tuple-element.150) | copy-start | bytes 1572868
  594.4 6.8 %copy-start.1 = (bf16[256,1024]{1,0:T(8,128)(2,1)S(1)}, bf16[256,1024]{1,0:T(8,128)(2,1)}, u32[]{:S(2)}) copy-start(bf16[256,1024]{1,0:T(8,128)(2,1)} %get-tuple-element.195) | copy-start | bytes 1572868
Sparse Core Ops, SparseCore 0:
  12.1 56.3 all-gather.10
  70.6 46.0 all-gather.12
  118.9 48.2 all-gather.8
  169.2 46.0 all-gather.6
  300.0 51.0 reduce-scatter.6
  353.3 53.1 reduce-scatter.4
  441.1 58.1 reduce-scatter.8
  501.6 53.1 reduce-scatter.10

commit v4 on v3

--- a/solution.py
+++ b/solution.py
@@ -226,7 +226,7 @@
     )(length, x, gain, shift, rate, coef, skip)
 
 
-def average_backward_work(r):
+def average_backward_work(beside, r):
     length = r.length[0]
     count, own = r.z.shape
     dims = r.rate.shape[0]
@@ -235,11 +235,12 @@
     groups = own // LANES
     part_size = dims // 2
     gain_ref, shift_ref = r.norm.at[0:1, :], r.norm.at[1:2, :]
-    peers = plane()
-    sems, piece = (r.send, r.recv), block_piece(r.whole)
-    r.whole[peers[0]] = r.block[...]
-    greet(peers[1], peers[2])
-    begun = [gather_begin(r.whole, piece, peers, sems, half) for half in range(2)]
+    if beside:
+        peers = plane()
+        sems, piece = (r.send, r.recv), block_piece(r.whole)
+        r.whole[peers[0]] = r.block[...]
+        greet(peers[1], peers[2])
+        begun = [gather_begin(r.whole, piece, peers, sems, half) for half in range(2)]
 
     def load_strip(i, carry):
         start = pl.multiple_of(i * STRIP, STRIP)
@@ -303,7 +304,7 @@
             return states
 
         lax.fori_loop(0, steps, back_outputs, starts, unroll=UNROLL)
-        if passed is None:
+        if beside and passed is None:
             passed = gather_forward(r.whole, piece, peers, sems, *begun)
 
     ones = jnp.ones((CHUNKS, own), BF16)
@@ -342,7 +343,8 @@
     r.sums[last + 1 : last + 2, :] = of_shift
     r.sums[last + 2 : last + 3, :] = of_skip
     r.sums[last + 3 : last + 8, :] = jnp.zeros((5, own), F32)
-    gather_finish(r.whole, piece, peers, sems, *begun, passed)
+    if beside:
+        gather_finish(r.whole, piece, peers, sems, *begun, passed)
 
 
 def average_backward(
@@ -363,18 +365,23 @@
         rate=rate,
         coef=coef,
         skip=skip,
-        block=block,
     )
+    beside = block is not None
+    outs, held = {}, {}
+    if beside:
+        given.update(block=block)
+        outs.update(whole=(shape((4,) + block.shape, BF16), VMEM))
+        held.update(send=sems, recv=sems)
     return transfer(
-        average_backward_work,
+        functools.partial(average_backward_work, beside),
         dict(length=(length, SMEM), **{name: (a, VMEM) for name, a in given.items()}),
         dict(
             z=(shape((count, own), BF16), VMEM),
             stats=(shape((CHUNKS, count), F32), VMEM),
             sums=(shape((2 * dims + 8, own), F32), VMEM),
-            whole=(shape((4,) + block.shape, BF16), VMEM),
+            **outs,
         ),
-        dict(m_buf=buffer, g_buf=buffer, r_buf=buffer, send=sems, recv=sems),
+        dict(m_buf=buffer, g_buf=buffer, r_buf=buffer, **held),
         ident,
         17,
         after,
@@ -684,7 +691,7 @@
     return stage[...] + got[1]
 
 
-def transfer(work, ins, outs, scratch, ident, microseconds, after=(), first=None):
+def transfer(work, ins, outs, scratch, ident, microseconds, after=(), first=None, rows=ROWS):
     order = [n for kind in (FETCH, BLOCKS, LATE, OWN_PART) for n in ins if ins[n][1] == kind]
     stored = [n for n, (_, how) in outs.items() if how == STORE]
     buffers, places, low = {}, {}, 0
@@ -696,7 +703,7 @@
             columns = array.shape[1] // (4 if how == OWN_PART else 1)
             buffers[name] = pltpu.VMEM((array.shape[0], columns), array.dtype)
         places[name] = low
-        low += ins[name][0].shape[0] // ROWS if name in ins and ins[name][1] == BLOCKS else 1
+        low += ins[name][0].shape[0] // rows if name in ins and ins[name][1] == BLOCKS else 1
     by_blocks = [n for n in order if ins[n][1] == BLOCKS]
 
     def kernel(*refs):
@@ -718,7 +725,7 @@
             return pltpu.make_async_copy(given[name], held[name], sem)
 
         def block_copy(name, block):
-            here = rows_of(block)
+            here = rows_of(block, rows)
             source, target = given[name].at[here, :], held[name].at[here, :]
             return pltpu.make_async_copy(source, target, local.at[places[name] + block])
 
@@ -735,7 +742,7 @@
         if first:
             first(r)
         if by_blocks:
-            for block in range(ins[by_blocks[0]][0].shape[0] // ROWS):
+            for block in range(ins[by_blocks[0]][0].shape[0] // rows):
                 for name in by_blocks:
                     block_copy(name, block).start()
         start(LATE, OWN_PART)
@@ -756,26 +763,22 @@
         + [pltpu.SemaphoreType.DMA((max(low, 1),))]
         + list(scratch.values()),
         cost_estimate=lasting(microseconds),
-        compiler_params=comm_params(ident),
+        compiler_params=params() if ident is None else comm_params(ident),
     )(*after, *[a for a, _ in ins.values()])
 
 
-def rows_of(block):
-    return pl.ds(pl.multiple_of(block * ROWS, ROWS), ROWS)
-
-
-def half_rows(block):
-    return pl.ds(pl.multiple_of(block * (ROWS // 2), ROWS // 2), ROWS // 2)
-
-
-def owned(block, owner, half, own):
-    start = pl.multiple_of(block * ROWS + half * (ROWS // 2), ROWS // 2)
-    return pl.ds(start, ROWS // 2), pl.ds(pl.multiple_of(owner * own, LANES), own)
-
-
-def sum_scratch(name, count, own):
+def rows_of(block, rows=ROWS):
+    return pl.ds(pl.multiple_of(block * rows, rows), rows)
+
+
+def owned(block, owner, half, own, rows):
+    start = pl.multiple_of(block * rows + half * (rows // 2), rows // 2)
+    return pl.ds(start, rows // 2), pl.ds(pl.multiple_of(owner * own, LANES), own)
+
+
+def sum_scratch(name, count, own, rows=ROWS):
     buffer = pltpu.VMEM((2, count // 2, own), BF16)
-    sems = pltpu.SemaphoreType.DMA((6 * (count // ROWS),))
+    sems = pltpu.SemaphoreType.DMA((6 * (count // rows),))
     return {
         name + "_early": buffer,
         name + "_direct": buffer,
@@ -786,9 +789,10 @@
     }
 
 
-def block_sum(r, name, part, peers, own, piece=None, place=half_rows):
+def block_sum(r, name, part, peers, own, piece=None, place=None, rows=ROWS):
     if piece is None:
-        piece = functools.partial(owned, own=own)
+        piece = functools.partial(owned, own=own, rows=rows)
+        place = functools.partial(rows_of, rows=rows // 2)
     me, across, along, far = peers
     early, direct, late, stage, send, recv = (
         getattr(r, name + end) for end in ("_early", "_direct", "_late", "_stage", "_send", "_recv")
@@ -853,7 +857,7 @@
     me, across, along, far = peers
 
     def copy(block, owner, half, index, other):
-        place = out.at[owned(block, owner, half, own)]
+        place = out.at[owned(block, owner, half, own, ROWS)]
         return link(place, place, sems, block * 6 + index, other)
 
     def own_copy(block, half, way):
@@ -886,8 +890,8 @@
     return types.SimpleNamespace(begin=begin, forward=forward, arrive=arrive, sent=sent)
 
 
-def pipeline(count, compute, sums, finish, gather, extra=None, between=None, before=None):
-    blocks = count // ROWS
+def pipeline(count, compute, sums, finish, gather, extra=None, between=None, before=None, rows=ROWS):
+    blocks = count // rows
     if before:
         before.begin(0)
         before.begin(1)
@@ -953,23 +957,24 @@
     lax.fori_loop(0, blocks, close, 0)
 
 
-def finish_strips(one, block, work):
+def finish_strips(one, block, work, rows=ROWS):
     for half in range(2):
         one.arrived(block, half)
 
         def strip(start):
-            row = pl.multiple_of(block * ROWS + half * (ROWS // 2), ROWS // 2) + start
+            row = pl.multiple_of(block * rows + half * (rows // 2), rows // 2) + start
             work(pl.ds(row, STRIP), one.total(block, half, start))
 
-        strips(ROWS // 2, strip)
-
-
-def views(refs, block):
-    return [ref.at[rows_of(block), :] for ref in refs]
-
-
-def attention_forward(length, normed, mixed_own, packed, bias, pair, offset, x, shards, ident):
+        strips(rows // 2, strip)
+
+
+def views(refs, block, rows=ROWS):
+    return [ref.at[rows_of(block, rows), :] for ref in refs]
+
+
+def attention_forward(length, normed, mixed, packed, bias, pair, offset, x, shards, ident):
     count, width = normed.shape
+    apart = mixed.shape[1] == width
     own = width // 4
     wide = width // 2
     keyed = pair.shape[1]
@@ -986,9 +991,12 @@
         peers = plane()
         mine = pl.ds(pl.multiple_of(peers[0] * own, LANES), own)
         real = r.length[0]
-        r.mixed[:, mine] = r.mixed_own[...]
+        mixing = None
+        if not apart:
+            r.mixed[:, mine] = r.mixed_own[...]
         greet(peers[1], peers[2])
-        mixing = block_gather(r.mixed, peers, own, (r.mixed_send, r.mixed_recv))
+        if not apart:
+            mixing = block_gather(r.mixed, peers, own, (r.mixed_send, r.mixed_recv))
         total = block_sum(r, "sum", r.part, peers, own)
         gather = block_gather(r.out, peers, own, (r.gather_send, r.gather_recv))
         saved = (r.update, r.shared, r.reset, r.cand, r.value, r.att, r.gated, r.probs)
@@ -1029,7 +1037,9 @@
 
             @pl.when(i == count // ROWS)
             def _():
-                r.store("mixed", "update", "shared", "reset", "value", "att", "gated", "probs")
+                if not apart:
+                    r.store("mixed")
+                r.store("update", "shared", "reset", "value", "att", "gated", "probs")
 
         pipeline(count, compute, (total,), finish, gather, extra, before=mixing)
 
@@ -1040,7 +1050,7 @@
             length=(length, SMEM),
             packed=(packed, RAW),
             normed=(normed, BLOCKS),
-            mixed_own=(mixed_own, VMEM),
+            **(dict(mixed=(mixed, BLOCKS)) if apart else dict(mixed_own=(mixed, VMEM))),
             x=(x, OWN_PART),
             bias=(bias, VMEM),
             pair=(pair, VMEM),
@@ -1049,7 +1059,7 @@
         dict(
             out=(shape((count, width), BF16), VMEM),
             hidden=(shape((count, own), BF16), VMEM),
-            mixed=rows(width),
+            **({} if apart else dict(mixed=rows(width))),
             update=rows(own),
             shared=rows(keyed),
             reset=rows(wide),
@@ -1074,6 +1084,38 @@
         54,
         first=first,
     )
+
+
+def gather_kernel(waits, *refs):
+    own_ref, out_ref, send, recv = refs[waits:]
+    count, own = own_ref.shape
+    peers = plane()
+    mine = pl.ds(pl.multiple_of(peers[0] * own, LANES), own)
+    out_ref[:, mine] = own_ref[...]
+    greet(peers[1], peers[2])
+    whole = block_gather(out_ref, peers, own, (send, recv))
+    blocks = count // ROWS
+    for block in range(blocks):
+        whole.begin(block)
+        if block:
+            whole.forward(block - 1)
+    whole.forward(blocks - 1)
+    for block in range(blocks):
+        whole.arrive(block)
+        whole.sent(block)
+
+
+def gather_columns(own, ident, after=()):
+    count, width = own.shape
+    return pl.pallas_call(
+        functools.partial(gather_kernel, len(after)),
+        out_shape=shape((count, width * 4), BF16),
+        in_specs=[hbm()] * len(after) + [vmem()],
+        out_specs=vmem(),
+        scratch_shapes=[gather_sems(count), gather_sems(count)],
+        cost_estimate=lasting(20),
+        compiler_params=comm_params(ident),
+    )(*after, own)
 
 
 def feed_forward_joined(x, gain, shift, weights, bias, own_out, ident):
@@ -1423,7 +1465,8 @@
     wide = width // 2
     keyed = pair.shape[1]
     total = packed.shape[1] - width // 2
-    blocks = count // ROWS
+    rows = 2 * ROWS
+    blocks = count // rows
     few = wide // shards
     block_rows = width // shards
 
@@ -1441,8 +1484,8 @@
         greet(peers[1], peers[2])
         r.bias[...] = jnp.zeros_like(r.bias)
         r.pairs[...] = jnp.zeros_like(r.pairs)
-        one = block_sum(r, "one", r.gmixed_part, peers, own)
-        two = block_sum(r, "two", r.gvalue_part, peers, own)
+        one = block_sum(r, "one", r.gmixed_part, peers, own, rows=rows)
+        two = block_sum(r, "two", r.gvalue_part, peers, own, rows=rows)
 
         def compute(block):
             @pl.when(block == 0)
@@ -1453,13 +1496,13 @@
             r.wait_block(block)
             attention_backward_block(
                 real,
-                block * ROWS,
+                block * rows,
                 mine,
-                *views((r.gout, r.gupdate, r.shared, r.reset, r.value, r.att, r.probs), block),
+                *views((r.gout, r.gupdate, r.shared, r.reset, r.value, r.att, r.probs), block, rows),
                 r.in_w,
                 r.pair,
                 r.offset,
-                *views((r.gmixed_part, r.gvalue_part, r.gbase, r.gvalue), block),
+                *views((r.gmixed_part, r.gvalue_part, r.gbase, r.gvalue), block, rows),
                 r.bias,
                 r.pairs,
                 r.out_w,
@@ -1472,8 +1515,8 @@
 
                 return strip
 
-            finish_strips(one, block, keep(r.gmixed))
-            finish_strips(two, block, keep(r.gnormed))
+            finish_strips(one, block, keep(r.gmixed), rows)
+            finish_strips(two, block, keep(r.gnormed), rows)
 
         def value_grad(rows, value):
             r.grad[rows, :wide] = value
@@ -1493,8 +1536,8 @@
         def small_grads():
             last = total + width // 2
             r.grad[:, last:] = jnp.zeros((width, LANES), BF16)
-            rows = [r.bias[0:1, i * LANES : (i + 1) * LANES] for i in range(total // LANES)]
-            block = jnp.concatenate(rows + [r.pairs[0:3, :]], axis=0).astype(BF16)
+            pieces = [r.bias[0:1, i * LANES : (i + 1) * LANES] for i in range(total // LANES)]
+            block = jnp.concatenate(pieces + [r.pairs[0:3, :]], axis=0).astype(BF16)
             for shard in range(shards):
                 r.grad[shard * block_rows : shard * block_rows + SMALL, last:] = block
 
@@ -1512,7 +1555,7 @@
                 grad_tiles(r.gated, r.gout, out_grad, 0, wide // TILE)
                 r.store("grad")
 
-        pipeline(count, compute, (one, two), finish, None, extra, between)
+        pipeline(count, compute, (one, two), finish, None, extra, between, rows=rows)
 
     return transfer(
         work,
@@ -1547,13 +1590,14 @@
             in_w=pltpu.VMEM((width, total), BF16),
             out_w=pltpu.VMEM((wide, width), BF16),
             fold=pltpu.SemaphoreType.DMA((2 * shards + 1,)),
-            **sum_scratch("one", count, own),
-            **sum_scratch("two", count, own),
+            **sum_scratch("one", count, own, rows),
+            **sum_scratch("two", count, own, rows),
         ),
         ident,
         40,
         after,
         first,
+        rows,
     )
 
 
@@ -1756,7 +1800,9 @@
     lax.fori_loop(0, rows // SMALL, strip, 0)
 
 
-def attention_outputs(shards, part, value_ref, base_ref, out_ref, small_ref):
+def attention_outputs(shards, layer, part, extras, outs):
+    value_ref, base_ref, out_ref, value_bias_ref, base_bias_ref, pair_ref, query_ref = outs[:7]
+    norm_outs, average_outs = outs[7:10], outs[10:]
     sections = part.shape[0]
     width = out_ref.shape[2]
     wide = value_ref.shape[2] // sections
@@ -1788,10 +1834,62 @@
             out_ref[0, k * few : (k + 1) * few, columns] = part[
                 k, half * few : (half + 1) * few, total : total + width // 2
             ].astype(F32)
-        small_ref[0, k] = part[k, :SMALL, total + width // 2 :].astype(F32)
-
-
-def feed_outputs(shards, feed, in_ref, out_ref, small_ref):
+    slot = lax.axis_index("dp")
+    row = slice(layer, layer + 1)
+    blocks = [part[k, :SMALL, total + width // 2 :].astype(F32) for k in range(sections)]
+    lines = [
+        jnp.concatenate([b[i : i + 1] for i in range(total // LANES)], axis=1) for b in blocks
+    ]
+    summed = sum(blocks[1:], blocks[0])
+
+    def mine(line):
+        size = line.shape[1] // shards
+        return chosen([line[:, d * size : (d + 1) * size] for d in range(shards)], slot)
+
+    value_bias_ref[row, :] = jnp.concatenate([mine(line[:, :wide]) for line in lines], axis=1)
+    low = edge + keyed
+    base_line = jnp.concatenate(
+        [line[:, wide:edge] for line in lines]
+        + [sum((line[:, edge:low] for line in lines[1:]), lines[0][:, edge:low])]
+        + [
+            line[:, low + d * few : low + (d + 1) * few]
+            for d in range(shards)
+            for line in lines
+        ]
+        + [line[:, low + wide :] for line in lines],
+        axis=1,
+    )
+    base_bias_ref[row, :] = mine(base_line)
+    first = total // LANES
+    for k in range(2):
+        pair_ref[layer, k : k + 1, :] = mine(summed[first + k : first + k + 1])
+    query_ref[row, :] = mine(summed[first + 2 : first + 3])
+
+    channels_ref, decay_ref, input_ref, output_ref = extras
+    dims, size = decay_ref.shape[1:]
+    holders = own // size
+    low = layer * (2 * dims + 8)
+
+    def channels(start, count):
+        here = slice(low + start, low + start + count)
+        pieces = [channels_ref[here, k * size : (k + 1) * size] for k in range(holders)]
+        return chosen(pieces, slot % holders)
+
+    sums = channels(2 * dims, 8)
+    for k, ref in enumerate(norm_outs):
+        ref[row, :] = sums[k : k + 1]
+    of_states, of_slopes = channels(0, dims), channels(dims, dims)
+    rate = sigmoid(decay_ref[layer])
+    drive = (1.0 - rate) * input_ref[layer]
+    gdrive = output_ref[layer] * of_states
+    grate = drive * output_ref[layer] * of_slopes - input_ref[layer] * gdrive
+    average_outs[0][layer] = grate * rate * (1.0 - rate)
+    average_outs[1][layer] = (1.0 - rate) * gdrive
+    average_outs[2][layer] = drive * of_states
+
+
+def feed_outputs(shards, layer, feed, extras, outs):
+    in_ref, out_ref, gain_ref, shift_ref, out_bias_ref, in_bias_ref = outs
     sections, rows = feed.shape[:2]
     width = out_ref.shape[2]
     hidden = in_ref.shape[2] // sections
@@ -1802,35 +1900,48 @@
     by_strips(rows, strip)
     for k in range(sections):
         out_ref[0, k * rows : (k + 1) * rows, :] = feed[k, :, hidden : hidden + width].astype(F32)
-        small_ref[0, k] = feed[k, :SMALL, hidden + width :].astype(F32)
-
-
-def assemble_kernel(work, shards, layers, *refs):
+    size = width // shards
+    row = slice(layer, layer + 1)
+    blocks = [feed[k, :SMALL, hidden + width :].astype(F32)[:, :size] for k in range(sections)]
+    summed = sum(blocks[1:], blocks[0])
+    gain_ref[row, :] = summed[0:1]
+    shift_ref[row, :] = summed[1:2]
+    out_bias_ref[row, :] = blocks[0][2:3]
+    in_bias_ref[row, :] = jnp.concatenate([b[3:4] for b in blocks], axis=1)
+
+
+def assemble_kernel(work, shards, layers, more, *refs):
+    extras, outs = refs[layers : layers + more], refs[layers + more :]
     for layer in range(layers):
 
         @pl.when(pl.program_id(0) == layer)
         def _():
-            work(shards, refs[layer], *refs[layers:])
-
-
-def assemble(work, gathered, dims, shards):
+            work(shards, layer, refs[layer], extras, outs)
+
+
+def assemble(work, gathered, extras, dims, small_dims, shards):
     layers = len(gathered)
-    dims = dims + ((gathered[0].shape[0], SMALL, LANES),)
+
+    def whole(dims):
+        return pl.BlockSpec(dims, lambda i, n=len(dims): (0,) * n)
+
     return pl.pallas_call(
-        functools.partial(assemble_kernel, work, shards, layers),
+        functools.partial(assemble_kernel, work, shards, layers, len(extras)),
         grid=(layers,),
-        out_shape=tuple(shape((layers,) + d, F32) for d in dims),
-        in_specs=[pl.BlockSpec(a.shape, lambda i: (0, 0, 0)) for a in gathered],
+        out_shape=tuple(shape((layers,) + d, F32) for d in dims + small_dims),
+        in_specs=[whole(a.shape) for a in gathered + extras],
         out_specs=tuple(
             pl.BlockSpec((1,) + d, lambda i, n=len(d): (i,) + (0,) * n) for d in dims
-        ),
+        )
+        + tuple(whole((layers,) + d) for d in small_dims),
         cost_estimate=lasting(6),
         compiler_params=params(),
-    )(*gathered)
-
-
-def chosen(pieces):
-    section = lax.axis_index("section")
+    )(*gathered, *extras)
+
+
+def chosen(pieces, section=None):
+    if section is None:
+        section = lax.axis_index("section")
     result = pieces[0]
     for k in range(1, len(pieces)):
         result = jnp.where(section == k, pieces[k], result)
@@ -1897,17 +2008,22 @@
     packed_ref[:, hidden:] = out_ref[0, pl.ds(start, size), :]
 
 
-def pack(kernel, layer, columns, shards, sections, *arrays):
+def pack(work, layer, columns, shards, sections, arrays, after=()):
     rows = arrays[0].shape[1]
+
+    def kernel(*refs):
+        work(shards, sections, *refs[len(after) :])
+
     return pl.pallas_call(
-        functools.partial(kernel, shards, sections),
+        kernel,
         grid=(1,),
         out_shape=shape((rows, columns), BF16),
-        in_specs=[pl.BlockSpec((1,) + a.shape[1:], lambda i: (layer, 0, 0)) for a in arrays],
+        in_specs=[hbm()] * len(after)
+        + [pl.BlockSpec((1,) + a.shape[1:], lambda i: (layer, 0, 0)) for a in arrays],
         out_specs=pl.BlockSpec((rows, columns), lambda i: (0, 0)),
         cost_estimate=lasting(3),
         compiler_params=params(),
-    )(*arrays)
+    )(*after, *arrays)
 
 
 def unpack_kernel(layers, shards, sections, places, everyone_ref, *refs):
@@ -2094,28 +2210,18 @@
     def over_dp(array):
         return lax.all_gather(array, "dp", axis=0, tiled=True)
 
-    weights = []
-    for layer in range(layers):
-        attention = pack(
-            pack_attention_kernel,
-            layer,
-            total + width // 2,
-            shards,
-            sections,
-            value_weight,
-            base_weight,
-            out_weight,
-        )
-        feed = pack(
-            pack_feed_kernel,
-            layer,
-            hidden // sections + width,
-            shards,
-            sections,
-            feed_in_weight,
-            feed_out_weight,
-        )
-        weights.append((over_dp(attention), over_dp(feed)))
+    def attention_weights(layer, after=()):
+        arrays = (value_weight, base_weight, out_weight)
+        columns = total + width // 2
+        return pack(pack_attention_kernel, layer, columns, shards, sections, arrays, after)
+
+    def feed_weights(layer, after=()):
+        arrays = (feed_in_weight, feed_out_weight)
+        columns = hidden // sections + width
+        return pack(pack_feed_kernel, layer, columns, shards, sections, arrays, after)
+
+    weights = [[None, None] for _ in range(layers)]
+    weights[0][0] = over_dp(attention_weights(0))
 
     smalls = dict(
         norm_gain=norm_gain,
@@ -2151,16 +2257,19 @@
     x0 = x = tokens[0]
     kept = []
     for layer in range(layers):
-        attention_w, feed_w = weights[layer]
         p = small[layer]
         normed, mixed_own, pre, own_n, scale = average_forward(
             lengths, x, p.gain, p.shift, p.rate, p.coef, p.skip
         )
-        middle, hidden_pre, mixed, update, shared, reset, value, att, gated, probs = attention_forward(
+        if not layer:
+            packed_feed = feed_weights(0, (mixed_own,))
+            weights[0][1] = over_dp(packed_feed)
+            mixed = mixed_own = gather_columns(mixed_own, next(idents), (packed_feed,))
+        middle, hidden_pre, *mixed_out, update, shared, reset, value, att, gated, probs = attention_forward(
             lengths,
             normed,
             mixed_own,
-            attention_w,
+            weights[layer][0],
             p.bias,
             p.pair,
             p.offset,
@@ -2168,6 +2277,14 @@
             shards,
             next(idents),
         )
+        if layer:
+            (mixed,) = mixed_out
+        if layer + 1 < layers:
+            weights[layer + 1] = [
+                over_dp(attention_weights(layer + 1, (hidden_pre,))),
+                over_dp(feed_weights(layer + 1, (hidden_pre,))),
+            ]
+        attention_w, feed_w = weights[layer]
         feed_saved = [None] * 4
         x_next = None
         if layer + 1 < layers:
@@ -2203,12 +2320,11 @@
     feed_grads = [None] * layers
     attention_grads = [None] * layers
     channel_sums = [None] * layers
-    gathered = [None] * layers
     for layer in reversed(range(layers)):
         attention_w, feed_w = weights[layer]
         k, p = kept[layer], small[layer]
         gout, gupdate, resid, feed_grad, *last = feed_backward(
-            given, k, p, feed_w, shards, next(idents)
+            given, k, p, feed_w, shards, next(idents), () if layer else (feed_grads[1],)
         )
         if last:
             block_out = last[0]
@@ -2226,7 +2342,7 @@
             () if layer else (attention_grads[1],),
         )
         attention_grads[layer] = scattered(attention_grad)
-        z, zstats, channel_sums[layer], gathered[layer] = average_backward(
+        z, zstats, channel_sums[layer], *attention_one = average_backward(
             lengths,
             gmixed,
             gnormed,
@@ -2236,15 +2352,15 @@
             p.rate,
             p.coef,
             p.skip,
-            feed_grads[1] if layer else attention_grads[1],
-            next(idents),
+            None if layer else attention_grads[1],
+            None if layer else next(idents),
         )
         if layer:
             given = (z, zstats, k.x)
 
-    attention_one, feed_one = gathered
-    input_grad, feed_zero = final_exchange(
-        z, zstats, x0, [feed_grads[0]], sections, next(idents)
+    (attention_one,) = attention_one
+    input_grad, feed_one, feed_zero = final_exchange(
+        z, zstats, x0, [feed_grads[1], feed_grads[0]], sections, next(idents)
     )
     channels, attention_zero = gather_sums(
         jnp.concatenate(channel_sums, axis=0),
@@ -2254,61 +2370,28 @@
         own * shards // width,
         next(idents),
     )
-    shard = lax.axis_index("dp")
     size = width // shards
-    rows = channels.shape[0]
-    channels = lax.dynamic_slice_in_dim(channels, shard * size % own, size, axis=1)
-    channels = channels.reshape(layers, rows // layers, size)
-    g_feed_in, g_feed_out, feed_smalls = assemble(
+    dims = average_decay.shape[1]
+    g_feed_in, g_feed_out, g_feed_gain, g_feed_shift, g_feed_out_bias, g_feed_in_bias = assemble(
         feed_outputs,
         (feed_zero, feed_one),
+        (),
         ((size, hidden), (hidden // shards, width)),
+        ((size,), (size,), (size,), (hidden // shards,)),
         shards,
     )
-    g_value, g_base, g_out, smalls_out = assemble(
+    base = base_weight.shape[2]
+    g_value, g_base, g_out, g_value_bias, g_base_bias, g_pair, g_query, *rest = assemble(
         attention_outputs,
         (attention_zero, attention_one),
-        ((size, wide), (size, base_weight.shape[2]), (wide // shards, width)),
+        (channels, average_decay, average_input, average_output),
+        ((size, wide), (size, base), (wide // shards, width)),
+        ((wide // shards,), (base // shards,), (2, keyed // shards), (keyed // shards,))
+        + ((size,),) * 3
+        + ((dims, size),) * 3,
         shards,
     )
-
-    def of_shard(array):
-        part = array.shape[-1] // shards
-        return lax.dynamic_slice_in_dim(array, shard * part, part, axis=array.ndim - 1)
-
-    def woven(array):
-        split = array.reshape(layers, sections, shards, -1)
-        return split.transpose(0, 2, 1, 3).reshape(layers, -1)
-
-    of_states, of_slopes, sums = channels[:, :dims], channels[:, dims : 2 * dims], channels[:, 2 * dims :]
-    rate = jax.nn.sigmoid(average_decay)
-    gdrive = average_output * of_states
-    drive = (1.0 - rate) * average_input
-    grate = drive * average_output * of_slopes - average_input * gdrive
-    g_gain, g_shift, g_skip = sums[:, 0], sums[:, 1], sums[:, 2]
-    g_decay, g_input, g_output = grate * rate * (1.0 - rate), (1.0 - rate) * gdrive, drive * of_states
-
-    edge = share + own
-    bias_rows = total // LANES
-    bias = smalls_out[:, :, :bias_rows].reshape(layers, sections, total)
-    pairs = of_shard(jnp.sum(smalls_out[:, :, bias_rows : bias_rows + 3], axis=1))
-    g_pair, g_query = pairs[:, :2], pairs[:, 2]
-    g_value_bias = of_shard(woven(bias[..., :share]))
-    g_base_bias = of_shard(
-        jnp.concatenate(
-            (
-                bias[..., share:edge].reshape(layers, -1),
-                jnp.sum(bias[..., edge : edge + keyed], axis=1),
-                woven(bias[..., edge + keyed : edge + keyed + share]),
-                bias[..., edge + keyed + share :].reshape(layers, -1),
-            ),
-            axis=1,
-        )
-    )
-    g_feed_gain = jnp.sum(feed_smalls[:, :, 0, :size], axis=1)
-    g_feed_shift = jnp.sum(feed_smalls[:, :, 1, :size], axis=1)
-    g_feed_out_bias = feed_smalls[:, 0, 2, :size]
-    g_feed_in_bias = feed_smalls[:, :, 3, :size].reshape(layers, -1)
+    g_gain, g_shift, g_skip, g_decay, g_input, g_output = rest
     return (
         block_out[None],
         input_grad[None],

time: 610 us -> 591 us (0.969)
  waiting for transfers between devices: 18.2 us -> 0.24 us
    pallas_call x9, Pallas kernels: 426 us -> 394 us  [transfer(): pl.pallas_call(kernel, out_shape=tuple((o for o, _ in outs.values())), in...]
    pallas_call x6 -> x7, Pallas kernels: 27.2 us -> 51.7 us  [the longest x1 23.8 us: gather_columns(): pl.pallas_call(functools.partial(gather_kernel, len(after)), out_shape=sh...]
    pallas_call x1, Pallas kernels: 29.9 us -> 43.5 us  [final_exchange(): pl.pallas_call(functools.partial(final_kernel, number), out_shape=(shape(...]
    all_gather x4, waiting for transfers between devices: 10.7 us -> 0.06 us  [over_dp(): return lax.all_gather(array, 'dp', axis=0, tiled=True)]
    reduce_scatter x4, waiting for transfers between devices: 7.29 us -> 0.04 us  [scattered(): return lax.psum_scatter(grad, 'dp', scatter_dimension=0, tiled=True)]
  transfers between devices with their start and end apart: 8 -> 8, of which waited for: 3 -> 0; matrix products, arithmetic and copies ran while one was open for 1% -> 0% of each run, Pallas kernels for 72% -> 75%
where the time goes in v4:
time: 591 us; the launch traced here: 586 us
  Pallas kernels  547 us (93%)
  blocking collectives  18.6 us (3%)
  between operations  15.7 us (3%)
    pallas_call x9, Pallas kernels, transfer(): pl.pallas_call(kernel, out_shape=tuple((o for o, _ in outs.values())), in...  394 us
    pallas_call x1, Pallas kernels, final_exchange(): pl.pallas_call(functools.partial(final_kernel, number), out_shape=(shape(...  43.5 us
    pallas_call x1, Pallas kernels, gather_sums(): pl.pallas_call(functools.partial(sums_kernel, shards, holders), out_shape...  31.1 us
    pallas_call x2, Pallas kernels, average_forward(): pl.pallas_call(average_forward_kernel, out_shape=(shape((count, width), B...  23.8 us
    pallas_call x1, Pallas kernels, gather_columns(): pl.pallas_call(functools.partial(gather_kernel, len(after)), out_shape=sh...  23.8 us
    all_gather x1, blocking collectives, body(): lax.all_gather(packed, 'dp', axis=0)  18.6 us
    pallas_call x4, Pallas kernels, pack(): pl.pallas_call(kernel, grid=(1,), out_shape=shape((rows, columns), BF16),...  14.5 us
    pallas_call x2, Pallas kernels, assemble(): pl.pallas_call(functools.partial(assemble_kernel, work, shards, layers, l...  13.4 us
  transfers between devices with their start and end apart: 8, of which 0 were waited for; matrix products, arithmetic and copies ran while one was open for 0% of the time, Pallas kernels for 75%

profile of v4, /device:TPU:0, one launch (start us, length us, event | category | flops | bytes accessed | tf_op | source)
XLA Modules:
  0.0 585.7 jit_solution(16168231913208544222)
XLA Ops:
  7.3 0.0 all-gather.7.cloned.1.call-start
  7.4 4.7 shard_map.373
  12.1 0.0 all-gather.7.cloned.1.call-update
  12.1 0.0 all-gather.13.cloned.1.call-start
  12.8 0.1 reshape.57
  13.1 0.1 concatenate.6
  13.2 18.6 %all-gather.1.everyone_ref = f32[8,2,8256]{2,1,0:T(2,128)} all-gather(f32[1,2,8256]{2,1,0:T(2,128)S(1)} %bitcast.17), channel_id=2, replica_groups=mesh['section'=4,'dp'=8] {'dp'}, dimensions={0}, use_global_device_ids=true | all-gather | bytes 594432 | tf_op jit(solution)/shard_map/all_gather | solution.py:2250
  31.8 2.7 shard_map.374
  34.5 11.9 %shard_map.375 = (bf16[1024,1024]{1,0:T(8,128)(2,1)}, bf16[1024,256]{1,0:T(8,128)(2,1)}, bf16[1024,256]{1,0:T(8,128)(2,1)}, f32[1024,256]{1,0:T(8,128)}, f32[1024,128]{1,0:T(8,128)}) custom-call(s32[1]{0:T(128)S(6)} %copy.52.length_ref.refs_0_.refs_1_, bf16[1024,1024]{1,0:T(8,128)(2,1)} %bitcast.23, f32[1,1024]{1,0:T(1,128)} %get-tuple-element.127.gain_ref, ...), custom_call_target="tpu_custom_call" | custom-call | flops 12999999488 | bytes 39000000 | tf_op jit(solution)/shard_map/pallas_call | solution.py:208
  46.5 2.6 shard_map.376.refs_0_
  49.0 0.0 all-gather.13.cloned.1.call-update
  49.0 0.0 all-gather.11.cloned.1.call-start
  49.1 23.8 %shard_map.377.refs_3_.refs_11_ = bf16[1024,1024]{1,0:T(8,128)(2,1)} custom-call(bf16[128,2048]{1,0:T(8,128)(2,1)} %shard_map.376.refs_0_, bf16[1024,256]{1,0:T(8,128)(2,1)} %get-tuple-element.133.refs_0_.refs_1_), custom_call_target="tpu_custom_call" | custom-call | flops 20000000000 | bytes 60000000 | tf_op jit(solution)/shard_map/pallas_call | solution.py:1110
  72.9 0.0 all-gather.7.cloned.1.call-done.refs_1_.refs_2_
  72.9 44.6 %shard_map.378 = (bf16[1024,1024]{1,0:T(8,128)(2,1)}, bf16[1024,256]{1,0:T(8,128)(2,1)}, bf16[1024,256]{1,0:T(8,128)(2,1)}, bf16[1024,128]{1,0:T(8,128)(2,1)}, b...) custom-call(s32[1]{0:T(128)S(6)} %copy.52.length_ref.refs_0_.refs_1_, ...), custom_call_target="tpu_custom_call" | custom-call | flops 54000001024 | bytes 162000000 | tf_op jit(solution)/shard_map/pallas_call | solution.py:757
  117.6 4.7 shard_map.380
  122.3 0.0 all-gather.11.cloned.1.call-update
  122.3 0.0 all-gather.9.cloned.1.call-start
  122.4 2.5 shard_map.379
  124.9 0.0 all-gather.9.cloned.1.call-update
  124.9 0.2 reduce-scatter.7.cloned.1.call-start
  125.1 0.0 all-gather.13.cloned.1.call-done.refs_1_
  125.2 42.4 %shard_map.381 = (bf16[1024,1024]{1,0:T(8,128)(2,1)}, bf16[1024,1024]{1,0:T(8,128)(2,1)}, bf16[1024,1024]{1,0:T(8,128)(2,1)}, bf16[1024,1024]{1,0:T(8,128)(2,1)}, f32[1024,128]{1,0:T(8,128)}) custom-call(bf16[1024,1024]{1,0:T(8,128)(2,1)} %get-tuple-element.138.refs_0_, bf16[1024,2048]{1,0:T(8,128)(2,1)} %all-gather.13.cloned.1.call-done.refs_1_, ...), custom_call_target="tpu_custom_call" | custom-call | flops 40000000000 | bytes 120000000 | tf_op jit(solution)/shard_map/pallas_call | solution.py:757
  167.5 11.9 %shard_map.382 = (bf16[1024,1024]{1,0:T(8,128)(2,1)}, bf16[1024,256]{1,0:T(8,128)(2,1)}, bf16[1024,256]{1,0:T(8,128)(2,1)}, f32[1024,256]{1,0:T(8,128)}, f32[1024,128]{1,0:T(8,128)}) custom-call(s32[1]{0:T(128)S(6)} %copy.52.length_ref.refs_0_.refs_1_, bf16[1024,1024]{1,0:T(8,128)(2,1)} %get-tuple-element.143.x_ref.refs_4_.refs_8_.refs_3_, ...), custom_call_target="tpu_custom_call" | custom-call | flops 12999999488 | bytes 39000000 | tf_op jit(solution)/shard_map/pallas_call | solution.py:208
  179.5 57.0 %shard_map.383 = (bf16[1024,1024]{1,0:T(8,128)(2,1)}, bf16[1024,256]{1,0:T(8,128)(2,1)}, bf16[1024,1024]{1,0:T(8,128)(2,1)}, bf16[1024,256]{1,0:T(8,128)(2,1)}, ...) custom-call(s32[1]{0:T(128)S(6)} %copy.52.length_ref.refs_0_.refs_1_, ...), custom_call_target="tpu_custom_call" | custom-call | flops 54000001024 | bytes 162000000 | tf_op jit(solution)/shard_map/pallas_call | solution.py:757
  236.5 0.0 all-gather.9.cloned.1.call-done.refs_0_
  236.5 62.5 %shard_map.384 = (bf16[1024,1024]{1,0:T(8,128)(2,1)}, bf16[1024,256]{1,0:T(8,128)(2,1)}, f32[1024,256]{1,0:T(8,128)}, bf16[1024,2176]{1,0:T(8,128)(2,1)}, bf16[256,1024]{1,0:T(8,128)(2,1)}) custom-call(bf16[1024,2048]{1,0:T(8,128)(2,1)} %all-gather.9.cloned.1.call-done.refs_0_, bf16[1024,1024]{1,0:T(8,128)(2,1)} %bitcast.22, ...), custom_call_target="tpu_custom_call" | custom-call | flops 46000001024 | bytes 138000000 | tf_op jit(solution)/shard_map/pallas_call | solution.py:757
  299.0 0.0 reduce-scatter.7.cloned.1.call-update
  299.0 0.3 reduce-scatter.5.cloned.1.call-start
  299.3 44.5 %shard_map.385 = (f32[1024,256]{1,0:T(8,128)}, f32[1024,256]{1,0:T(8,128)}, bf16[1024,2304]{1,0:T(8,128)(2,1)}) custom-call(s32[1]{0:T(128)S(6)} %copy.52.length_ref.refs_0_.refs_1_, bf16[1024,2176]{1,0:T(8,128)(2,1)} %all-gather.11.cloned.1.call-done.refs_1_, bf16[1024,1024]{1,0:T(8,128)(2,1)} %get-tuple-element.163.refs_2_, ...), custom_call_target="tpu_custom_call" | custom-call | flops 40000000000 | bytes 120000000 | tf_op jit(solution)/shard_map/pallas_call | solution.py:757
  343.7 0.0 reduce-scatter.5.cloned.1.call-update
  343.8 0.0 reduce-scatter.9.cloned.1.call-start
  343.8 15.9 %shard_map.386 = (bf16[1024,256]{1,0:T(8,128)(2,1)}, f32[8,1024]{1,0:T(8,128)}, f32[40,256]{1,0:T(8,128)}) custom-call(s32[1]{0:T(128)S(6)} %copy.52.length_ref.refs_0_.refs_1_, f32[1024,256]{1,0:T(8,128)} %get-tuple-element.174.refs_1_, f32[1024,256]{1,0:T(8,128)} %get-tuple-element.175.refs_2_, bf16[1024,256]{1,0:T(8,128)(2,1)} %get-tuple-element.176.refs_3_, ...), custom_call_target="tpu_custom_call" | custom-call | flops 16999999488 | bytes 51000000 | tf_op jit(solution)/shard_map/pallas_call | solution.py:757
  359.7 0.0 reduce-scatter.7.cloned.1.call-done.refs_0_
  359.7 65.3 %shard_map.387 = (bf16[1024,1024]{1,0:T(8,128)(2,1)}, bf16[1024,256]{1,0:T(8,128)(2,1)}, f32[1024,256]{1,0:T(8,128)}, bf16[1024,2176]{1,0:T(8,128)(2,1)}) custom-call(bf16[128,2176]{1,0:T(8,128)(2,1)} %reduce-scatter.7.cloned.1.call-done.refs_0_, bf16[1024,2048]{1,0:T(8,128)(2,1)} %all-gather.13.cloned.1.call-done.refs_1_, ...), custom_call_target="tpu_custom_call" | custom-call | flops 46000001024 | bytes 138000000 | tf_op jit(solution)/shard_map/pallas_call | solution.py:757
  425.1 0.0 reduce-scatter.9.cloned.1.call-update
  425.1 0.3 reduce-scatter.11.cloned.1.call-start
  425.4 0.0 reduce-scatter.5.cloned.1.call-done.refs_0_.refs_11_
  425.4 40.5 %shard_map.388 = (f32[1024,256]{1,0:T(8,128)}, f32[1024,256]{1,0:T(8,128)}, bf16[1024,2304]{1,0:T(8,128)(2,1)}) custom-call(bf16[128,2304]{1,0:T(8,128)(2,1)} %reduce-scatter.5.cloned.1.call-done.refs_0_.refs_11_, s32[1]{0:T(128)S(6)} %copy.52.length_ref.refs_0_.refs_1_, bf16[1024,2176]{1,0:T(8,128)(2,1)} %all-gather.7.cloned.1.call-done.refs_1_.refs_2_, ...), custom_call_target="tpu_custom_call" | custom-call | flops 40000000000 | bytes 120000000 | tf_op jit(solution)/shard_map/pallas_call | solution.py:757
  466.0 0.0 reduce-scatter.11.cloned.1.call-update
  466.0 21.3 %shard_map.389 = (bf16[1024,256]{1,0:T(8,128)(2,1)}, f32[8,1024]{1,0:T(8,128)}, f32[40,256]{1,0:T(8,128)}, bf16[4,128,2304]{2,1,0:T(8,128)(2,1)}) custom-call(s32[1]{0:T(128)S(6)} %copy.52.length_ref.refs_0_.refs_1_, f32[1024,256]{1,0:T(8,128)} %get-tuple-element.196.refs_1_, f32[1024,256]{1,0:T(8,128)} %get-tuple-element.197.refs_2_, ...), custom_call_target="tpu_custom_call" | custom-call | flops 16999999488 | bytes 51000000 | tf_op jit(solution)/shard_map/pallas_call | solution.py:757
  487.3 1.4 pad_maximum_fusion.sums_ref
  488.7 43.5 %shard_map.390 = (bf16[256,1024]{1,0:T(8,128)(2,1)}, bf16[4,128,2176]{2,1,0:T(8,128)(2,1)}, bf16[4,128,2176]{2,1,0:T(8,128)(2,1)}) custom-call(bf16[1024,256]{1,0:T(8,128)(2,1)} %get-tuple-element.202.z_ref, f32[8,1024]{1,0:T(8,128)} %get-tuple-element.203.stats_ref, bf16[1024,1024]{1,0:T(8,128)(2,1)} %bitcast.26, ...), custom_call_target="tpu_custom_call" | custom-call | flops 49999998976 | bytes 150000000 | tf_op jit(solution)/shard_map/pallas_call | solution.py:1666
  532.3 6.0 %shard_map.393 = (f32[2,128,4096]{2,1,0:T(8,128)}, f32[2,512,1024]{2,1,0:T(8,128)}, f32[2,128]{1,0:T(2,128)}, f32[2,128]{1,0:T(2,128)}, f32[2,128]{1,0:T(2,128)}, /*index=5*/f32[2,512]{1,0:T(2,128)}) custom-call(bf16[4,128,2176]{2,1,0:T(8,128)(2,1)} %get-tuple-element.225.refs_0_, bf16[4,128,2176]{2,1,0:T(8,128)(2,1)} %get-tuple-element.226.refs_1_), custom_call_target="tpu_custom_call" | custom-call | flops 6000000000 | bytes 18000000 | tf_op jit(solution)/shard_map/pallas_call | solution.py:1928
  538.3 31.1 %shard_map.391 = (f32[80,256]{1,0:T(8,128)}, bf16[4,128,2304]{2,1,0:T(8,128)(2,1)}) custom-call(f32[80,256]{1,0:T(8,128)} %pad_maximum_fusion.sums_ref, bf16[128,2304]{1,0:T(8,128)(2,1)} %reduce-scatter.11.cloned.1.call-done.block_ref), custom_call_target="tpu_custom_call" | custom-call | flops 24999999488 | bytes 75000000 | tf_op jit(solution)/shard_map/pallas_call | solution.py:1763
  569.4 7.4 %shard_map.392 = (f32[2,128,2048]{2,1,0:T(8,128)}, f32[2,128,4224]{2,1,0:T(8,128)}, f32[2,256,1024]{2,1,0:T(8,128)}, f32[2,256]{1,0:T(2,128)}, f32[2,528]{1,0:T(...) custom-call(bf16[4,128,2304]{2,1,0:T(8,128)(2,1)} %get-tuple-element, ...), custom_call_target="tpu_custom_call" | custom-call | flops 6000000000 | bytes 18000000 | tf_op jit(solution)/shard_map/pallas_call | solution.py:1928
  576.8 0.8 copy.53
  577.6 0.8 copy.54
  (39 shorter events, 0.1 us)
Async XLA Ops:
  7.2 5.6 copy-start.9
  7.2 5.7 copy-start.3
  7.2 5.7 copy-start.5
  7.2 5.7 copy-start.4
  7.2 5.7 copy-start.15
  7.3 5.7 copy-start.7
  7.3 5.7 copy-start.14
  7.3 5.7 copy-start.13
  7.3 5.7 copy-start.16
  7.3 5.7 copy-start.6
  7.3 5.7 copy-start.8
  7.3 5.7 copy-start.12
  7.3 5.7 copy-start.11
  7.3 5.7 copy-start.10
  7.3 65.6 %all-gather.7.cloned.1.call-start = ((), (), s32[]{:S(2)}) async-start(), calls=%async_computation.4 | async-start | bytes 5013504 | tf_op jit(solution)/shard_map/all_gather | solution.py:2211
  12.1 113.0 %all-gather.13.cloned.1.call-start = ((), (), s32[]{:S(2)}) async-start(), calls=%async_computation.7 | async-start | bytes 4718592 | tf_op jit(solution)/shard_map/all_gather | solution.py:2211
  49.0 130.4 %all-gather.11.cloned.1.call-start = ((), (), s32[]{:S(2)}) async-start(), calls=%async_computation.6 | async-start | bytes 5013504 | tf_op jit(solution)/shard_map/all_gather | solution.py:2211
  122.3 114.2 %all-gather.9.cloned.1.call-start = ((), (), s32[]{:S(2)}) async-start(), calls=%async_computation.5 | async-start | bytes 4718592 | tf_op jit(solution)/shard_map/all_gather | solution.py:2211
  124.9 234.8 %reduce-scatter.7.cloned.1.call-start = ((), (), s32[]{:S(2)}) async-start(), calls=%async_computation.9 | async-start | bytes 5013504 | tf_op jit(solution)/shard_map/reduce_scatter | solution.py:2317
  299.0 126.4 %reduce-scatter.5.cloned.1.call-start = ((), (), s32[]{:S(2)}) async-start(), calls=%async_computation.8 | async-start | bytes 5308416 | tf_op jit(solution)/shard_map/reduce_scatter | solution.py:2317
  343.8 145.0 %reduce-scatter.9.cloned.1.call-start = ((), (), s32[]{:S(2)}) async-start(), calls=%async_computation.10 | async-start | bytes 5013504 | tf_op jit(solution)/shard_map/reduce_scatter | solution.py:2317
  425.1 113.2 %reduce-scatter.11.cloned.1.call-start = ((), (), s32[]{:S(2)}) async-start(), calls=%async_computation.11 | async-start | bytes 5308416 | tf_op jit(solution)/shard_map/reduce_scatter | solution.py:2317
  466.0 21.3 %copy-start.2 = (f32[40,256]{1,0:T(8,128)S(1)}, f32[40,256]{1,0:T(8,128)}, u32[]{:S(2)}) copy-start(f32[40,256]{1,0:T(8,128)} %get-tuple-element.207) | copy-start | bytes 122884
  569.4 7.4 %copy-start = (bf16[256,1024]{1,0:T(8,128)(2,1)S(1)}, bf16[256,1024]{1,0:T(8,128)(2,1)}, u32[]{:S(2)}) copy-start(bf16[256,1024]{1,0:T(8,128)(2,1)} %get-tuple-element.162) | copy-start | bytes 1572868
  569.4 8.2 %copy-start.1 = (bf16[256,1024]{1,0:T(8,128)(2,1)S(1)}, bf16[256,1024]{1,0:T(8,128)(2,1)}, u32[]{:S(2)}) copy-start(bf16[256,1024]{1,0:T(8,128)(2,1)} %get-tuple-element.205) | copy-start | bytes 1572868
Sparse Core Ops, SparseCore 0:
  12.2 53.4 all-gather.6
  67.9 46.0 all-gather.12
  122.4 50.1 all-gather.10
  174.6 45.9 all-gather.8
  299.1 53.0 reduce-scatter.6
  354.4 53.1 reduce-scatter.4
  425.2 53.8 reduce-scatter.8
  481.4 53.1 reduce-scatter.10

commit v5 on v4

--- a/solution.py
+++ b/solution.py
@@ -233,7 +233,6 @@
     steps = count // CHUNKS
     pitch = steps + 1
     groups = own // LANES
-    part_size = dims // 2
     gain_ref, shift_ref = r.norm.at[0:1, :], r.norm.at[1:2, :]
     if beside:
         peers = plane()
@@ -257,6 +256,7 @@
         return carry
 
     lax.fori_loop(0, count // STRIP, load_strip, 0)
+    r.store("m_buf", "g_buf")
 
     passed = None
     for group in range(groups):
@@ -274,28 +274,8 @@
         ends, end_slopes = lax.fori_loop(0, steps, back_finals, (blank, blank), unroll=UNROLL)
         starts = entering(ends, rates, steps, reverse=True)
 
-        for half in range(2):
-            first = half * part_size
-            some = r.rate[first : first + part_size, :, lanes]
-            empty = jnp.zeros_like(some)
-
-            def sweep(t, carry):
-                states, slopes, of_states, of_slopes = carry
-                x = m_part[pl.ds(t, CHUNKS, stride=pitch), :]
-                g = g_part[pl.ds(t, CHUNKS, stride=pitch), :]
-                slopes = some * slopes + states
-                states = some * states + x
-                return states, slopes, of_states + g * states, of_slopes + g * slopes
-
-            states, slopes, of_states, of_slopes = lax.fori_loop(
-                0, steps, sweep, (empty,) * 4, unroll=UNROLL
-            )
-            back, back_slope = ends[first : first + part_size], end_slopes[first : first + part_size]
-            state, slope = entering_pair(states, slopes, some, steps)
-            of_states = of_states + state * (some * back)
-            of_slopes = of_slopes + slope * (some * back) + state * (back + some * back_slope)
-            r.sums[first : first + part_size, lanes] = jnp.sum(of_states, axis=1)
-            r.sums[dims + first : dims + first + part_size, lanes] = jnp.sum(of_slopes, axis=1)
+        r.back[0, :, :, lanes] = ends
+        r.back[1, :, :, lanes] = end_slopes
 
         def back_outputs(t, states):
             here = pl.ds(steps - 1 - t, CHUNKS, stride=pitch)
@@ -338,13 +318,46 @@
     of_gain, of_shift, of_skip = lax.fori_loop(
         0, count // LANES, finish, (blank_row, blank_row, blank_row)
     )
-    last = 2 * dims
-    r.sums[last : last + 1, :] = of_gain
-    r.sums[last + 1 : last + 2, :] = of_shift
-    r.sums[last + 2 : last + 3, :] = of_skip
-    r.sums[last + 3 : last + 8, :] = jnp.zeros((5, own), F32)
+    r.sums[0:1, :] = of_gain
+    r.sums[1:2, :] = of_shift
+    r.sums[2:3, :] = of_skip
+    r.sums[3:8, :] = jnp.zeros((5, own), F32)
     if beside:
         gather_finish(r.whole, piece, peers, sems, *begun, passed)
+
+
+def average_sums(m_ref, g_ref, rate_ref, back_ref, sums_ref, low):
+    dims, _, own = rate_ref.shape
+    pitch = m_ref.shape[1] // CHUNKS
+    steps = pitch - 1
+    part_size = dims // 2
+    for group in range(own // LANES):
+        lanes = slice(group * LANES, (group + 1) * LANES)
+        m_part, g_part = m_ref.at[group], g_ref.at[group]
+        for half in range(2):
+            some = slice(half * part_size, (half + 1) * part_size)
+            rates = rate_ref[some, :, lanes]
+            empty = jnp.zeros_like(rates)
+
+            def sweep(t, carry):
+                states, slopes, of_states, of_slopes = carry
+                x = m_part[pl.ds(t, CHUNKS, stride=pitch), :]
+                g = g_part[pl.ds(t, CHUNKS, stride=pitch), :]
+                slopes = rates * slopes + states
+                states = rates * states + x
+                return states, slopes, of_states + g * states, of_slopes + g * slopes
+
+            states, slopes, of_states, of_slopes = lax.fori_loop(
+                0, steps, sweep, (empty,) * 4, unroll=UNROLL
+            )
+            back, back_slope = back_ref[0, some, :, lanes], back_ref[1, some, :, lanes]
+            state, slope = entering_pair(states, slopes, rates, steps)
+            of_states = of_states + state * (rates * back)
+            of_slopes = of_slopes + slope * (rates * back) + state * (back + rates * back_slope)
+            first = low + half * part_size
+            sums_ref[first : first + part_size, lanes] = jnp.sum(of_states, axis=1)
+            first += dims
+            sums_ref[first : first + part_size, lanes] = jnp.sum(of_slopes, axis=1)
 
 
 def average_backward(
@@ -352,7 +365,7 @@
 ):
     count, own = gmixed.shape
     dims = rate.shape[0]
-    buffer = pltpu.VMEM((own // LANES, count + CHUNKS, LANES), F32)
+    held_dims = (own // LANES, count + CHUNKS, LANES)
     sems = pltpu.SemaphoreType.DMA((6,))
     given = dict(
         gmixed=gmixed,
@@ -378,10 +391,13 @@
         dict(
             z=(shape((count, own), BF16), VMEM),
             stats=(shape((CHUNKS, count), F32), VMEM),
-            sums=(shape((2 * dims + 8, own), F32), VMEM),
+            sums=(shape((8, own), F32), VMEM),
+            m_buf=(shape(held_dims, F32), STORE),
+            g_buf=(shape(held_dims, F32), STORE),
+            back=(shape((2, dims, CHUNKS, own), F32), VMEM),
             **outs,
         ),
-        dict(m_buf=buffer, g_buf=buffer, r_buf=buffer, **held),
+        dict(r_buf=pltpu.VMEM(held_dims, F32), **held),
         ident,
         17,
         after,
@@ -1609,12 +1625,14 @@
     return piece
 
 
-def final_kernel(number, z_ref, stats_ref, x_ref, *refs):
+def final_kernel(number, layers, z_ref, stats_ref, x_ref, *refs):
     blocks, refs = refs[:number], refs[number:]
-    out_ref, refs = refs[0], refs[1:]
+    average_ins, refs = refs[: 5 * layers], refs[5 * layers :]
+    (out_ref, sums_ref), refs = refs[:2], refs[2:]
     gathered, refs = refs[:number], refs[number:]
     land, x_own, got, stats_stage, total_buf, local_sem, send, recv = refs[:8]
-    block_sems = [refs[8 + 2 * i : 10 + 2 * i] for i in range(number)]
+    m_buf, g_buf, held_sems = refs[8:11]
+    block_sems = [refs[11 + 2 * i : 13 + 2 * i] for i in range(number)]
     count, own = z_ref.shape
     quarter, width = out_ref.shape
     peers = plane()
@@ -1626,6 +1644,23 @@
     mine = pl.ds(pl.multiple_of(me * own, LANES), own)
     fetch = pltpu.make_async_copy(x_ref.at[rows(me), :], x_own, local_sem)
     fetch.start()
+    held = []
+    for layer in range(layers):
+        for k, buffer in enumerate((m_buf, g_buf)):
+            source = average_ins[5 * layer + k]
+            sem = held_sems.at[2 * layer + k]
+            held.append(pltpu.make_async_copy(source, buffer.at[layer], sem))
+            held[-1].start()
+
+    def sums_of(layer):
+        rate, back, rest = average_ins[5 * layer + 2 : 5 * layer + 5]
+        dims = rate.shape[0]
+        low = layer * (2 * dims + 8)
+        held[2 * layer].wait()
+        held[2 * layer + 1].wait()
+        average_sums(m_buf.at[layer], g_buf.at[layer], rate, back, sums_ref, low)
+        sums_ref[low + 2 * dims : low + 2 * dims + 8, :] = rest[...]
+
     land[:, mine] = z_ref[rows(me), :]
     for block, whole in zip(blocks, gathered):
         whole[me] = block[...]
@@ -1648,27 +1683,38 @@
     n, scale = normalise(x_own[...].astype(F32))
     g = land[...].astype(F32) - scale * (means[:, 0:1] + n * means[:, 1:2])
     out_ref[...] = g.astype(BF16)
+    for layer in range(1, layers):
+        sums_of(layer)
     passed = [
         gather_forward(whole, block_piece(whole), peers, k, zero, one)
         for whole, k, (zero, one) in zip(gathered, block_sems, begun)
     ]
+    sums_of(0)
     for whole, k, (zero, one), two in zip(gathered, block_sems, begun, passed):
         gather_finish(whole, block_piece(whole), peers, k, zero, one, two)
     for copy in copies:
         copy.wait_send()
 
 
-def final_exchange(z, stats, x, blocks, sections, ident):
+def final_exchange(z, stats, x, blocks, averages, sections, ident):
+    layers = len(averages)
+    dims, _, own = averages[0][2].shape
+    held_dims = (layers,) + averages[0][0].shape
     count, own = z.shape
     width = x.shape[1]
     quarter = count // 4
     number = len(blocks)
     return pl.pallas_call(
-        functools.partial(final_kernel, number),
-        out_shape=(shape((quarter, width), BF16),)
+        functools.partial(final_kernel, number, layers),
+        out_shape=(
+            shape((quarter, width), BF16),
+            shape((layers * (2 * dims + 8), own), F32),
+        )
         + tuple(shape((sections,) + a.shape, BF16) for a in blocks),
-        in_specs=[vmem(), vmem(), hbm()] + [vmem()] * number,
-        out_specs=(vmem(),) * (1 + number),
+        in_specs=[vmem(), vmem(), hbm()]
+        + [vmem()] * number
+        + [hbm(), hbm(), vmem(), vmem(), vmem()] * layers,
+        out_specs=(vmem(),) * (2 + number),
         scratch_shapes=[
             pltpu.VMEM((quarter, width), BF16),
             pltpu.VMEM((quarter, width), BF16),
@@ -1678,10 +1724,15 @@
             pltpu.SemaphoreType.DMA,
         ]
         + copy_sems(5)
+        + [
+            pltpu.VMEM(held_dims, F32),
+            pltpu.VMEM(held_dims, F32),
+            pltpu.SemaphoreType.DMA((2 * layers,)),
+        ]
         + copy_sems(6) * number,
         cost_estimate=lasting(10 + 20 * number),
         compiler_params=comm_params(ident),
-    )(z, stats, x, *blocks)
+    )(z, stats, x, *blocks, *[a for one in averages for a in one])
 
 
 def sums_kernel(shards, holders, sums_ref, block_ref, channels_ref, whole_ref, *refs):
@@ -1951,8 +2002,18 @@
 def pick(ref, index, low, size, shards, sections):
     step = size // (shards * sections)
     parts = []
+    section = lax.axis_index("section")
     for shard in range(shards):
         start = low + shard * sections * step
+        if 2 * step == LANES and start % LANES == 0:
+            pair = pl.ds(pl.multiple_of(start + section // 2 * LANES, LANES), LANES)
+            both = ref[index + (pair,)]
+            parts.append(jnp.where(section % 2 == 0, both[:, :step], both[:, step:]))
+            continue
+        if step == LANES and start % LANES == 0:
+            one = pl.ds(pl.multiple_of(start + section * LANES, LANES), LANES)
+            parts.append(ref[index + (one,)])
+            continue
         parts.append(
             chosen([ref[index + (slice(start + k * step, start + (k + 1) * step),)] for k in range(sections)])
         )
@@ -2319,7 +2380,7 @@
     given = cotangent[0]
     feed_grads = [None] * layers
     attention_grads = [None] * layers
-    channel_sums = [None] * layers
+    averages = [None] * layers
     for layer in reversed(range(layers)):
         attention_w, feed_w = weights[layer]
         k, p = kept[layer], small[layer]
@@ -2342,7 +2403,7 @@
             () if layer else (attention_grads[1],),
         )
         attention_grads[layer] = scattered(attention_grad)
-        z, zstats, channel_sums[layer], *attention_one = average_backward(
+        z, zstats, norm_sums, m_buf, g_buf, back, *attention_one = average_backward(
             lengths,
             gmixed,
             gnormed,
@@ -2355,15 +2416,16 @@
             None if layer else attention_grads[1],
             None if layer else next(idents),
         )
+        averages[layer] = (m_buf, g_buf, p.rate, back, norm_sums)
         if layer:
             given = (z, zstats, k.x)
 
     (attention_one,) = attention_one
-    input_grad, feed_one, feed_zero = final_exchange(
-        z, zstats, x0, [feed_grads[1], feed_grads[0]], sections, next(idents)
+    input_grad, channel_sums, feed_one, feed_zero = final_exchange(
+        z, zstats, x0, [feed_grads[1], feed_grads[0]], averages, sections, next(idents)
     )
     channels, attention_zero = gather_sums(
-        jnp.concatenate(channel_sums, axis=0),
+        channel_sums,
         attention_grads[0],
         sections,
         shards,

time: 591 us -> 582 us (0.985)
  Pallas kernels: 547 us -> 540 us
  transfers between devices with their start and end apart: 8 -> 8, of which waited for: 0 -> 0; matrix products, arithmetic and copies ran while one was open for 0% -> 0% of each run, Pallas kernels for 75% -> 76%
where the time goes in v5:
time: 582 us; the launch traced here: 577 us
  Pallas kernels  540 us (93%)
  blocking collectives  18.6 us (3%)
  between operations  15.6 us (3%)
    pallas_call x9, Pallas kernels, transfer(): pl.pallas_call(kernel, out_shape=tuple((o for o, _ in outs.values())), in...  391 us
    pallas_call x1, Pallas kernels, final_exchange(): pl.pallas_call(functools.partial(final_kernel, number, layers), out_shape...  43.4 us
    pallas_call x1, Pallas kernels, gather_sums(): pl.pallas_call(functools.partial(sums_kernel, shards, holders), out_shape...  29.5 us
    pallas_call x2, Pallas kernels, average_forward(): pl.pallas_call(average_forward_kernel, out_shape=(shape((count, width), B...  23.8 us
    pallas_call x1, Pallas kernels, gather_columns(): pl.pallas_call(functools.partial(gather_kernel, len(after)), out_shape=sh...  23.8 us
    all_gather x1, blocking collectives, body(): lax.all_gather(packed, 'dp', axis=0)  18.6 us
    pallas_call x2, Pallas kernels, assemble(): pl.pallas_call(functools.partial(assemble_kernel, work, shards, layers, l...  13.4 us
    pallas_call x4, Pallas kernels, pack(): pl.pallas_call(kernel, grid=(1,), out_shape=shape((rows, columns), BF16),...  12.4 us
  transfers between devices with their start and end apart: 8, of which 0 were waited for; matrix products, arithmetic and copies ran while one was open for 0% of the time, Pallas kernels for 76%

profile of v5, /device:TPU:0, one launch (start us, length us, event | category | flops | bytes accessed | tf_op | source)
XLA Modules:
  0.0 577.2 jit_solution(5491614972420153255)
XLA Ops:
  7.3 0.0 all-gather.7.cloned.1.call-start
  7.4 3.6 shard_map.373
  11.0 0.0 all-gather.7.cloned.1.call-update
  11.1 0.0 all-gather.13.cloned.1.call-start
  11.8 0.1 reshape.57
  12.0 0.1 concatenate.3
  12.1 18.6 %all-gather.1.everyone_ref = f32[8,2,8256]{2,1,0:T(2,128)} all-gather(f32[1,2,8256]{2,1,0:T(2,128)S(1)} %bitcast.17), channel_id=2, replica_groups=mesh['section'=4,'dp'=8] {'dp'}, dimensions={0}, use_global_device_ids=true | all-gather | bytes 594432 | tf_op jit(solution)/shard_map/all_gather | solution.py:2311
  30.7 2.4 shard_map.374
  33.1 11.9 %shard_map.375 = (bf16[1024,1024]{1,0:T(8,128)(2,1)}, bf16[1024,256]{1,0:T(8,128)(2,1)}, bf16[1024,256]{1,0:T(8,128)(2,1)}, f32[1024,256]{1,0:T(8,128)}, f32[1024,128]{1,0:T(8,128)}) custom-call(s32[1]{0:T(128)S(6)} %copy.52.length_ref.refs_0_.refs_1_, bf16[1024,1024]{1,0:T(8,128)(2,1)} %bitcast.23, f32[1,1024]{1,0:T(1,128)} %get-tuple-element.134.gain_ref, ...), custom_call_target="tpu_custom_call" | custom-call | flops 12999999488 | bytes 39000000 | tf_op jit(solution)/shard_map/pallas_call | solution.py:208
  45.1 2.6 shard_map.376.refs_0_
  47.6 0.0 all-gather.13.cloned.1.call-update
  47.7 0.0 all-gather.11.cloned.1.call-start
  47.7 23.8 %shard_map.377.refs_3_.refs_11_ = bf16[1024,1024]{1,0:T(8,128)(2,1)} custom-call(bf16[128,2048]{1,0:T(8,128)(2,1)} %shard_map.376.refs_0_, bf16[1024,256]{1,0:T(8,128)(2,1)} %get-tuple-element.140.refs_0_.refs_1_), custom_call_target="tpu_custom_call" | custom-call | flops 20000000000 | bytes 60000000 | tf_op jit(solution)/shard_map/pallas_call | solution.py:1126
  71.6 0.0 all-gather.7.cloned.1.call-done.refs_1_.refs_2_
  71.6 44.7 %shard_map.378 = (bf16[1024,1024]{1,0:T(8,128)(2,1)}, bf16[1024,256]{1,0:T(8,128)(2,1)}, bf16[1024,256]{1,0:T(8,128)(2,1)}, bf16[1024,128]{1,0:T(8,128)(2,1)}, b...) custom-call(s32[1]{0:T(128)S(6)} %copy.52.length_ref.refs_0_.refs_1_, ...), custom_call_target="tpu_custom_call" | custom-call | flops 54000001024 | bytes 162000000 | tf_op jit(solution)/shard_map/pallas_call | solution.py:773
  116.3 3.6 shard_map.380
  119.9 0.0 all-gather.11.cloned.1.call-update
  120.0 0.0 all-gather.9.cloned.1.call-start
  120.0 2.5 shard_map.379
  122.5 0.0 all-gather.9.cloned.1.call-update
  122.6 0.2 reduce-scatter.7.cloned.1.call-start
  122.8 0.0 all-gather.13.cloned.1.call-done.refs_1_
  122.8 42.3 %shard_map.381 = (bf16[1024,1024]{1,0:T(8,128)(2,1)}, bf16[1024,1024]{1,0:T(8,128)(2,1)}, bf16[1024,1024]{1,0:T(8,128)(2,1)}, bf16[1024,1024]{1,0:T(8,128)(2,1)}, f32[1024,128]{1,0:T(8,128)}) custom-call(bf16[1024,1024]{1,0:T(8,128)(2,1)} %get-tuple-element.145.refs_0_, bf16[1024,2048]{1,0:T(8,128)(2,1)} %all-gather.13.cloned.1.call-done.refs_1_, ...), custom_call_target="tpu_custom_call" | custom-call | flops 40000000000 | bytes 120000000 | tf_op jit(solution)/shard_map/pallas_call | solution.py:773
  165.1 11.9 %shard_map.382 = (bf16[1024,1024]{1,0:T(8,128)(2,1)}, bf16[1024,256]{1,0:T(8,128)(2,1)}, bf16[1024,256]{1,0:T(8,128)(2,1)}, f32[1024,256]{1,0:T(8,128)}, f32[1024,128]{1,0:T(8,128)}) custom-call(s32[1]{0:T(128)S(6)} %copy.52.length_ref.refs_0_.refs_1_, bf16[1024,1024]{1,0:T(8,128)(2,1)} %get-tuple-element.150.x_ref.refs_4_.refs_8_.refs_3_, ...), custom_call_target="tpu_custom_call" | custom-call | flops 12999999488 | bytes 39000000 | tf_op jit(solution)/shard_map/pallas_call | solution.py:208
  177.1 57.2 %shard_map.383 = (bf16[1024,1024]{1,0:T(8,128)(2,1)}, bf16[1024,256]{1,0:T(8,128)(2,1)}, bf16[1024,1024]{1,0:T(8,128)(2,1)}, bf16[1024,256]{1,0:T(8,128)(2,1)}, ...) custom-call(s32[1]{0:T(128)S(6)} %copy.52.length_ref.refs_0_.refs_1_, ...), custom_call_target="tpu_custom_call" | custom-call | flops 54000001024 | bytes 162000000 | tf_op jit(solution)/shard_map/pallas_call | solution.py:773
  234.2 0.0 all-gather.9.cloned.1.call-done.refs_0_
  234.2 62.4 %shard_map.384 = (bf16[1024,1024]{1,0:T(8,128)(2,1)}, bf16[1024,256]{1,0:T(8,128)(2,1)}, f32[1024,256]{1,0:T(8,128)}, bf16[1024,2176]{1,0:T(8,128)(2,1)}, bf16[256,1024]{1,0:T(8,128)(2,1)}) custom-call(bf16[1024,2048]{1,0:T(8,128)(2,1)} %all-gather.9.cloned.1.call-done.refs_0_, bf16[1024,1024]{1,0:T(8,128)(2,1)} %bitcast.22, ...), custom_call_target="tpu_custom_call" | custom-call | flops 46000001024 | bytes 138000000 | tf_op jit(solution)/shard_map/pallas_call | solution.py:773
  296.7 0.0 reduce-scatter.7.cloned.1.call-update
  296.7 0.3 reduce-scatter.5.cloned.1.call-start
  297.0 44.4 %shard_map.385 = (f32[1024,256]{1,0:T(8,128)}, f32[1024,256]{1,0:T(8,128)}, bf16[1024,2304]{1,0:T(8,128)(2,1)}) custom-call(s32[1]{0:T(128)S(6)} %copy.52.length_ref.refs_0_.refs_1_, bf16[1024,2176]{1,0:T(8,128)(2,1)} %all-gather.11.cloned.1.call-done.refs_1_, bf16[1024,1024]{1,0:T(8,128)(2,1)} %get-tuple-element.170.refs_2_, ...), custom_call_target="tpu_custom_call" | custom-call | flops 40000000000 | bytes 120000000 | tf_op jit(solution)/shard_map/pallas_call | solution.py:773
  341.4 0.0 reduce-scatter.5.cloned.1.call-update
  341.4 0.0 reduce-scatter.9.cloned.1.call-start
  341.5 11.1 %shard_map.386 = (bf16[1024,256]{1,0:T(8,128)(2,1)}, f32[8,1024]{1,0:T(8,128)}, f32[8,256]{1,0:T(8,128)}, f32[2,1032,128]{2,1,0:T(8,128)}, f32[2,1032,128]{2,1,0:T(8,128)}, /*index=5*/f32[2,16,8,256]{3,2,1,0:T(8,128)}) custom-call(s32[1]{0:T(128)S(6)} %copy.52.length_ref.refs_0_.refs_1_, f32[1024,256]{1,0:T(8,128)} %get-tuple-element.181.refs_1_, ...), custom_call_target="tpu_custom_call" | custom-call | flops 16999999488 | bytes 51000000 | tf_op jit(solution)/shard_map/pallas_call | solution.py:773
  352.5 0.0 reduce-scatter.7.cloned.1.call-done.refs_0_
  352.6 66.2 %shard_map.387 = (bf16[1024,1024]{1,0:T(8,128)(2,1)}, bf16[1024,256]{1,0:T(8,128)(2,1)}, f32[1024,256]{1,0:T(8,128)}, bf16[1024,2176]{1,0:T(8,128)(2,1)}) custom-call(bf16[128,2176]{1,0:T(8,128)(2,1)} %reduce-scatter.7.cloned.1.call-done.refs_0_, bf16[1024,2048]{1,0:T(8,128)(2,1)} %all-gather.13.cloned.1.call-done.refs_1_, ...), custom_call_target="tpu_custom_call" | custom-call | flops 46000001024 | bytes 138000000 | tf_op jit(solution)/shard_map/pallas_call | solution.py:773
  418.8 0.0 reduce-scatter.9.cloned.1.call-update
  418.8 0.3 reduce-scatter.11.cloned.1.call-start
  419.1 0.0 reduce-scatter.5.cloned.1.call-done.refs_0_.refs_11_
  419.2 39.6 %shard_map.388 = (f32[1024,256]{1,0:T(8,128)}, f32[1024,256]{1,0:T(8,128)}, bf16[1024,2304]{1,0:T(8,128)(2,1)}) custom-call(bf16[128,2304]{1,0:T(8,128)(2,1)} %reduce-scatter.5.cloned.1.call-done.refs_0_.refs_11_, s32[1]{0:T(128)S(6)} %copy.52.length_ref.refs_0_.refs_1_, bf16[1024,2176]{1,0:T(8,128)(2,1)} %all-gather.7.cloned.1.call-done.refs_1_.refs_2_, ...), custom_call_target="tpu_custom_call" | custom-call | flops 40000000000 | bytes 120000000 | tf_op jit(solution)/shard_map/pallas_call | solution.py:773
  458.7 0.0 reduce-scatter.11.cloned.1.call-update
  458.8 23.2 %shard_map.389 = (bf16[1024,256]{1,0:T(8,128)(2,1)}, f32[8,1024]{1,0:T(8,128)}, f32[8,256]{1,0:T(8,128)}, f32[2,1032,128]{2,1,0:T(8,128)}, f32[2,1032,128]{2,1,0...) custom-call(s32[1]{0:T(128)S(6)} %copy.52.length_ref.refs_0_.refs_1_, ...), custom_call_target="tpu_custom_call" | custom-call | flops 16999999488 | bytes 51000000 | tf_op jit(solution)/shard_map/pallas_call | solution.py:773
  482.0 0.0 reduce-scatter.9.cloned.1.call-done.refs_1_
  482.0 43.4 %shard_map.390 = (bf16[256,1024]{1,0:T(8,128)(2,1)}, f32[80,256]{1,0:T(8,128)}, bf16[4,128,2176]{2,1,0:T(8,128)(2,1)}, bf16[4,128,2176]{2,1,0:T(8,128)(2,1)}) custom-call(bf16[1024,256]{1,0:T(8,128)(2,1)} %get-tuple-element.209.z_ref, f32[8,1024]{1,0:T(8,128)} %get-tuple-element.210.stats_ref, bf16[1024,1024]{1,0:T(8,128)(2,1)} %bitcast.26, ...), custom_call_target="tpu_custom_call" | custom-call | flops 49999998976 | bytes 150000000 | tf_op jit(solution)/shard_map/pallas_call | solution.py:1707
  525.5 6.0 %shard_map.393 = (f32[2,128,4096]{2,1,0:T(8,128)}, f32[2,512,1024]{2,1,0:T(8,128)}, f32[2,128]{1,0:T(2,128)}, f32[2,128]{1,0:T(2,128)}, f32[2,128]{1,0:T(2,128)}, /*index=5*/f32[2,512]{1,0:T(2,128)}) custom-call(bf16[4,128,2176]{2,1,0:T(8,128)(2,1)} %get-tuple-element.239.refs_0_, bf16[4,128,2176]{2,1,0:T(8,128)(2,1)} %get-tuple-element.240.refs_1_), custom_call_target="tpu_custom_call" | custom-call | flops 6000000000 | bytes 18000000 | tf_op jit(solution)/shard_map/pallas_call | solution.py:1979
  531.5 29.5 %shard_map.391 = (f32[80,256]{1,0:T(8,128)}, bf16[4,128,2304]{2,1,0:T(8,128)(2,1)}) custom-call(f32[80,256]{1,0:T(8,128)} %get-tuple-element.221.sums_ref, bf16[128,2304]{1,0:T(8,128)(2,1)} %reduce-scatter.11.cloned.1.call-done.block_ref), custom_call_target="tpu_custom_call" | custom-call | flops 24999999488 | bytes 75000000 | tf_op jit(solution)/shard_map/pallas_call | solution.py:1814
  561.0 7.4 %shard_map.392 = (f32[2,128,2048]{2,1,0:T(8,128)}, f32[2,128,4224]{2,1,0:T(8,128)}, f32[2,256,1024]{2,1,0:T(8,128)}, f32[2,256]{1,0:T(2,128)}, f32[2,528]{1,0:T(...) custom-call(bf16[4,128,2304]{2,1,0:T(8,128)(2,1)} %get-tuple-element, ...), custom_call_target="tpu_custom_call" | custom-call | flops 6000000000 | bytes 18000000 | tf_op jit(solution)/shard_map/pallas_call | solution.py:1979
  568.4 0.8 copy.53
  569.2 0.8 copy.54
  (36 shorter events, 0.1 us)
Async XLA Ops:
  7.2 4.6 copy-start.8
  7.2 4.6 copy-start.2
  7.2 4.6 copy-start.4
  7.2 4.6 copy-start.3
  7.2 4.7 copy-start.14
  7.3 4.7 copy-start.6
  7.3 4.7 copy-start.13
  7.3 4.7 copy-start.12
  7.3 4.7 copy-start.15
  7.3 4.7 copy-start.5
  7.3 4.7 copy-start.7
  7.3 4.7 copy-start.11
  7.3 4.7 copy-start.10
  7.3 4.7 copy-start.9
  7.3 64.2 %all-gather.7.cloned.1.call-start = ((), (), s32[]{:S(2)}) async-start(), calls=%async_computation.4 | async-start | bytes 5013504 | tf_op jit(solution)/shard_map/all_gather | solution.py:2272
  11.1 111.8 %all-gather.13.cloned.1.call-start = ((), (), s32[]{:S(2)}) async-start(), calls=%async_computation.7 | async-start | bytes 4718592 | tf_op jit(solution)/shard_map/all_gather | solution.py:2272
  47.7 129.4 %all-gather.11.cloned.1.call-start = ((), (), s32[]{:S(2)}) async-start(), calls=%async_computation.6 | async-start | bytes 5013504 | tf_op jit(solution)/shard_map/all_gather | solution.py:2272
  120.0 114.3 %all-gather.9.cloned.1.call-start = ((), (), s32[]{:S(2)}) async-start(), calls=%async_computation.5 | async-start | bytes 4718592 | tf_op jit(solution)/shard_map/all_gather | solution.py:2272
  122.6 230.0 %reduce-scatter.7.cloned.1.call-start = ((), (), s32[]{:S(2)}) async-start(), calls=%async_computation.9 | async-start | bytes 5013504 | tf_op jit(solution)/shard_map/reduce_scatter | solution.py:2378
  296.7 122.4 %reduce-scatter.5.cloned.1.call-start = ((), (), s32[]{:S(2)}) async-start(), calls=%async_computation.8 | async-start | bytes 5308416 | tf_op jit(solution)/shard_map/reduce_scatter | solution.py:2378
  341.4 140.6 %reduce-scatter.9.cloned.1.call-start = ((), (), s32[]{:S(2)}) async-start(), calls=%async_computation.10 | async-start | bytes 5013504 | tf_op jit(solution)/shard_map/reduce_scatter | solution.py:2378
  418.8 112.7 %reduce-scatter.11.cloned.1.call-start = ((), (), s32[]{:S(2)}) async-start(), calls=%async_computation.11 | async-start | bytes 5308416 | tf_op jit(solution)/shard_map/reduce_scatter | solution.py:2378
  561.0 7.4 %copy-start = (bf16[256,1024]{1,0:T(8,128)(2,1)S(1)}, bf16[256,1024]{1,0:T(8,128)(2,1)}, u32[]{:S(2)}) copy-start(bf16[256,1024]{1,0:T(8,128)(2,1)} %get-tuple-element.169) | copy-start | bytes 1572868
  561.0 8.2 %copy-start.1 = (bf16[256,1024]{1,0:T(8,128)(2,1)S(1)}, bf16[256,1024]{1,0:T(8,128)(2,1)}, u32[]{:S(2)}) copy-start(bf16[256,1024]{1,0:T(8,128)(2,1)} %get-tuple-element.220) | copy-start | bytes 1572868
Sparse Core Ops, SparseCore 0:
  11.2 53.4 all-gather.6
  66.8 46.0 all-gather.12
  120.1 49.9 all-gather.10
  172.1 45.9 all-gather.8
  296.8 52.7 reduce-scatter.6
  351.8 53.1 reduce-scatter.4
  418.9 51.7 reduce-scatter.8
  473.1 53.0 reduce-scatter.10

commit v6 on v5

--- a/solution.py
+++ b/solution.py
@@ -20,7 +20,7 @@
 LOCAL = "local"
 UNROLL = 16
 SMALL = 16
-SMEM, VMEM, RAW, FETCH, BLOCKS, LATE, OWN_PART, STORE = range(8)
+SMEM, VMEM, RAW, FETCH, BLOCKS, LATE, OWN_PART, STORE, STORE_BLOCKS = range(9)
 EPS = 1e-05
 NEGATIVE = -1000000000.0
 VMEM_BYTES = 56 * 1024 * 1024
@@ -128,23 +128,10 @@
     return shifted(last, 1), shifted(slope, 1)
 
 
-def average_forward_kernel(
-    length_ref,
-    x_ref,
-    gain_ref,
-    shift_ref,
-    rate_ref,
-    coef_ref,
-    skip_ref,
-    normed_ref,
-    mixed_ref,
-    pre_ref,
-    own_ref,
-    scale_ref,
-    rows_buf,
-    m_buf,
-    y_buf,
-):
+def average_forward_work(r):
+    length_ref, x_ref, gain_ref, shift_ref, skip_ref = r.length, r.x, r.gain, r.shift, r.skip
+    rate_ref, coef_ref, rows_buf, m_buf, y_buf = r.rate, r.coef, r.rows_buf, r.m_buf, r.y_buf
+    normed_ref, mixed_ref, pre_ref, own_ref, scale_ref = r.normed, r.mixed, r.pre, r.own_n, r.scale
     length = length_ref[0]
     count, width = x_ref.shape
     own = mixed_ref.shape[1]
@@ -167,7 +154,11 @@
             m_buf[group, pl.ds(start + start // steps, STRIP), :] = masked[:, group * LANES : (group + 1) * LANES]
         return carry
 
-    lax.fori_loop(0, count // STRIP, norm_strip, 0)
+    share = ROWS // STRIP
+    for block in range(count // ROWS):
+        r.wait_block(block)
+        lax.fori_loop(block * share, (block + 1) * share, norm_strip, 0)
+    r.store("normed", "own_n", "scale")
 
     for group in range(own // LANES):
         lanes = slice(group * LANES, (group + 1) * LANES)
@@ -204,26 +195,26 @@
 def average_forward(length, x, gain, shift, rate, coef, skip):
     count, width = x.shape
     own = skip.shape[1]
-    groups = own // LANES
-    return pl.pallas_call(
-        average_forward_kernel,
-        out_shape=(
-            shape((count, width), BF16),
-            shape((count, own), BF16),
-            shape((count, own), BF16),
-            shape((count, own), F32),
-            shape((count, LANES), F32),
+    buffer = pltpu.VMEM((own // LANES, count + CHUNKS, LANES), F32)
+    small = dict(gain=gain, shift=shift, rate=rate, coef=coef, skip=skip)
+    return transfer(
+        average_forward_work,
+        dict(
+            length=(length, SMEM),
+            x=(x, BLOCKS),
+            **{name: (a, VMEM) for name, a in small.items()},
         ),
-        in_specs=[smem()] + [vmem()] * 6,
-        out_specs=(vmem(),) * 5,
-        scratch_shapes=[
-            pltpu.VMEM((STRIP, width), F32),
-            pltpu.VMEM((groups, count + CHUNKS, LANES), F32),
-            pltpu.VMEM((groups, count + CHUNKS, LANES), F32),
-        ],
-        cost_estimate=lasting(13),
-        compiler_params=params(),
-    )(length, x, gain, shift, rate, coef, skip)
+        dict(
+            normed=(shape((count, width), BF16), STORE),
+            mixed=(shape((count, own), BF16), VMEM),
+            pre=(shape((count, own), BF16), VMEM),
+            own_n=(shape((count, own), F32), STORE),
+            scale=(shape((count, LANES), F32), STORE),
+        ),
+        dict(rows_buf=pltpu.VMEM((STRIP, width), F32), m_buf=buffer, y_buf=buffer),
+        None,
+        12,
+    )
 
 
 def average_backward_work(beside, r):
@@ -237,9 +228,12 @@
     if beside:
         peers = plane()
         sems, piece = (r.send, r.recv), block_piece(r.whole)
+        r.wait("block")
         r.whole[peers[0]] = r.block[...]
         greet(peers[1], peers[2])
         begun = [gather_begin(r.whole, piece, peers, sems, half) for half in range(2)]
+
+    r.wait("own_n", "pre", "gmixed", "gvalue", "scale", "resid")
 
     def load_strip(i, carry):
         start = pl.multiple_of(i * STRIP, STRIP)
@@ -368,26 +362,27 @@
     held_dims = (own // LANES, count + CHUNKS, LANES)
     sems = pltpu.SemaphoreType.DMA((6,))
     given = dict(
+        own_n=k.own_n,
+        pre=k.pre,
         gmixed=gmixed,
         gvalue=gvalue,
-        pre=k.pre,
-        own_n=k.own_n,
         scale=k.scale,
         resid=resid,
-        norm=norm,
-        rate=rate,
-        coef=coef,
-        skip=skip,
     )
+    small = dict(norm=norm, rate=rate, coef=coef, skip=skip)
     beside = block is not None
     outs, held = {}, {}
     if beside:
-        given.update(block=block)
+        given = dict(block=block, **given)
         outs.update(whole=(shape((4,) + block.shape, BF16), VMEM))
         held.update(send=sems, recv=sems)
     return transfer(
         functools.partial(average_backward_work, beside),
-        dict(length=(length, SMEM), **{name: (a, VMEM) for name, a in given.items()}),
+        dict(
+            length=(length, SMEM),
+            **{name: (a, FETCH) for name, a in given.items()},
+            **{name: (a, VMEM) for name, a in small.items()},
+        ),
         dict(
             z=(shape((count, own), BF16), VMEM),
             stats=(shape((CHUNKS, count), F32), VMEM),
@@ -709,7 +704,7 @@
 
 def transfer(work, ins, outs, scratch, ident, microseconds, after=(), first=None, rows=ROWS):
     order = [n for kind in (FETCH, BLOCKS, LATE, OWN_PART) for n in ins if ins[n][1] == kind]
-    stored = [n for n, (_, how) in outs.items() if how == STORE]
+    stored = [n for n, (_, how) in outs.items() if how in (STORE, STORE_BLOCKS)]
     buffers, places, low = {}, {}, 0
     for name in order + stored:
         if name in stored:
@@ -719,7 +714,8 @@
             columns = array.shape[1] // (4 if how == OWN_PART else 1)
             buffers[name] = pltpu.VMEM((array.shape[0], columns), array.dtype)
         places[name] = low
-        low += ins[name][0].shape[0] // rows if name in ins and ins[name][1] == BLOCKS else 1
+        array, how = ins[name] if name in ins else outs[name]
+        low += array.shape[0] // rows if how in (BLOCKS, STORE_BLOCKS) else 1
     by_blocks = [n for n in order if ins[n][1] == BLOCKS]
 
     def kernel(*refs):
@@ -743,6 +739,11 @@
         def block_copy(name, block):
             here = rows_of(block, rows)
             source, target = given[name].at[here, :], held[name].at[here, :]
+            return pltpu.make_async_copy(source, target, local.at[places[name] + block])
+
+        def store_block(name, block):
+            here = rows_of(block, rows)
+            source, target = held[name].at[here, :], given[name].at[here, :]
             return pltpu.make_async_copy(source, target, local.at[places[name] + block])
 
         def start(*kinds):
@@ -765,9 +766,14 @@
         r.wait = lambda *which: [copy(n).wait() for n in which]
         r.store = lambda *which: [copy(n).start() for n in which]
         r.wait_block = wait_block
+        r.store_block = lambda name, block: store_block(name, block).start()
         work(r)
         for name in stored:
-            copy(name).wait()
+            if outs[name][1] == STORE:
+                copy(name).wait()
+                continue
+            for block in range(outs[name][0].shape[0] // rows):
+                store_block(name, block).wait()
 
     spec = {SMEM: smem, VMEM: vmem}
     return pl.pallas_call(
@@ -869,11 +875,11 @@
     return pltpu.SemaphoreType.DMA((6 * (count // ROWS),))
 
 
-def block_gather(out, peers, own, sems):
+def block_gather(out, peers, own, sems, rows=ROWS):
     me, across, along, far = peers
 
     def copy(block, owner, half, index, other):
-        place = out.at[owned(block, owner, half, own, ROWS)]
+        place = out.at[owned(block, owner, half, own, rows)]
         return link(place, place, sems, block * 6 + index, other)
 
     def own_copy(block, half, way):
@@ -906,7 +912,7 @@
     return types.SimpleNamespace(begin=begin, forward=forward, arrive=arrive, sent=sent)
 
 
-def pipeline(count, compute, sums, finish, gather, extra=None, between=None, before=None, rows=ROWS):
+def pipeline(count, compute, sums, finish, gather, extra=None, between=None, before=None, rows=ROWS, arrived=None):
     blocks = count // rows
     if before:
         before.begin(0)
@@ -965,6 +971,8 @@
             one.end(i)
         if gather:
             gather.arrive(i)
+            if arrived:
+                arrived(i)
             gather.sent(i)
         if before:
             before.sent(i)
@@ -1057,7 +1065,16 @@
                     r.store("mixed")
                 r.store("update", "shared", "reset", "value", "att", "gated", "probs")
 
-        pipeline(count, compute, (total,), finish, gather, extra, before=mixing)
+        pipeline(
+            count,
+            compute,
+            (total,),
+            finish,
+            gather,
+            extra,
+            before=mixing,
+            arrived=lambda block: r.store_block("out", block),
+        )
 
     rows = lambda columns: (shape((count, columns), BF16), STORE)
     return transfer(
@@ -1073,7 +1090,7 @@
             offset=(offset, VMEM),
         ),
         dict(
-            out=(shape((count, width), BF16), VMEM),
+            out=(shape((count, width), BF16), STORE_BLOCKS),
             hidden=(shape((count, own), BF16), VMEM),
             **({} if apart else dict(mixed=rows(width))),
             update=rows(own),
@@ -1164,7 +1181,15 @@
             def _():
                 r.store("pre", "n", "normed", "scale")
 
-        pipeline(count, compute, (total,), finish, gather, extra)
+        pipeline(
+            count,
+            compute,
+            (total,),
+            finish,
+            gather,
+            extra,
+            arrived=lambda block: r.store_block("out", block),
+        )
 
     rows = lambda columns, kind=BF16: (shape((count, columns), kind), STORE)
     return transfer(
@@ -1178,7 +1203,7 @@
             own_out=(own_out, VMEM),
         ),
         dict(
-            out=(shape((count, width), BF16), VMEM),
+            out=(shape((count, width), BF16), STORE_BLOCKS),
             pre=rows(hidden),
             n=rows(width),
             normed=rows(width),
@@ -1202,7 +1227,8 @@
     own = width // 4
     hidden = p.feed_in.shape[1]
     norms, gain = p.own, p.feed_gain
-    blocks = count // ROWS
+    rows = ROWS
+    blocks = count // rows
 
     def work(r):
         peers = plane()
@@ -1213,11 +1239,11 @@
         greet(across, along)
         before = None
         if corrected:
-            before = block_gather(r.z, peers, own, (r.z_send, r.z_recv))
+            before = block_gather(r.z, peers, own, (r.z_send, r.z_recv), rows)
         r.sums[...] = jnp.zeros_like(r.sums)
         r.bias[...] = jnp.zeros_like(r.bias)
-        total = block_sum(r, "sum", r.part, peers, own)
-        gather = block_gather(r.out, peers, own, (r.gather_send, r.gather_recv))
+        total = block_sum(r, "sum", r.part, peers, own, rows=rows)
+        gather = block_gather(r.out, peers, own, (r.gather_send, r.gather_recv), rows)
 
         def quarter(block, owner, half):
             size = count // 4
@@ -1245,23 +1271,32 @@
                 strips(count // 4, strip)
 
         def stats_copy(block, step):
-            lanes = rows_of(block)
+            lanes = rows_of(block, rows)
             source = (r.stats, r.stats_stage)[step].at[:, lanes]
             sems = (r.stats_send, r.stats_recv)
             other = (across, along)[step]
             return link(source, r.stats_got.at[step, :, lanes], sems, 2 * block + step, other)
 
+        def mean_copy(step):
+            source = (r.z_stats, r.means_stage)[step]
+            other = (across, along)[step]
+            return link(source, r.means_got.at[step], (r.means_send, r.means_recv), step, other)
+
+        if corrected:
+            mean_copy(0).start()
+
         def compute(block):
-            here = rows_of(block)
+            here = rows_of(block, rows)
 
             @pl.when(block == 0)
             def _():
                 r.wait("weights")
                 if corrected:
-                    sems = (r.means_send, r.means_recv)
-                    r.means[...] = stats_total(
-                        r.z_stats, r.means_got, r.means_stage, peers, sems, 0
-                    )
+                    mean_copy(0).wait_recv()
+                    r.means_stage[...] = r.z_stats[...] + r.means_got[0]
+                    mean_copy(1).start()
+                    mean_copy(1).wait_recv()
+                    r.means[...] = r.means_stage[...] + r.means_got[1]
 
             r.wait_block(block)
             if corrected:
@@ -1271,10 +1306,10 @@
                 g = z - xscale * (means[:, 0:1] + xn * means[:, 1:2])
                 r.g[here, :] = g.astype(BF16)
             if both_ways:
-                x_rows, *made = views((r.middle, r.made, r.pre, r.n, r.normed, r.scale), block)
+                x_rows, *made = views((r.middle, r.made, r.pre, r.n, r.normed, r.scale), block, rows)
                 feed_forward_kernel(x_rows, r.gain, r.shift, r.weights, r.in_bias, *made)
-            g_rows, pre_rows, n_rows = views((r.g, r.pre, r.n), block)
-            part, gpre, act = views((r.part, r.gpre, r.act), block)
+            g_rows, pre_rows, n_rows = views((r.g, r.pre, r.n), block, rows)
+            part, gpre, act = views((r.part, r.gpre, r.act), block, rows)
             feed_backward_block(
                 g_rows,
                 pre_rows,
@@ -1292,7 +1327,7 @@
             stats_copy(block, 0).start()
 
         def finish(block):
-            here = rows_of(block)
+            here = rows_of(block, rows)
             stats_copy(block, 1).wait_recv()
             every = r.stats_stage[:, here] + r.stats_got[1, :, here]
             r.columns[here, :] = every.T * (1.0 / width)
@@ -1311,7 +1346,7 @@
                 r.resid[here, :] = g * (1.0 - u)
                 r.out[here, mine] = (g * u * (s * (1.0 + pre * (1.0 - s)))).astype(BF16)
 
-            finish_strips(total, block, strip)
+            finish_strips(total, block, strip, rows)
 
         def small_grads():
             r.grad[:, hidden + width :] = jnp.zeros((width, LANES), BF16)
@@ -1333,7 +1368,7 @@
         def extra(i):
             @pl.when((i >= 1) & (i <= blocks))
             def _():
-                here = rows_of(i - 1)
+                here = rows_of(i - 1, rows)
                 stats_copy(i - 1, 0).wait_recv()
                 r.stats_stage[:, here] = r.stats[:, here] + r.stats_got[0, :, here]
                 stats_copy(i - 1, 1).start()
@@ -1371,7 +1406,18 @@
                 grad_tiles(r.act, r.g, out_grad, 0, hidden // TILE)
                 r.store("grad")
 
-        pipeline(count, compute, (total,), finish, gather, extra, between, before)
+        pipeline(
+            count,
+            compute,
+            (total,),
+            finish,
+            gather,
+            extra,
+            between,
+            before,
+            rows,
+            arrived=lambda block: r.store_block("out", block),
+        )
 
         def close(i, carry):
             stats_copy(i, 0).wait_send()
@@ -1379,6 +1425,9 @@
             return carry
 
         lax.fori_loop(0, blocks, close, 0)
+        if corrected:
+            mean_copy(0).wait_send()
+            mean_copy(1).wait_send()
 
     if corrected:
         z_own, z_stats, x_full = given
@@ -1408,14 +1457,14 @@
             out_bias=(p.feed_out, VMEM),
         )
         extra_outs.update(block_out=(shape((count // 4, width), BF16), VMEM))
-        rows = pltpu.VMEM((count, width), BF16)
+        buffer = pltpu.VMEM((count, width), BF16)
         slot = pltpu.VMEM((2, count // 4, width // 2), BF16)
         ends = pltpu.SemaphoreType.DMA((6,))
         extra_scratch.update(
-            made=rows,
+            made=buffer,
             pre=pltpu.VMEM((count, hidden), BF16),
-            n=rows,
-            normed=rows,
+            n=buffer,
+            normed=buffer,
             scale=pltpu.VMEM((count, LANES), F32),
             last_early=slot,
             last_direct=slot,
@@ -1445,7 +1494,7 @@
             norms=(norms, VMEM),
         ),
         dict(
-            out=(shape((count, width), BF16), VMEM),
+            out=(shape((count, width), BF16), STORE_BLOCKS),
             gupdate=(shape((count, own), BF16), STORE),
             resid=(shape((count, own), F32), STORE),
             grad=(shape((width, hidden + width + LANES), BF16), STORE),
@@ -1464,13 +1513,14 @@
             stats_send=sems,
             stats_recv=sems,
             **extra_scratch,
-            **sum_scratch("sum", count, own),
+            **sum_scratch("sum", count, own, rows),
             gather_send=gather_sems(count),
             gather_recv=gather_sems(count),
         ),
         ident,
         46,
         after,
+        rows=rows,
     )
 
 

time: 582 us -> 579 us (level)
    pallas_call x2 -> x0, Pallas kernels: 23.8 us -> none  [average_forward(): pl.pallas_call(average_forward_kernel, out_shape=(shape((count, width), B...]
    pallas_call x9 -> x11, Pallas kernels: 391 us -> 408 us  [transfer(): pl.pallas_call(kernel, out_shape=tuple((o for o, _ in outs.values())), in...]
  transfers between devices with their start and end apart: 8 -> 8, of which waited for: 0 -> 0; matrix products, arithmetic and copies ran while one was open for 0% -> 0% of each run, Pallas kernels for 76% -> 75%
where the time goes in v6:
time: 579 us; the launch traced here: 574 us
  Pallas kernels  537 us (93%)
  blocking collectives  18.6 us (3%)
  between operations  15.7 us (3%)
    pallas_call x11, Pallas kernels, transfer(): pl.pallas_call(kernel, out_shape=tuple((o for o, _ in outs.values())), in...  408 us
    pallas_call x1, Pallas kernels, final_exchange(): pl.pallas_call(functools.partial(final_kernel, number, layers), out_shape...  46.8 us
    pallas_call x1, Pallas kernels, gather_sums(): pl.pallas_call(functools.partial(sums_kernel, shards, holders), out_shape...  29.7 us
    pallas_call x1, Pallas kernels, gather_columns(): pl.pallas_call(functools.partial(gather_kernel, len(after)), out_shape=sh...  23.9 us
    all_gather x1, blocking collectives, body(): lax.all_gather(packed, 'dp', axis=0)  18.6 us
    pallas_call x2, Pallas kernels, assemble(): pl.pallas_call(functools.partial(assemble_kernel, work, shards, layers, l...  13.4 us
    pallas_call x4, Pallas kernels, pack(): pl.pallas_call(kernel, grid=(1,), out_shape=shape((rows, columns), BF16),...  12.3 us
  transfers between devices with their start and end apart: 8, of which 0 were waited for; matrix products, arithmetic and copies ran while one was open for 0% of the time, Pallas kernels for 75%

profile of v6, /device:TPU:0, one launch (start us, length us, event | category | flops | bytes accessed | tf_op | source)
XLA Modules:
  0.0 574.0 jit_solution(10677821214275462722)
XLA Ops:
  7.3 0.0 all-gather.7.cloned.1.call-start
  7.4 3.6 shard_map.373
  11.0 0.0 all-gather.7.cloned.1.call-update
  11.1 0.0 all-gather.13.cloned.1.call-start
  11.8 0.1 reshape.57
  12.0 0.1 concatenate.3
  12.1 18.6 %all-gather.1.everyone_ref = f32[8,2,8256]{2,1,0:T(2,128)} all-gather(f32[1,2,8256]{2,1,0:T(2,128)S(1)} %bitcast.17), channel_id=2, replica_groups=mesh['section'=4,'dp'=8] {'dp'}, dimensions={0}, use_global_device_ids=true | all-gather | bytes 594432 | tf_op jit(solution)/shard_map/all_gather | solution.py:2361
  30.7 2.4 shard_map.374
  33.1 11.1 %shard_map.375 = (bf16[1024,1024]{1,0:T(8,128)(2,1)}, bf16[1024,256]{1,0:T(8,128)(2,1)}, bf16[1024,256]{1,0:T(8,128)(2,1)}, f32[1024,256]{1,0:T(8,128)}, f32[1024,128]{1,0:T(8,128)}) custom-call(s32[1]{0:T(128)S(6)} %copy.52.refs_0_.refs_1_, bf16[1024,1024]{1,0:T(8,128)(2,1)} %bitcast.23, f32[1,1024]{1,0:T(1,128)} %get-tuple-element.134.refs_2_, ...), custom_call_target="tpu_custom_call" | custom-call | flops 12000000000 | bytes 36000000 | tf_op jit(solution)/shard_map/pallas_call | solution.py:779
  44.3 2.5 shard_map.376.refs_0_
  46.8 0.0 all-gather.13.cloned.1.call-update
  46.8 0.0 all-gather.11.cloned.1.call-start
  46.9 23.9 %shard_map.377.refs_3_.refs_11_ = bf16[1024,1024]{1,0:T(8,128)(2,1)} custom-call(bf16[128,2048]{1,0:T(8,128)(2,1)} %shard_map.376.refs_0_, bf16[1024,256]{1,0:T(8,128)(2,1)} %get-tuple-element.140.refs_0_.refs_1_), custom_call_target="tpu_custom_call" | custom-call | flops 20000000000 | bytes 60000000 | tf_op jit(solution)/shard_map/pallas_call | solution.py:1143
  70.8 0.0 all-gather.7.cloned.1.call-done.refs_1_.refs_2_
  70.8 44.8 %shard_map.378 = (bf16[1024,1024]{1,0:T(8,128)(2,1)}, bf16[1024,256]{1,0:T(8,128)(2,1)}, bf16[1024,256]{1,0:T(8,128)(2,1)}, bf16[1024,128]{1,0:T(8,128)(2,1)}, b...) custom-call(s32[1]{0:T(128)S(6)} %copy.52.refs_0_.refs_1_, ...), custom_call_target="tpu_custom_call" | custom-call | flops 54000001024 | bytes 162000000 | tf_op jit(solution)/shard_map/pallas_call | solution.py:779
  115.6 3.6 shard_map.380
  119.2 0.0 all-gather.11.cloned.1.call-update
  119.3 0.0 all-gather.9.cloned.1.call-start
  119.3 2.5 shard_map.379
  121.9 0.2 reduce-scatter.7.cloned.1.call-start
  122.1 0.0 all-gather.13.cloned.1.call-done.refs_1_
  122.1 41.8 %shard_map.381 = (bf16[1024,1024]{1,0:T(8,128)(2,1)}, bf16[1024,1024]{1,0:T(8,128)(2,1)}, bf16[1024,1024]{1,0:T(8,128)(2,1)}, bf16[1024,1024]{1,0:T(8,128)(2,1)}, f32[1024,128]{1,0:T(8,128)}) custom-call(bf16[1024,1024]{1,0:T(8,128)(2,1)} %get-tuple-element.145.refs_0_, bf16[1024,2048]{1,0:T(8,128)(2,1)} %all-gather.13.cloned.1.call-done.refs_1_, ...), custom_call_target="tpu_custom_call" | custom-call | flops 40000000000 | bytes 120000000 | tf_op jit(solution)/shard_map/pallas_call | solution.py:779
  163.9 11.1 %shard_map.382 = (bf16[1024,1024]{1,0:T(8,128)(2,1)}, bf16[1024,256]{1,0:T(8,128)(2,1)}, bf16[1024,256]{1,0:T(8,128)(2,1)}, f32[1024,256]{1,0:T(8,128)}, f32[1024,128]{1,0:T(8,128)}) custom-call(s32[1]{0:T(128)S(6)} %copy.52.refs_0_.refs_1_, bf16[1024,1024]{1,0:T(8,128)(2,1)} %get-tuple-element.150.refs_1_.refs_4_.refs_8_.refs_3_, ...), custom_call_target="tpu_custom_call" | custom-call | flops 12000000000 | bytes 36000000 | tf_op jit(solution)/shard_map/pallas_call | solution.py:779
  175.0 0.0 all-gather.11.cloned.1.call-done.refs_1_
  175.0 57.1 %shard_map.383 = (bf16[1024,1024]{1,0:T(8,128)(2,1)}, bf16[1024,256]{1,0:T(8,128)(2,1)}, bf16[1024,1024]{1,0:T(8,128)(2,1)}, bf16[1024,256]{1,0:T(8,128)(2,1)}, ...) custom-call(s32[1]{0:T(128)S(6)} %copy.52.refs_0_.refs_1_, ...), custom_call_target="tpu_custom_call" | custom-call | flops 54000001024 | bytes 162000000 | tf_op jit(solution)/shard_map/pallas_call | solution.py:779
  232.2 0.0 all-gather.9.cloned.1.call-done.refs_0_
  232.2 62.6 %shard_map.384 = (bf16[1024,1024]{1,0:T(8,128)(2,1)}, bf16[1024,256]{1,0:T(8,128)(2,1)}, f32[1024,256]{1,0:T(8,128)}, bf16[1024,2176]{1,0:T(8,128)(2,1)}, bf16[256,1024]{1,0:T(8,128)(2,1)}) custom-call(bf16[1024,2048]{1,0:T(8,128)(2,1)} %all-gather.9.cloned.1.call-done.refs_0_, bf16[1024,1024]{1,0:T(8,128)(2,1)} %bitcast.22, ...), custom_call_target="tpu_custom_call" | custom-call | flops 46000001024 | bytes 138000000 | tf_op jit(solution)/shard_map/pallas_call | solution.py:779
  294.8 0.0 reduce-scatter.7.cloned.1.call-update
  294.8 0.3 reduce-scatter.5.cloned.1.call-start
  295.1 44.2 %shard_map.385 = (f32[1024,256]{1,0:T(8,128)}, f32[1024,256]{1,0:T(8,128)}, bf16[1024,2304]{1,0:T(8,128)(2,1)}) custom-call(s32[1]{0:T(128)S(6)} %copy.52.refs_0_.refs_1_, bf16[1024,2176]{1,0:T(8,128)(2,1)} %all-gather.11.cloned.1.call-done.refs_1_, bf16[1024,1024]{1,0:T(8,128)(2,1)} %get-tuple-element.170.refs_2_, ...), custom_call_target="tpu_custom_call" | custom-call | flops 40000000000 | bytes 120000000 | tf_op jit(solution)/shard_map/pallas_call | solution.py:779
  339.3 0.0 reduce-scatter.5.cloned.1.call-update
  339.4 0.0 reduce-scatter.9.cloned.1.call-start
  339.4 12.0 %shard_map.386 = (bf16[1024,256]{1,0:T(8,128)(2,1)}, f32[8,1024]{1,0:T(8,128)}, f32[8,256]{1,0:T(8,128)}, f32[2,1032,128]{2,1,0:T(8,128)}, f32[2,1032,128]{2,1,0:T(8,128)}, /*index=5*/f32[2,16,8,256]{3,2,1,0:T(8,128)}) custom-call(s32[1]{0:T(128)S(6)} %copy.52.refs_0_.refs_1_, f32[1024,256]{1,0:T(8,128)} %get-tuple-element.183.refs_1_, ...), custom_call_target="tpu_custom_call" | custom-call | flops 16999999488 | bytes 51000000 | tf_op jit(solution)/shard_map/pallas_call | solution.py:779
  351.4 0.0 reduce-scatter.7.cloned.1.call-done.refs_0_
  351.4 62.1 %shard_map.387 = (bf16[1024,1024]{1,0:T(8,128)(2,1)}, bf16[1024,256]{1,0:T(8,128)(2,1)}, f32[1024,256]{1,0:T(8,128)}, bf16[1024,2176]{1,0:T(8,128)(2,1)}) custom-call(bf16[128,2176]{1,0:T(8,128)(2,1)} %reduce-scatter.7.cloned.1.call-done.refs_0_, bf16[1024,2048]{1,0:T(8,128)(2,1)} %all-gather.13.cloned.1.call-done.refs_1_, ...), custom_call_target="tpu_custom_call" | custom-call | flops 46000001024 | bytes 138000000 | tf_op jit(solution)/shard_map/pallas_call | solution.py:779
  413.6 0.0 reduce-scatter.9.cloned.1.call-update
  413.6 0.3 reduce-scatter.11.cloned.1.call-start
  413.9 0.0 reduce-scatter.5.cloned.1.call-done.refs_0_.refs_1_
  413.9 41.5 %shard_map.388 = (f32[1024,256]{1,0:T(8,128)}, f32[1024,256]{1,0:T(8,128)}, bf16[1024,2304]{1,0:T(8,128)(2,1)}) custom-call(bf16[128,2304]{1,0:T(8,128)(2,1)} %reduce-scatter.5.cloned.1.call-done.refs_0_.refs_1_, s32[1]{0:T(128)S(6)} %copy.52.refs_0_.refs_1_, bf16[1024,2176]{1,0:T(8,128)(2,1)} %all-gather.7.cloned.1.call-done.refs_1_.refs_2_, ...), custom_call_target="tpu_custom_call" | custom-call | flops 40000000000 | bytes 120000000 | tf_op jit(solution)/shard_map/pallas_call | solution.py:779
  455.5 0.0 reduce-scatter.11.cloned.1.call-update
  455.5 19.7 %shard_map.389 = (bf16[1024,256]{1,0:T(8,128)(2,1)}, f32[8,1024]{1,0:T(8,128)}, f32[8,256]{1,0:T(8,128)}, f32[2,1032,128]{2,1,0:T(8,128)}, f32[2,1032,128]{2,1,0...) custom-call(s32[1]{0:T(128)S(6)} %copy.52.refs_0_.refs_1_, ...), custom_call_target="tpu_custom_call" | custom-call | flops 16999999488 | bytes 51000000 | tf_op jit(solution)/shard_map/pallas_call | solution.py:779
  475.2 0.0 reduce-scatter.9.cloned.1.call-done.refs_1_
  475.2 46.8 %shard_map.390 = (bf16[256,1024]{1,0:T(8,128)(2,1)}, f32[80,256]{1,0:T(8,128)}, bf16[4,128,2176]{2,1,0:T(8,128)(2,1)}, bf16[4,128,2176]{2,1,0:T(8,128)(2,1)}) custom-call(bf16[1024,256]{1,0:T(8,128)(2,1)} %get-tuple-element.209.z_ref, f32[8,1024]{1,0:T(8,128)} %get-tuple-element.210.stats_ref, bf16[1024,1024]{1,0:T(8,128)(2,1)} %bitcast.26, ...), custom_call_target="tpu_custom_call" | custom-call | flops 49999998976 | bytes 150000000 | tf_op jit(solution)/shard_map/pallas_call | solution.py:1757
  522.0 6.0 %shard_map.393 = (f32[2,128,4096]{2,1,0:T(8,128)}, f32[2,512,1024]{2,1,0:T(8,128)}, f32[2,128]{1,0:T(2,128)}, f32[2,128]{1,0:T(2,128)}, f32[2,128]{1,0:T(2,128)}, /*index=5*/f32[2,512]{1,0:T(2,128)}) custom-call(bf16[4,128,2176]{2,1,0:T(8,128)(2,1)} %get-tuple-element.239.refs_0_, bf16[4,128,2176]{2,1,0:T(8,128)(2,1)} %get-tuple-element.240.refs_1_), custom_call_target="tpu_custom_call" | custom-call | flops 6000000000 | bytes 18000000 | tf_op jit(solution)/shard_map/pallas_call | solution.py:2029
  528.1 29.7 %shard_map.391 = (f32[80,256]{1,0:T(8,128)}, bf16[4,128,2304]{2,1,0:T(8,128)(2,1)}) custom-call(f32[80,256]{1,0:T(8,128)} %get-tuple-element.221.sums_ref, bf16[128,2304]{1,0:T(8,128)(2,1)} %reduce-scatter.11.cloned.1.call-done.block_ref), custom_call_target="tpu_custom_call" | custom-call | flops 24999999488 | bytes 75000000 | tf_op jit(solution)/shard_map/pallas_call | solution.py:1864
  557.8 7.4 %shard_map.392 = (f32[2,128,2048]{2,1,0:T(8,128)}, f32[2,128,4224]{2,1,0:T(8,128)}, f32[2,256,1024]{2,1,0:T(8,128)}, f32[2,256]{1,0:T(2,128)}, f32[2,528]{1,0:T(...) custom-call(bf16[4,128,2304]{2,1,0:T(8,128)(2,1)} %get-tuple-element, ...), custom_call_target="tpu_custom_call" | custom-call | flops 6000000000 | bytes 18000000 | tf_op jit(solution)/shard_map/pallas_call | solution.py:2029
  565.2 0.8 copy.53
  566.0 0.8 copy.54
  (36 shorter events, 0.1 us)
Async XLA Ops:
  7.2 4.6 copy-start.8
  7.2 4.6 copy-start.2
  7.2 4.6 copy-start.4
  7.2 4.6 copy-start.3
  7.2 4.7 copy-start.14
  7.3 4.7 copy-start.6
  7.3 4.7 copy-start.13
  7.3 4.7 copy-start.12
  7.3 4.7 copy-start.15
  7.3 4.7 copy-start.5
  7.3 4.7 copy-start.7
  7.3 4.7 copy-start.11
  7.3 4.7 copy-start.10
  7.3 4.7 copy-start.9
  7.3 63.5 %all-gather.7.cloned.1.call-start = ((), (), s32[]{:S(2)}) async-start(), calls=%async_computation.4 | async-start | bytes 5013504 | tf_op jit(solution)/shard_map/all_gather | solution.py:2322
  11.1 111.1 %all-gather.13.cloned.1.call-start = ((), (), s32[]{:S(2)}) async-start(), calls=%async_computation.7 | async-start | bytes 4718592 | tf_op jit(solution)/shard_map/all_gather | solution.py:2322
  46.8 128.2 %all-gather.11.cloned.1.call-start = ((), (), s32[]{:S(2)}) async-start(), calls=%async_computation.6 | async-start | bytes 5013504 | tf_op jit(solution)/shard_map/all_gather | solution.py:2322
  119.3 112.9 %all-gather.9.cloned.1.call-start = ((), (), s32[]{:S(2)}) async-start(), calls=%async_computation.5 | async-start | bytes 4718592 | tf_op jit(solution)/shard_map/all_gather | solution.py:2322
  121.9 229.6 %reduce-scatter.7.cloned.1.call-start = ((), (), s32[]{:S(2)}) async-start(), calls=%async_computation.9 | async-start | bytes 5013504 | tf_op jit(solution)/shard_map/reduce_scatter | solution.py:2428
  294.8 119.1 %reduce-scatter.5.cloned.1.call-start = ((), (), s32[]{:S(2)}) async-start(), calls=%async_computation.8 | async-start | bytes 5308416 | tf_op jit(solution)/shard_map/reduce_scatter | solution.py:2428
  339.4 135.8 %reduce-scatter.9.cloned.1.call-start = ((), (), s32[]{:S(2)}) async-start(), calls=%async_computation.10 | async-start | bytes 5013504 | tf_op jit(solution)/shard_map/reduce_scatter | solution.py:2428
  413.6 114.4 %reduce-scatter.11.cloned.1.call-start = ((), (), s32[]{:S(2)}) async-start(), calls=%async_computation.11 | async-start | bytes 5308416 | tf_op jit(solution)/shard_map/reduce_scatter | solution.py:2428
  557.8 7.4 %copy-start = (bf16[256,1024]{1,0:T(8,128)(2,1)S(1)}, bf16[256,1024]{1,0:T(8,128)(2,1)}, u32[]{:S(2)}) copy-start(bf16[256,1024]{1,0:T(8,128)(2,1)} %get-tuple-element.169) | copy-start | bytes 1572868
  557.8 8.2 %copy-start.1 = (bf16[256,1024]{1,0:T(8,128)(2,1)S(1)}, bf16[256,1024]{1,0:T(8,128)(2,1)}, u32[]{:S(2)}) copy-start(bf16[256,1024]{1,0:T(8,128)(2,1)} %get-tuple-element.220) | copy-start | bytes 1572868
Sparse Core Ops, SparseCore 0:
  11.2 53.4 all-gather.6
  66.8 46.0 all-gather.12
  119.4 50.0 all-gather.10
  171.5 45.8 all-gather.8
  295.0 52.7 reduce-scatter.6
  350.0 53.1 reduce-scatter.4
  413.7 53.4 reduce-scatter.8
  469.5 53.1 reduce-scatter.10
